TPU v7x, 32 devices: a whole 2x2x4 slice. The times are simulated.
32 devices in a mesh: dp: 16 (over z, y, core), tensor: 2 (over x).
Axes of the slice: x: 2, y: 2, z: 4, core: 2. Of those that a mesh axis runs over, the one named last changes fastest.
Arguments:
- tokens: bfloat16 [32768, 1536], P(('dp', 'tensor')), may hold values from -6 to 6
- norm_gains: float32 [1536], replicated, may hold values from 0.5 to 1.5
- w_query: bfloat16 [1536, 1536], P(None, 'tensor'), may hold values from -0.15625 to 0.15625
- w_key: bfloat16 [1536, 512], P(None, 'tensor'), may hold values from -0.15625 to 0.15625
- w_value: bfloat16 [1536, 512], P(None, 'tensor'), may hold values from -0.15625 to 0.15625
- w_out: bfloat16 [1536, 1536], P('tensor'), may hold values from -2.5 to 2.5
- mix_gains: float32 [1536], replicated, may hold values from 0.5 to 1.5
- w_router: bfloat16 [1536, 40], replicated, may hold values from -0.078125 to 0.078125
- w_gate: bfloat16 [40, 1536, 512], P('tensor'), may hold values from -0.15625 to 0.15625
- w_up: bfloat16 [40, 1536, 512], P('tensor'), may hold values from -0.15625 to 0.15625
- w_down: bfloat16 [40, 512, 1536], P('tensor'), may hold values from -1 to 1
- routes: int32 [32768, 8], P('dp'), may hold values from 0 to 39, all different within a row; in each aligned block of 2048 rows (0 to 2047, 2048 to 4095, ...) at most 614 rows name the same one
- starts: int32 [32, 2], P('dp'), may hold values from 0 to 768, as said below
- cotangent: bfloat16 [32768, 1536], P(('dp', 'tensor')), may hold values from -6 to 6
Outputs:
- output: bfloat16 [32768, 1536], P(('dp', 'tensor'))
- balance: float32 [40], replicated
- input_grad: float32 [32768, 1536], P(('dp', 'tensor'))
- norm_gain_grad: float32 [1536], replicated
- query_weight_grad: float32 [1536, 1536], P('dp', 'tensor')
- key_weight_grad: float32 [1536, 512], P('dp', 'tensor')
- value_weight_grad: float32 [1536, 512], P('dp', 'tensor')
- out_weight_grad: float32 [1536, 1536], P('tensor', 'dp')
- mix_gain_grad: float32 [1536], replicated
- router_grad: float32 [1536, 40], replicated
- gate_weight_grad: float32 [40, 1536, 512], P('tensor', 'dp')
- up_weight_grad: float32 [40, 1536, 512], P('tensor', 'dp')
- down_weight_grad: float32 [40, 512, 1536], P('tensor', None, 'dp')
Inputs may be any that keep to these rules, and one draw needn't show every extreme that they name: `routes`: each row names 8 different experts. In each aligned block of 2048 rows (the tokens of one index of dp) no expert is named by more than 614 rows, a bound that some block reaches. Row s holds the first positions of the 2 picture pieces of sequence s, each 256 tokens long; piece k starts between k * 512 and (k + 1) * 512 - 256.
All inputs are finite; a program needn't handle non-finite values.
Results may differ from a plain program's by a relative error of at most 0.02.
Values may be sent and summed in bfloat16 or wider, within the bound.
No kernel may reach another device: no remote copies, remote signals or barrier semaphores. Data moves between devices by JAX's collectives and lax.ppermute only.
A program may use at most 896 MiB of HBM per device.

v0:
```python
import jax
import jax.numpy as jnp
from jax import lax
from jax.sharding import PartitionSpec as P

HD = 64
PIECE = 256
CAP = 614


EPSILON = 1e-06
ALPHA = 0.01
HIGHEST = lax.Precision.HIGHEST


def normalize(values, gains):
    return values * lax.rsqrt(jnp.mean(values * values, axis=-1, keepdims=True) + EPSILON) * gains


def softmax_rows(values):
    shifted = jnp.exp(values - jnp.max(values, axis=-1, keepdims=True))
    return shifted / jnp.sum(shifted, axis=-1, keepdims=True)


def contract_rows(left, right):
    return lax.dot_general(
        left, right, (((0,), (0,)), ((), ())), preferred_element_type=jnp.float32
    )


def contract_cols(left, right):
    return lax.dot_general(
        left, right, (((1,), (1,)), ((), ())), preferred_element_type=jnp.float32
    )


def rope_tables(sequence_length, head_width):
    half_width = head_width // 2
    frequency = 10000.0 ** (-(jnp.arange(half_width, dtype=jnp.float32) * 2.0 / head_width))
    angles = jnp.arange(sequence_length, dtype=jnp.float32)[:, None] * frequency[None, :]
    return (jnp.cos(angles), jnp.sin(angles))


def rotate(values, cosine, sine_table):
    half_width = values.shape[-1] // 2
    first_half = values[..., :half_width]
    second_half = values[..., half_width:]
    cosine_rows = cosine[:, None, :]
    sine_rows = sine_table[:, None, :]
    return jnp.concatenate(
        [
            first_half * cosine_rows - second_half * sine_rows,
            second_half * cosine_rows + first_half * sine_rows,
        ],
        axis=-1,
    )


def allowed_pairs(starts_row, sequence_length, piece_length):
    position = jnp.arange(sequence_length, dtype=jnp.int32)
    labels = jnp.full((sequence_length,), -1, jnp.int32)
    for piece_index in range(starts_row.shape[0]):
        inside = (position >= starts_row[piece_index]) & (
            position < starts_row[piece_index] + piece_length
        )
        labels = jnp.where(inside, piece_index, labels)
    causal = position[None, :] <= position[:, None]
    shared = (labels[:, None] == labels[None, :]) & (labels[:, None] >= 0)
    return causal | shared


def slot_table(routes, expert_count, capacity):
    flattened = routes.reshape(-1)
    onehot = (flattened[:, None] == jnp.arange(expert_count, dtype=jnp.int32)[None, :]).astype(
        jnp.int32
    )
    placed = jnp.sum((jnp.cumsum(onehot, axis=0) - 1) * onehot, axis=1)
    entries = jnp.arange(flattened.shape[0], dtype=jnp.int32)
    return (
        jnp.full((expert_count * capacity,), flattened.shape[0], jnp.int32)
        .at[flattened * capacity + placed]
        .set(entries)
    )


def expert_forward(expert_inputs, w_gate, w_up, w_down):
    gate_proj = jnp.einsum(
        "ecd,edf->ecf", expert_inputs, w_gate, preferred_element_type=jnp.float32
    )
    up_proj = jnp.einsum("ecd,edf->ecf", expert_inputs, w_up, preferred_element_type=jnp.float32)
    activated = (gate_proj * jax.nn.sigmoid(gate_proj) * up_proj).astype(jnp.bfloat16)
    returned = jnp.einsum("ecf,efd->ecd", activated, w_down, preferred_element_type=jnp.float32)
    return (gate_proj, up_proj, activated, returned)


def scores_of(query_block, key_block, allowed, score_scale):
    raw_scores = (
        jnp.einsum("qkgd,skd->kgqs", query_block, key_block, preferred_element_type=jnp.float32)
        * score_scale
    )
    return jnp.where(allowed, raw_scores, -1e30)


def shards(
    tokens,
    norm_gains,
    w_query,
    w_key,
    w_value,
    w_out,
    mix_gains,
    w_router,
    w_gate,
    w_up,
    w_down,
    routes,
    starts,
    cotangent,
):
    share_rows = tokens.shape[0]
    model_width = tokens.shape[1]
    head_width = HD
    query_width = w_query.shape[1]
    key_width = w_key.shape[1]
    heads_here = query_width // head_width
    groups_here = key_width // head_width
    per_group = heads_here // groups_here
    experts_here = w_gate.shape[0]
    group_rows = routes.shape[0]
    choices_count = routes.shape[1]
    sequences_here = starts.shape[0]
    sequence_length = group_rows // sequences_here
    expert_count = w_router.shape[1]
    tensor_rank = lax.axis_index("tensor")
    total_tokens = group_rows * lax.axis_size("dp")
    score_scale = head_width ** (-0.5)
    inputs_share = tokens.astype(jnp.float32)
    normed_share = normalize(inputs_share, norm_gains).astype(jnp.bfloat16)
    normed = lax.all_gather(normed_share, "tensor", axis=0, tiled=True)
    joined_weights = jnp.concatenate([w_query, w_key, w_value], axis=1)
    projected = jnp.dot(normed, joined_weights, preferred_element_type=jnp.float32)
    cosine, sine_table = rope_tables(sequence_length, head_width)
    cosine_rows = jnp.tile(cosine, (sequences_here, 1))
    sine_rows = jnp.tile(sine_table, (sequences_here, 1))
    query_rows = rotate(
        projected[:, :query_width].reshape(group_rows, heads_here, head_width),
        cosine_rows,
        sine_rows,
    ).astype(jnp.bfloat16)
    key_rows = rotate(
        projected[:, query_width : query_width + key_width].reshape(
            group_rows, groups_here, head_width
        ),
        cosine_rows,
        sine_rows,
    ).astype(jnp.bfloat16)
    value_rows = (
        projected[:, query_width + key_width :]
        .astype(jnp.bfloat16)
        .reshape(group_rows, groups_here, head_width)
    )
    attended_parts = []
    logsum_parts = []
    for sequence in range(sequences_here):
        first_row = sequence * sequence_length
        query_block = query_rows[first_row : first_row + sequence_length].reshape(
            sequence_length, groups_here, per_group, head_width
        )
        key_block = key_rows[first_row : first_row + sequence_length]
        value_block = value_rows[first_row : first_row + sequence_length]
        allowed = allowed_pairs(starts[sequence], sequence_length, PIECE)
        scores = scores_of(query_block, key_block, allowed, score_scale)
        highest = jnp.max(scores, axis=-1, keepdims=True)
        shifted = jnp.exp(scores - highest)
        totals = jnp.sum(shifted, axis=-1, keepdims=True)
        weights = (shifted / totals).astype(jnp.bfloat16)
        mixed_values = jnp.einsum(
            "kgqs,skd->qkgd", weights, value_block, preferred_element_type=jnp.float32
        )
        attended_parts.append(
            mixed_values.reshape(sequence_length, query_width).astype(jnp.bfloat16)
        )
        logsum_parts.append(highest + jnp.log(totals))
    attended = jnp.concatenate(attended_parts, axis=0)
    attention_share = lax.psum_scatter(
        jnp.dot(attended, w_out, preferred_element_type=jnp.float32),
        "tensor",
        scatter_dimension=0,
        tiled=True,
    )
    middle_share = inputs_share + attention_share
    mixed_share = normalize(middle_share, mix_gains).astype(jnp.bfloat16)
    share_routes = lax.dynamic_slice_in_dim(routes, tensor_rank * share_rows, share_rows, 0)
    route_onehot = (
        share_routes[:, :, None] == jnp.arange(expert_count, dtype=jnp.int32)[None, None, :]
    ).astype(jnp.float32)
    logits = jnp.dot(mixed_share, w_router, preferred_element_type=jnp.float32)
    probabilities = softmax_rows(logits)
    chosen = jnp.sum(logits[:, None, :] * route_onehot, axis=-1)
    gate_soft = softmax_rows(chosen)
    gate_low = gate_soft.astype(jnp.bfloat16)
    counts, prob_sums = lax.psum(
        (jnp.sum(route_onehot, axis=(0, 1)), jnp.sum(probabilities, axis=0)), ("dp", "tensor")
    )
    fractions = counts / (total_tokens * choices_count)
    balance = expert_count * expert_count * fractions * prob_sums / total_tokens
    mixed_rows, gate_rows = (
        lax.all_gather(mixed_share, "tensor", axis=0, tiled=True),
        lax.all_gather(gate_low, "tensor", axis=0, tiled=True),
    )
    slots_all = slot_table(routes, expert_count, CAP)
    slots = lax.dynamic_slice_in_dim(
        slots_all, tensor_rank * experts_here * CAP, experts_here * CAP, 0
    )
    owners = slots // choices_count
    padded_rows = jnp.concatenate([mixed_rows, jnp.zeros((1, model_width), jnp.bfloat16)], axis=0)
    padded_gates = jnp.concatenate(
        [gate_rows.reshape(-1).astype(jnp.float32), jnp.zeros((1,), jnp.float32)], axis=0
    )
    slot_gates = padded_gates[slots]
    expert_inputs = padded_rows[owners].reshape(experts_here, CAP, model_width)
    gate_proj, up_proj, activated, returned = expert_forward(expert_inputs, w_gate, w_up, w_down)
    returned_flat = returned.reshape(experts_here * CAP, model_width)
    expert_partial = jax.ops.segment_sum(
        slot_gates[:, None] * returned_flat, owners, num_segments=group_rows + 1
    )[:group_rows]
    expert_share = lax.psum_scatter(
        expert_partial.astype(jnp.bfloat16), "tensor", scatter_dimension=0, tiled=True
    ).astype(jnp.float32)
    output_share = (middle_share + expert_share).astype(jnp.bfloat16)
    upstream = cotangent.astype(jnp.float32)
    upstream_rows = lax.all_gather(cotangent, "tensor", axis=0, tiled=True)
    padded_upstream = jnp.concatenate(
        [upstream_rows, jnp.zeros((1, model_width), jnp.bfloat16)], axis=0
    )
    slot_upstream = padded_upstream[owners].astype(jnp.float32)
    slot_cotangent = (
        (slot_gates[:, None] * slot_upstream)
        .astype(jnp.bfloat16)
        .reshape(experts_here, CAP, model_width)
    )
    slot_gate_grad = jnp.sum(slot_upstream * returned_flat, axis=1)
    activated_grad = jnp.einsum(
        "ecd,efd->ecf", slot_cotangent, w_down, preferred_element_type=jnp.float32
    )
    down_grad = jnp.einsum(
        "ecf,ecd->efd", activated, slot_cotangent, preferred_element_type=jnp.float32
    )
    sigmoid_gate = jax.nn.sigmoid(gate_proj)
    gate_proj_low = (
        activated_grad * up_proj * sigmoid_gate * (1.0 + gate_proj * (1.0 - sigmoid_gate))
    ).astype(jnp.bfloat16)
    up_proj_low = (activated_grad * gate_proj * sigmoid_gate).astype(jnp.bfloat16)
    inputs_grad = jnp.einsum(
        "ecf,edf->ecd", gate_proj_low, w_gate, preferred_element_type=jnp.float32
    ) + jnp.einsum("ecf,edf->ecd", up_proj_low, w_up, preferred_element_type=jnp.float32)
    gate_grad = jnp.einsum(
        "ecd,ecf->edf", expert_inputs, gate_proj_low, preferred_element_type=jnp.float32
    )
    up_grad = jnp.einsum(
        "ecd,ecf->edf", expert_inputs, up_proj_low, preferred_element_type=jnp.float32
    )
    mixed_partial = jax.ops.segment_sum(
        inputs_grad.reshape(experts_here * CAP, model_width), owners, num_segments=group_rows + 1
    )[:group_rows]
    gate_partial = jax.ops.segment_sum(
        slot_gate_grad, slots, num_segments=group_rows * choices_count + 1
    )[: group_rows * choices_count].reshape(group_rows, choices_count)
    mixed_grad_share, gates_grad_share = (
        lax.psum_scatter(mixed_partial, "tensor", scatter_dimension=0, tiled=True),
        lax.psum_scatter(gate_partial, "tensor", scatter_dimension=0, tiled=True),
    )
    gate_total, up_total = (
        lax.psum_scatter(
            gate_grad.astype(jnp.bfloat16), "dp", scatter_dimension=1, tiled=True
        ).astype(jnp.float32),
        lax.psum_scatter(
            up_grad.astype(jnp.bfloat16), "dp", scatter_dimension=1, tiled=True
        ).astype(jnp.float32),
    )
    down_total = lax.psum_scatter(
        down_grad.astype(jnp.bfloat16), "dp", scatter_dimension=2, tiled=True
    ).astype(jnp.float32)
    chosen_grad = gate_soft * (
        gates_grad_share - jnp.sum(gate_soft * gates_grad_share, axis=-1, keepdims=True)
    )
    logit_grad = jnp.sum(chosen_grad[:, :, None] * route_onehot, axis=1)
    prob_target = ALPHA * expert_count * fractions / total_tokens
    logit_grad = logit_grad + probabilities * (
        prob_target[None, :] - jnp.sum(probabilities * prob_target[None, :], axis=-1, keepdims=True)
    )
    mixed_float = mixed_share.astype(jnp.float32)
    router_grad = jnp.dot(
        mixed_float.T, logit_grad, precision=HIGHEST, preferred_element_type=jnp.float32
    )
    mixed_grad_share = mixed_grad_share + jnp.dot(
        logit_grad,
        w_router.astype(jnp.float32).T,
        precision=HIGHEST,
        preferred_element_type=jnp.float32,
    )
    mix_pullback = jax.vjp(normalize, middle_share, mix_gains)[1]
    middle_from_norm, mix_gain_grad = mix_pullback(mixed_grad_share)
    middle_grad = upstream + middle_from_norm
    middle_low = middle_grad.astype(jnp.bfloat16)
    middle_rows = lax.all_gather(middle_low, "tensor", axis=0, tiled=True)
    out_grad = contract_rows(attended, middle_rows)
    attended_grad = contract_cols(middle_rows, w_out).astype(jnp.bfloat16)
    query_parts = []
    key_parts = []
    value_parts = []
    for sequence in range(sequences_here):
        first_row = sequence * sequence_length
        query_block = query_rows[first_row : first_row + sequence_length].reshape(
            sequence_length, groups_here, per_group, head_width
        )
        key_block = key_rows[first_row : first_row + sequence_length]
        value_block = value_rows[first_row : first_row + sequence_length]
        allowed = allowed_pairs(starts[sequence], sequence_length, PIECE)
        scores = scores_of(query_block, key_block, allowed, score_scale)
        weights_full = jnp.exp(scores - logsum_parts[sequence])
        weights_low = weights_full.astype(jnp.bfloat16)
        grad_block = attended_grad[first_row : first_row + sequence_length].reshape(
            sequence_length, groups_here, per_group, head_width
        )
        value_parts.append(
            jnp.einsum(
                "kgqs,qkgd->skd", weights_low, grad_block, preferred_element_type=jnp.float32
            )
        )
        weight_grad = jnp.einsum(
            "qkgd,skd->kgqs", grad_block, value_block, preferred_element_type=jnp.float32
        )
        score_low = (
            weights_full
            * (weight_grad - jnp.sum(weights_full * weight_grad, axis=-1, keepdims=True))
        ).astype(jnp.bfloat16)
        query_parts.append(
            jnp.einsum("kgqs,skd->qkgd", score_low, key_block, preferred_element_type=jnp.float32)
            * score_scale
        )
        key_parts.append(
            jnp.einsum("kgqs,qkgd->skd", score_low, query_block, preferred_element_type=jnp.float32)
            * score_scale
        )
    query_grads = (
        rotate(
            jnp.concatenate(query_parts, axis=0).reshape(group_rows, heads_here, head_width),
            cosine_rows,
            -sine_rows,
        )
        .astype(jnp.bfloat16)
        .reshape(group_rows, query_width)
    )
    key_grads = (
        rotate(jnp.concatenate(key_parts, axis=0), cosine_rows, -sine_rows)
        .astype(jnp.bfloat16)
        .reshape(group_rows, key_width)
    )
    value_grads = (
        jnp.concatenate(value_parts, axis=0).astype(jnp.bfloat16).reshape(group_rows, key_width)
    )
    joined_grads = jnp.concatenate([query_grads, key_grads, value_grads], axis=1)
    joined_weight_grad = contract_rows(normed, joined_grads)
    normed_grad_share = lax.psum_scatter(
        contract_cols(joined_grads, joined_weights).astype(jnp.bfloat16),
        "tensor",
        scatter_dimension=0,
        tiled=True,
    ).astype(jnp.float32)
    input_pullback = jax.vjp(normalize, inputs_share, norm_gains)[1]
    input_from_norm, norm_gain_grad = input_pullback(normed_grad_share)
    input_grad_share = middle_grad + input_from_norm
    query_total, key_total, value_total, out_turned = (
        lax.psum_scatter(
            joined_weight_grad[:, :query_width].astype(jnp.bfloat16),
            "dp",
            scatter_dimension=0,
            tiled=True,
        ).astype(jnp.float32),
        lax.psum_scatter(
            joined_weight_grad[:, query_width : query_width + key_width].astype(jnp.bfloat16),
            "dp",
            scatter_dimension=0,
            tiled=True,
        ).astype(jnp.float32),
        lax.psum_scatter(
            joined_weight_grad[:, query_width + key_width :].astype(jnp.bfloat16),
            "dp",
            scatter_dimension=0,
            tiled=True,
        ).astype(jnp.float32),
        lax.psum_scatter(
            out_grad.T.astype(jnp.bfloat16), "dp", scatter_dimension=0, tiled=True
        ).astype(jnp.float32),
    )
    out_total = out_turned.T
    norm_gain_total, mix_gain_total, router_total = lax.psum(
        (norm_gain_grad, mix_gain_grad, router_grad), ("dp", "tensor")
    )
    return (
        output_share,
        balance,
        input_grad_share,
        norm_gain_total,
        query_total,
        key_total,
        value_total,
        out_total,
        mix_gain_total,
        router_total,
        gate_total,
        up_total,
        down_total,
    )


def solution(mesh):
    return jax.shard_map(
        shards,
        mesh=mesh,
        in_specs=(
            P(("dp", "tensor"), None),
            P(),
            P(None, "tensor"),
            P(None, "tensor"),
            P(None, "tensor"),
            P("tensor", None),
            P(),
            P(),
            P("tensor", None, None),
            P("tensor", None, None),
            P("tensor", None, None),
            P("dp", None),
            P("dp", None),
            P(("dp", "tensor"), None),
        ),
        out_specs=(
            P(("dp", "tensor"), None),
            P(),
            P(("dp", "tensor"), None),
            P(),
            P("dp", "tensor"),
            P("dp", "tensor"),
            P("dp", "tensor"),
            P("tensor", "dp"),
            P(),
            P(),
            P("tensor", "dp", None),
            P("tensor", "dp", None),
            P("tensor", None, "dp"),
        ),
        check_vma=False,
    )
```

profile of v0, /device:TPU:0, one launch (start us, length us, event | category | flops | bytes accessed | tf_op | source)
XLA Modules:
  0.0 3364.2 jit_solution(3808868114864663489)
XLA Ops:
  33.4 65.4 %all-gather.5.cloned.1.call-done = bf16[2048,1536]{1,0:T(8,128)(2,1)} async-done(((bf16[1024,1536]{1,0:T(8,128)(2,1)}), bf16[2048,1536]{1,0:T(8,128)(2,1)}) %all-gather.5.cloned.1.call-update) | async-done | bytes 6291472 | tf_op jit(solution)/shard_map/all_gather | solution.py:139
  265.4 138.6 %reduce-scatter.13.cloned.1.call-done = f32[1024,1536]{1,0:T(8,128)} async-done(((f32[2048,1536]{1,0:T(8,128)}), f32[1024,1536]{1,0:T(8,128)}) %reduce-scatter.13.cloned.1.call-update) | async-done | bytes 6291472 | tf_op jit(solution)/shard_map/reduce_scatter | solution.py:185
  427.7 60.4 %scatter_custom_fusion = s32[24560]{0:T(1024)S(1)} fusion(s32[16384]{0:T(1024)S(1)} %bitcast.249, s32[16384]{0:T(1024)S(1)} %iota.108, s32[]{:T(128)} %constant.42.clone.1), kind=kCustom, calls=%fused_computation.164 | custom fusion | bytes 98244 | tf_op jit(solution)/shard_map/scatter | solution.py:82
  494.9 78.1 %gather_fusion.2 = bf16[12280,1536]{1,0:T(8,128)(2,1)} fusion(bf16[2049,1536]{1,0:T(8,128)(2,1)} %concatenate.59, s32[12288]{0:T(1024)S(1)} %pad_clamp_fusion), kind=kCustom, calls=%fused_computation.2 | custom fusion | bytes 75497440 | tf_op jit(solution)/shard_map/gather | solution.py:236
  573.1 50.8 %reshape.361 = f32[20,614,1536]{2,1,0:T(8,128)} reshape(bf16[12280,1536]{1,0:T(8,128)(2,1)} %gather_fusion.2) | data formatting | bytes 113172480 | tf_op jit(solution)/shard_map/convert_element_type | solution.py:236
  634.2 68.2 %gather_fusion = f32[12280]{0:T(1024)S(1)} fusion(f32[16385]{0:T(1024)S(1)} %maximum_convert_fusion, s32[12288]{0:T(1024)S(1)} %pad_clamp_fusion.1), kind=kCustom, calls=%fused_computation | custom fusion | bytes 147360 | tf_op jit(solution)/shard_map/gather | solution.py:220
  708.9 77.1 %gather_fusion.1 = bf16[12280,1536]{1,0:T(8,128)(2,1)} fusion(bf16[2049,1536]{1,0:T(8,128)(2,1)} %concatenate.58, s32[12288]{0:T(1024)S(1)} %pad_clamp_fusion), kind=kCustom, calls=%fused_computation.1 | custom fusion | bytes 75497440 | tf_op jit(solution)/shard_map/gather | solution.py:221
  895.7 62.8 %multiply_convert_fusion.1 = (bf16[20,614,512]{2,1,0:T(8,128)(2,1)}, bf16[20,614,512]{2,1,0:T(8,128)(2,1)}, bf16[20,614,512]{2,1,0:T(8,128)(2,1)}) fusion(f32[20,614,512]{2,1,0:T(8,128)} %fusion.118, f32[20,614,512]{2,1,0:T(8,128)} %fusion.119, bf16[20,512,1536]{2,1,0:T(8,128)(2,1)} %param.24, f32[20,614,1536]{2,1,0:T(8,128)} %reshape.361, ...), kind=kOutput, calls=%fused_computation.38 | convolution fusion | flops 19453091840 | bytes 194977760 | tf_op jit(solution)/shard_map/ecd,efd->ecf/dot_general | solution.py:243
  958.5 62.0 %multiply_reduce_fusion = (f32[20,614]{1,0:T(8,128)S(1)}, f32[20,614,1536]{2,1,0:T(8,128)}) fusion(f32[20,614,1536]{2,1,0:T(8,128)} %reshape.361, bf16[20,614,512]{2,1,0:T(8,128)(2,1)} %get-tuple-element.30, bf16[20,512,1536]{2,1,0:T(8,128)(2,1)} %param.24), kind=kOutput, calls=%fused_computation.7 | convolution fusion | flops 19352481792 | bytes 194977760 | tf_op jit(solution)/shard_map/ecf,efd->ecd/dot_general | solution.py:92
  1020.5 84.3 %scatter_custom_fusion.3 = f32[16385]{0:T(1024)S(1)} fusion(s32[12280]{0:T(1024)} %copy-done.51, f32[12280]{0:T(1024)S(1)} %reshape.414, f32[]{:T(128)} %constant.30.clone.1), kind=kCustom, calls=%fused_computation.168 | custom fusion | flops 12280 | bytes 66052 | tf_op jit(solution)/shard_map/scatter-add | solution.py:266
  1106.4 44.2 %fusion.120 = f32[20,614,1536]{2,1,0:T(8,128)} fusion(bf16[20,614,512]{2,1,0:T(8,128)(2,1)} %get-tuple-element.29, bf16[20,1536,512]{2,1,0:T(8,128)(2,1)} %param.22), kind=kOutput, calls=%fused_computation.234 | convolution fusion | flops 19314769920 | bytes 119480320 | tf_op jit(solution)/shard_map/ecf,edf->ecd/dot_general | solution.py:254
  1150.6 61.6 %convolution_add_fusion = f32[20,614,1536]{2,1,0:T(8,128)} fusion(f32[20,614,1536]{2,1,0:T(8,128)} %fusion.120, bf16[20,614,512]{2,1,0:T(8,128)(2,1)} %get-tuple-element.28, bf16[20,1536,512]{2,1,0:T(8,128)(2,1)} %param.23), kind=kOutput, calls=%fused_computation.34 | convolution fusion | flops 19333632000 | bytes 194928640 | tf_op jit(solution)/shard_map/ecf,edf->ecd/dot_general | solution.py:256
  1212.2 61.2 %reshape.406 = f32[12280,1536]{1,0:T(8,128)} reshape(f32[20,614,1536]{2,1,0:T(8,128)} %convolution_add_fusion) | data formatting | bytes 150896640 | tf_op jit(solution)/shard_map/reshape | solution.py:264
  1273.5 124.6 %scatter_custom_fusion.2 = f32[2049,1536]{1,0:T(8,128)} fusion(s32[12280]{0:T(1024)} %get-tuple-element.50, f32[12280,1536]{1,0:T(8,128)} %reshape.406, f32[]{:T(128)} %constant.30.clone.1), kind=kCustom, calls=%fused_computation.65 | custom fusion | flops 18862080 | bytes 12589568 | tf_op jit(solution)/shard_map/scatter-add | solution.py:263
  1452.2 102.1 %reduce-scatter.17.cloned.1.call-done = f32[1024,1536]{1,0:T(8,128)} async-done(((f32[2048,1536]{1,0:T(8,128)}), f32[1024,1536]{1,0:T(8,128)}) %reduce-scatter.17.cloned.1.call-update) | async-done | bytes 6291472 | tf_op jit(solution)/shard_map/reduce_scatter | solution.py:270
  1571.5 79.5 %all-gather.11.cloned.1.call-done = bf16[2048,1536]{1,0:T(8,128)(2,1)} async-done(((bf16[1024,1536]{1,0:T(8,128)(2,1)}), bf16[2048,1536]{1,0:T(8,128)(2,1)}) %all-gather.11.cloned.1.call-update) | async-done | bytes 6291472 | tf_op jit(solution)/shard_map/all_gather | solution.py:306
  1842.4 41.1 %fusion.4 = bf16[4,3,1024,1024]{2,3,1,0:T(8,128)(2,1)} fusion(f32[4,1024,1024,3]{2,1,3,0:T(8,128)} %get-tuple-element.69, f32[4,3,1024]{2,1,0:T(4,128)S(1)} %get-tuple-element.68, f32[4,3,1024]{2,1,0:T(4,128)S(1)} %log_add_fusion, f32[4,1024,1024,3]{2,1,3,0:T(8,128)} %get-tuple-element.60, pred[1024,1024]{0,1:T(8,128)(4,1)S(1)} %copy-done.3), kind=kLoop, calls=%fused_computation.15 | loop fusion | flops 75497472 | bytes 126976000 | tf_op jit(solution)/shard_map/convert_element_type | solution.py:337
  1954.4 61.9 %reshape.355 = f32[12280,1536]{1,0:T(8,128)} reshape(f32[20,614,1536]{2,1,0:T(8,128)} %get-tuple-element.64) | data formatting | bytes 150896640 | tf_op jit(solution)/shard_map/reshape | solution.py:223
  2016.3 132.7 %scatter_custom_fusion.1 = f32[2049,1536]{1,0:T(8,128)} fusion(s32[12280]{0:T(1024)} %get-tuple-element.50, f32[12280,1536]{1,0:T(8,128)} %reshape.355, f32[12280]{0:T(1024)S(1)} %copy-done.40, f32[]{:T(128)} %constant.30.clone.1), kind=kCustom, calls=%fused_computation.9 | custom fusion | flops 37724160 | bytes 88087008 | tf_op jit(solution)/shard_map/scatter-add | solution.py:224
  2157.8 47.0 %convolution_convert_fusion = bf16[20,512,1536]{1,2,0:T(8,128)(2,1)} fusion(bf16[20,614,512]{2,1,0:T(8,128)(2,1)} %get-tuple-element.30, f32[20,614,1536]{2,1,0:T(8,128)} %reshape.361, f32[20,614]{1,0:T(8,128)S(1)} %copy-done.32), kind=kOutput, calls=%fused_computation.35 | convolution fusion | flops 19368222720 | bytes 119529440 | tf_op jit(solution)/shard_map/ecf,ecd->efd/dot_general | solution.py:246
  2348.6 282.6 %reduce-scatter.35.cloned.1.call-done = bf16[20,512,96]{1,2,0:T(8,128)(2,1)} async-done(((bf16[20,512,1536]{1,2,0:T(8,128)(2,1)}), bf16[20,512,96]{1,2,0:T(8,128)(2,1)}) %reduce-scatter.35.cloned.1.call-update) | async-done | bytes 1966096 | tf_op jit(solution)/shard_map/reduce_scatter | solution.py:281
  2635.2 293.9 %reduce-scatter.33.cloned.1.call-done = bf16[20,96,512]{2,1,0:T(8,128)(2,1)} async-done(((bf16[20,1536,512]{2,1,0:T(8,128)(2,1)}), bf16[20,96,512]{2,1,0:T(8,128)(2,1)}) %reduce-scatter.33.cloned.1.call-update) | async-done | bytes 1966096 | tf_op jit(solution)/shard_map/reduce_scatter | solution.py:277
  2933.1 293.9 %reduce-scatter.31.cloned.1.call-done = bf16[20,96,512]{2,1,0:T(8,128)(2,1)} async-done(((bf16[20,1536,512]{2,1,0:T(8,128)(2,1)}), bf16[20,96,512]{2,1,0:T(8,128)(2,1)}) %reduce-scatter.31.cloned.1.call-update) | async-done | bytes 1966096 | tf_op jit(solution)/shard_map/reduce_scatter | solution.py:274
  3231.0 124.7 %all-reduce.5.cloned.1.call-done = f32[1536,40]{0,1:T(8,128)} async-done(((f32[1536,40]{0,1:T(8,128)}), f32[1536,40]{0,1:T(8,128)}) %all-reduce.5.cloned.1.call-update) | async-done | bytes 245776 | tf_op jit(solution)/shard_map/psum | solution.py:398
  (351 shorter events, 847.4 us)
Async XLA Ops:
  7.2 242.1 %copy-start = (bf16[768,1536]{1,0:T(8,128)(2,1)S(1)}, bf16[768,1536]{1,0:T(8,128)(2,1)}, u32[]{:S(2)}) copy-start(bf16[768,1536]{1,0:T(8,128)(2,1)} %param.19) | copy-start | bytes 7077892
  7.2 91.6 %all-gather.5.cloned.1.call-start = ((), (), s32[]{:S(2)}) async-start(), calls=%async_computation.12 | async-start | bytes 9437184 | tf_op jit(solution)/shard_map/all_gather | solution.py:139
  15.5 388.5 %reduce-scatter.13.cloned.1.call-start = ((), (), s32[]{:S(2)}) async-start(), calls=%async_computation.13 | async-start | bytes 18874368 | tf_op jit(solution)/shard_map/reduce_scatter | solution.py:185
  259.4 229.6 %all-gather.9.cloned.1.call-start = ((), (), s32[]{:S(2)}) async-start(), calls=%async_computation.16 | async-start | bytes 9437184 | tf_op jit(solution)/shard_map/all_gather | solution.py:232
  260.1 443.1 %all-gather.7.cloned.1.call-start = ((), (), s32[]{:S(2)}) async-start(), calls=%async_computation.14 | async-start | bytes 9437184 | tf_op jit(solution)/shard_map/all_gather | solution.py:208
  265.4 145.9 %copy-start.52 = (f32[1536]{0:T(1024)S(1)}, f32[1536]{0:T(1024)}, u32[]{:S(2)}) copy-start(f32[1536]{0:T(1024)} %param.20) | copy-start | bytes 18436
  413.6 995.8 %reduce-scatter.19.cloned.1.call-start = ((), (), s32[]{:S(2)}) async-start(), calls=%async_computation.18 | async-start | bytes 98304 | tf_op jit(solution)/shard_map/reduce_scatter | solution.py:271
  1106.4 448.0 %reduce-scatter.17.cloned.1.call-start = ((), (), s32[]{:S(2)}) async-start(), calls=%async_computation.17 | async-start | bytes 18874368 | tf_op jit(solution)/shard_map/reduce_scatter | solution.py:270
  1408.4 145.9 %copy-start.38 = (bf16[1536,40]{0,1:T(8,128)(2,1)S(1)}, bf16[1536,40]{0,1:T(8,128)(2,1)}, u32[]{:S(2)}) copy-start(bf16[1536,40]{0,1:T(8,128)(2,1)} %param.21) | copy-start | bytes 368644
  1408.5 145.9 %copy-start.53 = (f32[1536]{0:T(1024)S(1)}, f32[1536]{0:T(1024)}, u32[]{:S(2)}) copy-start(f32[1536]{0:T(1024)} %param.20) | copy-start | bytes 18436
  1408.5 145.9 %copy-start.60 = (f32[1024]{0:T(1024)S(1)}, f32[1024]{0:T(1024)}, u32[]{:S(2)}) copy-start(f32[1024]{0:T(1024)} %copy-done.59) | copy-start | bytes 12292
  1408.5 242.5 %all-gather.11.cloned.1.call-start = ((), (), s32[]{:S(2)}) async-start(), calls=%async_computation.19 | async-start | bytes 9437184 | tf_op jit(solution)/shard_map/all_gather | solution.py:306
  1409.4 153.3 %copy-start.64 = (f32[1024]{0:T(1024)}, f32[1024]{0:T(1024)S(1)}, u32[]{:S(2)}) copy-start(f32[1024]{0:T(1024)S(1)} %fusion.67) | copy-start | bytes 12292
  1411.3 151.3 %copy-start.26 = (f32[1024,40]{0,1:T(8,128)}, f32[1024,40]{0,1:T(8,128)S(1)}, u32[]{:S(2)}) copy-start(f32[1024,40]{0,1:T(8,128)S(1)} %get-tuple-element.19) | copy-start | bytes 491524
  1570.6 712.2 %reduce-scatter.25.cloned.1.call-start = ((), (), s32[]{:S(2)}) async-start(), calls=%async_computation.22 | async-start | bytes 835584 | tf_op jit(solution)/shard_map/reduce_scatter | solution.py:381
  1925.2 359.1 %reduce-scatter.27.cloned.1.call-start = ((), (), s32[]{:S(2)}) async-start(), calls=%async_computation.23 | async-start | bytes 835584 | tf_op jit(solution)/shard_map/reduce_scatter | solution.py:387
  1926.0 359.8 %reduce-scatter.29.cloned.1.call-start = ((), (), s32[]{:S(2)}) async-start(), calls=%async_computation.24 | async-start | bytes 2506752 | tf_op jit(solution)/shard_map/reduce_scatter | solution.py:393
  1935.7 351.7 %reduce-scatter.23.cloned.1.call-start = ((), (), s32[]{:S(2)}) async-start(), calls=%async_computation.21 | async-start | bytes 2506752 | tf_op jit(solution)/shard_map/reduce_scatter | solution.py:375
  1939.0 350.1 %reduce-scatter.21.cloned.1.call-start = ((), (), s32[]{:S(2)}) async-start(), calls=%async_computation.20 | async-start | bytes 9437184 | tf_op jit(solution)/shard_map/reduce_scatter | solution.py:365
  1954.3 379.0 %reduce-scatter.15.cloned.1.call-start = ((), (), s32[]{:S(2)}) async-start(), calls=%async_computation.15 | async-start | bytes 9437184 | tf_op jit(solution)/shard_map/reduce_scatter | solution.py:227
  2157.0 474.2 %reduce-scatter.35.cloned.1.call-start = ((), (), s32[]{:S(2)}) async-start(), calls=%async_computation.28 | async-start | bytes 33423360 | tf_op jit(solution)/shard_map/reduce_scatter | solution.py:281
  2204.8 724.3 %reduce-scatter.33.cloned.1.call-start = ((), (), s32[]{:S(2)}) async-start(), calls=%async_computation.27 | async-start | bytes 33423360 | tf_op jit(solution)/shard_map/reduce_scatter | solution.py:277
  2240.8 986.2 %reduce-scatter.31.cloned.1.call-start = ((), (), s32[]{:S(2)}) async-start(), calls=%async_computation.26 | async-start | bytes 33423360 | tf_op jit(solution)/shard_map/reduce_scatter | solution.py:274
  2277.7 1078.1 %all-reduce.5.cloned.1.call-start = ((), (), s32[]{:S(2)}) async-start(), calls=%async_computation.25 | async-start | bytes 491520 | tf_op jit(solution)/shard_map/psum | solution.py:398
  (83 other events, 1404.9 us)
Sparse Core Ops, SparseCore 0:
  15.6 83.0 all-gather.4
  259.5 144.4 reduce-scatter.12
  405.5 80.3 all-gather.8
  487.9 80.3 all-gather.6
  1106.5 9.6 reduce-scatter.18
  1408.6 145.6 reduce-scatter.16
  1570.8 80.1 all-gather.10
  1925.3 56.5 reduce-scatter.24
  1985.9 55.5 reduce-scatter.26
  2045.1 61.9 reduce-scatter.28
  2111.3 62.0 reduce-scatter.22
  2175.6 76.0 reduce-scatter.20
  2254.1 77.9 reduce-scatter.14
  2336.0 295.1 reduce-scatter.34
  2635.2 293.8 reduce-scatter.32
  2933.1 293.8 reduce-scatter.30
  3232.9 122.7 all-reduce.4
where the time goes:
time: 3370 us; the launch traced here: 3360 us
  waiting for transfers between devices  1380 us (41%)
  matrix products  752 us (22%)
  local copies, waits for them, and re-layouts  575 us (17%)
  other arithmetic  552 us (16%)
  blocking collectives  83.5 us (2%)
    reduce_scatter x1, waiting for transfers between devices, shards(): lax.psum_scatter(gate_grad.astype(jnp.bfloat16), 'dp', scatter_dimension=...  294 us
    reduce_scatter x1, waiting for transfers between devices, shards(): lax.psum_scatter(up_grad.astype(jnp.bfloat16), 'dp', scatter_dimension=1,...  294 us
    reduce_scatter x1, waiting for transfers between devices, shards(): lax.psum_scatter(down_grad.astype(jnp.bfloat16), 'dp', scatter_dimension=...  283 us
    reduce_scatter x1, waiting for transfers between devices, shards(): lax.psum_scatter(jnp.dot(attended, w_out, preferred_element_type=jnp.floa...  139 us
    scatter-add x1, other arithmetic, shards(): jax.ops.segment_sum(slot_gates[:, None] * returned_flat, owners, num_segm...  133 us
    psum x1, waiting for transfers between devices, shards(): lax.psum((norm_gain_grad, mix_gain_grad, router_grad), ('dp', 'tensor'))  125 us
    scatter-add x1, other arithmetic, shards(): jax.ops.segment_sum(inputs_grad.reshape(experts_here * CAP, model_width),...  125 us
    reduce_scatter x1, waiting for transfers between devices, shards(): lax.psum_scatter(mixed_partial, 'tensor', scatter_dimension=0, tiled=True)  102 us
  transfers between devices with their start and end apart: 17, of which 8 were waited for; matrix products, arithmetic and copies ran while one was open for 30% of the time, Pallas kernels for 0%

commit v1 on v0

--- a/solution.py
+++ b/solution.py
@@ -1,6 +1,10 @@
+import functools
+
 import jax
 import jax.numpy as jnp
 from jax import lax
+from jax.experimental import pallas as pl
+from jax.experimental.pallas import tpu as pltpu
 from jax.sharding import PartitionSpec as P
 
 HD = 64
@@ -69,6 +73,559 @@
     return causal | shared
 
 
+def scores_of(query_block, key_block, allowed, score_scale):
+    raw_scores = (
+        jnp.einsum("qkgd,skd->kgqs", query_block, key_block, preferred_element_type=jnp.float32)
+        * score_scale
+    )
+    return jnp.where(allowed, raw_scores, -1e30)
+
+
+BLOCK = 256
+PART = 128
+PIECE_ROWS = 64
+GROUP = BLOCK // PIECE_ROWS
+VMEM_LIMIT = 60 * 1024 * 1024
+
+
+def dot_nt(left, right):
+    return lax.dot_general(
+        left, right, (((1,), (1,)), ((), ())), preferred_element_type=jnp.float32
+    )
+
+
+def dot_tn(left, right):
+    return lax.dot_general(
+        left, right, (((0,), (0,)), ((), ())), preferred_element_type=jnp.float32
+    )
+
+
+def round_up(value, multiple):
+    return -(-value // multiple) * multiple
+
+
+def placement(routes_rows, gates_rows, first_expert, experts):
+    rows = routes_rows.shape[0]
+    tiles = rows // BLOCK
+    turned = routes_rows.T
+    names = first_expert + jnp.arange(experts, dtype=jnp.int32)
+    hit = turned[None, :, :] == names[:, None, None]
+    member = jnp.any(hit, axis=1)
+    upper = jnp.triu(jnp.ones((BLOCK, BLOCK), jnp.bfloat16))
+    inside = jnp.dot(
+        member.astype(jnp.bfloat16).reshape(experts * tiles, BLOCK),
+        upper,
+        preferred_element_type=jnp.float32,
+    ).astype(jnp.int32).reshape(experts, tiles, BLOCK)
+    sums = inside[:, :, -1]
+    ends = jnp.cumsum(sums, axis=1)
+    begins = ends - sums
+    place = jnp.where(
+        member.reshape(experts, tiles, BLOCK), begins[:, :, None] + inside - 1, -1
+    )
+    place = jnp.concatenate(
+        [place, jnp.full((1, tiles, BLOCK), -1, jnp.int32)], axis=0
+    ).reshape(experts + 1, tiles, 1, BLOCK)
+    gates = None
+    if gates_rows is not None:
+        gates = jnp.sum(
+            jnp.where(hit, gates_rows.astype(jnp.float32).T[None, :, :], 0.0), axis=1
+        ).reshape(experts, tiles, 1, BLOCK)
+    return place, begins, ends, gates
+
+
+def gather_tables(begins, ends, slots):
+    counts = ends[:, -1]
+    parts = jnp.arange(slots // PART, dtype=jnp.int32) * PART
+    low = jnp.sum((ends[:, None, :] <= parts[None, :, None]).astype(jnp.int32), axis=2)
+    high = jnp.sum((begins[:, None, :] < parts[None, :, None] + PART).astype(jnp.int32), axis=2)
+    high = jnp.where(parts[None, :] < counts[:, None], high, low)
+    blocks = jnp.maximum(-(-counts // BLOCK), 1)
+    return low, high, blocks
+
+
+def combine_tables(begins, ends, slots):
+    experts, tiles = begins.shape
+    width = round_up(experts * (BLOCK // PIECE_ROWS + 1), GROUP)
+    first = begins // PIECE_ROWS
+    amount = jnp.where(ends > begins, (ends - 1) // PIECE_ROWS - first + 1, 0)
+    stop = jnp.cumsum(amount, axis=0)
+    place = jnp.arange(width, dtype=jnp.int32)
+    owner = jnp.sum(
+        (stop.T[:, None, :] <= place[None, :, None]).astype(jnp.int32), axis=2
+    )
+    chosen = owner[:, :, None] == jnp.arange(experts, dtype=jnp.int32)[None, None, :]
+    offset = jnp.sum(
+        jnp.where(chosen, (first - (stop - amount)).T[:, None, :], 0), axis=2
+    )
+    valid = owner < experts
+    piece = jnp.where(valid, offset + place[None, :], 0)
+    source = jnp.where(valid, owner, 0) * (slots // PIECE_ROWS) + piece
+    groups = jnp.maximum(-(-stop[-1] // GROUP), 1)
+    return owner, piece, source, groups, width
+
+
+def gather_kernel(
+    experts, slots, sources, with_gates, low_ref, high_ref, blocks_ref, place_ref, *rest
+):
+    if with_gates:
+        gates_ref, rest = rest[0], rest[1:]
+    inputs, rest = rest[:sources], rest[sources:]
+    if with_gates:
+        out_ref, gate_out_ref, rest = rest[0], rest[1], rest[2:]
+    else:
+        out_ref, rest = rest[0], rest[1:]
+    held, total, gate_total, sems = rest
+    expert = pl.program_id(0)
+    part = pl.program_id(1)
+    share = inputs[0].shape[0]
+
+    @pl.when((expert == 0) & (part == 0))
+    def _():
+        copies = [
+            pltpu.make_async_copy(ref, held.at[pl.ds(i * share, share)], sems.at[i])
+            for i, ref in enumerate(inputs)
+        ]
+        for copy in copies:
+            copy.start()
+        for copy in copies:
+            copy.wait()
+
+    @pl.when(part * PART < blocks_ref[expert] * BLOCK)
+    def _():
+        total[...] = jnp.zeros_like(total)
+        if with_gates:
+            gate_total[...] = jnp.zeros_like(gate_total)
+        rows = lax.broadcasted_iota(jnp.int32, (PART, BLOCK), 0) + part * PART
+
+        def step(tile, carry):
+            match = rows == place_ref[expert, tile]
+            pick = jnp.where(match, 1.0, 0.0)
+            start = pl.multiple_of(tile * BLOCK, BLOCK)
+            total[...] += jnp.dot(
+                pick.astype(jnp.bfloat16),
+                held[pl.ds(start, BLOCK), :],
+                preferred_element_type=jnp.float32,
+            )
+            if with_gates:
+                weighted = pick * gates_ref[expert, tile]
+                gate_total[...] += jnp.broadcast_to(
+                    jnp.sum(weighted, axis=1, keepdims=True), gate_total.shape
+                )
+            return carry
+
+        lax.fori_loop(low_ref[expert, part], high_ref[expert, part], step, 0)
+        out_ref[...] = total[...].astype(out_ref.dtype)
+        if with_gates:
+            gate_out_ref[...] = gate_total[...]
+
+
+def gather_rows(tables, place, gates, sources, slots, first, count):
+    low, high, blocks = tables
+    low, high, blocks = (t[first : first + count] for t in (low, high, blocks))
+    place = place[first : first + count]
+    tiles = place.shape[1]
+    rows = tiles * BLOCK
+    width = sources[0].shape[1]
+    with_gates = gates is not None
+    if with_gates:
+        gates = gates[first : first + count]
+    parts = slots // PART
+
+    def out_index(expert, part, low, high, blocks):
+        return (expert * parts + jnp.minimum(part, blocks[expert] * (BLOCK // PART) - 1), 0)
+
+    def whole(array):
+        zeros = (0,) * array.ndim
+        return pl.BlockSpec(array.shape, lambda *_: zeros)
+
+    operands = [place] + ([gates] if with_gates else [])
+    in_specs = [whole(a) for a in operands] + [pl.BlockSpec(memory_space=pl.ANY)] * len(sources)
+    out_shape = [jax.ShapeDtypeStruct((count * slots, width), jnp.bfloat16)]
+    out_specs = [pl.BlockSpec((PART, width), out_index)]
+    if with_gates:
+        out_shape.append(jax.ShapeDtypeStruct((count * slots, 128), jnp.float32))
+        out_specs.append(pl.BlockSpec((PART, 128), out_index))
+    return pl.pallas_call(
+        functools.partial(gather_kernel, count, slots, len(sources), with_gates),
+        grid_spec=pltpu.PrefetchScalarGridSpec(
+            num_scalar_prefetch=3,
+            grid=(count, parts),
+            in_specs=in_specs,
+            out_specs=out_specs,
+            scratch_shapes=[
+                pltpu.VMEM((rows, width), jnp.bfloat16),
+                pltpu.VMEM((PART, width), jnp.float32),
+                pltpu.VMEM((PART, 128), jnp.float32),
+                pltpu.SemaphoreType.DMA((len(sources),)),
+            ],
+        ),
+        out_shape=out_shape,
+        compiler_params=pltpu.CompilerParams(vmem_limit_bytes=VMEM_LIMIT),
+        cost_estimate=pl.CostEstimate(
+            flops=count * rows * 6 * PART * width, bytes_accessed=rows * width * 6, transcendentals=0
+        ),
+    )(low, high, blocks, *operands, *sources)
+
+
+def expert_kernel(
+    first, split, depth, blocks_ref, misc_ref, x_ref, c_ref, sg_ref, wg_ref, wu_ref, wd_ref, *rest
+):
+    if len(rest) == 3 + (2 if split else 1) + 2 + 3:
+        rest = rest[3:]
+    y_ref, dx_ref, gg_ref = rest[:3]
+    rest = rest[3:]
+    if split:
+        send_ref, keep_ref = rest[:2]
+        rest = rest[2:]
+    else:
+        grads_ref = rest[0]
+        rest = rest[1:]
+    total_gu, total_d = rest
+    block = pl.program_id(1)
+    hidden = wg_ref.shape[2]
+
+    @pl.when(block == 0)
+    def _():
+        total_gu[...] = jnp.zeros_like(total_gu)
+        total_d[...] = jnp.zeros_like(total_d)
+
+    @pl.when(block < blocks_ref[first + pl.program_id(0)])
+    def _():
+        x = x_ref[...]
+        c = c_ref[...]
+        gate = jnp.concatenate([sg_ref[...]] * (hidden // 128), axis=1)
+        gate_proj = jnp.dot(x, wg_ref[0], preferred_element_type=jnp.float32)
+        up_proj = jnp.dot(x, wu_ref[0], preferred_element_type=jnp.float32)
+        sigmoid = 1.0 / (1.0 + jnp.exp(-gate_proj))
+        silu = gate_proj * sigmoid
+        activated = (silu * up_proj).astype(jnp.bfloat16).astype(jnp.float32)
+        pulled = dot_nt(c, wd_ref[0])
+        gate_grad = jnp.sum(activated * pulled, axis=1, keepdims=True)
+        gg_ref[...] = jnp.broadcast_to(gate_grad, gg_ref.shape)
+        gated = (gate * activated).astype(jnp.bfloat16)
+        y_ref[...] = jnp.dot(gated, wd_ref[0], preferred_element_type=jnp.float32).astype(
+            y_ref.dtype
+        )
+        activated_grad = gate * pulled
+        gate_low = (
+            activated_grad * up_proj * sigmoid * (1.0 + gate_proj * (1.0 - sigmoid))
+        ).astype(jnp.bfloat16)
+        up_low = (activated_grad * silu).astype(jnp.bfloat16)
+        dx_ref[...] = (dot_nt(gate_low, wg_ref[0]) + dot_nt(up_low, wu_ref[0])).astype(
+            dx_ref.dtype
+        )
+        total_gu[...] += dot_tn(x, jnp.concatenate([gate_low, up_low], axis=1))
+        total_d[...] += dot_tn(c, gated)
+
+    @pl.when(block == pl.num_programs(1) - 1)
+    def _():
+        parts = (
+            (total_gu, 0),
+            (total_gu, hidden),
+            (total_d, 0),
+        )
+        for which, (ref, column) in enumerate(parts):
+            if split:
+                side = misc_ref[1]
+                for index in range(keep_ref.shape[2]):
+                    for out, chosen in ((keep_ref, side), (send_ref, 1 - side)):
+                        start = pl.multiple_of((2 * index + chosen) * depth, 64)
+                        out[0, which, index] = ref[
+                            pl.ds(start, depth), pl.ds(column, hidden)
+                        ].astype(out.dtype)
+            else:
+                grads_ref[0, which] = ref[:, pl.ds(column, hidden)].astype(grads_ref.dtype)
+
+
+def expert_call(blocks, misc, x, c, sg, weights, carried, slots, first, count, x_first, c_first, depth):
+    w_gate, w_up, w_down = weights
+    experts = blocks.shape[0]
+    width = x.shape[1]
+    hidden = w_gate.shape[2]
+    most = slots // BLOCK
+    split = depth is not None
+
+    def rows_index(base):
+        def index(expert, block, blocks, misc):
+            limit = blocks[first + expert] - 1
+            return ((first - base + expert) * most + jnp.minimum(block, limit), 0)
+
+        return index
+
+    def weight_index(expert, block, blocks, misc):
+        return (misc[0] + first + expert, 0, 0)
+
+    def grads_index(expert, block, blocks, misc):
+        return (expert, 0, 0, 0, 0)
+
+    out_shape = [
+        jax.ShapeDtypeStruct((experts * slots, width), jnp.bfloat16),
+        jax.ShapeDtypeStruct((experts * slots, width), jnp.bfloat16),
+        jax.ShapeDtypeStruct((experts * slots, 128), jnp.float32),
+    ]
+    out_specs = [
+        pl.BlockSpec((BLOCK, width), rows_index(0)),
+        pl.BlockSpec((BLOCK, width), rows_index(0)),
+        pl.BlockSpec((BLOCK, 128), rows_index(0)),
+    ]
+    if split:
+        cuts = width // depth // 2
+        out_shape += [jax.ShapeDtypeStruct((count, 3, cuts, depth, hidden), jnp.bfloat16)] * 2
+        out_specs += [pl.BlockSpec((1, 3, cuts, depth, hidden), grads_index)] * 2
+    else:
+        out_shape += [jax.ShapeDtypeStruct((count, 3, width, hidden), jnp.bfloat16)]
+        out_specs += [pl.BlockSpec((1, 3, width, hidden), lambda e, b, *_: (e, 0, 0, 0))]
+    operands = [x, c, sg, w_gate, w_up, w_down]
+    in_specs = [
+        pl.BlockSpec((BLOCK, width), rows_index(x_first)),
+        pl.BlockSpec((BLOCK, width), rows_index(c_first)),
+        pl.BlockSpec((BLOCK, 128), rows_index(x_first)),
+        pl.BlockSpec((1, width, hidden), weight_index),
+        pl.BlockSpec((1, width, hidden), weight_index),
+        pl.BlockSpec((1, hidden, width), weight_index),
+    ]
+    aliases = {}
+    if carried is not None:
+        operands += list(carried)
+        in_specs += [pl.BlockSpec(memory_space=pl.ANY)] * 3
+        aliases = {8: 0, 9: 1, 10: 2}
+    rows = count * 820
+    return pl.pallas_call(
+        functools.partial(expert_kernel, first, split, depth),
+        grid_spec=pltpu.PrefetchScalarGridSpec(
+            num_scalar_prefetch=2,
+            grid=(count, most),
+            in_specs=in_specs,
+            out_specs=out_specs,
+            scratch_shapes=[
+                pltpu.VMEM((width, 2 * hidden), jnp.float32),
+                pltpu.VMEM((width, hidden), jnp.float32),
+            ],
+        ),
+        out_shape=out_shape,
+        input_output_aliases=aliases,
+        compiler_params=pltpu.CompilerParams(vmem_limit_bytes=VMEM_LIMIT),
+        cost_estimate=pl.CostEstimate(
+            flops=18 * rows * width * hidden,
+            bytes_accessed=8 * rows * width + 12 * count * width * hidden,
+            transcendentals=rows * hidden,
+        ),
+    )(blocks, misc, *operands)
+
+
+def combine_kernel(
+    first, width, owner_ref, piece_ref, source_ref, groups_ref, begin_ref, place_ref, y_ref, dx_ref,
+    gg_ref, y_out, dx_out, gate_out, y_buf, dx_buf, gg_buf, y_total, dx_total, sems,
+):
+    step = pl.program_id(0)
+    tile = first + step
+
+    def copies(which_tile, group, slot):
+        made = []
+        for i in range(GROUP):
+            source = pl.multiple_of(
+                source_ref[which_tile, group * GROUP + i] * PIECE_ROWS, PIECE_ROWS
+            )
+            for kind, (ref, buf) in enumerate(((y_ref, y_buf), (dx_ref, dx_buf), (gg_ref, gg_buf))):
+                made.append(
+                    pltpu.make_async_copy(
+                        ref.at[pl.ds(source, PIECE_ROWS)],
+                        buf.at[slot, pl.ds(i * PIECE_ROWS, PIECE_ROWS)],
+                        sems.at[slot, kind, i],
+                    )
+                )
+        return made
+
+    @pl.when(step == 0)
+    def _():
+        for copy in copies(tile, 0, begin_ref[tile] % 2):
+            copy.start()
+
+    y_total[...] = jnp.zeros_like(y_total)
+    dx_total[...] = jnp.zeros_like(dx_total)
+    gate_out[...] = jnp.zeros_like(gate_out)
+
+    def one(group, carry):
+        slot = (begin_ref[tile] + group) % 2
+        last = group + 1 == groups_ref[tile]
+        next_tile = jnp.where(last, tile + 1, tile)
+        next_group = jnp.where(last, 0, group + 1)
+
+        @pl.when(jnp.logical_not(last & (step == pl.num_programs(0) - 1)))
+        def _():
+            for copy in copies(next_tile, next_group, 1 - slot):
+                copy.start()
+
+        for copy in copies(tile, group, slot):
+            copy.wait()
+        picks = []
+        for i in range(GROUP):
+            entry = group * GROUP + i
+            expert = owner_ref[tile, entry]
+            rows = (
+                lax.broadcasted_iota(jnp.int32, (PIECE_ROWS, BLOCK), 0)
+                + piece_ref[tile, entry] * PIECE_ROWS
+            )
+            pick = jnp.where(rows == place_ref[expert, step], 1.0, 0.0)
+            picks.append(pick.astype(jnp.bfloat16))
+            grads = gg_buf[slot, pl.ds(i * PIECE_ROWS, PIECE_ROWS), :]
+            grads = jnp.concatenate([grads] * (BLOCK // 128), axis=1)
+            gate_out[expert, 0] += jnp.sum(pick * grads, axis=0, keepdims=True)
+        picked = jnp.concatenate(picks, axis=0)
+        y_total[...] += dot_tn(picked, y_buf[slot])
+        dx_total[...] += dot_tn(picked, dx_buf[slot])
+        return carry
+
+    lax.fori_loop(0, groups_ref[tile], one, 0)
+    y_out[...] = y_total[...].astype(y_out.dtype)
+    dx_out[...] = dx_total[...].astype(dx_out.dtype)
+
+
+def combine_rows(tables, place, y, dx, gg, first, count):
+    owner, piece, source, groups, width = tables
+    begin = jnp.cumsum(groups) - groups
+    experts = place.shape[0]
+    columns = y.shape[1]
+    return pl.pallas_call(
+        functools.partial(combine_kernel, first, width),
+        grid_spec=pltpu.PrefetchScalarGridSpec(
+            num_scalar_prefetch=5,
+            grid=(count,),
+            in_specs=[pl.BlockSpec((experts, count, 1, BLOCK), lambda *_: (0, first // count, 0, 0))]
+            + [pl.BlockSpec(memory_space=pl.ANY)] * 3,
+            out_specs=[
+                pl.BlockSpec((BLOCK, columns), lambda t, *_: (t, 0)),
+                pl.BlockSpec((BLOCK, columns), lambda t, *_: (t, 0)),
+                pl.BlockSpec((experts, 1, 1, BLOCK), lambda t, *_: (0, t, 0, 0)),
+            ],
+            scratch_shapes=[
+                pltpu.VMEM((2, BLOCK, columns), jnp.bfloat16),
+                pltpu.VMEM((2, BLOCK, columns), jnp.bfloat16),
+                pltpu.VMEM((2, BLOCK, 128), jnp.float32),
+                pltpu.VMEM((BLOCK, columns), jnp.float32),
+                pltpu.VMEM((BLOCK, columns), jnp.float32),
+                pltpu.SemaphoreType.DMA((2, 3, GROUP)),
+            ],
+        ),
+        out_shape=[
+            jax.ShapeDtypeStruct((count * BLOCK, columns), jnp.bfloat16),
+            jax.ShapeDtypeStruct((count * BLOCK, columns), jnp.bfloat16),
+            jax.ShapeDtypeStruct((experts, count, 1, BLOCK), jnp.float32),
+        ],
+        compiler_params=pltpu.CompilerParams(vmem_limit_bytes=VMEM_LIMIT),
+        cost_estimate=pl.CostEstimate(
+            flops=count * 20 * PIECE_ROWS * BLOCK * columns * 4,
+            bytes_accessed=count * 20 * PIECE_ROWS * columns * 4,
+            transcendentals=0,
+        ),
+    )(owner, piece, source, groups, begin, place, y, dx, gg)
+
+
+def flip(value, bit):
+    size = lax.axis_size("dp")
+    return lax.ppermute(value, "dp", [(i, i ^ bit) for i in range(size)])
+
+
+def swap(value):
+    return lax.ppermute(value, "tensor", [(0, 1), (1, 0)])
+
+
+def add_low(left, right):
+    return (left.astype(jnp.float32) + right.astype(jnp.float32)).astype(jnp.bfloat16)
+
+
+def pick_index(value, index, axis):
+    return lax.dynamic_index_in_dim(value, index, axis, keepdims=False)
+
+
+def chip_sum(send, keep, rank):
+    low_bit, high_bit = (rank // 4) % 2, rank // 8
+    count, kinds, cuts, depth, hidden = keep.shape
+    got = flip(send, 2)
+    view = (count, kinds, cuts // 2, 2, depth, hidden)
+    keep, got = keep.reshape(view), got.reshape(view)
+    send = add_low(pick_index(keep, 1 - low_bit, 3), pick_index(got, 1 - low_bit, 3))
+    keep = add_low(pick_index(keep, low_bit, 3), pick_index(got, low_bit, 3))
+    got = flip(send, 4)
+    send = add_low(pick_index(keep, 1 - high_bit, 2), pick_index(got, 1 - high_bit, 2))
+    keep = add_low(pick_index(keep, high_bit, 2), pick_index(got, high_bit, 2))
+    got = flip(send, 8)
+    return add_low(keep, got)
+
+
+def attend_half(normed, joined_weights, sizes, tables, allowed, score_scale):
+    query_width, key_width, head_width = sizes
+    rows = normed.shape[0]
+    heads_here = query_width // head_width
+    groups_here = key_width // head_width
+    per_group = heads_here // groups_here
+    cosine, sine_table = tables
+    projected = jnp.dot(normed, joined_weights, preferred_element_type=jnp.float32)
+    query_rows = rotate(
+        projected[:, :query_width].reshape(rows, heads_here, head_width), cosine, sine_table
+    ).astype(jnp.bfloat16)
+    key_rows = rotate(
+        projected[:, query_width : query_width + key_width].reshape(rows, groups_here, head_width),
+        cosine,
+        sine_table,
+    ).astype(jnp.bfloat16)
+    value_rows = (
+        projected[:, query_width + key_width :]
+        .astype(jnp.bfloat16)
+        .reshape(rows, groups_here, head_width)
+    )
+    query_block = query_rows.reshape(rows, groups_here, per_group, head_width)
+    scores = scores_of(query_block, key_rows, allowed, score_scale)
+    highest = jnp.max(scores, axis=-1, keepdims=True)
+    shifted = jnp.exp(scores - highest)
+    totals = jnp.sum(shifted, axis=-1, keepdims=True)
+    weights = (shifted / totals).astype(jnp.bfloat16)
+    mixed_values = jnp.einsum(
+        "kgqs,skd->qkgd", weights, value_rows, preferred_element_type=jnp.float32
+    )
+    attended = mixed_values.reshape(rows, query_width).astype(jnp.bfloat16)
+    return attended, (query_block, key_rows, value_rows, highest + jnp.log(totals))
+
+
+def attend_half_back(saved, attended_grad, sizes, tables, allowed, score_scale):
+    query_width, key_width, head_width = sizes
+    query_block, key_block, value_block, logsum = saved
+    rows = key_block.shape[0]
+    cosine, sine_table = tables
+    scores = scores_of(query_block, key_block, allowed, score_scale)
+    weights_full = jnp.exp(scores - logsum)
+    weights_low = weights_full.astype(jnp.bfloat16)
+    grad_block = attended_grad.reshape(query_block.shape)
+    value_grad = jnp.einsum(
+        "kgqs,qkgd->skd", weights_low, grad_block, preferred_element_type=jnp.float32
+    )
+    weight_grad = jnp.einsum(
+        "qkgd,skd->kgqs", grad_block, value_block, preferred_element_type=jnp.float32
+    )
+    score_low = (
+        weights_full * (weight_grad - jnp.sum(weights_full * weight_grad, axis=-1, keepdims=True))
+    ).astype(jnp.bfloat16)
+    query_grad = (
+        jnp.einsum("kgqs,skd->qkgd", score_low, key_block, preferred_element_type=jnp.float32)
+        * score_scale
+    )
+    key_grad = (
+        jnp.einsum("kgqs,qkgd->skd", score_low, query_block, preferred_element_type=jnp.float32)
+        * score_scale
+    )
+    query_grads = (
+        rotate(query_grad.reshape(rows, -1, head_width), cosine, -sine_table)
+        .astype(jnp.bfloat16)
+        .reshape(rows, query_width)
+    )
+    key_grads = (
+        rotate(key_grad, cosine, -sine_table).astype(jnp.bfloat16).reshape(rows, key_width)
+    )
+    value_grads = value_grad.astype(jnp.bfloat16).reshape(rows, key_width)
+    return jnp.concatenate([query_grads, key_grads, value_grads], axis=1)
+
+
 def slot_table(routes, expert_count, capacity):
     flattened = routes.reshape(-1)
     onehot = (flattened[:, None] == jnp.arange(expert_count, dtype=jnp.int32)[None, :]).astype(
@@ -93,15 +650,7 @@
     return (gate_proj, up_proj, activated, returned)
 
 
-def scores_of(query_block, key_block, allowed, score_scale):
-    raw_scores = (
-        jnp.einsum("qkgd,skd->kgqs", query_block, key_block, preferred_element_type=jnp.float32)
-        * score_scale
-    )
-    return jnp.where(allowed, raw_scores, -1e30)
-
-
-def shards(
+def shards_wide(
     tokens,
     norm_gains,
     w_query,
@@ -415,9 +964,239 @@
     )
 
 
+def all_sum(value):
+    for bit in (1, 2, 4, 8):
+        value = value + flip(value, bit)
+    return value + swap(value)
+
+
+def spread(value):
+    across = swap(value)
+    return [value, across, flip(value, 1), flip(across, 1)]
+
+
+CHUNK = 2
+
+
+def shards_pair(
+    tokens,
+    norm_gains,
+    w_query,
+    w_key,
+    w_value,
+    w_out,
+    mix_gains,
+    w_router,
+    w_gate,
+    w_up,
+    w_down,
+    routes,
+    starts,
+    cotangent,
+):
+    share_rows, model_width = tokens.shape
+    query_width = w_query.shape[1]
+    key_width = w_key.shape[1]
+    sizes = (query_width, key_width, HD)
+    experts_here = w_gate.shape[0]
+    experts = experts_here // 2
+    choices_count = routes.shape[1]
+    expert_count = w_router.shape[1]
+    dp_size = lax.axis_size("dp")
+    rank = lax.axis_index("dp")
+    core, side = rank % 2, (rank // 2) % 2
+    tensor_rank = lax.axis_index("tensor")
+    total_tokens = routes.shape[0] * dp_size
+    score_scale = HD ** (-0.5)
+    depth = model_width // dp_size * 2
+    slots = round_up(2 * CAP, BLOCK)
+
+    joined_own = jnp.concatenate([w_query, w_key, w_value], axis=1)
+    part_rows = model_width // dp_size
+    out_rows = query_width // dp_size
+    joined_other = lax.all_gather(
+        swap(lax.dynamic_slice_in_dim(joined_own, rank * part_rows, part_rows, 0)),
+        "dp",
+        axis=0,
+        tiled=True,
+    )
+    out_other = lax.all_gather(
+        swap(lax.dynamic_slice_in_dim(w_out, rank * out_rows, out_rows, 0)),
+        "dp",
+        axis=0,
+        tiled=True,
+    )
+
+    own_routes = lax.dynamic_slice_in_dim(routes, tensor_rank * share_rows, share_rows, 0)
+    across_routes = lax.dynamic_slice_in_dim(routes, (1 - tensor_rank) * share_rows, share_rows, 0)
+    both_routes = jnp.concatenate([own_routes, across_routes], axis=0)
+    group_routes = jnp.concatenate([both_routes, flip(both_routes, 1)], axis=0)
+    first_expert = tensor_rank * experts_here + core * experts
+
+    cotangent_rows = spread(cotangent)
+
+    inputs_share = tokens.astype(jnp.float32)
+    normed = normalize(inputs_share, norm_gains).astype(jnp.bfloat16)
+    tables = rope_tables(share_rows, HD)
+    starts_row = lax.dynamic_index_in_dim(starts, tensor_rank, 0, keepdims=False)
+    allowed = allowed_pairs(starts_row, share_rows, PIECE)
+    attended_own, saved_own = attend_half(normed, joined_own, sizes, tables, allowed, score_scale)
+    attended_other, saved_other = attend_half(
+        normed, joined_other, sizes, tables, allowed, score_scale
+    )
+    middle_share = (
+        inputs_share
+        + jnp.dot(attended_own, w_out, preferred_element_type=jnp.float32)
+        + jnp.dot(attended_other, out_other, preferred_element_type=jnp.float32)
+    )
+    mixed_share = normalize(middle_share, mix_gains).astype(jnp.bfloat16)
+
+    route_onehot = (
+        own_routes[:, :, None] == jnp.arange(expert_count, dtype=jnp.int32)[None, None, :]
+    ).astype(jnp.float32)
+    logits = jnp.dot(mixed_share, w_router, preferred_element_type=jnp.float32)
+    probabilities = softmax_rows(logits)
+    chosen = jnp.sum(logits[:, None, :] * route_onehot, axis=-1)
+    gate_soft = softmax_rows(chosen)
+    gate_low = gate_soft.astype(jnp.bfloat16)
+    counts = all_sum(jnp.sum(route_onehot, axis=(0, 1)))
+    prob_sums = all_sum(jnp.sum(probabilities, axis=0))
+    fractions = counts / (total_tokens * choices_count)
+    balance = expert_count * expert_count * fractions * prob_sums / total_tokens
+
+    mixed_rows = spread(mixed_share)
+    group_gates = jnp.concatenate(spread(gate_low), axis=0)
+    place, begins, ends, gates = placement(group_routes, group_gates, first_expert, experts)
+    gather_from = gather_tables(begins, ends, slots)
+    blocks = gather_from[2]
+    cot_slots = gather_rows(gather_from, place, None, cotangent_rows, slots, 0, experts)[0]
+    misc = jnp.stack([core * experts, side])
+    weights = (w_gate, w_up, w_down)
+    carried = None
+    sums = []
+    first_part = gather_rows(gather_from, place, gates, mixed_rows, slots, 0, CHUNK)
+    later_part = gather_rows(gather_from, place, gates, mixed_rows, slots, CHUNK, experts - CHUNK)
+    for first in range(0, experts, CHUNK):
+        (x_slots, slot_gates), x_first = (
+            (first_part, 0) if first == 0 else (later_part, CHUNK)
+        )
+        *carried, send, keep = expert_call(
+            blocks, misc, x_slots, cot_slots, slot_gates, weights, carried, slots,
+            first, CHUNK, x_first, 0, depth,
+        )
+        sums.append(chip_sum(send, keep, rank))
+
+    combine_from = combine_tables(begins, ends, slots)
+    tiles = place.shape[1] // 2
+    turned_routes = group_routes.T
+    names = first_expert + jnp.arange(experts, dtype=jnp.int32)
+
+    def combined(half):
+        y, dx, gate_grads = combine_rows(combine_from, place, *carried, half * tiles, tiles)
+        gate_grads = gate_grads[:experts].reshape(experts, 1, tiles * BLOCK)
+        rows = turned_routes[:, half * tiles * BLOCK : (half + 1) * tiles * BLOCK]
+        hit = rows[None, :, :] == names[:, None, None]
+        return y, dx, jnp.sum(jnp.where(hit, gate_grads, 0.0), axis=0)
+
+    y_far, dx_far, gg_far = combined(1)
+    y_far, dx_far, gg_far = flip(y_far, 1), flip(dx_far, 1), flip(gg_far, 1)
+    y_near, dx_near, gg_near = combined(0)
+    dx_across = swap(add_low(dx_near[share_rows:], dx_far[share_rows:]))
+    gg_across = swap(gg_near[:, share_rows:] + gg_far[:, share_rows:])
+    y_across = swap(add_low(y_near[share_rows:], y_far[share_rows:]))
+    mixed_grad_share = (
+        dx_near[:share_rows].astype(jnp.float32)
+        + dx_far[:share_rows].astype(jnp.float32)
+        + dx_across.astype(jnp.float32)
+    )
+    gates_grad_share = (gg_near[:, :share_rows] + gg_far[:, :share_rows] + gg_across).T
+    expert_share = (
+        y_near[:share_rows].astype(jnp.float32)
+        + y_far[:share_rows].astype(jnp.float32)
+        + y_across.astype(jnp.float32)
+    )
+    output_share = (middle_share + expert_share).astype(jnp.bfloat16)
+
+    upstream = cotangent.astype(jnp.float32)
+    chosen_grad = gate_soft * (
+        gates_grad_share - jnp.sum(gate_soft * gates_grad_share, axis=-1, keepdims=True)
+    )
+    logit_grad = jnp.sum(chosen_grad[:, :, None] * route_onehot, axis=1)
+    prob_target = ALPHA * expert_count * fractions / total_tokens
+    logit_grad = logit_grad + probabilities * (
+        prob_target[None, :] - jnp.sum(probabilities * prob_target[None, :], axis=-1, keepdims=True)
+    )
+    router_grad = jnp.dot(
+        mixed_share.astype(jnp.float32).T,
+        logit_grad,
+        precision=HIGHEST,
+        preferred_element_type=jnp.float32,
+    )
+    mixed_grad_share = mixed_grad_share + jnp.dot(
+        logit_grad,
+        w_router.astype(jnp.float32).T,
+        precision=HIGHEST,
+        preferred_element_type=jnp.float32,
+    )
+    mix_pullback = jax.vjp(normalize, middle_share, mix_gains)[1]
+    middle_from_norm, mix_gain_grad = mix_pullback(mixed_grad_share)
+    middle_grad = upstream + middle_from_norm
+    middle_low = middle_grad.astype(jnp.bfloat16)
+
+    def half_back(saved, attended, joined_weights, out_weights):
+        attended_grad = dot_nt(middle_low, out_weights).astype(jnp.bfloat16)
+        joined_grads = attend_half_back(saved, attended_grad, sizes, tables, allowed, score_scale)
+        weight_grads = jnp.concatenate(
+            [dot_tn(normed, joined_grads), dot_tn(middle_low, attended)], axis=1
+        )
+        return weight_grads.astype(jnp.bfloat16), dot_nt(joined_grads, joined_weights)
+
+    other_grads, other_normed = half_back(saved_other, attended_other, joined_other, out_other)
+    own_grads, own_normed = half_back(saved_own, attended_own, joined_own, w_out)
+    attention_grads = add_low(own_grads, swap(other_grads))
+    attention_total = lax.psum_scatter(
+        attention_grads, "dp", scatter_dimension=0, tiled=True
+    ).astype(jnp.float32)
+    input_pullback = jax.vjp(normalize, inputs_share, norm_gains)[1]
+    input_from_norm, norm_gain_grad = input_pullback(other_normed + own_normed)
+    input_grad_share = middle_grad + input_from_norm
+    key_end = query_width + key_width
+    joined_end = key_end + key_width
+
+    router_total = all_sum(router_grad)
+    mix_gain_total = all_sum(mix_gain_grad)
+    norm_gain_total = all_sum(norm_gain_grad)
+
+    mine = jnp.concatenate(sums, axis=0).reshape(experts, 3, 2, depth // 2, -1)
+    theirs = flip(pick_index(mine, 1 - core, 2), 1)
+    mine = pick_index(mine, core, 2)
+    expert_total = jnp.where(
+        core == 0,
+        jnp.concatenate([mine, theirs], axis=0),
+        jnp.concatenate([theirs, mine], axis=0),
+    ).astype(jnp.float32)
+    return (
+        output_share,
+        balance,
+        input_grad_share,
+        norm_gain_total,
+        attention_total[:, :query_width],
+        attention_total[:, query_width:key_end],
+        attention_total[:, key_end:joined_end],
+        attention_total[:, joined_end:].T,
+        mix_gain_total,
+        router_total,
+        expert_total[:, 0],
+        expert_total[:, 1],
+        expert_total[:, 2].transpose(0, 2, 1),
+    )
+
+
 def solution(mesh):
+    sizes = dict(mesh.shape)
+    paired = sizes["tensor"] == 2 and sizes["dp"] == 16
     return jax.shard_map(
-        shards,
+        shards_pair if paired else shards_wide,
         mesh=mesh,
         in_specs=(
             P(("dp", "tensor"), None),

time: 3370 us -> 2090 us (0.62)
  waiting for transfers between devices: 1380 us -> 759 us
  Pallas kernels: 0 us -> 488 us
  local copies, waits for them, and re-layouts: 575 us -> 113 us
  matrix products: 752 us -> 379 us
  other arithmetic: 552 us -> 253 us
  blocking collectives: 83.5 us -> 0 us
  starting transfers between devices: 0.7 us -> 69.6 us
    reduce_scatter x12 -> x0, waiting for transfers between devices: 1110 us -> none  [the longest x1 294 us: shards(): lax.psum_scatter(gate_grad.astype(jnp.bfloat16), 'dp', scatter_dimension=...]
    ppermute x0 -> x60, waiting for transfers between devices: none -> 759 us  [the longest x46 546 us: flip(): return lax.ppermute(value, 'dp', [(i, i ^ bit) for i in range(size)])]
    pallas_call x0 -> x10, Pallas kernels: none -> 488 us  [the longest x5 218 us: expert_call(): pl.pallas_call(functools.partial(expert_kernel, first, split, depth), gri...]
    dot_general x28 -> x26, matrix products: 709 us -> 324 us  [the longest x2 88.9 us: attend_half_back(): jnp.einsum('qkgd,skd->kgqs', grad_block, value_block, preferred_element_t...]
    scatter-add x3 -> x0, other arithmetic: 342 us -> none  [the longest x1 133 us: shards(): jax.ops.segment_sum(slot_gates[:, None] * returned_flat, owners, num_segm...]
    gather x3 -> x0, local copies, waits for them, and re-layouts: 223 us -> none  [the longest x1 78.1 us: shards(): slot_upstream = padded_upstream[owners].astype(jnp.float32)]
    reshape x5 -> x4, local copies, waits for them, and re-layouts: 165 us -> 5.72 us  [the longest x1 1.75 us: placement(): inside = jnp.dot(member.astype(jnp.bfloat16).reshape(experts * tiles, BLO...]
    all_gather x4 -> x2, waiting for transfers between devices: 145 us -> 0.04 us  [the longest x1 0.02 us: shards_pair(): lax.all_gather(swap(lax.dynamic_slice_in_dim(w_out, rank * out_rows, out_...]
  transfers between devices with their start and end apart: 17 -> 63, of which waited for: 8 -> 25; matrix products, arithmetic and copies ran while one was open for 30% -> 35% of each run, Pallas kernels for 0% -> 6%
where the time goes in v1:
time: 2090 us; the launch traced here: 2080 us
  waiting for transfers between devices  759 us (36%)
  Pallas kernels  488 us (23%)
  matrix products  379 us (18%)
  other arithmetic  253 us (12%)
  local copies, waits for them, and re-layouts  113 us (5%)
  starting transfers between devices  69.6 us (3%)
    ppermute x46, waiting for transfers between devices, flip(): return lax.ppermute(value, 'dp', [(i, i ^ bit) for i in range(size)])  546 us
    pallas_call x5, Pallas kernels, expert_call(): pl.pallas_call(functools.partial(expert_kernel, first, split, depth), gri...  218 us
    ppermute x14, waiting for transfers between devices, swap(): return lax.ppermute(value, 'tensor', [(0, 1), (1, 0)])  214 us
    pallas_call x3, Pallas kernels, gather_rows(): pl.pallas_call(functools.partial(gather_kernel, count, slots, len(sources...  174 us
    pallas_call x2, Pallas kernels, combine_rows(): pl.pallas_call(functools.partial(combine_kernel, first, width), grid_spec...  95.8 us
    dot_general x2, matrix products, attend_half_back(): jnp.einsum('qkgd,skd->kgqs', grad_block, value_block, preferred_element_t...  88.9 us
    convert_element_type x1, other arithmetic, attend_half_back(): score_low = (weights_full * (weight_grad - jnp.sum(weights_full * weight_...  80.7 us
    ppermute x46, starting transfers between devices, flip(): return lax.ppermute(value, 'dp', [(i, i ^ bit) for i in range(size)])  58 us
  transfers between devices with their start and end apart: 63, of which 25 were waited for; matrix products, arithmetic and copies ran while one was open for 35% of the time, Pallas kernels for 6%

profile of v1, /device:TPU:0, one launch (start us, length us, event | category | flops | bytes accessed | tf_op | source)
XLA Modules:
  0.0 2079.0 jit_solution(9791548934358739805)
XLA Ops:
  146.4 33.6 %fusion.19 = (f32[4,3,1024]{2,1,0:T(4,128)S(1)}, f32[4,3,1024]{2,1,0:T(4,128)S(1)}, f32[4,1024,1024,3]{2,1,3,0:T(8,128)}) fusion(pred[1024,1024]{0,1:T(8,128)(4,1)S(1)} %fusion.30, f32[4,1024,1024,3]{2,1,3,0:T(8,128)} %fusion.87, bf16[1024,4,3,32]{0,3,2,1:T(8,128)(2,1)} %bitcast.365, bf16[1024,4,3,32]{0,3,2,1:T(8,128)(2,1)} %bitcast.367, ...), kind=kOutput, calls=%fused_computation.29 | convolution fusion | flops 1690279936 | bytes 103907328 | tf_op jit(solution)/shard_map/qkgd,skd->kgqs/dot_general | solution.py:78
  180.0 32.3 %fusion.7 = (f32[4,3,1024]{2,1,0:T(4,128)S(1)}, f32[4,3,1024]{2,1,0:T(4,128)S(1)}) fusion(f32[4,3,1024]{2,1,0:T(4,128)S(1)} %get-tuple-element.143, f32[4,1024,1024,3]{2,1,3,0:T(8,128)} %get-tuple-element.217, pred[1024,1024]{0,1:T(8,128)(4,1)S(1)} %fusion.30, f32[4,3,1024]{2,1,0:T(4,128)S(1)} %get-tuple-element.144, f32[4,1024,1024,3]{2,1,3,0:T(8,128)} %fusion.87), kind=kLoop, calls=%fused_computation.19 | loop fusion | flops 100638720 | bytes 101908480 | tf_op jit(solution)/shard_map/reduce_sum | solution.py:582
  240.2 21.9 %fusion.51 = bf16[4,64,3,1024]{3,1,2,0:T(8,128)(2,1)} fusion(bf16[1024,4,64,1]{0,2,3,1:T(8,128)(2,1)S(1)} %bitcast.394, f32[4,3,1024]{2,1,0:T(4,128)S(1)} %get-tuple-element.141, f32[4,3,1024]{2,1,0:T(4,128)S(1)} %get-tuple-element.143, f32[4,1024,1024,3]{2,1,3,0:T(8,128)} %get-tuple-element.217, pred[1024,1024]{0,1:T(8,128)(4,1)S(1)} %fusion.30), kind=kOutput, calls=%fused_computation.121 | convolution fusion | flops 1674313728 | bytes 53575680 | tf_op jit(solution)/shard_map/kgqs,skd->qkgd/dot_general | solution.py:584
  289.7 55.5 %collective-permute-done.3 = bf16[1024,8]{0,1:T(8,128)(2,1)S(1)} collective-permute-done((bf16[1024,8]{0,1:T(8,128)(2,1)S(1)}, bf16[1024,8]{0,1:T(8,128)(2,1)S(1)}, u32[]{:S(2)}, u32[]{:S(2)}) %collective-permute-start.3) | collective-permute-done | bytes 16416 | tf_op jit(solution)/shard_map/ppermute | solution.py:531
  345.7 82.1 %shard_map.238.c_ref = bf16[12800,1536]{1,0:T(8,128)(2,1)} custom-call(s32[10,10]{1,0:T(8,128)} %convert_reduce_fusion.2.low_ref, s32[10,10]{1,0:T(8,128)} %copy-done.99, s32[10]{0:T(128)} %copy-done.104, s32[10,16,1,256]{3,2,1,0:T(1,128)} %add_select_fusion.place_ref, bf16[1024,1536]{1,0:T(8,128)(2,1)} %rest_0_.1, ...), custom_call_target="tpu_custom_call" | custom-call | flops 48318382080 | bytes 37748736 | tf_op jit(solution)/shard_map/pallas_call | solution.py:249
  429.9 23.0 %shard_map.239 = (bf16[2560,1536]{1,0:T(8,128)(2,1)}, f32[2560,128]{1,0:T(8,128)}) custom-call(s32[2,10]{1,0:T(2,128)} %slice.287.low_ref, s32[2,10]{1,0:T(2,128)} %slice.288.high_ref, s32[2]{0:T(128)} %bitcast.416, s32[2,16,1,256]{3,2,1,0:T(1,128)} %copy.215.place_ref, f32[2,16,1,256]{3,2,1,0:T(1,128)} %slice.234.rest_0_, ...), custom_call_target="tpu_custom_call" | custom-call | flops 9663676416 | bytes 37748736 | tf_op jit(solution)/shard_map/pallas_call | solution.py:249
  452.9 46.9 %shard_map.240 = (bf16[12800,1536]{1,0:T(8,128)(2,1)}, bf16[12800,1536]{1,0:T(8,128)(2,1)}, f32[12800,128]{1,0:T(8,128)}, bf16[2,3,4,192,512]{4,3,2,1,0:T(8,128)(2,1)}, bf16[2,3,4,192,512]{4,3,2,1,0:T(8,128)(2,1)}) custom-call(s32[10]{0:T(128)} %copy-done.104, s32[2]{0:T(128)} %pad_add_fusion.1.misc_ref, bf16[2560,1536]{1,0:T(8,128)(2,1)} %get-tuple-element.50.x_ref, ...), custom_call_target="tpu_custom_call" | custom-call | flops 23215472640 | bytes 39026688 | tf_op jit(solution)/shard_map/pallas_call | solution.py:394
  499.8 68.7 %shard_map.237 = (bf16[10240,1536]{1,0:T(8,128)(2,1)}, f32[10240,128]{1,0:T(8,128)}) custom-call(s32[8,10]{1,0:T(8,128)} %slice.283.low_ref, s32[8,10]{1,0:T(8,128)} %slice.284.high_ref, s32[8]{0:T(128)} %slice.223.blocks_ref, s32[8,16,1,256]{3,2,1,0:T(1,128)} %copy.213.place_ref, f32[8,16,1,256]{3,2,1,0:T(1,128)} %slice.227.rest_0_, ...), custom_call_target="tpu_custom_call" | custom-call | flops 38654705664 | bytes 37748736 | tf_op jit(solution)/shard_map/pallas_call | solution.py:249
  568.5 46.3 %shard_map.241 = (bf16[12800,1536]{1,0:T(8,128)(2,1)}, bf16[12800,1536]{1,0:T(8,128)(2,1)}, f32[12800,128]{1,0:T(8,128)}, bf16[2,3,4,192,512]{4,3,2,1,0:T(8,128)(2,1)}, bf16[2,3,4,192,512]{4,3,2,1,0:T(8,128)(2,1)}) custom-call(s32[10]{0:T(128)} %copy-done.104, s32[2]{0:T(128)} %pad_add_fusion.1.misc_ref, ...), custom_call_target="tpu_custom_call", output_to_operand_aliasing={{0}: (8, {}), {1}: (9, {}), {2}: (10, {})} | custom-call | flops 23215472640 | bytes 39026688 | tf_op jit(solution)/shard_map/pallas_call | solution.py:394
  614.8 35.2 %shard_map.242 = (bf16[12800,1536]{1,0:T(8,128)(2,1)}, bf16[12800,1536]{1,0:T(8,128)(2,1)}, f32[12800,128]{1,0:T(8,128)}, bf16[2,3,4,192,512]{4,3,2,1,0:T(8,128)(2,1)}, bf16[2,3,4,192,512]{4,3,2,1,0:T(8,128)(2,1)}) custom-call(s32[10]{0:T(128)} %copy-done.104, s32[2]{0:T(128)} %pad_add_fusion.1.misc_ref, ...), custom_call_target="tpu_custom_call", output_to_operand_aliasing={{0}: (8, {}), {1}: (9, {}), {2}: (10, {})} | custom-call | flops 23215472640 | bytes 39026688 | tf_op jit(solution)/shard_map/pallas_call | solution.py:394
  649.9 46.8 %shard_map.243 = (bf16[12800,1536]{1,0:T(8,128)(2,1)}, bf16[12800,1536]{1,0:T(8,128)(2,1)}, f32[12800,128]{1,0:T(8,128)}, bf16[2,3,4,192,512]{4,3,2,1,0:T(8,128)(2,1)}, bf16[2,3,4,192,512]{4,3,2,1,0:T(8,128)(2,1)}) custom-call(s32[10]{0:T(128)} %copy-done.104, s32[2]{0:T(128)} %pad_add_fusion.1.misc_ref, ...), custom_call_target="tpu_custom_call", output_to_operand_aliasing={{0}: (8, {}), {1}: (9, {}), {2}: (10, {})} | custom-call | flops 23215472640 | bytes 39026688 | tf_op jit(solution)/shard_map/pallas_call | solution.py:394
  696.7 43.2 %shard_map.244 = (bf16[12800,1536]{1,0:T(8,128)(2,1)}, bf16[12800,1536]{1,0:T(8,128)(2,1)}, f32[12800,128]{1,0:T(8,128)}, bf16[2,3,4,192,512]{4,3,2,1,0:T(8,128)(2,1)}, bf16[2,3,4,192,512]{4,3,2,1,0:T(8,128)(2,1)}) custom-call(s32[10]{0:T(128)} %copy-done.104, s32[2]{0:T(128)} %pad_add_fusion.1.misc_ref, ...), custom_call_target="tpu_custom_call", output_to_operand_aliasing={{0}: (8, {}), {1}: (9, {}), {2}: (10, {})} | custom-call | flops 23215472640 | bytes 39026688 | tf_op jit(solution)/shard_map/pallas_call | solution.py:394
  740.0 48.9 %shard_map.246 = (bf16[2048,1536]{1,0:T(8,128)(2,1)}, bf16[2048,1536]{1,0:T(8,128)(2,1)}, f32[11,8,1,256]{3,2,1,0:T(1,128)}) custom-call(s32[16,52]{1,0:T(8,128)} %convert_reduce_fusion.3.owner_ref, s32[16,52]{1,0:T(8,128)} %get-tuple-element.211.piece_ref, s32[16,52]{1,0:T(8,128)} %get-tuple-element.210.source_ref, s32[16]{0:T(128)} %get-tuple-element.152.groups_ref, ...), custom_call_target="tpu_custom_call" | custom-call | flops 16106127360 | bytes 62914560 | tf_op jit(solution)/shard_map/pallas_call | solution.py:490
  812.9 47.0 %shard_map.245 = (bf16[2048,1536]{1,0:T(8,128)(2,1)}, bf16[2048,1536]{1,0:T(8,128)(2,1)}, f32[11,8,1,256]{3,2,1,0:T(1,128)}) custom-call(s32[16,52]{1,0:T(8,128)} %convert_reduce_fusion.3.owner_ref, s32[16,52]{1,0:T(8,128)} %get-tuple-element.211.piece_ref, s32[16,52]{1,0:T(8,128)} %get-tuple-element.210.source_ref, s32[16]{0:T(128)} %get-tuple-element.152.groups_ref, ...), custom_call_target="tpu_custom_call" | custom-call | flops 16106127360 | bytes 62914560 | tf_op jit(solution)/shard_map/pallas_call | solution.py:490
  870.5 246.6 %collective-permute-done.15 = f32[40]{0:T(128)S(1)} collective-permute-done((f32[40]{0:T(128)S(1)}, f32[40]{0:T(128)S(1)}, u32[]{:S(2)}, u32[]{:S(2)}) %collective-permute-start.15) | collective-permute-done | bytes 192 | tf_op jit(solution)/shard_map/ppermute | solution.py:527
  1253.5 68.2 %fusion.3 = (f32[4,3,1024]{2,1,0:T(4,128)}, f32[4,3,1024]{2,1,0:T(4,128)}, f32[4,1024,1024,3]{2,1,3,0:T(8,128)}) fusion(f32[4,3,1024]{2,1,0:T(4,128)S(1)} %get-tuple-element.226, f32[4,1024,1024,3]{2,1,3,0:T(8,128)} %get-tuple-element.217, pred[1024,1024]{0,1:T(8,128)(4,1)S(1)} %copy-done.2, f32[4,1024,1024,3]{2,1,3,0:T(8,128)} %fusion.156, ...), kind=kOutput, calls=%fused_computation.7 | convolution fusion | flops 1736417280 | bytes 204668928 | tf_op jit(solution)/shard_map/qkgd,skd->kgqs/dot_general | solution.py:603
  1321.7 80.7 %fusion.5 = (bf16[4,3,1024,1024]{2,3,1,0:T(8,128)(2,1)}, bf16[4,3,1024,1024]{2,3,1,0:T(8,128)(2,1)}) fusion(f32[4,1024,1024,3]{2,1,3,0:T(8,128)} %get-tuple-element.223, f32[4,3,1024]{2,1,0:T(4,128)} %get-tuple-element.139, f32[4,3,1024]{2,1,0:T(4,128)S(1)} %get-tuple-element.226, f32[4,1024,1024,3]{2,1,3,0:T(8,128)} %get-tuple-element.217, ...), kind=kLoop, calls=%fused_computation.9 | loop fusion | flops 150994944 | bytes 252903424 | tf_op jit(solution)/shard_map/convert_element_type | solution.py:608
  1465.9 21.9 %fusion.67 = bf16[4,64,1024]{2,1,0:T(8,128)(2,1)} fusion(bf16[1024,4,3,64]{0,3,2,1:T(8,128)(2,1)} %bitcast.390, f32[4,3,1024]{2,1,0:T(4,128)S(1)} %get-tuple-element.226, f32[4,1024,1024,3]{2,1,3,0:T(8,128)} %get-tuple-element.217, pred[1024,1024]{0,1:T(8,128)(4,1)S(1)} %copy-done.2), kind=kOutput, calls=%fused_computation.151 | convolution fusion | flops 1661206528 | bytes 53526528 | tf_op jit(solution)/shard_map/kgqs,qkgd->skd/dot_general | solution.py:600
  1517.3 22.0 %fusion.64 = bf16[4,64,1024]{2,1,0:T(8,128)(2,1)} fusion(bf16[1024,4,3,64]{0,3,2,1:T(8,128)(2,1)} %bitcast.396, f32[4,3,1024]{2,1,0:T(4,128)S(1)} %get-tuple-element.225, f32[4,1024,1024,3]{2,1,3,0:T(8,128)} %fusion.87, pred[1024,1024]{0,1:T(8,128)(4,1)S(1)} %copy-done.2), kind=kOutput, calls=%fused_computation.150 | convolution fusion | flops 1661206528 | bytes 53526528 | tf_op jit(solution)/shard_map/kgqs,qkgd->skd/dot_general | solution.py:600
  1551.4 83.8 %collective-permute-done.33 = bf16[1536,2048]{0,1:T(8,128)(2,1)} collective-permute-done((bf16[1536,2048]{0,1:T(8,128)(2,1)}, bf16[1536,2048]{0,1:T(8,128)(2,1)}, u32[]{:S(2)}, u32[]{:S(2)}) %collective-permute-start.33) | collective-permute-done | bytes 6291488 | tf_op jit(solution)/shard_map/ppermute | solution.py:531
  1671.0 60.1 %collective-permute-done.51 = bf16[2,3,2,192,512]{4,3,1,0,2:T(8,128)(2,1)} collective-permute-done((bf16[2,3,2,192,512]{4,3,1,0,2:T(8,128)(2,1)}, bf16[2,3,2,192,512]{4,3,1,0,2:T(8,128)(2,1)}, u32[]{:S(2)}, u32[]{:S(2)}) %collective-permute-start.51) | collective-permute-done | bytes 2359328 | tf_op jit(solution)/shard_map/ppermute | solution.py:527
  1741.2 140.5 %collective-permute-done.46 = bf16[2,3,192,512]{3,2,1,0:T(8,128)(2,1)S(1)} collective-permute-done((bf16[2,3,192,512]{3,2,1,0:T(8,128)(2,1)S(1)}, bf16[2,3,192,512]{3,2,1,0:T(8,128)(2,1)S(1)}, u32[]{:S(2)}, u32[]{:S(2)}) %collective-permute-start.46) | collective-permute-done | bytes 1179680 | tf_op jit(solution)/shard_map/ppermute | solution.py:527
  1885.8 68.5 %collective-permute-done.52 = bf16[2,3,192,512]{3,2,1,0:T(8,128)(2,1)S(1)} collective-permute-done((bf16[2,3,192,512]{3,2,1,0:T(8,128)(2,1)}, bf16[2,3,192,512]{3,2,1,0:T(8,128)(2,1)S(1)}, u32[]{:S(2)}, u32[]{:S(2)}) %collective-permute-start.52) | collective-permute-done | bytes 1179680 | tf_op jit(solution)/shard_map/ppermute | solution.py:527
  1990.4 31.2 %collective-permute-done.23 = f32[40]{0:T(128)S(1)} collective-permute-done((f32[40]{0:T(128)S(1)}, f32[40]{0:T(128)S(1)}, u32[]{:S(2)}, u32[]{:S(2)}) %collective-permute-start.23) | collective-permute-done | bytes 192 | tf_op jit(solution)/shard_map/ppermute | solution.py:531
  (598 shorter events, 607.2 us)
Async XLA Ops:
  24.3 237.8 %all-gather.5.cloned.1.call-start = ((), (), s32[]{:S(2)}) async-start(), calls=%async_computation.2 | async-start | bytes 2506752 | tf_op jit(solution)/shard_map/all_gather | solution.py:1023
  24.3 264.8 %collective-permute-start.10 = (bf16[1024,1536]{1,0:T(8,128)(2,1)}, bf16[1024,1536]{1,0:T(8,128)(2,1)}, u32[]{:S(2)}, u32[]{:S(2)}) collective-permute-start(bf16[1024,1536]{1,0:T(8,128)(2,1)} %rest_0_.1), channel_id=1, source_target_pairs={{0,2},{2,0},{4,6},{6,4},{8,10},{10,8},{12,14},{14,12},{16,18},{18,... | collective-permute-start | bytes 9437192 | tf_op jit(solution)/shard_map/ppermute | solution.py:527
  98.4 1967.2 %reduce-scatter.4.cloned.1.call-start = ((), (), s32[]{:S(2)}) async-start(), calls=%async_computation.3 | async-start | bytes 6684672
  98.5 247.2 %collective-permute-start.11 = (bf16[1024,1536]{1,0:T(8,128)(2,1)}, bf16[1024,1536]{1,0:T(8,128)(2,1)}, u32[]{:S(2)}, u32[]{:S(2)}) collective-permute-start(bf16[1024,1536]{1,0:T(8,128)(2,1)} %collective-permute-done.9.rest_1_), channel_id=1, source_target_pairs={{0,2},{2,0},{4,6},{6,4},{8,10},{10,8},{12,14},{14,12},{16,18},{18,... | collective-permute-start | bytes 9437192 | tf_op jit(solution)/shard_map/ppermute | solution.py:527
  289.2 138.7 %collective-permute-start.4 = (bf16[1024,8]{0,1:T(8,128)(2,1)S(1)}, bf16[1024,8]{0,1:T(8,128)(2,1)S(1)}, u32[]{:S(2)}, u32[]{:S(2)}) collective-permute-start(bf16[1024,8]{0,1:T(8,128)(2,1)S(1)} %fusion.139), channel_id=1, source_target_pairs={{0,2},{2,0},{4,6},{6,4},{8,10},{10,8},{12,14},{14,12},{16,18},{18,... | collective-permute-start | bytes 49160 | tf_op jit(solution)/shard_map/ppermute | solution.py:527
  289.2 140.7 %collective-permute-start.7 = (bf16[1024,1536]{1,0:T(8,128)(2,1)}, bf16[1024,1536]{1,0:T(8,128)(2,1)}, u32[]{:S(2)}, u32[]{:S(2)}) collective-permute-start(bf16[1024,1536]{1,0:T(8,128)(2,1)} %multiply_convert_fusion.rest_1_), channel_id=1, source_target_pairs={{0,2},{2,0},{4,6},{6,4},{8,10},{10,8},{12,14},{14,12},{16,18},{18,... | collective-permute-start | bytes 9437192 | tf_op jit(solution)/shard_map/ppermute | solution.py:527
  788.8 344.8 %collective-permute-start.24 = (bf16[2048,1536]{1,0:T(8,128)(2,1)}, bf16[2048,1536]{1,0:T(8,128)(2,1)}, u32[]{:S(2)}, u32[]{:S(2)}) collective-permute-start(bf16[2048,1536]{1,0:T(8,128)(2,1)} %get-tuple-element.70), channel_id=1, source_target_pairs={{0,2},{2,0},{4,6},{6,4},{8,10},{10,8},{12,14},{14,12},{16,18},{18,... | collective-permute-start | bytes 18874376 | tf_op jit(solution)/shard_map/ppermute | solution.py:527
  810.7 364.6 %collective-permute-start.44 = (bf16[2,3,4,192,512]{4,3,2,1,0:T(8,128)(2,1)}, bf16[2,3,4,192,512]{4,3,2,1,0:T(8,128)(2,1)}, u32[]{:S(2)}, u32[]{:S(2)}) collective-permute-start(bf16[2,3,4,192,512]{4,3,2,1,0:T(8,128)(2,1)} %get-tuple-element.74), channel_id=1, source_target_pairs={{0,4},{2,6},{4,0},{6,2},{8,12},{10,14},{12,8},{14,10},{16,20},{18,... | collective-permute-start | bytes 14155784 | tf_op jit(solution)/shard_map/ppermute | solution.py:527
  810.9 366.2 %collective-permute-start.47 = (bf16[2,3,4,192,512]{4,3,2,1,0:T(8,128)(2,1)}, bf16[2,3,4,192,512]{4,3,2,1,0:T(8,128)(2,1)}, u32[]{:S(2)}, u32[]{:S(2)}) collective-permute-start(bf16[2,3,4,192,512]{4,3,2,1,0:T(8,128)(2,1)} %get-tuple-element.76), channel_id=1, source_target_pairs={{0,4},{2,6},{4,0},{6,2},{8,12},{10,14},{12,8},{14,10},{16,20},{18,... | collective-permute-start | bytes 14155784 | tf_op jit(solution)/shard_map/ppermute | solution.py:527
  859.9 327.0 %collective-permute-start.56 = (bf16[2,3,4,192,512]{4,3,2,1,0:T(8,128)(2,1)}, bf16[2,3,4,192,512]{4,3,2,1,0:T(8,128)(2,1)}, u32[]{:S(2)}, u32[]{:S(2)}) collective-permute-start(bf16[2,3,4,192,512]{4,3,2,1,0:T(8,128)(2,1)} %get-tuple-element.82), channel_id=1, source_target_pairs={{0,4},{2,6},{4,0},{6,2},{8,12},{10,14},{12,8},{14,10},{16,20},{18,... | collective-permute-start | bytes 14155784 | tf_op jit(solution)/shard_map/ppermute | solution.py:527
  868.5 248.6 %collective-permute-start.15 = (f32[40]{0:T(128)S(1)}, f32[40]{0:T(128)S(1)}, u32[]{:S(2)}, u32[]{:S(2)}) collective-permute-start(f32[40]{0:T(128)S(1)} %add.508), channel_id=1, source_target_pairs={{0,4},{2,6},{4,0},{6,2},{8,12},{10,14},{12,8},{14,10},{16,20},{18,... | collective-permute-start | bytes 488 | tf_op jit(solution)/shard_map/ppermute | solution.py:527
  1174.3 323.7 %collective-permute-start.50 = (bf16[2,3,4,192,512]{4,3,2,1,0:T(8,128)(2,1)}, bf16[2,3,4,192,512]{4,3,2,1,0:T(8,128)(2,1)}, u32[]{:S(2)}, u32[]{:S(2)}) collective-permute-start(bf16[2,3,4,192,512]{4,3,2,1,0:T(8,128)(2,1)} %get-tuple-element.78), channel_id=1, source_target_pairs={{0,4},{2,6},{4,0},{6,2},{8,12},{10,14},{12,8},{14,10},{16,20},{18,... | collective-permute-start | bytes 14155784 | tf_op jit(solution)/shard_map/ppermute | solution.py:527
  1175.3 322.7 %collective-permute-start.53 = (bf16[2,3,4,192,512]{4,3,2,1,0:T(8,128)(2,1)}, bf16[2,3,4,192,512]{4,3,2,1,0:T(8,128)(2,1)}, u32[]{:S(2)}, u32[]{:S(2)}) collective-permute-start(bf16[2,3,4,192,512]{4,3,2,1,0:T(8,128)(2,1)} %get-tuple-element.80), channel_id=1, source_target_pairs={{0,4},{2,6},{4,0},{6,2},{8,12},{10,14},{12,8},{14,10},{16,20},{18,... | collective-permute-start | bytes 14155784 | tf_op jit(solution)/shard_map/ppermute | solution.py:527
  1177.1 558.4 %collective-permute-start.12 = (bf16[2048,1536]{1,0:T(8,128)(2,1)}, bf16[2048,1536]{1,0:T(8,128)(2,1)}, u32[]{:S(2)}, u32[]{:S(2)}) collective-permute-start(bf16[2048,1536]{1,0:T(8,128)(2,1)} %get-tuple-element.68), channel_id=1, source_target_pairs={{0,2},{2,0},{4,6},{6,4},{8,10},{10,8},{12,14},{14,12},{16,18},{18,... | collective-permute-start | bytes 18874376 | tf_op jit(solution)/shard_map/ppermute | solution.py:527
  1186.9 359.7 %collective-permute-start.48 = (bf16[2,3,2,192,512]{4,3,1,0,2:T(8,128)(2,1)}, bf16[2,3,2,192,512]{4,3,1,0,2:T(8,128)(2,1)}, u32[]{:S(2)}, u32[]{:S(2)}) collective-permute-start(bf16[2,3,2,192,512]{4,3,1,0,2:T(8,128)(2,1)} %fusion.32), channel_id=1, source_target_pairs={{0,8},{2,10},{4,12},{6,14},{8,0},{10,2},{12,4},{14,6},{16,24},{18,... | collective-permute-start | bytes 7077896 | tf_op jit(solution)/shard_map/ppermute | solution.py:527
  1208.9 453.2 %collective-permute-start.45 = (bf16[2,3,2,192,512]{4,3,1,0,2:T(8,128)(2,1)}, bf16[2,3,2,192,512]{4,3,1,0,2:T(8,128)(2,1)}, u32[]{:S(2)}, u32[]{:S(2)}) collective-permute-start(bf16[2,3,2,192,512]{4,3,1,0,2:T(8,128)(2,1)} %fusion.31), channel_id=1, source_target_pairs={{0,8},{2,10},{4,12},{6,14},{8,0},{10,2},{12,4},{14,6},{16,24},{18,... | collective-permute-start | bytes 7077896 | tf_op jit(solution)/shard_map/ppermute | solution.py:527
  1498.0 166.2 %collective-permute-start.57 = (bf16[2,3,2,192,512]{4,3,2,1,0:T(8,128)(2,1)}, bf16[2,3,2,192,512]{4,3,2,1,0:T(8,128)(2,1)}, u32[]{:S(2)}, u32[]{:S(2)}) collective-permute-start(bf16[2,3,2,192,512]{4,3,2,1,0:T(8,128)(2,1)} %fusion.35), channel_id=1, source_target_pairs={{0,8},{2,10},{4,12},{6,14},{8,0},{10,2},{12,4},{14,6},{16,24},{18,... | collective-permute-start | bytes 7077896 | tf_op jit(solution)/shard_map/ppermute | solution.py:527
  1498.0 137.2 %collective-permute-start.33 = (bf16[1536,2048]{0,1:T(8,128)(2,1)}, bf16[1536,2048]{0,1:T(8,128)(2,1)}, u32[]{:S(2)}, u32[]{:S(2)}) collective-permute-start(bf16[1536,2048]{0,1:T(8,128)(2,1)} %pad_maximum_fusion), channel_id=1, source_target_pairs={{0,1},{1,0},{2,3},{3,2},{4,5},{5,4},{6,7},{7,6},{8,9},{9,8},{10,11... | collective-permute-start | bytes 18874376 | tf_op jit(solution)/shard_map/ppermute | solution.py:531
  1662.1 221.3 %collective-permute-start.49 = (bf16[2,3,192,512]{3,2,1,0:T(8,128)(2,1)S(1)}, bf16[2,3,192,512]{3,2,1,0:T(8,128)(2,1)S(1)}, u32[]{:S(2)}, u32[]{:S(2)}) collective-permute-start(bf16[2,3,192,512]{3,2,1,0:T(8,128)(2,1)S(1)} %fusion.75), channel_id=1, source_target_pairs={{0,16},{2,18},{4,20},{6,22},{8,24},{10,26},{12,28},{14,30},{16,0},... | collective-permute-start | bytes 3538952 | tf_op jit(solution)/shard_map/ppermute | solution.py:527
  1664.2 217.4 %collective-permute-start.46 = (bf16[2,3,192,512]{3,2,1,0:T(8,128)(2,1)S(1)}, bf16[2,3,192,512]{3,2,1,0:T(8,128)(2,1)S(1)}, u32[]{:S(2)}, u32[]{:S(2)}) collective-permute-start(bf16[2,3,192,512]{3,2,1,0:T(8,128)(2,1)S(1)} %fusion.72), channel_id=1, source_target_pairs={{0,16},{2,18},{4,20},{6,22},{8,24},{10,26},{12,28},{14,30},{16,0},... | collective-permute-start | bytes 3538952 | tf_op jit(solution)/shard_map/ppermute | solution.py:527
  1668.7 289.7 %collective-permute-start.58 = (bf16[2,3,192,512]{3,2,1,0:T(8,128)(2,1)S(1)}, bf16[2,3,192,512]{3,2,1,0:T(8,128)(2,1)S(1)}, u32[]{:S(2)}, u32[]{:S(2)}) collective-permute-start(bf16[2,3,192,512]{3,2,1,0:T(8,128)(2,1)S(1)} %fusion.84), channel_id=1, source_target_pairs={{0,16},{2,18},{4,20},{6,22},{8,24},{10,26},{12,28},{14,30},{16,0},... | collective-permute-start | bytes 3538952 | tf_op jit(solution)/shard_map/ppermute | solution.py:527
  1731.2 225.4 %collective-permute-start.55 = (bf16[2,3,192,512]{3,2,1,0:T(8,128)(2,1)S(1)}, bf16[2,3,192,512]{3,2,1,0:T(8,128)(2,1)S(1)}, u32[]{:S(2)}, u32[]{:S(2)}) collective-permute-start(bf16[2,3,192,512]{3,2,1,0:T(8,128)(2,1)S(1)} %fusion.81), channel_id=1, source_target_pairs={{0,16},{2,18},{4,20},{6,22},{8,24},{10,26},{12,28},{14,30},{16,0},... | collective-permute-start | bytes 3538952 | tf_op jit(solution)/shard_map/ppermute | solution.py:527
  1735.5 218.8 %collective-permute-start.52 = (bf16[2,3,192,512]{3,2,1,0:T(8,128)(2,1)}, bf16[2,3,192,512]{3,2,1,0:T(8,128)(2,1)S(1)}, u32[]{:S(2)}, u32[]{:S(2)}) collective-permute-start(bf16[2,3,192,512]{3,2,1,0:T(8,128)(2,1)} %fusion.78), channel_id=1, source_target_pairs={{0,16},{2,18},{4,20},{6,22},{8,24},{10,26},{12,28},{14,30},{16,0},... | collective-permute-start | bytes 3538952 | tf_op jit(solution)/shard_map/ppermute | solution.py:527
  1883.5 138.6 %collective-permute-start.43 = (f32[1536,40]{0,1:T(8,128)S(1)}, f32[1536,40]{0,1:T(8,128)S(1)}, u32[]{:S(2)}, u32[]{:S(2)}) collective-permute-start(f32[1536,40]{0,1:T(8,128)S(1)} %copy-done.50), channel_id=1, source_target_pairs={{0,1},{1,0},{2,3},{3,2},{4,5},{5,4},{6,7},{7,6},{8,9},{9,8},{10,11... | collective-permute-start | bytes 737288 | tf_op jit(solution)/shard_map/ppermute | solution.py:531
  (173 other events, 5142.7 us)
Sparse Core Ops, SparseCore 0:
  24.4 50.3 all-gather.2
  98.6 43.7 all-gather.4
  1653.3 224.0 reduce-scatter.3

commit v2 on v1

--- a/solution.py
+++ b/solution.py
@@ -82,10 +82,15 @@
 
 
 BLOCK = 256
-PART = 128
+PART = 256
 PIECE_ROWS = 64
 GROUP = BLOCK // PIECE_ROWS
 VMEM_LIMIT = 60 * 1024 * 1024
+COST = 0.6
+
+
+def cost(micros):
+    return pl.CostEstimate(flops=0, bytes_accessed=int(micros * 3e6), transcendentals=0)
 
 
 def dot_nt(left, right):
@@ -166,11 +171,11 @@
 
 
 def gather_kernel(
-    experts, slots, sources, with_gates, low_ref, high_ref, blocks_ref, place_ref, *rest
+    experts, slots, sources, with_gates, after, low_ref, high_ref, blocks_ref, place_ref, *rest
 ):
     if with_gates:
         gates_ref, rest = rest[0], rest[1:]
-    inputs, rest = rest[:sources], rest[sources:]
+    inputs, rest = rest[:sources], rest[sources + after :]
     if with_gates:
         out_ref, gate_out_ref, rest = rest[0], rest[1], rest[2:]
     else:
@@ -220,7 +225,7 @@
             gate_out_ref[...] = gate_total[...]
 
 
-def gather_rows(tables, place, gates, sources, slots, first, count):
+def gather_rows(tables, place, gates, sources, slots, first, count, after=()):
     low, high, blocks = tables
     low, high, blocks = (t[first : first + count] for t in (low, high, blocks))
     place = place[first : first + count]
@@ -240,14 +245,16 @@
         return pl.BlockSpec(array.shape, lambda *_: zeros)
 
     operands = [place] + ([gates] if with_gates else [])
-    in_specs = [whole(a) for a in operands] + [pl.BlockSpec(memory_space=pl.ANY)] * len(sources)
+    in_specs = [whole(a) for a in operands] + [pl.BlockSpec(memory_space=pl.ANY)] * (
+        len(sources) + len(after)
+    )
     out_shape = [jax.ShapeDtypeStruct((count * slots, width), jnp.bfloat16)]
     out_specs = [pl.BlockSpec((PART, width), out_index)]
     if with_gates:
         out_shape.append(jax.ShapeDtypeStruct((count * slots, 128), jnp.float32))
         out_specs.append(pl.BlockSpec((PART, 128), out_index))
     return pl.pallas_call(
-        functools.partial(gather_kernel, count, slots, len(sources), with_gates),
+        functools.partial(gather_kernel, count, slots, len(sources), with_gates, len(after)),
         grid_spec=pltpu.PrefetchScalarGridSpec(
             num_scalar_prefetch=3,
             grid=(count, parts),
@@ -262,19 +269,16 @@
         ),
         out_shape=out_shape,
         compiler_params=pltpu.CompilerParams(vmem_limit_bytes=VMEM_LIMIT),
-        cost_estimate=pl.CostEstimate(
-            flops=count * rows * 6 * PART * width, bytes_accessed=rows * width * 6, transcendentals=0
-        ),
-    )(low, high, blocks, *operands, *sources)
+        cost_estimate=cost(COST * count * 5.5),
+    )(low, high, blocks, *operands, *sources, *after)
 
 
 def expert_kernel(
-    first, split, depth, blocks_ref, misc_ref, x_ref, c_ref, sg_ref, wg_ref, wu_ref, wd_ref, *rest
+    first, split, depth, far_first, extra, blocks_ref, misc_ref, x_ref, c_ref, sg_ref, wg_ref, wu_ref, wd_ref, *rest
 ):
-    if len(rest) == 3 + (2 if split else 1) + 2 + 3:
-        rest = rest[3:]
-    y_ref, dx_ref, gg_ref = rest[:3]
-    rest = rest[3:]
+    yd_ref, gg_ref = rest[extra : extra + 2]
+    rest = rest[extra + 2 :]
+    width = x_ref.shape[1]
     if split:
         send_ref, keep_ref = rest[:2]
         rest = rest[2:]
@@ -304,16 +308,16 @@
         gate_grad = jnp.sum(activated * pulled, axis=1, keepdims=True)
         gg_ref[...] = jnp.broadcast_to(gate_grad, gg_ref.shape)
         gated = (gate * activated).astype(jnp.bfloat16)
-        y_ref[...] = jnp.dot(gated, wd_ref[0], preferred_element_type=jnp.float32).astype(
-            y_ref.dtype
-        )
+        yd_ref[:, :width] = jnp.dot(
+            gated, wd_ref[0], preferred_element_type=jnp.float32
+        ).astype(yd_ref.dtype)
         activated_grad = gate * pulled
         gate_low = (
             activated_grad * up_proj * sigmoid * (1.0 + gate_proj * (1.0 - sigmoid))
         ).astype(jnp.bfloat16)
         up_low = (activated_grad * silu).astype(jnp.bfloat16)
-        dx_ref[...] = (dot_nt(gate_low, wg_ref[0]) + dot_nt(up_low, wu_ref[0])).astype(
-            dx_ref.dtype
+        yd_ref[:, width:] = (dot_nt(gate_low, wg_ref[0]) + dot_nt(up_low, wu_ref[0])).astype(
+            yd_ref.dtype
         )
         total_gu[...] += dot_tn(x, jnp.concatenate([gate_low, up_low], axis=1))
         total_d[...] += dot_tn(c, gated)
@@ -327,18 +331,22 @@
         )
         for which, (ref, column) in enumerate(parts):
             if split:
-                side = misc_ref[1]
-                for index in range(keep_ref.shape[2]):
-                    for out, chosen in ((keep_ref, side), (send_ref, 1 - side)):
-                        start = pl.multiple_of((2 * index + chosen) * depth, 64)
-                        out[0, which, index] = ref[
-                            pl.ds(start, depth), pl.ds(column, hidden)
-                        ].astype(out.dtype)
+                side = misc_ref[1 + far_first]
+                for high in range(2):
+                    for low in range(2):
+                        for out, chosen in ((keep_ref, side), (send_ref, 1 - side)):
+                            middle, last = (chosen, low) if far_first else (low, chosen)
+                            start = ((high * 2 + middle) * 2 + last) * depth
+                            out[0, which, high, low] = ref[
+                                pl.ds(pl.multiple_of(start, 64), depth), pl.ds(column, hidden)
+                            ].astype(out.dtype)
             else:
                 grads_ref[0, which] = ref[:, pl.ds(column, hidden)].astype(grads_ref.dtype)
 
 
-def expert_call(blocks, misc, x, c, sg, weights, carried, slots, first, count, x_first, c_first, depth):
+def expert_call(
+    blocks, misc, x, c, sg, weights, carried, slots, first, count, x_first, c_first, depth, far_first=0, after=()
+):
     w_gate, w_up, w_down = weights
     experts = blocks.shape[0]
     width = x.shape[1]
@@ -357,22 +365,19 @@
         return (misc[0] + first + expert, 0, 0)
 
     def grads_index(expert, block, blocks, misc):
-        return (expert, 0, 0, 0, 0)
+        return (expert, 0, 0, 0, 0, 0)
 
     out_shape = [
-        jax.ShapeDtypeStruct((experts * slots, width), jnp.bfloat16),
-        jax.ShapeDtypeStruct((experts * slots, width), jnp.bfloat16),
+        jax.ShapeDtypeStruct((experts * slots, 2 * width), jnp.bfloat16),
         jax.ShapeDtypeStruct((experts * slots, 128), jnp.float32),
     ]
     out_specs = [
-        pl.BlockSpec((BLOCK, width), rows_index(0)),
-        pl.BlockSpec((BLOCK, width), rows_index(0)),
+        pl.BlockSpec((BLOCK, 2 * width), rows_index(0)),
         pl.BlockSpec((BLOCK, 128), rows_index(0)),
     ]
     if split:
-        cuts = width // depth // 2
-        out_shape += [jax.ShapeDtypeStruct((count, 3, cuts, depth, hidden), jnp.bfloat16)] * 2
-        out_specs += [pl.BlockSpec((1, 3, cuts, depth, hidden), grads_index)] * 2
+        out_shape += [jax.ShapeDtypeStruct((count, 3, 2, 2, depth, hidden), jnp.bfloat16)] * 2
+        out_specs += [pl.BlockSpec((1, 3, 2, 2, depth, hidden), grads_index)] * 2
     else:
         out_shape += [jax.ShapeDtypeStruct((count, 3, width, hidden), jnp.bfloat16)]
         out_specs += [pl.BlockSpec((1, 3, width, hidden), lambda e, b, *_: (e, 0, 0, 0))]
@@ -388,11 +393,12 @@
     aliases = {}
     if carried is not None:
         operands += list(carried)
-        in_specs += [pl.BlockSpec(memory_space=pl.ANY)] * 3
-        aliases = {8: 0, 9: 1, 10: 2}
-    rows = count * 820
+        aliases = {8: 0, 9: 1}
+    operands += list(after)
+    extra = len(operands) - 6
+    in_specs += [pl.BlockSpec(memory_space=pl.ANY)] * extra
     return pl.pallas_call(
-        functools.partial(expert_kernel, first, split, depth),
+        functools.partial(expert_kernel, first, split, depth, far_first, extra),
         grid_spec=pltpu.PrefetchScalarGridSpec(
             num_scalar_prefetch=2,
             grid=(count, most),
@@ -406,18 +412,15 @@
         out_shape=out_shape,
         input_output_aliases=aliases,
         compiler_params=pltpu.CompilerParams(vmem_limit_bytes=VMEM_LIMIT),
-        cost_estimate=pl.CostEstimate(
-            flops=18 * rows * width * hidden,
-            bytes_accessed=8 * rows * width + 12 * count * width * hidden,
-            transcendentals=rows * hidden,
-        ),
+        cost_estimate=cost(COST * count * 21.0),
     )(blocks, misc, *operands)
 
 
 def combine_kernel(
-    first, width, owner_ref, piece_ref, source_ref, groups_ref, begin_ref, place_ref, y_ref, dx_ref,
-    gg_ref, y_out, dx_out, gate_out, y_buf, dx_buf, gg_buf, y_total, dx_total, sems,
+    first, owner_ref, piece_ref, source_ref, groups_ref, begin_ref, place_ref, yd_ref, gg_ref, *rest
 ):
+    y_out, dx_out, gate_out, yd_buf, gg_buf, total, sems = rest[-7:]
+    columns = y_out.shape[1]
     step = pl.program_id(0)
     tile = first + step
 
@@ -427,7 +430,7 @@
             source = pl.multiple_of(
                 source_ref[which_tile, group * GROUP + i] * PIECE_ROWS, PIECE_ROWS
             )
-            for kind, (ref, buf) in enumerate(((y_ref, y_buf), (dx_ref, dx_buf), (gg_ref, gg_buf))):
+            for kind, (ref, buf) in enumerate(((yd_ref, yd_buf), (gg_ref, gg_buf))):
                 made.append(
                     pltpu.make_async_copy(
                         ref.at[pl.ds(source, PIECE_ROWS)],
@@ -442,8 +445,7 @@
         for copy in copies(tile, 0, begin_ref[tile] % 2):
             copy.start()
 
-    y_total[...] = jnp.zeros_like(y_total)
-    dx_total[...] = jnp.zeros_like(dx_total)
+    total[...] = jnp.zeros_like(total)
     gate_out[...] = jnp.zeros_like(gate_out)
 
     def one(group, carry):
@@ -473,39 +475,36 @@
             grads = jnp.concatenate([grads] * (BLOCK // 128), axis=1)
             gate_out[expert, 0] += jnp.sum(pick * grads, axis=0, keepdims=True)
         picked = jnp.concatenate(picks, axis=0)
-        y_total[...] += dot_tn(picked, y_buf[slot])
-        dx_total[...] += dot_tn(picked, dx_buf[slot])
+        total[...] += dot_tn(picked, yd_buf[slot])
         return carry
 
     lax.fori_loop(0, groups_ref[tile], one, 0)
-    y_out[...] = y_total[...].astype(y_out.dtype)
-    dx_out[...] = dx_total[...].astype(dx_out.dtype)
-
-
-def combine_rows(tables, place, y, dx, gg, first, count):
+    y_out[...] = total[:, :columns].astype(y_out.dtype)
+    dx_out[...] = total[:, columns:].astype(dx_out.dtype)
+
+
+def combine_rows(tables, place, yd, gg, first, count, after=()):
     owner, piece, source, groups, width = tables
     begin = jnp.cumsum(groups) - groups
     experts = place.shape[0]
-    columns = y.shape[1]
+    columns = yd.shape[1] // 2
     return pl.pallas_call(
-        functools.partial(combine_kernel, first, width),
+        functools.partial(combine_kernel, first),
         grid_spec=pltpu.PrefetchScalarGridSpec(
             num_scalar_prefetch=5,
             grid=(count,),
             in_specs=[pl.BlockSpec((experts, count, 1, BLOCK), lambda *_: (0, first // count, 0, 0))]
-            + [pl.BlockSpec(memory_space=pl.ANY)] * 3,
+            + [pl.BlockSpec(memory_space=pl.ANY)] * (2 + len(after)),
             out_specs=[
                 pl.BlockSpec((BLOCK, columns), lambda t, *_: (t, 0)),
                 pl.BlockSpec((BLOCK, columns), lambda t, *_: (t, 0)),
                 pl.BlockSpec((experts, 1, 1, BLOCK), lambda t, *_: (0, t, 0, 0)),
             ],
             scratch_shapes=[
-                pltpu.VMEM((2, BLOCK, columns), jnp.bfloat16),
-                pltpu.VMEM((2, BLOCK, columns), jnp.bfloat16),
+                pltpu.VMEM((2, BLOCK, 2 * columns), jnp.bfloat16),
                 pltpu.VMEM((2, BLOCK, 128), jnp.float32),
-                pltpu.VMEM((BLOCK, columns), jnp.float32),
-                pltpu.VMEM((BLOCK, columns), jnp.float32),
-                pltpu.SemaphoreType.DMA((2, 3, GROUP)),
+                pltpu.VMEM((BLOCK, 2 * columns), jnp.float32),
+                pltpu.SemaphoreType.DMA((2, 2, GROUP)),
             ],
         ),
         out_shape=[
@@ -514,12 +513,8 @@
             jax.ShapeDtypeStruct((experts, count, 1, BLOCK), jnp.float32),
         ],
         compiler_params=pltpu.CompilerParams(vmem_limit_bytes=VMEM_LIMIT),
-        cost_estimate=pl.CostEstimate(
-            flops=count * 20 * PIECE_ROWS * BLOCK * columns * 4,
-            bytes_accessed=count * 20 * PIECE_ROWS * columns * 4,
-            transcendentals=0,
-        ),
-    )(owner, piece, source, groups, begin, place, y, dx, gg)
+        cost_estimate=cost(COST * 45.0),
+    )(owner, piece, source, groups, begin, place, yd, gg, *after)
 
 
 def flip(value, bit):
@@ -531,6 +526,10 @@
     return lax.ppermute(value, "tensor", [(0, 1), (1, 0)])
 
 
+def order(value, *after):
+    return lax.optimization_barrier((value, *after))[0] if after else value
+
+
 def add_low(left, right):
     return (left.astype(jnp.float32) + right.astype(jnp.float32)).astype(jnp.bfloat16)
 
@@ -539,91 +538,328 @@
     return lax.dynamic_index_in_dim(value, index, axis, keepdims=False)
 
 
-def chip_sum(send, keep, rank):
+def sum_stage(parts, bit, axis, chosen, after):
+    send, keep = parts
+    got = order(flip(send, bit), *after)
+    return (
+        add_low(pick_index(keep, 1 - chosen, axis), pick_index(got, 1 - chosen, axis)),
+        add_low(pick_index(keep, chosen, axis), pick_index(got, chosen, axis)),
+    )
+
+
+class ChipSum:
+    def __init__(self, parts, rank, far_first):
+        side, low_bit, high_bit = (rank // 2) % 2, (rank // 4) % 2, rank // 8
+        self.parts = parts
+        self.first = (4, 2, high_bit) if far_first else (2, 3, low_bit)
+        self.second = (8, 2, side) if far_first else (4, 2, high_bit)
+        self.last = 2 if far_first else 8
+
+    def one(self, *after):
+        self.parts = sum_stage(self.parts, *self.first, after)
+        return self.parts[0]
+
+    def two(self, *after):
+        self.parts = sum_stage(self.parts, *self.second, after)
+        return self.parts[0]
+
+    def three(self, *after):
+        send, keep = self.parts
+        return add_low(keep, order(flip(send, self.last), *after))
+
+
+def sum_heads(own, other, rank, marks=((), (), ())):
+    core, side = rank % 2, (rank // 2) % 2
     low_bit, high_bit = (rank // 4) % 2, rank // 8
-    count, kinds, cuts, depth, hidden = keep.shape
-    got = flip(send, 2)
-    view = (count, kinds, cuts // 2, 2, depth, hidden)
-    keep, got = keep.reshape(view), got.reshape(view)
-    send = add_low(pick_index(keep, 1 - low_bit, 3), pick_index(got, 1 - low_bit, 3))
-    keep = add_low(pick_index(keep, low_bit, 3), pick_index(got, low_bit, 3))
-    got = flip(send, 4)
-    send = add_low(pick_index(keep, 1 - high_bit, 2), pick_index(got, 1 - high_bit, 2))
-    keep = add_low(pick_index(keep, high_bit, 2), pick_index(got, high_bit, 2))
-    got = flip(send, 8)
-    return add_low(keep, got)
-
-
-def attend_half(normed, joined_weights, sizes, tables, allowed, score_scale):
-    query_width, key_width, head_width = sizes
-    rows = normed.shape[0]
-    heads_here = query_width // head_width
-    groups_here = key_width // head_width
-    per_group = heads_here // groups_here
-    cosine, sine_table = tables
-    projected = jnp.dot(normed, joined_weights, preferred_element_type=jnp.float32)
-    query_rows = rotate(
-        projected[:, :query_width].reshape(rows, heads_here, head_width), cosine, sine_table
-    ).astype(jnp.bfloat16)
-    key_rows = rotate(
-        projected[:, query_width : query_width + key_width].reshape(rows, groups_here, head_width),
-        cosine,
-        sine_table,
-    ).astype(jnp.bfloat16)
-    value_rows = (
-        projected[:, query_width + key_width :]
-        .astype(jnp.bfloat16)
-        .reshape(rows, groups_here, head_width)
-    )
-    query_block = query_rows.reshape(rows, groups_here, per_group, head_width)
-    scores = scores_of(query_block, key_rows, allowed, score_scale)
-    highest = jnp.max(scores, axis=-1, keepdims=True)
-    shifted = jnp.exp(scores - highest)
-    totals = jnp.sum(shifted, axis=-1, keepdims=True)
-    weights = (shifted / totals).astype(jnp.bfloat16)
-    mixed_values = jnp.einsum(
-        "kgqs,skd->qkgd", weights, value_rows, preferred_element_type=jnp.float32
-    )
-    attended = mixed_values.reshape(rows, query_width).astype(jnp.bfloat16)
-    return attended, (query_block, key_rows, value_rows, highest + jnp.log(totals))
-
-
-def attend_half_back(saved, attended_grad, sizes, tables, allowed, score_scale):
-    query_width, key_width, head_width = sizes
-    query_block, key_block, value_block, logsum = saved
-    rows = key_block.shape[0]
-    cosine, sine_table = tables
-    scores = scores_of(query_block, key_block, allowed, score_scale)
-    weights_full = jnp.exp(scores - logsum)
-    weights_low = weights_full.astype(jnp.bfloat16)
-    grad_block = attended_grad.reshape(query_block.shape)
-    value_grad = jnp.einsum(
-        "kgqs,qkgd->skd", weights_low, grad_block, preferred_element_type=jnp.float32
-    )
-    weight_grad = jnp.einsum(
-        "qkgd,skd->kgqs", grad_block, value_block, preferred_element_type=jnp.float32
-    )
-    score_low = (
-        weights_full * (weight_grad - jnp.sum(weights_full * weight_grad, axis=-1, keepdims=True))
-    ).astype(jnp.bfloat16)
-    query_grad = (
-        jnp.einsum("kgqs,skd->qkgd", score_low, key_block, preferred_element_type=jnp.float32)
-        * score_scale
-    )
-    key_grad = (
-        jnp.einsum("kgqs,qkgd->skd", score_low, query_block, preferred_element_type=jnp.float32)
-        * score_scale
-    )
-    query_grads = (
-        rotate(query_grad.reshape(rows, -1, head_width), cosine, -sine_table)
-        .astype(jnp.bfloat16)
-        .reshape(rows, query_width)
-    )
-    key_grads = (
-        rotate(key_grad, cosine, -sine_table).astype(jnp.bfloat16).reshape(rows, key_width)
-    )
-    value_grads = value_grad.astype(jnp.bfloat16).reshape(rows, key_width)
-    return jnp.concatenate([query_grads, key_grads, value_grads], axis=1)
+    rows, columns = own.shape
+    part = rows // 16
+    view = (8, 2, part, columns)
+    parts = []
+    for value in (other, own):
+        value = value.reshape(view)
+        got = order(flip(pick_index(value, 1 - core, 1).astype(jnp.bfloat16), 1), *marks[0])
+        parts.append(add_low(pick_index(value, core, 1), got))
+    held = parts[0]
+    total = add_low(parts[1], order(swap(parts[0]), *marks[1])).reshape(4, 2, part, columns)
+    got = order(flip(pick_index(total, 1 - side, 1), 2), *marks[2])
+    total = add_low(pick_index(total, side, 1), got).reshape(2, 2, part, columns)
+    got = flip(pick_index(total, 1 - low_bit, 1), 4)
+    total = add_low(pick_index(total, low_bit, 1), got)
+    got = flip(pick_index(total, 1 - high_bit, 0), 8)
+    return pick_index(total, high_bit, 0).astype(jnp.float32) + got.astype(jnp.float32), held
+
+
+def fetch_other(weights, core, side):
+    rows = weights.shape[0] // 4
+    pieces = swap(lax.dynamic_slice_in_dim(weights, (side * 2 + core) * rows, rows, 0))
+    turned = flip(pieces, 2)
+    result = jnp.zeros_like(weights)
+    first = pieces
+    for value, place in (
+        (pieces, side * 2 + core),
+        (turned, (1 - side) * 2 + core),
+        (flip(pieces, 1), side * 2 + 1 - core),
+        (flip(turned, 1), (1 - side) * 2 + 1 - core),
+    ):
+        result = lax.dynamic_update_slice_in_dim(result, value, place * rows, 0)
+    return result, first
+
+
+ROWS = 256
+HALF = 512
+
+
+def lane_swap(values):
+    width = values.shape[1]
+    lane = lax.broadcasted_iota(jnp.int32, values.shape, 1) % HD
+    ahead = pltpu.roll(values, width - HD // 2, 1)
+    behind = pltpu.roll(values, HD // 2, 1)
+    return jnp.where(lane < HD // 2, ahead, behind)
+
+
+def turn_tables(rows):
+    cosine, sine = rope_tables(rows, HD)
+    return (
+        jnp.concatenate([cosine] * 4, axis=1),
+        jnp.concatenate([-sine, sine, -sine, sine], axis=1),
+    )
+
+
+def project_kernel(sizes, score_scale, normed_ref, weights_ref, cosine_ref, sine_ref, *outs):
+    query_ref, key_ref, value_ref = outs
+    query_width, key_width = sizes
+    projected = jnp.dot(normed_ref[...], weights_ref[...], preferred_element_type=jnp.float32)
+    cosine, sine = cosine_ref[...], sine_ref[...]
+    for start in range(0, query_width + key_width, 128):
+        piece = projected[:, start : start + 128]
+        turned = piece * cosine + lane_swap(piece) * sine
+        if start < query_width:
+            query_ref[:, start : start + 128] = (turned * score_scale).astype(jnp.bfloat16)
+        else:
+            begin = start - query_width
+            key_ref[:, begin : begin + 128] = turned.astype(jnp.bfloat16)
+    value_ref[...] = projected[:, query_width + key_width :].astype(jnp.bfloat16)
+
+
+def project(normed, weights, tables, query_width, key_width, score_scale):
+    rows, depth = normed.shape
+    width = weights.shape[1]
+    row_spec = lambda columns: pl.BlockSpec((ROWS, columns), lambda i: (i, 0))
+    return pl.pallas_call(
+        functools.partial(project_kernel, (query_width, key_width), score_scale),
+        grid=(rows // ROWS,),
+        in_specs=[
+            row_spec(depth),
+            pl.BlockSpec((depth, width), lambda i: (0, 0)),
+            row_spec(128),
+            row_spec(128),
+        ],
+        out_specs=[row_spec(query_width), row_spec(key_width), row_spec(key_width)],
+        out_shape=[
+            jax.ShapeDtypeStruct((rows, query_width), jnp.bfloat16),
+            jax.ShapeDtypeStruct((rows, key_width), jnp.bfloat16),
+            jax.ShapeDtypeStruct((rows, key_width), jnp.bfloat16),
+        ],
+        compiler_params=pltpu.CompilerParams(vmem_limit_bytes=VMEM_LIMIT),
+        cost_estimate=cost(COST * 9.0),
+    )(normed, weights, *tables)
+
+
+def attend_kernel(per_pair, query_ref, key_ref, value_ref, limit_ref, out_ref, lse_ref):
+    step = pl.program_id(1)
+
+    def work(keys):
+        columns = lax.broadcasted_iota(jnp.int32, (ROWS, HALF), 1) + (keys - HALF)
+        allowed = columns <= limit_ref[...]
+        lanes = lax.broadcasted_iota(jnp.int32, (ROWS, 128), 1)
+        sums = jnp.zeros((ROWS, 128), jnp.float32)
+        pieces = []
+        for head in range(per_pair):
+            group = head // (per_pair // 2)
+            query = query_ref[:, head * HD : (head + 1) * HD]
+            key = key_ref[:keys, group * HD : (group + 1) * HD]
+            value = value_ref[:keys, group * HD : (group + 1) * HD]
+            scores = dot_nt(query, key)
+            last = jnp.where(allowed, scores[:, keys - HALF :], -1e30)
+            scores = last if keys == HALF else jnp.concatenate([scores[:, : keys - HALF], last], 1)
+            highest = jnp.max(scores, axis=1, keepdims=True)
+            shifted = jnp.exp(scores - highest)
+            total = jnp.sum(shifted, axis=1, keepdims=True)
+            mixed = jnp.dot(
+                shifted.astype(jnp.bfloat16), value, preferred_element_type=jnp.float32
+            )
+            pieces.append((mixed / total).astype(jnp.bfloat16))
+            sums = jnp.where(lanes == head, highest + jnp.log(total), sums)
+        out_ref[...] = jnp.concatenate(pieces, axis=1)
+        lse_ref[0] = sums
+
+    halfway = pl.num_programs(1) // 2
+
+    @pl.when(step < halfway)
+    def _():
+        work(HALF)
+
+    @pl.when(step >= halfway)
+    def _():
+        work(2 * HALF)
+
+
+def attend(query, key, value, limits):
+    rows, query_width = query.shape
+    pairs = key.shape[1] // 128
+    wide = query_width // pairs
+    return pl.pallas_call(
+        functools.partial(attend_kernel, wide // HD),
+        grid=(pairs, rows // ROWS),
+        in_specs=[
+            pl.BlockSpec((ROWS, wide), lambda p, i: (i, p)),
+            pl.BlockSpec((rows, 128), lambda p, i: (0, p)),
+            pl.BlockSpec((rows, 128), lambda p, i: (0, p)),
+            pl.BlockSpec((ROWS, 1), lambda p, i: (i, 0)),
+        ],
+        out_specs=[
+            pl.BlockSpec((ROWS, wide), lambda p, i: (i, p)),
+            pl.BlockSpec((1, ROWS, 128), lambda p, i: (p, i, 0)),
+        ],
+        out_shape=[
+            jax.ShapeDtypeStruct((rows, query_width), jnp.bfloat16),
+            jax.ShapeDtypeStruct((pairs, rows, 128), jnp.float32),
+        ],
+        compiler_params=pltpu.CompilerParams(vmem_limit_bytes=VMEM_LIMIT),
+        cost_estimate=cost(COST * 24.0),
+    )(query, key, value, limits)
+
+
+def back_kernel(
+    per_pair, score_scale, after, query_ref, key_ref, value_ref, turned_key_ref, grad_ref, lse_ref,
+    limit_ref, cosine_ref, sine_ref, all_cosine_ref, all_sine_ref, *rest
+):
+    query_out, key_out, value_out, key_total, value_total = rest[after:]
+    step = pl.program_id(1)
+    halfway = pl.num_programs(1) // 2
+
+    @pl.when(step == 0)
+    def _():
+        key_total[...] = jnp.zeros_like(key_total)
+        value_total[...] = jnp.zeros_like(value_total)
+
+    def work(keys):
+        rows = lax.broadcasted_iota(jnp.int32, (HALF, ROWS), 0) + (keys - HALF)
+        allowed = rows <= limit_ref[...]
+        made = []
+        key_parts, value_parts = [], []
+        for group in range(2):
+            span = slice(group * HD, (group + 1) * HD)
+            key, value = key_ref[:keys, span], value_ref[:keys, span]
+            key_part = value_part = 0.0
+            for head in range(group * per_pair // 2, (group + 1) * per_pair // 2):
+                query = query_ref[:, head * HD : (head + 1) * HD]
+                grad = grad_ref[:, head * HD : (head + 1) * HD]
+                scores = dot_nt(key, query)
+                last = jnp.where(allowed, scores[keys - HALF :], -1e30)
+                scores = (
+                    last
+                    if keys == HALF
+                    else jnp.concatenate([scores[: keys - HALF], last], axis=0)
+                )
+                weights = jnp.exp(scores - lse_ref[0, head : head + 1, :])
+                pulled = dot_nt(value, grad)
+                inner = jnp.sum(weights * pulled, axis=0, keepdims=True)
+                score_low = (weights * (pulled - inner)).astype(jnp.bfloat16)
+                value_part += jnp.dot(
+                    weights.astype(jnp.bfloat16), grad, preferred_element_type=jnp.float32
+                )
+                key_part += jnp.dot(score_low, query, preferred_element_type=jnp.float32)
+                made.append(
+                    jnp.dot(
+                        turned_key_ref[0, span, :keys],
+                        score_low,
+                        preferred_element_type=jnp.float32,
+                    )
+                )
+            key_parts.append(key_part)
+            value_parts.append(value_part)
+        key_total[:keys] += jnp.concatenate(key_parts, axis=1)
+        value_total[:keys] += jnp.concatenate(value_parts, axis=1)
+        cosine, sine = cosine_ref[...], sine_ref[...]
+        for index in range(per_pair // 2):
+            both = jnp.concatenate(made[2 * index : 2 * index + 2], axis=0).T * score_scale
+            query_out[:, index * 128 : (index + 1) * 128] = (
+                both * cosine - lane_swap(both) * sine
+            ).astype(jnp.bfloat16)
+
+    @pl.when(step < halfway)
+    def _():
+        work(HALF)
+
+    @pl.when(step >= halfway)
+    def _():
+        work(2 * HALF)
+
+    @pl.when(step == pl.num_programs(1) - 1)
+    def _():
+        total = key_total[...]
+        key_out[...] = (
+            total * all_cosine_ref[...] - lane_swap(total) * all_sine_ref[...]
+        ).astype(jnp.bfloat16)
+        value_out[...] = value_total[...].astype(jnp.bfloat16)
+
+
+def attend_back(saved, attended_grad, limits, tables, score_scale, after=()):
+    query, key, value, lse = saved
+    rows, query_width = query.shape
+    pairs = key.shape[1] // 128
+    wide = query_width // pairs
+    turned_key = key.T.reshape(pairs, 128, rows)
+    lse_rows = lse[:, :, :8].transpose(0, 2, 1)
+    cosine, sine = tables
+    block = lambda columns: pl.BlockSpec((ROWS, columns), lambda p, i: (i, p))
+    whole = pl.BlockSpec((rows, 128), lambda p, i: (0, p))
+    table = pl.BlockSpec((ROWS, 128), lambda p, i: (i, 0))
+    full_table = pl.BlockSpec((rows, 128), lambda p, i: (0, 0))
+    return pl.pallas_call(
+        functools.partial(back_kernel, wide // HD, score_scale, len(after)),
+        grid=(pairs, rows // ROWS),
+        in_specs=[
+            block(wide),
+            whole,
+            whole,
+            pl.BlockSpec((1, 128, rows), lambda p, i: (p, 0, 0)),
+            block(wide),
+            pl.BlockSpec((1, 8, ROWS), lambda p, i: (p, 0, i)),
+            pl.BlockSpec((1, ROWS), lambda p, i: (0, i)),
+            table,
+            table,
+            full_table,
+            full_table,
+        ]
+        + [pl.BlockSpec(memory_space=pl.ANY)] * len(after),
+        out_specs=[block(wide), whole, whole],
+        out_shape=[
+            jax.ShapeDtypeStruct((rows, query_width), jnp.bfloat16),
+            jax.ShapeDtypeStruct((rows, key.shape[1]), jnp.bfloat16),
+            jax.ShapeDtypeStruct((rows, key.shape[1]), jnp.bfloat16),
+        ],
+        scratch_shapes=[
+            pltpu.VMEM((rows, 128), jnp.float32),
+            pltpu.VMEM((rows, 128), jnp.float32),
+        ],
+        compiler_params=pltpu.CompilerParams(vmem_limit_bytes=VMEM_LIMIT),
+        cost_estimate=cost(COST * 40.0),
+    )(
+        query, key, value, turned_key, attended_grad, lse_rows, limits.T, cosine, sine, cosine,
+        sine, *after,
+    )
+
+
+def piece_limits(starts_row, rows):
+    position = jnp.arange(rows, dtype=jnp.int32)
+    limits = position
+    for index in range(starts_row.shape[0]):
+        start = starts_row[index]
+        inside = (position >= start) & (position < start + PIECE)
+        limits = jnp.where(inside, start + PIECE - 1, limits)
+    return limits[:, None]
 
 
 def slot_table(routes, expert_count, capacity):
@@ -975,7 +1211,8 @@
     return [value, across, flip(value, 1), flip(across, 1)]
 
 
-CHUNK = 2
+FIRST_PART = 2
+FAR_FIRST = (2, 5)
 
 
 def shards_pair(
@@ -1012,20 +1249,8 @@
     slots = round_up(2 * CAP, BLOCK)
 
     joined_own = jnp.concatenate([w_query, w_key, w_value], axis=1)
-    part_rows = model_width // dp_size
-    out_rows = query_width // dp_size
-    joined_other = lax.all_gather(
-        swap(lax.dynamic_slice_in_dim(joined_own, rank * part_rows, part_rows, 0)),
-        "dp",
-        axis=0,
-        tiled=True,
-    )
-    out_other = lax.all_gather(
-        swap(lax.dynamic_slice_in_dim(w_out, rank * out_rows, out_rows, 0)),
-        "dp",
-        axis=0,
-        tiled=True,
-    )
+    joined_other, joined_piece = fetch_other(joined_own, core, side)
+    out_other, out_piece = fetch_other(w_out, core, side)
 
     own_routes = lax.dynamic_slice_in_dim(routes, tensor_rank * share_rows, share_rows, 0)
     across_routes = lax.dynamic_slice_in_dim(routes, (1 - tensor_rank) * share_rows, share_rows, 0)
@@ -1033,17 +1258,27 @@
     group_routes = jnp.concatenate([both_routes, flip(both_routes, 1)], axis=0)
     first_expert = tensor_rank * experts_here + core * experts
 
-    cotangent_rows = spread(cotangent)
+    route_onehot = (
+        own_routes[:, :, None] == jnp.arange(expert_count, dtype=jnp.int32)[None, None, :]
+    ).astype(jnp.float32)
+    counts = all_sum(jnp.sum(route_onehot, axis=(0, 1)))
+    cotangent_rows = spread(order(cotangent, joined_piece, out_piece))
 
     inputs_share = tokens.astype(jnp.float32)
     normed = normalize(inputs_share, norm_gains).astype(jnp.bfloat16)
-    tables = rope_tables(share_rows, HD)
+    tables = turn_tables(share_rows)
     starts_row = lax.dynamic_index_in_dim(starts, tensor_rank, 0, keepdims=False)
-    allowed = allowed_pairs(starts_row, share_rows, PIECE)
-    attended_own, saved_own = attend_half(normed, joined_own, sizes, tables, allowed, score_scale)
-    attended_other, saved_other = attend_half(
-        normed, joined_other, sizes, tables, allowed, score_scale
-    )
+    limits = piece_limits(starts_row, share_rows)
+
+    def half_forward(joined_weights):
+        query, key, value = project(
+            normed, joined_weights, tables, query_width, key_width, score_scale
+        )
+        attended, lse = attend(query, key, value, limits)
+        return attended, (query, key, value, lse)
+
+    attended_own, saved_own = half_forward(joined_own)
+    attended_other, saved_other = half_forward(joined_other)
     middle_share = (
         inputs_share
         + jnp.dot(attended_own, w_out, preferred_element_type=jnp.float32)
@@ -1051,71 +1286,85 @@
     )
     mixed_share = normalize(middle_share, mix_gains).astype(jnp.bfloat16)
 
-    route_onehot = (
-        own_routes[:, :, None] == jnp.arange(expert_count, dtype=jnp.int32)[None, None, :]
-    ).astype(jnp.float32)
     logits = jnp.dot(mixed_share, w_router, preferred_element_type=jnp.float32)
     probabilities = softmax_rows(logits)
     chosen = jnp.sum(logits[:, None, :] * route_onehot, axis=-1)
     gate_soft = softmax_rows(chosen)
     gate_low = gate_soft.astype(jnp.bfloat16)
-    counts = all_sum(jnp.sum(route_onehot, axis=(0, 1)))
-    prob_sums = all_sum(jnp.sum(probabilities, axis=0))
     fractions = counts / (total_tokens * choices_count)
-    balance = expert_count * expert_count * fractions * prob_sums / total_tokens
-
-    mixed_rows = spread(mixed_share)
+
     group_gates = jnp.concatenate(spread(gate_low), axis=0)
     place, begins, ends, gates = placement(group_routes, group_gates, first_expert, experts)
     gather_from = gather_tables(begins, ends, slots)
     blocks = gather_from[2]
     cot_slots = gather_rows(gather_from, place, None, cotangent_rows, slots, 0, experts)[0]
-    misc = jnp.stack([core * experts, side])
+    mixed_across = order(swap(mixed_share), cot_slots)
+    mixed_rows = [mixed_share, mixed_across, flip(mixed_share, 1), flip(mixed_across, 1)]
+    misc = jnp.stack([core * experts, side, (rank // 4) % 2])
     weights = (w_gate, w_up, w_down)
+    first_part = gather_rows(
+        gather_from, place, gates, mixed_rows, slots, 0, FIRST_PART, (cot_slots, counts)
+    )
+    later_part = None
     carried = None
-    sums = []
-    first_part = gather_rows(gather_from, place, gates, mixed_rows, slots, 0, CHUNK)
-    later_part = gather_rows(gather_from, place, gates, mixed_rows, slots, CHUNK, experts - CHUNK)
-    for first in range(0, experts, CHUNK):
-        (x_slots, slot_gates), x_first = (
-            (first_part, 0) if first == 0 else (later_part, CHUNK)
-        )
+    chips = []
+    for index in range(experts):
+        if index == FIRST_PART:
+            later_part = gather_rows(
+                gather_from, place, gates, mixed_rows, slots, FIRST_PART, experts - FIRST_PART,
+                (carried[1],),
+            )
+        if later_part is None:
+            (x_slots, slot_gates), x_first = first_part, 0
+        else:
+            (x_slots, slot_gates), x_first = later_part, FIRST_PART
+        waits = []
+        if index == 2:
+            waits = [chips[0].one(slot_gates)]
+        elif index == 4:
+            waits = [chips[1].one(carried[1]), chips[0].two(carried[1])]
+        elif index == 6:
+            waits = [chips[2].one(carried[1])]
+        elif index == 7:
+            waits = [chips[3].one(carried[1]), chips[1].two(carried[1])]
+        elif index == 9:
+            waits = [chips[4].one(carried[1])]
+        far_first = int(index in FAR_FIRST)
         *carried, send, keep = expert_call(
             blocks, misc, x_slots, cot_slots, slot_gates, weights, carried, slots,
-            first, CHUNK, x_first, 0, depth,
+            index, 1, x_first, 0, depth, far_first, waits,
         )
-        sums.append(chip_sum(send, keep, rank))
+        chips.append(ChipSum((send, keep), rank, far_first))
+    waits = [chips[5].one(carried[1])] + [chips[i].two(carried[1]) for i in (2, 3)]
 
     combine_from = combine_tables(begins, ends, slots)
-    tiles = place.shape[1] // 2
+    tiles = place.shape[1] // 4
     turned_routes = group_routes.T
     names = first_expert + jnp.arange(experts, dtype=jnp.int32)
 
-    def combined(half):
-        y, dx, gate_grads = combine_rows(combine_from, place, *carried, half * tiles, tiles)
-        gate_grads = gate_grads[:experts].reshape(experts, 1, tiles * BLOCK)
-        rows = turned_routes[:, half * tiles * BLOCK : (half + 1) * tiles * BLOCK]
+    def combined(start, count, after):
+        y, dx, gate_grads = combine_rows(combine_from, place, *carried, start, count, after)
+        gate_grads = gate_grads[:experts].reshape(experts, 1, count * BLOCK)
+        rows = turned_routes[:, start * BLOCK : (start + count) * BLOCK]
         hit = rows[None, :, :] == names[:, None, None]
         return y, dx, jnp.sum(jnp.where(hit, gate_grads, 0.0), axis=0)
 
-    y_far, dx_far, gg_far = combined(1)
-    y_far, dx_far, gg_far = flip(y_far, 1), flip(dx_far, 1), flip(gg_far, 1)
-    y_near, dx_near, gg_near = combined(0)
-    dx_across = swap(add_low(dx_near[share_rows:], dx_far[share_rows:]))
-    gg_across = swap(gg_near[:, share_rows:] + gg_far[:, share_rows:])
-    y_across = swap(add_low(y_near[share_rows:], y_far[share_rows:]))
+    y_far, dx_far, gg_far = combined(2 * tiles, 2 * tiles, waits)
+    waits = [chips[6].one(dx_far), chips[4].two(dx_far)]
+    dx_far, y_far, gg_far = flip(dx_far, 1), flip(y_far, 1), flip(gg_far, 1)
+    y_cross, dx_cross, gg_cross = combined(tiles, tiles, waits)
+    dx_send = add_low(dx_cross, dx_far[share_rows:])
+    dx_across = swap(dx_send)
+    gg_across = swap(gg_cross + gg_far[:, share_rows:])
+    y_near, dx_near, gg_near = combined(0, tiles, [dx_send])
+    waits = [chips[7].one(dx_near)] + [chips[i].two(dx_near) for i in (5, 6)]
+    waits.append(chips[8].one(dx_near))
     mixed_grad_share = (
-        dx_near[:share_rows].astype(jnp.float32)
+        dx_near.astype(jnp.float32)
         + dx_far[:share_rows].astype(jnp.float32)
         + dx_across.astype(jnp.float32)
     )
-    gates_grad_share = (gg_near[:, :share_rows] + gg_far[:, :share_rows] + gg_across).T
-    expert_share = (
-        y_near[:share_rows].astype(jnp.float32)
-        + y_far[:share_rows].astype(jnp.float32)
-        + y_across.astype(jnp.float32)
-    )
-    output_share = (middle_share + expert_share).astype(jnp.bfloat16)
+    gates_grad_share = (gg_near + gg_far[:, :share_rows] + gg_across).T
 
     upstream = cotangent.astype(jnp.float32)
     chosen_grad = gate_soft * (
@@ -1143,29 +1392,47 @@
     middle_grad = upstream + middle_from_norm
     middle_low = middle_grad.astype(jnp.bfloat16)
 
-    def half_back(saved, attended, joined_weights, out_weights):
+    def half_back(saved, out_weights, after):
         attended_grad = dot_nt(middle_low, out_weights).astype(jnp.bfloat16)
-        joined_grads = attend_half_back(saved, attended_grad, sizes, tables, allowed, score_scale)
-        weight_grads = jnp.concatenate(
-            [dot_tn(normed, joined_grads), dot_tn(middle_low, attended)], axis=1
-        )
-        return weight_grads.astype(jnp.bfloat16), dot_nt(joined_grads, joined_weights)
-
-    other_grads, other_normed = half_back(saved_other, attended_other, joined_other, out_other)
-    own_grads, own_normed = half_back(saved_own, attended_own, joined_own, w_out)
-    attention_grads = add_low(own_grads, swap(other_grads))
-    attention_total = lax.psum_scatter(
-        attention_grads, "dp", scatter_dimension=0, tiled=True
-    ).astype(jnp.float32)
+        grads = attend_back(saved, attended_grad, limits, tables, score_scale, after)
+        return jnp.concatenate(grads, axis=1)
+
+    other_grads = half_back(saved_other, out_other, waits)
+    y_across = swap(order(add_low(y_cross, y_far[share_rows:]), other_grads))
+    expert_share = (
+        y_near.astype(jnp.float32)
+        + y_far[:share_rows].astype(jnp.float32)
+        + y_across.astype(jnp.float32)
+    )
+    output_share = (middle_share + expert_share).astype(jnp.bfloat16)
+    other_weight_grads = dot_tn(normed, other_grads)
+    waits = [chips[9].one(other_grads)] + [chips[i].two(other_grads) for i in (7, 8)]
+    out_grads = (
+        dot_tn(middle_low, attended_own),
+        dot_tn(order(middle_low, other_grads), attended_other),
+    )
+    own_grads = half_back(saved_own, w_out, waits)
+    out_total, _ = sum_heads(*out_grads, rank, ((), (), (own_grads,)))
+    own_weight_grads = dot_tn(normed, own_grads)
+    joined_total, _ = sum_heads(own_weight_grads, other_weight_grads, rank)
+    chips[9].two(own_weight_grads)
+    sums = [chip.three(own_weight_grads) for chip in chips]
+    other_normed = dot_nt(other_grads, joined_other)
+    own_normed = dot_nt(own_grads, joined_own)
     input_pullback = jax.vjp(normalize, inputs_share, norm_gains)[1]
     input_from_norm, norm_gain_grad = input_pullback(other_normed + own_normed)
     input_grad_share = middle_grad + input_from_norm
     key_end = query_width + key_width
-    joined_end = key_end + key_width
-
-    router_total = all_sum(router_grad)
-    mix_gain_total = all_sum(mix_gain_grad)
-    norm_gain_total = all_sum(norm_gain_grad)
+    small = all_sum(
+        jnp.concatenate(
+            [jnp.sum(probabilities, axis=0), mix_gain_grad, norm_gain_grad, router_grad.reshape(-1)]
+        )
+    )
+    prob_sums = small[:expert_count]
+    mix_gain_total = small[expert_count : expert_count + model_width]
+    norm_gain_total = small[expert_count + model_width : expert_count + 2 * model_width]
+    router_total = small[expert_count + 2 * model_width :].reshape(router_grad.shape)
+    balance = expert_count * expert_count * fractions * prob_sums / total_tokens
 
     mine = jnp.concatenate(sums, axis=0).reshape(experts, 3, 2, depth // 2, -1)
     theirs = flip(pick_index(mine, 1 - core, 2), 1)
@@ -1180,10 +1447,10 @@
         balance,
         input_grad_share,
         norm_gain_total,
-        attention_total[:, :query_width],
-        attention_total[:, query_width:key_end],
-        attention_total[:, key_end:joined_end],
-        attention_total[:, joined_end:].T,
+        joined_total[:, :query_width],
+        joined_total[:, query_width:key_end],
+        joined_total[:, key_end:],
+        out_total.T,
         mix_gain_total,
         router_total,
         expert_total[:, 0],

time: 2090 us -> 1480 us (0.71)
  waiting for transfers between devices: 759 us -> 312 us
  matrix products: 379 us -> 81.4 us
  Pallas kernels: 488 us -> 679 us
  other arithmetic: 253 us -> 162 us
  local copies, waits for them, and re-layouts: 113 us -> 148 us
    ppermute x46 -> x65, waiting for transfers between devices: 546 us -> 214 us  [flip(): return lax.ppermute(value, 'dp', [(i, i ^ bit) for i in range(size)])]
    dot_general x14 -> x0, matrix products: 300 us -> none  [the longest x2 88.9 us: attend_half_back(): jnp.einsum('qkgd,skd->kgqs', grad_block, value_block, preferred_element_t...]
    pallas_call x7 -> x19, Pallas kernels: 314 us -> 489 us  [the longest x10 241 us: expert_call(): pl.pallas_call(functools.partial(expert_kernel, first, split, depth, far_...]
    ppermute x14 -> x12, waiting for transfers between devices: 214 us -> 98.2 us  [swap(): return lax.ppermute(value, 'tensor', [(0, 1), (1, 0)])]
    convert_element_type x2 -> x1, other arithmetic: 81.7 us -> 2.45 us  [shards_pair(): normed = normalize(inputs_share, norm_gains).astype(jnp.bfloat16)]
    pallas_call x0 -> x12, local copies, waits for them, and re-layouts: none -> 34.9 us  [the longest x10 31 us: expert_call(): pl.pallas_call(functools.partial(expert_kernel, first, split, depth, far_...]
    reduce_sum x3 -> x2, other arithmetic: 32.6 us -> 1 us  [the longest x1 0.65 us: shards_pair(): jnp.sum(probabilities, axis=0)]
    convert_element_type x0 -> x14, local copies, waits for them, and re-layouts: none -> 28.8 us  [the longest x10 22.3 us: add_low(): (left.astype(jnp.float32) + right.astype(jnp.float32)).astype(jnp.bfloat16)]
  transfers between devices with their start and end apart: 63 -> 77, of which waited for: 25 -> 25; matrix products, arithmetic and copies ran while one was open for 35% -> 25% of each run, Pallas kernels for 6% -> 40%
where the time goes in v2:
time: 1480 us; the launch traced here: 1470 us
  Pallas kernels  679 us (46%)
  waiting for transfers between devices  312 us (21%)
  other arithmetic  162 us (11%)
  local copies, waits for them, and re-layouts  148 us (10%)
  starting transfers between devices  86 us (6%)
  matrix products  81.4 us (6%)
    pallas_call x10, Pallas kernels, expert_call(): pl.pallas_call(functools.partial(expert_kernel, first, split, depth, far_...  241 us
    ppermute x65, waiting for transfers between devices, flip(): return lax.ppermute(value, 'dp', [(i, i ^ bit) for i in range(size)])  214 us
    pallas_call x3, Pallas kernels, gather_rows(): pl.pallas_call(functools.partial(gather_kernel, count, slots, len(sources...  189 us
    pallas_call x3, Pallas kernels, combine_rows(): pl.pallas_call(functools.partial(combine_kernel, first), grid_spec=pltpu....  103 us
    ppermute x12, waiting for transfers between devices, swap(): return lax.ppermute(value, 'tensor', [(0, 1), (1, 0)])  98.2 us
    convert_element_type x30, other arithmetic, add_low(): (left.astype(jnp.float32) + right.astype(jnp.float32)).astype(jnp.bfloat16)  80.4 us
    pallas_call x2, Pallas kernels, attend_back(): pl.pallas_call(functools.partial(back_kernel, wide // HD, score_scale, le...  79.7 us
    ppermute x65, starting transfers between devices, flip(): return lax.ppermute(value, 'dp', [(i, i ^ bit) for i in range(size)])  62.5 us
  transfers between devices with their start and end apart: 77, of which 25 were waited for; matrix products, arithmetic and copies ran while one was open for 25% of the time, Pallas kernels for 40%

profile of v2, /device:TPU:0, one launch (start us, length us, event | category | flops | bytes accessed | tf_op | source)
XLA Modules:
  0.0 1473.2 jit_solution(10350115233470019006)
XLA Ops:
  37.6 24.4 %shard_map.238 = (bf16[1024,768]{1,0:T(8,128)(2,1)}, f32[2,1024,128]{2,1,0:T(8,128)}) custom-call(bf16[1024,768]{1,0:T(8,128)(2,1)} %get-tuple-element.117.query_ref, bf16[1024,256]{1,0:T(8,128)(2,1)} %get-tuple-element.118.key_ref, bf16[1024,256]{1,0:T(8,128)(2,1)} %get-tuple-element.119.value_ref, s32[1024,1]{1,0:T(8,128)} %select_select_fusion.limit_ref), custom_call_target="tpu_custom_call" | custom-call | bytes 43200000 | tf_op jit(solution)/shard_map/pallas_call | solution.py:711
  112.9 24.6 %shard_map.240 = (bf16[1024,768]{1,0:T(8,128)(2,1)}, f32[2,1024,128]{2,1,0:T(8,128)}) custom-call(bf16[1024,768]{1,0:T(8,128)(2,1)} %get-tuple-element.121.query_ref, bf16[1024,256]{1,0:T(8,128)(2,1)} %get-tuple-element.122.key_ref, bf16[1024,256]{1,0:T(8,128)(2,1)} %get-tuple-element.123.value_ref, s32[1024,1]{1,0:T(8,128)} %select_select_fusion.limit_ref), custom_call_target="tpu_custom_call" | custom-call | bytes 43200000 | tf_op jit(solution)/shard_map/pallas_call | solution.py:711
  157.9 90.0 %shard_map.241.rest_5_.c_ref = bf16[12800,1536]{1,0:T(8,128)(2,1)} custom-call(s32[10,5]{1,0:T(8,128)} %copy-done.68, s32[10,5]{1,0:T(8,128)} %compare_select_fusion.3.high_ref, s32[10]{0:T(128)} %negate_maximum_fusion.blocks_ref, s32[10,16,1,256]{3,2,1,0:T(1,128)} %add_select_fusion.place_ref, bf16[1024,1536]{1,0:T(8,128)(2,1)} %rest_0_, ...), custom_call_target="tpu_custom_call" | custom-call | bytes 99000000 | tf_op jit(solution)/shard_map/pallas_call | solution.py:256
  271.6 23.6 %shard_map.242 = (bf16[2560,1536]{1,0:T(8,128)(2,1)}, f32[2560,128]{1,0:T(8,128)}) custom-call(s32[2,5]{1,0:T(2,128)} %slice.185.low_ref, s32[2,5]{1,0:T(2,128)} %slice.186.high_ref, s32[2]{0:T(128)} %bitcast.408, s32[2,16,1,256]{3,2,1,0:T(1,128)} %copy.226.place_ref, f32[2,16,1,256]{3,2,1,0:T(1,128)} %slice.153.rest_0_, ...), custom_call_target="tpu_custom_call" | custom-call | bytes 19800000 | tf_op jit(solution)/shard_map/pallas_call | solution.py:256
  295.3 20.0 %shard_map.243 = (bf16[12800,3072]{1,0:T(8,128)(2,1)}, f32[12800,128]{1,0:T(8,128)}, bf16[1,3,2,2,192,512]{5,4,3,2,1,0:T(8,128)(2,1)}, bf16[1,3,2,2,192,512]{5,4,3,2,1,0:T(8,128)(2,1)}) custom-call(s32[10]{0:T(128)} %negate_maximum_fusion.blocks_ref, s32[3]{0:T(128)} %pad_add_fusion.1.misc_ref, bf16[2560,1536]{1,0:T(8,128)(2,1)} %get-tuple-element.127.x_ref, ...), custom_call_target="tpu_custom_call" | custom-call | bytes 37800000 | tf_op jit(solution)/shard_map/pallas_call | solution.py:400
  318.8 24.1 %shard_map.244 = (bf16[12800,3072]{1,0:T(8,128)(2,1)}, f32[12800,128]{1,0:T(8,128)}, bf16[1,3,2,2,192,512]{5,4,3,2,1,0:T(8,128)(2,1)}, bf16[1,3,2,2,192,512]{5,4,3,2,1,0:T(8,128)(2,1)}) custom-call(s32[10]{0:T(128)} %negate_maximum_fusion.blocks_ref, s32[3]{0:T(128)} %pad_add_fusion.1.misc_ref, ...), custom_call_target="tpu_custom_call", output_to_operand_aliasing={{0}: (8, {}), {1}: (9, {})} | custom-call | bytes 37800000 | tf_op jit(solution)/shard_map/pallas_call | solution.py:400
  349.5 75.7 %shard_map.245 = (bf16[10240,1536]{1,0:T(8,128)(2,1)}, f32[10240,128]{1,0:T(8,128)}) custom-call(s32[8,5]{1,0:T(8,128)} %slice.181.low_ref, s32[8,5]{1,0:T(8,128)} %slice.182.high_ref, s32[8]{0:T(128)} %slice.142.blocks_ref, s32[8,16,1,256]{3,2,1,0:T(1,128)} %copy.227.place_ref, f32[8,16,1,256]{3,2,1,0:T(1,128)} %slice.146.rest_0_, ...), custom_call_target="tpu_custom_call" | custom-call | bytes 79200000 | tf_op jit(solution)/shard_map/pallas_call | solution.py:256
  432.2 23.9 %shard_map.246 = (bf16[12800,3072]{1,0:T(8,128)(2,1)}, f32[12800,128]{1,0:T(8,128)}, bf16[1,3,2,2,192,512]{5,4,3,2,1,0:T(8,128)(2,1)}, bf16[1,3,2,2,192,512]{5,4,3,2,1,0:T(8,128)(2,1)}) custom-call(s32[10]{0:T(128)} %negate_maximum_fusion.blocks_ref, s32[3]{0:T(128)} %pad_add_fusion.1.misc_ref, ...), custom_call_target="tpu_custom_call", output_to_operand_aliasing={{0}: (8, {}), {1}: (9, {})} | custom-call | bytes 37800000 | tf_op jit(solution)/shard_map/pallas_call | solution.py:400
  463.5 20.2 %shard_map.247 = (bf16[12800,3072]{1,0:T(8,128)(2,1)}, f32[12800,128]{1,0:T(8,128)}, bf16[1,3,2,2,192,512]{5,4,3,2,1,0:T(8,128)(2,1)}, bf16[1,3,2,2,192,512]{5,4,3,2,1,0:T(8,128)(2,1)}) custom-call(s32[10]{0:T(128)} %negate_maximum_fusion.blocks_ref, s32[3]{0:T(128)} %pad_add_fusion.1.misc_ref, ...), custom_call_target="tpu_custom_call", output_to_operand_aliasing={{0}: (8, {}), {1}: (9, {})} | custom-call | bytes 37800000 | tf_op jit(solution)/shard_map/pallas_call | solution.py:400
  496.2 31.2 %collective-permute-done.25 = bf16[1,3,2,192,512]{4,3,1,2,0:T(8,128)(2,1)} collective-permute-done((bf16[1,3,2,192,512]{4,3,1,2,0:T(8,128)(2,1)}, bf16[1,3,2,192,512]{4,3,1,2,0:T(8,128)(2,1)}, u32[]{:S(2)}, u32[]{:S(2)}) %collective-permute-start.25) | collective-permute-done | bytes 1179680 | tf_op jit(solution)/shard_map/ppermute | solution.py:522
  529.4 19.9 %shard_map.248 = (bf16[12800,3072]{1,0:T(8,128)(2,1)}, f32[12800,128]{1,0:T(8,128)}, bf16[1,3,2,2,192,512]{5,4,3,2,1,0:T(8,128)(2,1)}, bf16[1,3,2,2,192,512]{5,4,3,2,1,0:T(8,128)(2,1)}) custom-call(s32[10]{0:T(128)} %negate_maximum_fusion.blocks_ref, s32[3]{0:T(128)} %pad_add_fusion.1.misc_ref, ...), custom_call_target="tpu_custom_call", output_to_operand_aliasing={{0}: (8, {}), {1}: (9, {})} | custom-call | bytes 37800000 | tf_op jit(solution)/shard_map/pallas_call | solution.py:400
  552.9 20.4 %shard_map.249 = (bf16[12800,3072]{1,0:T(8,128)(2,1)}, f32[12800,128]{1,0:T(8,128)}, bf16[1,3,2,2,192,512]{5,4,3,2,1,0:T(8,128)(2,1)}, bf16[1,3,2,2,192,512]{5,4,3,2,1,0:T(8,128)(2,1)}) custom-call(s32[10]{0:T(128)} %negate_maximum_fusion.blocks_ref, s32[3]{0:T(128)} %pad_add_fusion.1.misc_ref, ...), custom_call_target="tpu_custom_call", output_to_operand_aliasing={{0}: (8, {}), {1}: (9, {})} | custom-call | bytes 37800000 | tf_op jit(solution)/shard_map/pallas_call | solution.py:400
  592.8 28.1 %shard_map.250 = (bf16[12800,3072]{1,0:T(8,128)(2,1)}, f32[12800,128]{1,0:T(8,128)}, bf16[1,3,2,2,192,512]{5,4,3,2,1,0:T(8,128)(2,1)}, bf16[1,3,2,2,192,512]{5,4,3,2,1,0:T(8,128)(2,1)}) custom-call(s32[10]{0:T(128)} %negate_maximum_fusion.blocks_ref, s32[3]{0:T(128)} %pad_add_fusion.1.misc_ref, ...), custom_call_target="tpu_custom_call", output_to_operand_aliasing={{0}: (8, {}), {1}: (9, {})} | custom-call | bytes 37800000 | tf_op jit(solution)/shard_map/pallas_call | solution.py:400
  638.9 42.7 %collective-permute-done.28 = bf16[1,3,2,192,512]{4,3,1,2,0:T(8,128)(2,1)} collective-permute-done((bf16[1,3,2,192,512]{4,3,1,2,0:T(8,128)(2,1)}, bf16[1,3,2,192,512]{4,3,1,2,0:T(8,128)(2,1)}, u32[]{:S(2)}, u32[]{:S(2)}) %collective-permute-start.28) | collective-permute-done | bytes 1179680 | tf_op jit(solution)/shard_map/ppermute | solution.py:522
  683.7 27.9 %shard_map.251 = (bf16[12800,3072]{1,0:T(8,128)(2,1)}, f32[12800,128]{1,0:T(8,128)}, bf16[1,3,2,2,192,512]{5,4,3,2,1,0:T(8,128)(2,1)}, bf16[1,3,2,2,192,512]{5,4,3,2,1,0:T(8,128)(2,1)}) custom-call(s32[10]{0:T(128)} %negate_maximum_fusion.blocks_ref, s32[3]{0:T(128)} %pad_add_fusion.1.misc_ref, ...), custom_call_target="tpu_custom_call", output_to_operand_aliasing={{0}: (8, {}), {1}: (9, {})} | custom-call | bytes 37800000 | tf_op jit(solution)/shard_map/pallas_call | solution.py:400
  711.6 27.8 %shard_map.252 = (bf16[12800,3072]{1,0:T(8,128)(2,1)}, f32[12800,128]{1,0:T(8,128)}, bf16[1,3,2,2,192,512]{5,4,3,2,1,0:T(8,128)(2,1)}, bf16[1,3,2,2,192,512]{5,4,3,2,1,0:T(8,128)(2,1)}) custom-call(s32[10]{0:T(128)} %negate_maximum_fusion.blocks_ref, s32[3]{0:T(128)} %pad_add_fusion.1.misc_ref, ...), custom_call_target="tpu_custom_call", output_to_operand_aliasing={{0}: (8, {}), {1}: (9, {})} | custom-call | bytes 37800000 | tf_op jit(solution)/shard_map/pallas_call | solution.py:400
  746.3 28.3 %shard_map.253 = (bf16[12800,3072]{1,0:T(8,128)(2,1)}, f32[12800,128]{1,0:T(8,128)}, bf16[1,3,2,2,192,512]{5,4,3,2,1,0:T(8,128)(2,1)}, bf16[1,3,2,2,192,512]{5,4,3,2,1,0:T(8,128)(2,1)}) custom-call(s32[10]{0:T(128)} %negate_maximum_fusion.blocks_ref, s32[3]{0:T(128)} %pad_add_fusion.1.misc_ref, ...), custom_call_target="tpu_custom_call", output_to_operand_aliasing={{0}: (8, {}), {1}: (9, {})} | custom-call | bytes 37800000 | tf_op jit(solution)/shard_map/pallas_call | solution.py:400
  785.8 49.1 %shard_map.254 = (bf16[2048,1536]{1,0:T(8,128)(2,1)}, bf16[2048,1536]{1,0:T(8,128)(2,1)}, f32[11,8,1,256]{3,2,1,0:T(1,128)}) custom-call(s32[16,52]{1,0:T(8,128)} %copy-done.65, s32[16,52]{1,0:T(8,128)} %get-tuple-element.312.piece_ref, s32[16,52]{1,0:T(8,128)} %get-tuple-element.311.source_ref, s32[16]{0:T(128)} %get-tuple-element.273.groups_ref, ...), custom_call_target="tpu_custom_call" | custom-call | bytes 81000000 | tf_op jit(solution)/shard_map/pallas_call | solution.py:491
  851.3 41.9 %collective-permute-done.30 = bf16[1,3,2,2,192,512]{5,4,1,3,2,0:T(8,128)(2,1)} collective-permute-done((bf16[1,3,2,2,192,512]{5,4,1,3,2,0:T(8,128)(2,1)}, bf16[1,3,2,2,192,512]{5,4,1,3,2,0:T(8,128)(2,1)}, u32[]{:S(2)}, u32[]{:S(2)}) %collective-permute-start.30) | collective-permute-done | bytes 2359328 | tf_op jit(solution)/shard_map/ppermute | solution.py:522
  913.1 27.0 %shard_map.255 = (bf16[1024,1536]{1,0:T(8,128)(2,1)}, bf16[1024,1536]{1,0:T(8,128)(2,1)}, f32[11,4,1,256]{3,2,1,0:T(1,128)}) custom-call(s32[16,52]{1,0:T(8,128)} %copy-done.65, s32[16,52]{1,0:T(8,128)} %get-tuple-element.312.piece_ref, s32[16,52]{1,0:T(8,128)} %get-tuple-element.311.source_ref, s32[16]{0:T(128)} %get-tuple-element.273.groups_ref, ...), custom_call_target="tpu_custom_call" | custom-call | bytes 81000000 | tf_op jit(solution)/shard_map/pallas_call | solution.py:491
  955.8 26.5 %shard_map.256 = (bf16[1024,1536]{1,0:T(8,128)(2,1)}, bf16[1024,1536]{1,0:T(8,128)(2,1)}, f32[11,4,1,256]{3,2,1,0:T(1,128)}) custom-call(s32[16,52]{1,0:T(8,128)} %copy-done.65, s32[16,52]{1,0:T(8,128)} %get-tuple-element.312.piece_ref, s32[16,52]{1,0:T(8,128)} %get-tuple-element.311.source_ref, s32[16]{0:T(128)} %get-tuple-element.273.groups_ref, ...), custom_call_target="tpu_custom_call" | custom-call | bytes 81000000 | tf_op jit(solution)/shard_map/pallas_call | solution.py:491
  1056.0 39.8 %shard_map.257 = (bf16[1024,768]{1,0:T(8,128)(2,1)}, bf16[1024,256]{1,0:T(8,128)(2,1)}, bf16[1024,256]{1,0:T(8,128)(2,1)}) custom-call(bf16[1024,768]{1,0:T(8,128)(2,1)} %get-tuple-element.121.query_ref, bf16[1024,256]{1,0:T(8,128)(2,1)} %get-tuple-element.122.key_ref, bf16[1024,256]{1,0:T(8,128)(2,1)} %get-tuple-element.123.value_ref, ...), custom_call_target="tpu_custom_call" | custom-call | bytes 72000000 | tf_op jit(solution)/shard_map/pallas_call | solution.py:820
  1124.1 39.8 %shard_map.258 = (bf16[1024,768]{1,0:T(8,128)(2,1)}, bf16[1024,256]{1,0:T(8,128)(2,1)}, bf16[1024,256]{1,0:T(8,128)(2,1)}) custom-call(bf16[1024,768]{1,0:T(8,128)(2,1)} %get-tuple-element.117.query_ref, bf16[1024,256]{1,0:T(8,128)(2,1)} %get-tuple-element.118.key_ref, bf16[1024,256]{1,0:T(8,128)(2,1)} %get-tuple-element.119.value_ref, ...), custom_call_target="tpu_custom_call" | custom-call | bytes 72000000 | tf_op jit(solution)/shard_map/pallas_call | solution.py:820
  1310.1 71.7 %collective-permute-done.52 = f32[64552]{0:T(1024)S(1)} collective-permute-done((f32[64552]{0:T(1024)S(1)}, f32[64552]{0:T(1024)S(1)}, u32[]{:S(2)}, u32[]{:S(2)}) %collective-permute-start.52) | collective-permute-done | bytes 258240 | tf_op jit(solution)/shard_map/ppermute | solution.py:526
  (607 shorter events, 619.4 us)
Async XLA Ops:
  148.8 99.0 %collective-permute-start.12 = (bf16[1024,1536]{1,0:T(8,128)(2,1)}, bf16[1024,1536]{1,0:T(8,128)(2,1)}, u32[]{:S(2)}, u32[]{:S(2)}) collective-permute-start(bf16[1024,1536]{1,0:T(8,128)(2,1)} %multiply_convert_fusion.rest_1_), channel_id=1, source_target_pairs={{0,1},{1,0},{2,3},{3,2},{4,5},{5,4},{6,7},{7,6},{8,9},{9,8},{10,11... | collective-permute-start | bytes 9437192 | tf_op jit(solution)/shard_map/ppermute | solution.py:526
  157.7 114.0 %collective-permute-start.16 = (bf16[1024,1536]{1,0:T(8,128)(2,1)}, bf16[1024,1536]{1,0:T(8,128)(2,1)}, u32[]{:S(2)}, u32[]{:S(2)}) collective-permute-start(bf16[1024,1536]{1,0:T(8,128)(2,1)} %multiply_convert_fusion.rest_1_), channel_id=1, source_target_pairs={{0,2},{2,0},{4,6},{6,4},{8,10},{10,8},{12,14},{14,12},{16,18},{18,... | collective-permute-start | bytes 9437192 | tf_op jit(solution)/shard_map/ppermute | solution.py:522
  318.5 106.7 %collective-permute-start.23 = (bf16[1,3,2,2,192,512]{5,4,1,3,2,0:T(8,128)(2,1)}, bf16[1,3,2,2,192,512]{5,4,1,3,2,0:T(8,128)(2,1)}, u32[]{:S(2)}, u32[]{:S(2)}) collective-permute-start(bf16[1,3,2,2,192,512]{5,4,1,3,2,0:T(8,128)(2,1)} %copy.229), channel_id=1, source_target_pairs={{0,4},{2,6},{4,0},{6,2},{8,12},{10,14},{12,8},{14,10},{16,20},{18,... | collective-permute-start | bytes 7077896 | tf_op jit(solution)/shard_map/ppermute | solution.py:522
  346.1 143.2 %collective-permute-start.24 = (bf16[1,3,2,2,192,512]{5,4,1,3,2,0:T(8,128)(2,1)}, bf16[1,3,2,2,192,512]{5,4,1,3,2,0:T(8,128)(2,1)}, u32[]{:S(2)}, u32[]{:S(2)}) collective-permute-start(bf16[1,3,2,2,192,512]{5,4,1,3,2,0:T(8,128)(2,1)} %copy.232), channel_id=1, source_target_pairs={{0,4},{2,6},{4,0},{6,2},{8,12},{10,14},{12,8},{14,10},{16,20},{18,... | collective-permute-start | bytes 7077896 | tf_op jit(solution)/shard_map/ppermute | solution.py:522
  459.4 119.3 %collective-permute-start.26 = (bf16[1,3,2,2,192,512]{5,4,1,3,2,0:T(8,128)(2,1)}, bf16[1,3,2,2,192,512]{5,4,1,3,2,0:T(8,128)(2,1)}, u32[]{:S(2)}, u32[]{:S(2)}) collective-permute-start(bf16[1,3,2,2,192,512]{5,4,1,3,2,0:T(8,128)(2,1)} %copy.236), channel_id=1, source_target_pairs={{0,8},{2,10},{4,12},{6,14},{8,0},{10,2},{12,4},{14,6},{16,24},{18,... | collective-permute-start | bytes 7077896 | tf_op jit(solution)/shard_map/ppermute | solution.py:522
  486.9 134.0 %collective-permute-start.27 = (bf16[1,3,2,2,192,512]{5,4,1,3,2,0:T(8,128)(2,1)}, bf16[1,3,2,2,192,512]{5,4,1,3,2,0:T(8,128)(2,1)}, u32[]{:S(2)}, u32[]{:S(2)}) collective-permute-start(bf16[1,3,2,2,192,512]{5,4,1,3,2,0:T(8,128)(2,1)} %copy.239), channel_id=1, source_target_pairs={{0,4},{2,6},{4,0},{6,2},{8,12},{10,14},{12,8},{14,10},{16,20},{18,... | collective-permute-start | bytes 7077896 | tf_op jit(solution)/shard_map/ppermute | solution.py:522
  552.6 186.8 %collective-permute-start.29 = (bf16[1,3,2,2,192,512]{5,4,1,3,2,0:T(8,128)(2,1)}, bf16[1,3,2,2,192,512]{5,4,1,3,2,0:T(8,128)(2,1)}, u32[]{:S(2)}, u32[]{:S(2)}) collective-permute-start(bf16[1,3,2,2,192,512]{5,4,1,3,2,0:T(8,128)(2,1)} %copy.243), channel_id=1, source_target_pairs={{0,4},{2,6},{4,0},{6,2},{8,12},{10,14},{12,8},{14,10},{16,20},{18,... | collective-permute-start | bytes 7077896 | tf_op jit(solution)/shard_map/ppermute | solution.py:522
  576.6 198.1 %collective-permute-start.31 = (bf16[1,3,2,2,192,512]{5,4,1,3,2,0:T(8,128)(2,1)}, bf16[1,3,2,2,192,512]{5,4,1,3,2,0:T(8,128)(2,1)}, u32[]{:S(2)}, u32[]{:S(2)}) collective-permute-start(bf16[1,3,2,2,192,512]{5,4,1,3,2,0:T(8,128)(2,1)} %copy.248), channel_id=1, source_target_pairs={{0,8},{2,10},{4,12},{6,14},{8,0},{10,2},{12,4},{14,6},{16,24},{18,... | collective-permute-start | bytes 7077896 | tf_op jit(solution)/shard_map/ppermute | solution.py:522
  578.3 103.3 %collective-permute-start.28 = (bf16[1,3,2,192,512]{4,3,1,2,0:T(8,128)(2,1)}, bf16[1,3,2,192,512]{4,3,1,2,0:T(8,128)(2,1)}, u32[]{:S(2)}, u32[]{:S(2)}) collective-permute-start(bf16[1,3,2,192,512]{4,3,1,2,0:T(8,128)(2,1)} %get-tuple-element.300), channel_id=1, source_target_pairs={{0,8},{2,10},{4,12},{6,14},{8,0},{10,2},{12,4},{14,6},{16,24},{18,... | collective-permute-start | bytes 3538952 | tf_op jit(solution)/shard_map/ppermute | solution.py:522
  585.6 189.0 %collective-permute-start.32 = (bf16[1,3,2,192,512]{4,3,1,2,0:T(8,128)(2,1)}, bf16[1,3,2,192,512]{4,3,1,2,0:T(8,128)(2,1)}, u32[]{:S(2)}, u32[]{:S(2)}) collective-permute-start(bf16[1,3,2,192,512]{4,3,1,2,0:T(8,128)(2,1)} %get-tuple-element.298), channel_id=1, source_target_pairs={{0,16},{2,18},{4,20},{6,22},{8,24},{10,26},{12,28},{14,30},{16,0},... | collective-permute-start | bytes 3538952 | tf_op jit(solution)/shard_map/ppermute | solution.py:522
  625.5 149.1 %collective-permute-start.33 = (bf16[1,3,2,192,512]{4,3,1,2,0:T(8,128)(2,1)}, bf16[1,3,2,192,512]{4,3,1,2,0:T(8,128)(2,1)}, u32[]{:S(2)}, u32[]{:S(2)}) collective-permute-start(bf16[1,3,2,192,512]{4,3,1,2,0:T(8,128)(2,1)} %get-tuple-element.296), channel_id=1, source_target_pairs={{0,8},{2,10},{4,12},{6,14},{8,0},{10,2},{12,4},{14,6},{16,24},{18,... | collective-permute-start | bytes 3538952 | tf_op jit(solution)/shard_map/ppermute | solution.py:522
  835.0 169.9 %collective-permute-start.36 = (bf16[2048,1536]{1,0:T(8,128)(2,1)}, bf16[2048,1536]{1,0:T(8,128)(2,1)}, u32[]{:S(2)}, u32[]{:S(2)}) collective-permute-start(bf16[2048,1536]{1,0:T(8,128)(2,1)} %get-tuple-element.180), channel_id=1, source_target_pairs={{0,2},{2,0},{4,6},{6,4},{8,10},{10,8},{12,14},{14,12},{16,18},{18,... | collective-permute-start | bytes 18874376 | tf_op jit(solution)/shard_map/ppermute | solution.py:522
  843.4 102.2 %collective-permute-start.43 = (bf16[1,3,2,2,192,512]{5,4,1,3,2,0:T(8,128)(2,1)}, bf16[1,3,2,2,192,512]{5,4,1,3,2,0:T(8,128)(2,1)}, u32[]{:S(2)}, u32[]{:S(2)}) collective-permute-start(bf16[1,3,2,2,192,512]{5,4,1,3,2,0:T(8,128)(2,1)} %copy.261), channel_id=1, source_target_pairs={{0,4},{2,6},{4,0},{6,2},{8,12},{10,14},{12,8},{14,10},{16,20},{18,... | collective-permute-start | bytes 7077896 | tf_op jit(solution)/shard_map/ppermute | solution.py:522
  893.2 100.2 %collective-permute-start.40 = (bf16[1,3,2,2,192,512]{5,4,1,3,2,0:T(8,128)(2,1)}, bf16[1,3,2,2,192,512]{5,4,1,3,2,0:T(8,128)(2,1)}, u32[]{:S(2)}, u32[]{:S(2)}) collective-permute-start(bf16[1,3,2,2,192,512]{5,4,1,3,2,0:T(8,128)(2,1)} %copy.257), channel_id=1, source_target_pairs={{0,4},{2,6},{4,0},{6,2},{8,12},{10,14},{12,8},{14,10},{16,20},{18,... | collective-permute-start | bytes 7077896 | tf_op jit(solution)/shard_map/ppermute | solution.py:522
  982.3 225.4 %collective-permute-start.65 = (bf16[1,3,192,512]{3,2,1,0:T(8,128)(2,1)}, bf16[1,3,192,512]{3,2,1,0:T(8,128)(2,1)}, u32[]{:S(2)}, u32[]{:S(2)}) collective-permute-start(bf16[1,3,192,512]{3,2,1,0:T(8,128)(2,1)} %fusion.62.rest_3_), channel_id=1, source_target_pairs={{0,16},{2,18},{4,20},{6,22},{8,24},{10,26},{12,28},{14,30},{16,0},... | collective-permute-start | bytes 1769480 | tf_op jit(solution)/shard_map/ppermute | solution.py:522
  982.4 212.4 %collective-permute-start.66 = (bf16[1,3,192,512]{3,2,1,0:T(8,128)(2,1)}, bf16[1,3,192,512]{3,2,1,0:T(8,128)(2,1)}, u32[]{:S(2)}, u32[]{:S(2)}) collective-permute-start(bf16[1,3,192,512]{3,2,1,0:T(8,128)(2,1)} %fusion.63.rest_3_), channel_id=1, source_target_pairs={{0,16},{2,18},{4,20},{6,22},{8,24},{10,26},{12,28},{14,30},{16,0},... | collective-permute-start | bytes 1769480 | tf_op jit(solution)/shard_map/ppermute | solution.py:522
  996.7 117.5 %collective-permute-start.45 = (bf16[1,3,2,2,192,512]{5,4,1,3,2,0:T(8,128)(2,1)}, bf16[1,3,2,2,192,512]{5,4,1,3,2,0:T(8,128)(2,1)}, u32[]{:S(2)}, u32[]{:S(2)}) collective-permute-start(bf16[1,3,2,2,192,512]{5,4,1,3,2,0:T(8,128)(2,1)} %copy.267), channel_id=1, source_target_pairs={{0,4},{2,6},{4,0},{6,2},{8,12},{10,14},{12,8},{14,10},{16,20},{18,... | collective-permute-start | bytes 7077896 | tf_op jit(solution)/shard_map/ppermute | solution.py:522
  1097.7 119.8 %collective-permute-start.68 = (bf16[1,3,192,512]{3,2,1,0:T(8,128)(2,1)}, bf16[1,3,192,512]{3,2,1,0:T(8,128)(2,1)}, u32[]{:S(2)}, u32[]{:S(2)}) collective-permute-start(bf16[1,3,192,512]{3,2,1,0:T(8,128)(2,1)} %fusion.65.rest_2_), channel_id=1, source_target_pairs={{0,16},{2,18},{4,20},{6,22},{8,24},{10,26},{12,28},{14,30},{16,0},... | collective-permute-start | bytes 1769480 | tf_op jit(solution)/shard_map/ppermute | solution.py:522
  1101.8 85.8 %collective-permute-start.67 = (bf16[1,3,192,512]{3,2,1,0:T(8,128)(2,1)}, bf16[1,3,192,512]{3,2,1,0:T(8,128)(2,1)}, u32[]{:S(2)}, u32[]{:S(2)}) collective-permute-start(bf16[1,3,192,512]{3,2,1,0:T(8,128)(2,1)} %fusion.64.rest_1_), channel_id=1, source_target_pairs={{0,4},{2,6},{4,0},{6,2},{8,12},{10,14},{12,8},{14,10},{16,20},{18,... | collective-permute-start | bytes 1769480 | tf_op jit(solution)/shard_map/ppermute | solution.py:522
  1114.3 108.0 %collective-permute-start.69 = (bf16[1,3,192,512]{3,2,1,0:T(8,128)(2,1)}, bf16[1,3,192,512]{3,2,1,0:T(8,128)(2,1)}, u32[]{:S(2)}, u32[]{:S(2)}) collective-permute-start(bf16[1,3,192,512]{3,2,1,0:T(8,128)(2,1)} %fusion.66.rest_1_), channel_id=1, source_target_pairs={{0,16},{2,18},{4,20},{6,22},{8,24},{10,26},{12,28},{14,30},{16,0},... | collective-permute-start | bytes 1769480 | tf_op jit(solution)/shard_map/ppermute | solution.py:522
  1287.4 139.5 %collective-permute-start.44 = (bf16[1024,1536]{1,0:T(8,128)(2,1)}, bf16[1024,1536]{1,0:T(8,128)(2,1)}, u32[]{:S(2)}, u32[]{:S(2)}) collective-permute-start(bf16[1024,1536]{1,0:T(8,128)(2,1)} %add_convert_fusion.1), channel_id=1, source_target_pairs={{0,1},{1,0},{2,3},{3,2},{4,5},{5,4},{6,7},{7,6},{8,9},{9,8},{10,11... | collective-permute-start | bytes 9437192 | tf_op jit(solution)/shard_map/ppermute | solution.py:526
  1297.5 108.3 %collective-permute-start.53 = (bf16[8,96,1280]{2,1,0:T(8,128)(2,1)}, bf16[8,96,1280]{2,1,0:T(8,128)(2,1)}, u32[]{:S(2)}, u32[]{:S(2)}) collective-permute-start(bf16[8,96,1280]{2,1,0:T(8,128)(2,1)} %fusion.14), channel_id=1, source_target_pairs={{0,2},{2,0},{4,6},{6,4},{8,10},{10,8},{12,14},{14,12},{16,18},{18,... | collective-permute-start | bytes 5898248 | tf_op jit(solution)/shard_map/ppermute | solution.py:522
  1300.5 92.7 %collective-permute-start.75 = (bf16[1,3,192,512]{3,2,1,0:T(8,128)(2,1)}, bf16[1,3,192,512]{3,2,1,0:T(8,128)(2,1)}, u32[]{:S(2)}, u32[]{:S(2)}) collective-permute-start(bf16[1,3,192,512]{3,2,1,0:T(8,128)(2,1)} %fusion.91), channel_id=1, source_target_pairs={{0,16},{2,18},{4,20},{6,22},{8,24},{10,26},{12,28},{14,30},{16,0},... | collective-permute-start | bytes 1769480 | tf_op jit(solution)/shard_map/ppermute | solution.py:522
  1308.8 113.2 %collective-permute-start.55 = (bf16[8,96,1280]{2,1,0:T(8,128)(2,1)}, bf16[8,96,1280]{2,1,0:T(8,128)(2,1)}, u32[]{:S(2)}, u32[]{:S(2)}) collective-permute-start(bf16[8,96,1280]{2,1,0:T(8,128)(2,1)} %fusion.10), channel_id=1, source_target_pairs={{0,1},{1,0},{2,3},{3,2},{4,5},{5,4},{6,7},{7,6},{8,9},{9,8},{10,11... | collective-permute-start | bytes 5898248 | tf_op jit(solution)/shard_map/ppermute | solution.py:526
  (165 other events, 3903.4 us)

commit v3 on v2

--- a/solution.py
+++ b/solution.py
@@ -83,14 +83,9 @@
 
 BLOCK = 256
 PART = 256
-PIECE_ROWS = 64
-GROUP = BLOCK // PIECE_ROWS
+PIECE_ROWS = 32
+GROUP = 8
 VMEM_LIMIT = 60 * 1024 * 1024
-COST = 0.6
-
-
-def cost(micros):
-    return pl.CostEstimate(flops=0, bytes_accessed=int(micros * 3e6), transcendentals=0)
 
 
 def dot_nt(left, right):
@@ -109,7 +104,7 @@
     return -(-value // multiple) * multiple
 
 
-def placement(routes_rows, gates_rows, first_expert, experts):
+def placement(routes_rows, first_expert, experts):
     rows = routes_rows.shape[0]
     tiles = rows // BLOCK
     turned = routes_rows.T
@@ -131,12 +126,14 @@
     place = jnp.concatenate(
         [place, jnp.full((1, tiles, BLOCK), -1, jnp.int32)], axis=0
     ).reshape(experts + 1, tiles, 1, BLOCK)
-    gates = None
-    if gates_rows is not None:
-        gates = jnp.sum(
-            jnp.where(hit, gates_rows.astype(jnp.float32).T[None, :, :], 0.0), axis=1
-        ).reshape(experts, tiles, 1, BLOCK)
-    return place, begins, ends, gates
+    return place, begins, ends
+
+
+def gate_table(routes_rows, gates_rows, first_expert, experts):
+    names = first_expert + jnp.arange(experts, dtype=jnp.int32)
+    hit = routes_rows.T[None, :, :] == names[:, None, None]
+    table = jnp.sum(jnp.where(hit, gates_rows.astype(jnp.float32).T[None, :, :], 0.0), axis=1)
+    return jnp.pad(table, ((0, 128 - experts), (0, 0))).T.astype(jnp.bfloat16)
 
 
 def gather_tables(begins, ends, slots):
@@ -170,22 +167,19 @@
     return owner, piece, source, groups, width
 
 
-def gather_kernel(
-    experts, slots, sources, with_gates, after, low_ref, high_ref, blocks_ref, place_ref, *rest
-):
+def gather_kernel(sources, with_gates, after, low_ref, high_ref, blocks_ref, place_ref, *rest):
     if with_gates:
         gates_ref, rest = rest[0], rest[1:]
     inputs, rest = rest[:sources], rest[sources + after :]
     if with_gates:
-        out_ref, gate_out_ref, rest = rest[0], rest[1], rest[2:]
+        out_ref, gate_out_ref, held, buffer, gate_buffer, sems, out_sems = rest
     else:
-        out_ref, rest = rest[0], rest[1:]
-    held, total, gate_total, sems = rest
+        out_ref, held, buffer, sems, out_sems = rest
     expert = pl.program_id(0)
-    part = pl.program_id(1)
     share = inputs[0].shape[0]
-
-    @pl.when((expert == 0) & (part == 0))
+    slots = out_ref.shape[0] // pl.num_programs(0)
+
+    @pl.when(expert == 0)
     def _():
         copies = [
             pltpu.make_async_copy(ref, held.at[pl.ds(i * share, share)], sems.at[i])
@@ -196,88 +190,111 @@
         for copy in copies:
             copy.wait()
 
-    @pl.when(part * PART < blocks_ref[expert] * BLOCK)
-    def _():
-        total[...] = jnp.zeros_like(total)
+    def copies_of(part, slot):
+        start = pl.multiple_of(expert * slots + part * PART, PART)
+        made = [
+            pltpu.make_async_copy(
+                buffer.at[slot], out_ref.at[pl.ds(start, PART)], out_sems.at[0, slot]
+            )
+        ]
         if with_gates:
-            gate_total[...] = jnp.zeros_like(gate_total)
+            made.append(
+                pltpu.make_async_copy(
+                    gate_buffer.at[slot], gate_out_ref.at[pl.ds(start, PART)], out_sems.at[1, slot]
+                )
+            )
+        return made
+
+    parts = blocks_ref[expert] * (BLOCK // PART)
+
+    def one(part, carry):
+        slot = part % 2
+
+        @pl.when(part >= 2)
+        def _():
+            for copy in copies_of(part - 2, slot):
+                copy.wait()
+
+        buffer[slot] = jnp.zeros(buffer.shape[1:], buffer.dtype)
+        if with_gates:
+            gate_buffer[slot] = jnp.zeros(gate_buffer.shape[1:], gate_buffer.dtype)
         rows = lax.broadcasted_iota(jnp.int32, (PART, BLOCK), 0) + part * PART
 
-        def step(tile, carry):
-            match = rows == place_ref[expert, tile]
-            pick = jnp.where(match, 1.0, 0.0)
-            start = pl.multiple_of(tile * BLOCK, BLOCK)
-            total[...] += jnp.dot(
-                pick.astype(jnp.bfloat16),
-                held[pl.ds(start, BLOCK), :],
-                preferred_element_type=jnp.float32,
-            )
+        def step(pair, carry):
+            pick = jnp.concatenate(
+                [
+                    jnp.where(rows == place_ref[expert, 2 * pair + i], 1.0, 0.0)
+                    for i in range(2)
+                ],
+                axis=1,
+            ).astype(jnp.bfloat16)
+            start = pl.multiple_of(pair * 2 * BLOCK, 2 * BLOCK)
+            buffer[slot] += jnp.dot(
+                pick, held[pl.ds(start, 2 * BLOCK), :], preferred_element_type=jnp.float32
+            ).astype(buffer.dtype)
             if with_gates:
-                weighted = pick * gates_ref[expert, tile]
-                gate_total[...] += jnp.broadcast_to(
-                    jnp.sum(weighted, axis=1, keepdims=True), gate_total.shape
+                gate_buffer[slot] += jnp.dot(
+                    pick, gates_ref[pl.ds(start, 2 * BLOCK), :], preferred_element_type=jnp.float32
                 )
             return carry
 
-        lax.fori_loop(low_ref[expert, part], high_ref[expert, part], step, 0)
-        out_ref[...] = total[...].astype(out_ref.dtype)
-        if with_gates:
-            gate_out_ref[...] = gate_total[...]
+        lax.fori_loop(
+            low_ref[expert, part] // 2, (high_ref[expert, part] + 1) // 2, step, 0
+        )
+        for copy in copies_of(part, slot):
+            copy.start()
+        return carry
+
+    lax.fori_loop(0, parts, one, 0)
+    for back in (2, 1):
+        for copy in copies_of(parts - back, (parts - back) % 2):
+            copy.wait()
 
 
 def gather_rows(tables, place, gates, sources, slots, first, count, after=()):
     low, high, blocks = tables
     low, high, blocks = (t[first : first + count] for t in (low, high, blocks))
     place = place[first : first + count]
-    tiles = place.shape[1]
-    rows = tiles * BLOCK
+    rows = place.shape[1] * BLOCK
     width = sources[0].shape[1]
     with_gates = gates is not None
-    if with_gates:
-        gates = gates[first : first + count]
-    parts = slots // PART
-
-    def out_index(expert, part, low, high, blocks):
-        return (expert * parts + jnp.minimum(part, blocks[expert] * (BLOCK // PART) - 1), 0)
 
     def whole(array):
         zeros = (0,) * array.ndim
         return pl.BlockSpec(array.shape, lambda *_: zeros)
 
     operands = [place] + ([gates] if with_gates else [])
-    in_specs = [whole(a) for a in operands] + [pl.BlockSpec(memory_space=pl.ANY)] * (
-        len(sources) + len(after)
-    )
+    anywhere = pl.BlockSpec(memory_space=pl.ANY)
+    in_specs = [whole(a) for a in operands] + [anywhere] * (len(sources) + len(after))
     out_shape = [jax.ShapeDtypeStruct((count * slots, width), jnp.bfloat16)]
-    out_specs = [pl.BlockSpec((PART, width), out_index)]
+    scratch = [
+        pltpu.VMEM((rows, width), jnp.bfloat16),
+        pltpu.VMEM((2, PART, width), jnp.bfloat16),
+    ]
     if with_gates:
         out_shape.append(jax.ShapeDtypeStruct((count * slots, 128), jnp.float32))
-        out_specs.append(pl.BlockSpec((PART, 128), out_index))
+        scratch.append(pltpu.VMEM((2, PART, 128), jnp.float32))
     return pl.pallas_call(
-        functools.partial(gather_kernel, count, slots, len(sources), with_gates, len(after)),
+        functools.partial(gather_kernel, len(sources), with_gates, len(after)),
         grid_spec=pltpu.PrefetchScalarGridSpec(
             num_scalar_prefetch=3,
-            grid=(count, parts),
+            grid=(count,),
             in_specs=in_specs,
-            out_specs=out_specs,
-            scratch_shapes=[
-                pltpu.VMEM((rows, width), jnp.bfloat16),
-                pltpu.VMEM((PART, width), jnp.float32),
-                pltpu.VMEM((PART, 128), jnp.float32),
-                pltpu.SemaphoreType.DMA((len(sources),)),
-            ],
+            out_specs=[anywhere] * len(out_shape),
+            scratch_shapes=scratch
+            + [pltpu.SemaphoreType.DMA((len(sources),)), pltpu.SemaphoreType.DMA((2, 2))],
         ),
         out_shape=out_shape,
         compiler_params=pltpu.CompilerParams(vmem_limit_bytes=VMEM_LIMIT),
-        cost_estimate=cost(COST * count * 5.5),
     )(low, high, blocks, *operands, *sources, *after)
 
 
 def expert_kernel(
-    first, split, depth, far_first, extra, blocks_ref, misc_ref, x_ref, c_ref, sg_ref, wg_ref, wu_ref, wd_ref, *rest
+    first, split, depth, far_first, extra, blocks_ref, misc_ref, x_ref, c_ref, sg_ref, wg_ref,
+    wu_ref, wd_ref, *rest
 ):
-    yd_ref, gg_ref = rest[extra : extra + 2]
-    rest = rest[extra + 2 :]
+    yd_ref = rest[extra]
+    rest = rest[extra + 1 :]
     width = x_ref.shape[1]
     if split:
         send_ref, keep_ref = rest[:2]
@@ -285,28 +302,29 @@
     else:
         grads_ref = rest[0]
         rest = rest[1:]
-    total_gu, total_d = rest
+    total_gu, total_d, x_held, c_held, low_held, gated_held = rest
+    expert = first + pl.program_id(0)
     block = pl.program_id(1)
     hidden = wg_ref.shape[2]
-
-    @pl.when(block == 0)
-    def _():
-        total_gu[...] = jnp.zeros_like(total_gu)
-        total_d[...] = jnp.zeros_like(total_d)
-
-    @pl.when(block < blocks_ref[first + pl.program_id(0)])
+    blocks = blocks_ref[expert]
+    lanes = lax.broadcasted_iota(jnp.int32, (BLOCK, 128), 1)
+
+    @pl.when(block < blocks)
     def _():
         x = x_ref[...]
         c = c_ref[...]
-        gate = jnp.concatenate([sg_ref[...]] * (hidden // 128), axis=1)
+        gate = jnp.sum(jnp.where(lanes == expert, sg_ref[...], 0.0), axis=1, keepdims=True)
         gate_proj = jnp.dot(x, wg_ref[0], preferred_element_type=jnp.float32)
         up_proj = jnp.dot(x, wu_ref[0], preferred_element_type=jnp.float32)
+        pulled = dot_nt(c, wd_ref[0])
         sigmoid = 1.0 / (1.0 + jnp.exp(-gate_proj))
         silu = gate_proj * sigmoid
         activated = (silu * up_proj).astype(jnp.bfloat16).astype(jnp.float32)
-        pulled = dot_nt(c, wd_ref[0])
         gate_grad = jnp.sum(activated * pulled, axis=1, keepdims=True)
-        gg_ref[...] = jnp.broadcast_to(gate_grad, gg_ref.shape)
+        coarse = gate_grad.astype(jnp.bfloat16).astype(jnp.float32)
+        yd_ref[:, 2 * width :] = jnp.where(
+            lanes == expert, coarse, jnp.where(lanes == expert + 64, gate_grad - coarse, 0.0)
+        ).astype(yd_ref.dtype)
         gated = (gate * activated).astype(jnp.bfloat16)
         yd_ref[:, :width] = jnp.dot(
             gated, wd_ref[0], preferred_element_type=jnp.float32
@@ -316,11 +334,45 @@
             activated_grad * up_proj * sigmoid * (1.0 + gate_proj * (1.0 - sigmoid))
         ).astype(jnp.bfloat16)
         up_low = (activated_grad * silu).astype(jnp.bfloat16)
-        yd_ref[:, width:] = (dot_nt(gate_low, wg_ref[0]) + dot_nt(up_low, wu_ref[0])).astype(
-            yd_ref.dtype
-        )
-        total_gu[...] += dot_tn(x, jnp.concatenate([gate_low, up_low], axis=1))
-        total_d[...] += dot_tn(c, gated)
+        yd_ref[:, width : 2 * width] = (
+            dot_nt(gate_low, wg_ref[0]) + dot_nt(up_low, wu_ref[0])
+        ).astype(yd_ref.dtype)
+        start = pl.multiple_of((block % 2) * BLOCK, BLOCK)
+        held = pl.ds(start, BLOCK)
+        x_held[held, :] = x
+        c_held[held, :] = c
+        low_held[held, :hidden] = gate_low
+        low_held[held, hidden:] = up_low
+        gated_held[held, :] = gated
+
+    def gather(rows, fresh):
+        for begin in range(0, width, BLOCK):
+            span = slice(begin, begin + BLOCK)
+            for total, left, right in (
+                (total_gu, x_held, low_held),
+                (total_d, c_held, gated_held),
+            ):
+                term = dot_tn(left[:rows, span], right[:rows, :])
+                total[span, :] = term if fresh else total[span, :] + term
+
+    odd = block % 2 == 1
+    last = block == blocks - 1
+
+    @pl.when((block == 0) & last)
+    def _():
+        gather(BLOCK, True)
+
+    @pl.when((block == 1) & (block < blocks))
+    def _():
+        gather(2 * BLOCK, True)
+
+    @pl.when((block > 1) & odd & (block < blocks))
+    def _():
+        gather(2 * BLOCK, False)
+
+    @pl.when((block > 1) & jnp.logical_not(odd) & last)
+    def _():
+        gather(BLOCK, False)
 
     @pl.when(block == pl.num_programs(1) - 1)
     def _():
@@ -335,9 +387,13 @@
                 for high in range(2):
                     for low in range(2):
                         for out, chosen in ((keep_ref, side), (send_ref, 1 - side)):
-                            middle, last = (chosen, low) if far_first else (low, chosen)
-                            start = ((high * 2 + middle) * 2 + last) * depth
-                            out[0, which, high, low] = ref[
+                            if far_first:
+                                start = ((high * 2 + chosen) * 2 + low) * depth
+                                place = (high, low, which)
+                            else:
+                                start = ((high * 2 + low) * 2 + chosen) * depth
+                                place = (low, high, which)
+                            out[place] = ref[
                                 pl.ds(pl.multiple_of(start, 64), depth), pl.ds(column, hidden)
                             ].astype(out.dtype)
             else:
@@ -345,7 +401,8 @@
 
 
 def expert_call(
-    blocks, misc, x, c, sg, weights, carried, slots, first, count, x_first, c_first, depth, far_first=0, after=()
+    blocks, misc, x, c, sg, weights, carried, slots, first, count, x_first, c_first, depth,
+    far_first=0, after=()
 ):
     w_gate, w_up, w_down = weights
     experts = blocks.shape[0]
@@ -365,19 +422,13 @@
         return (misc[0] + first + expert, 0, 0)
 
     def grads_index(expert, block, blocks, misc):
-        return (expert, 0, 0, 0, 0, 0)
-
-    out_shape = [
-        jax.ShapeDtypeStruct((experts * slots, 2 * width), jnp.bfloat16),
-        jax.ShapeDtypeStruct((experts * slots, 128), jnp.float32),
-    ]
-    out_specs = [
-        pl.BlockSpec((BLOCK, 2 * width), rows_index(0)),
-        pl.BlockSpec((BLOCK, 128), rows_index(0)),
-    ]
+        return (0, 0, 0, 0, 0)
+
+    out_shape = [jax.ShapeDtypeStruct((experts * slots, 2 * width + 128), jnp.bfloat16)]
+    out_specs = [pl.BlockSpec((BLOCK, 2 * width + 128), rows_index(0))]
     if split:
-        out_shape += [jax.ShapeDtypeStruct((count, 3, 2, 2, depth, hidden), jnp.bfloat16)] * 2
-        out_specs += [pl.BlockSpec((1, 3, 2, 2, depth, hidden), grads_index)] * 2
+        out_shape += [jax.ShapeDtypeStruct((2, 2, 3, depth, hidden), jnp.bfloat16)] * 2
+        out_specs += [pl.BlockSpec((2, 2, 3, depth, hidden), grads_index)] * 2
     else:
         out_shape += [jax.ShapeDtypeStruct((count, 3, width, hidden), jnp.bfloat16)]
         out_specs += [pl.BlockSpec((1, 3, width, hidden), lambda e, b, *_: (e, 0, 0, 0))]
@@ -392,8 +443,8 @@
     ]
     aliases = {}
     if carried is not None:
-        operands += list(carried)
-        aliases = {8: 0, 9: 1}
+        operands.append(carried)
+        aliases = {8: 0}
     operands += list(after)
     extra = len(operands) - 6
     in_specs += [pl.BlockSpec(memory_space=pl.ANY)] * extra
@@ -407,19 +458,22 @@
             scratch_shapes=[
                 pltpu.VMEM((width, 2 * hidden), jnp.float32),
                 pltpu.VMEM((width, hidden), jnp.float32),
+                pltpu.VMEM((2 * BLOCK, width), jnp.bfloat16),
+                pltpu.VMEM((2 * BLOCK, width), jnp.bfloat16),
+                pltpu.VMEM((2 * BLOCK, 2 * hidden), jnp.bfloat16),
+                pltpu.VMEM((2 * BLOCK, hidden), jnp.bfloat16),
             ],
         ),
         out_shape=out_shape,
         input_output_aliases=aliases,
         compiler_params=pltpu.CompilerParams(vmem_limit_bytes=VMEM_LIMIT),
-        cost_estimate=cost(COST * count * 21.0),
     )(blocks, misc, *operands)
 
 
 def combine_kernel(
-    first, owner_ref, piece_ref, source_ref, groups_ref, begin_ref, place_ref, yd_ref, gg_ref, *rest
+    first, owner_ref, piece_ref, source_ref, groups_ref, begin_ref, place_ref, yd_ref, *rest
 ):
-    y_out, dx_out, gate_out, yd_buf, gg_buf, total, sems = rest[-7:]
+    y_out, dx_out, gate_out, buffer, total, sems = rest[-6:]
     columns = y_out.shape[1]
     step = pl.program_id(0)
     tile = first + step
@@ -430,23 +484,19 @@
             source = pl.multiple_of(
                 source_ref[which_tile, group * GROUP + i] * PIECE_ROWS, PIECE_ROWS
             )
-            for kind, (ref, buf) in enumerate(((yd_ref, yd_buf), (gg_ref, gg_buf))):
-                made.append(
-                    pltpu.make_async_copy(
-                        ref.at[pl.ds(source, PIECE_ROWS)],
-                        buf.at[slot, pl.ds(i * PIECE_ROWS, PIECE_ROWS)],
-                        sems.at[slot, kind, i],
-                    )
+            made.append(
+                pltpu.make_async_copy(
+                    yd_ref.at[pl.ds(source, PIECE_ROWS)],
+                    buffer.at[slot, pl.ds(i * PIECE_ROWS, PIECE_ROWS)],
+                    sems.at[slot, i],
                 )
+            )
         return made
 
     @pl.when(step == 0)
     def _():
         for copy in copies(tile, 0, begin_ref[tile] % 2):
             copy.start()
-
-    total[...] = jnp.zeros_like(total)
-    gate_out[...] = jnp.zeros_like(gate_out)
 
     def one(group, carry):
         slot = (begin_ref[tile] + group) % 2
@@ -459,62 +509,58 @@
             for copy in copies(next_tile, next_group, 1 - slot):
                 copy.start()
 
-        for copy in copies(tile, group, slot):
-            copy.wait()
         picks = []
         for i in range(GROUP):
             entry = group * GROUP + i
-            expert = owner_ref[tile, entry]
             rows = (
                 lax.broadcasted_iota(jnp.int32, (PIECE_ROWS, BLOCK), 0)
                 + piece_ref[tile, entry] * PIECE_ROWS
             )
-            pick = jnp.where(rows == place_ref[expert, step], 1.0, 0.0)
-            picks.append(pick.astype(jnp.bfloat16))
-            grads = gg_buf[slot, pl.ds(i * PIECE_ROWS, PIECE_ROWS), :]
-            grads = jnp.concatenate([grads] * (BLOCK // 128), axis=1)
-            gate_out[expert, 0] += jnp.sum(pick * grads, axis=0, keepdims=True)
-        picked = jnp.concatenate(picks, axis=0)
-        total[...] += dot_tn(picked, yd_buf[slot])
+            picks.append(jnp.where(rows == place_ref[owner_ref[tile, entry], step], 1.0, 0.0))
+        picked = jnp.concatenate(picks, axis=0).T.astype(jnp.bfloat16)
+        for copy in copies(tile, group, slot):
+            copy.wait()
+        fresh = group == 0
+        for begin in range(0, total.shape[1], 640):
+            span = slice(begin, begin + 640)
+            term = jnp.dot(picked, buffer[slot, :, span], preferred_element_type=jnp.float32)
+            total[:, span] = jnp.where(fresh, 0.0, total[:, span]) + term
         return carry
 
     lax.fori_loop(0, groups_ref[tile], one, 0)
     y_out[...] = total[:, :columns].astype(y_out.dtype)
-    dx_out[...] = total[:, columns:].astype(dx_out.dtype)
-
-
-def combine_rows(tables, place, yd, gg, first, count, after=()):
+    dx_out[...] = total[:, columns : 2 * columns].astype(dx_out.dtype)
+    gate_out[...] = total[:, 2 * columns :]
+
+
+def combine_rows(tables, place, yd, first, count, after=()):
     owner, piece, source, groups, width = tables
     begin = jnp.cumsum(groups) - groups
     experts = place.shape[0]
-    columns = yd.shape[1] // 2
+    whole_width = yd.shape[1]
+    columns = (whole_width - 128) // 2
+    row_block = lambda wide: pl.BlockSpec((BLOCK, wide), lambda t, *_: (t, 0))
     return pl.pallas_call(
         functools.partial(combine_kernel, first),
         grid_spec=pltpu.PrefetchScalarGridSpec(
             num_scalar_prefetch=5,
             grid=(count,),
             in_specs=[pl.BlockSpec((experts, count, 1, BLOCK), lambda *_: (0, first // count, 0, 0))]
-            + [pl.BlockSpec(memory_space=pl.ANY)] * (2 + len(after)),
-            out_specs=[
-                pl.BlockSpec((BLOCK, columns), lambda t, *_: (t, 0)),
-                pl.BlockSpec((BLOCK, columns), lambda t, *_: (t, 0)),
-                pl.BlockSpec((experts, 1, 1, BLOCK), lambda t, *_: (0, t, 0, 0)),
-            ],
+            + [pl.BlockSpec(memory_space=pl.ANY)] * (1 + len(after)),
+            out_specs=[row_block(columns), row_block(columns), row_block(128)],
             scratch_shapes=[
-                pltpu.VMEM((2, BLOCK, 2 * columns), jnp.bfloat16),
-                pltpu.VMEM((2, BLOCK, 128), jnp.float32),
-                pltpu.VMEM((BLOCK, 2 * columns), jnp.float32),
-                pltpu.SemaphoreType.DMA((2, 2, GROUP)),
+                pltpu.VMEM((2, GROUP * PIECE_ROWS, whole_width), jnp.bfloat16),
+                pltpu.VMEM((BLOCK, whole_width), jnp.float32),
+                pltpu.SemaphoreType.DMA((2, GROUP)),
             ],
         ),
         out_shape=[
             jax.ShapeDtypeStruct((count * BLOCK, columns), jnp.bfloat16),
             jax.ShapeDtypeStruct((count * BLOCK, columns), jnp.bfloat16),
-            jax.ShapeDtypeStruct((experts, count, 1, BLOCK), jnp.float32),
+            jax.ShapeDtypeStruct((count * BLOCK, 128), jnp.float32),
         ],
         compiler_params=pltpu.CompilerParams(vmem_limit_bytes=VMEM_LIMIT),
-        cost_estimate=cost(COST * 45.0),
-    )(owner, piece, source, groups, begin, place, yd, gg, *after)
+    )(owner, piece, source, groups, begin, place, yd, *after)
 
 
 def flip(value, bit):
@@ -538,12 +584,12 @@
     return lax.dynamic_index_in_dim(value, index, axis, keepdims=False)
 
 
-def sum_stage(parts, bit, axis, chosen, after):
+def sum_stage(parts, bit, chosen, after):
     send, keep = parts
     got = order(flip(send, bit), *after)
-    return (
-        add_low(pick_index(keep, 1 - chosen, axis), pick_index(got, 1 - chosen, axis)),
-        add_low(pick_index(keep, chosen, axis), pick_index(got, chosen, axis)),
+    return tuple(
+        add_low(pick_index(keep, which, 0), pick_index(got, which, 0))
+        for which in (1 - chosen, chosen)
     )
 
 
@@ -551,8 +597,8 @@
     def __init__(self, parts, rank, far_first):
         side, low_bit, high_bit = (rank // 2) % 2, (rank // 4) % 2, rank // 8
         self.parts = parts
-        self.first = (4, 2, high_bit) if far_first else (2, 3, low_bit)
-        self.second = (8, 2, side) if far_first else (4, 2, high_bit)
+        self.first = (4, high_bit) if far_first else (2, low_bit)
+        self.second = (8, side) if far_first else (4, high_bit)
         self.last = 2 if far_first else 8
 
     def one(self, *after):
@@ -568,33 +614,34 @@
         return add_low(keep, order(flip(send, self.last), *after))
 
 
-def sum_heads(own, other, rank, marks=((), (), ())):
-    core, side = rank % 2, (rank // 2) % 2
-    low_bit, high_bit = (rank // 4) % 2, rank // 8
-    rows, columns = own.shape
-    part = rows // 16
-    view = (8, 2, part, columns)
-    parts = []
-    for value in (other, own):
-        value = value.reshape(view)
-        got = order(flip(pick_index(value, 1 - core, 1).astype(jnp.bfloat16), 1), *marks[0])
-        parts.append(add_low(pick_index(value, core, 1), got))
-    held = parts[0]
-    total = add_low(parts[1], order(swap(parts[0]), *marks[1])).reshape(4, 2, part, columns)
-    got = order(flip(pick_index(total, 1 - side, 1), 2), *marks[2])
+def core_sum(value, core):
+    rows, columns = value.shape
+    value = value.reshape(8, 2, rows // 16, columns)
+    got = flip(pick_index(value, 1 - core, 1).astype(jnp.bfloat16), 1)
+    return add_low(pick_index(value, core, 1), got)
+
+
+def plane_sum(total, rank, *after):
+    side, low_bit, high_bit = (rank // 2) % 2, (rank // 4) % 2, rank // 8
+    part, columns = total.shape[1:]
+    total = total.reshape(4, 2, part, columns)
+    got = order(flip(pick_index(total, 1 - side, 1), 2), *after)
     total = add_low(pick_index(total, side, 1), got).reshape(2, 2, part, columns)
     got = flip(pick_index(total, 1 - low_bit, 1), 4)
     total = add_low(pick_index(total, low_bit, 1), got)
     got = flip(pick_index(total, 1 - high_bit, 0), 8)
-    return pick_index(total, high_bit, 0).astype(jnp.float32) + got.astype(jnp.float32), held
-
-
-def fetch_other(weights, core, side):
-    rows = weights.shape[0] // 4
-    pieces = swap(lax.dynamic_slice_in_dim(weights, (side * 2 + core) * rows, rows, 0))
+    return pick_index(total, high_bit, 0).astype(jnp.float32) + got.astype(jnp.float32)
+
+
+def fetch_other(weights, core, side, after=()):
+    rows = weights[0].shape[0] // 4
+    start = (side * 2 + core) * rows
+    own = jnp.concatenate(
+        [lax.dynamic_slice_in_dim(w, start, rows, 0) for w in weights], axis=1
+    )
+    pieces = swap(order(own, *after))
     turned = flip(pieces, 2)
-    result = jnp.zeros_like(weights)
-    first = pieces
+    result = jnp.zeros((4 * rows, own.shape[1]), own.dtype)
     for value, place in (
         (pieces, side * 2 + core),
         (turned, (1 - side) * 2 + core),
@@ -602,7 +649,7 @@
         (flip(turned, 1), (1 - side) * 2 + 1 - core),
     ):
         result = lax.dynamic_update_slice_in_dim(result, value, place * rows, 0)
-    return result, first
+    return result, own, pieces
 
 
 ROWS = 256
@@ -626,7 +673,7 @@
 
 
 def project_kernel(sizes, score_scale, normed_ref, weights_ref, cosine_ref, sine_ref, *outs):
-    query_ref, key_ref, value_ref = outs
+    query_ref, key_ref, value_ref = outs[-3:]
     query_width, key_width = sizes
     projected = jnp.dot(normed_ref[...], weights_ref[...], preferred_element_type=jnp.float32)
     cosine, sine = cosine_ref[...], sine_ref[...]
@@ -641,7 +688,7 @@
     value_ref[...] = projected[:, query_width + key_width :].astype(jnp.bfloat16)
 
 
-def project(normed, weights, tables, query_width, key_width, score_scale):
+def project(normed, weights, tables, query_width, key_width, score_scale, after=()):
     rows, depth = normed.shape
     width = weights.shape[1]
     row_spec = lambda columns: pl.BlockSpec((ROWS, columns), lambda i: (i, 0))
@@ -653,7 +700,8 @@
             pl.BlockSpec((depth, width), lambda i: (0, 0)),
             row_spec(128),
             row_spec(128),
-        ],
+        ]
+        + [pl.BlockSpec(memory_space=pl.ANY)] * len(after),
         out_specs=[row_spec(query_width), row_spec(key_width), row_spec(key_width)],
         out_shape=[
             jax.ShapeDtypeStruct((rows, query_width), jnp.bfloat16),
@@ -661,8 +709,7 @@
             jax.ShapeDtypeStruct((rows, key_width), jnp.bfloat16),
         ],
         compiler_params=pltpu.CompilerParams(vmem_limit_bytes=VMEM_LIMIT),
-        cost_estimate=cost(COST * 9.0),
-    )(normed, weights, *tables)
+    )(normed, weights, *tables, *after)
 
 
 def attend_kernel(per_pair, query_ref, key_ref, value_ref, limit_ref, out_ref, lse_ref):
@@ -726,7 +773,6 @@
             jax.ShapeDtypeStruct((pairs, rows, 128), jnp.float32),
         ],
         compiler_params=pltpu.CompilerParams(vmem_limit_bytes=VMEM_LIMIT),
-        cost_estimate=cost(COST * 24.0),
     )(query, key, value, limits)
 
 
@@ -805,7 +851,7 @@
         value_out[...] = value_total[...].astype(jnp.bfloat16)
 
 
-def attend_back(saved, attended_grad, limits, tables, score_scale, after=()):
+def attend_back(saved, attended_grad, limits, tables, score_scale, chosen, after=()):
     query, key, value, lse = saved
     rows, query_width = query.shape
     pairs = key.shape[1] // 128
@@ -813,20 +859,23 @@
     turned_key = key.T.reshape(pairs, 128, rows)
     lse_rows = lse[:, :, :8].transpose(0, 2, 1)
     cosine, sine = tables
-    block = lambda columns: pl.BlockSpec((ROWS, columns), lambda p, i: (i, p))
-    whole = pl.BlockSpec((rows, 128), lambda p, i: (0, p))
+    begin, count = chosen
+    block = lambda columns: pl.BlockSpec((ROWS, columns), lambda p, i: (i, p + begin))
+    whole = pl.BlockSpec((rows, 128), lambda p, i: (0, p + begin))
+    block_out = pl.BlockSpec((ROWS, wide), lambda p, i: (i, p))
+    whole_out = pl.BlockSpec((rows, 128), lambda p, i: (0, p))
     table = pl.BlockSpec((ROWS, 128), lambda p, i: (i, 0))
     full_table = pl.BlockSpec((rows, 128), lambda p, i: (0, 0))
     return pl.pallas_call(
         functools.partial(back_kernel, wide // HD, score_scale, len(after)),
-        grid=(pairs, rows // ROWS),
+        grid=(count, rows // ROWS),
         in_specs=[
             block(wide),
             whole,
             whole,
-            pl.BlockSpec((1, 128, rows), lambda p, i: (p, 0, 0)),
+            pl.BlockSpec((1, 128, rows), lambda p, i: (p + begin, 0, 0)),
             block(wide),
-            pl.BlockSpec((1, 8, ROWS), lambda p, i: (p, 0, i)),
+            pl.BlockSpec((1, 8, ROWS), lambda p, i: (p + begin, 0, i)),
             pl.BlockSpec((1, ROWS), lambda p, i: (0, i)),
             table,
             table,
@@ -834,18 +883,17 @@
             full_table,
         ]
         + [pl.BlockSpec(memory_space=pl.ANY)] * len(after),
-        out_specs=[block(wide), whole, whole],
+        out_specs=[block_out, whole_out, whole_out],
         out_shape=[
-            jax.ShapeDtypeStruct((rows, query_width), jnp.bfloat16),
-            jax.ShapeDtypeStruct((rows, key.shape[1]), jnp.bfloat16),
-            jax.ShapeDtypeStruct((rows, key.shape[1]), jnp.bfloat16),
+            jax.ShapeDtypeStruct((rows, count * wide), jnp.bfloat16),
+            jax.ShapeDtypeStruct((rows, count * 128), jnp.bfloat16),
+            jax.ShapeDtypeStruct((rows, count * 128), jnp.bfloat16),
         ],
         scratch_shapes=[
             pltpu.VMEM((rows, 128), jnp.float32),
             pltpu.VMEM((rows, 128), jnp.float32),
         ],
         compiler_params=pltpu.CompilerParams(vmem_limit_bytes=VMEM_LIMIT),
-        cost_estimate=cost(COST * 40.0),
     )(
         query, key, value, turned_key, attended_grad, lse_rows, limits.T, cosine, sine, cosine,
         sine, *after,
@@ -1249,8 +1297,8 @@
     slots = round_up(2 * CAP, BLOCK)
 
     joined_own = jnp.concatenate([w_query, w_key, w_value], axis=1)
-    joined_other, joined_piece = fetch_other(joined_own, core, side)
-    out_other, out_piece = fetch_other(w_out, core, side)
+    joined_other, joined_send, joined_piece = fetch_other([w_query, w_key, w_value], core, side)
+    out_other, _, out_piece = fetch_other([w_out], core, side, (joined_send,))
 
     own_routes = lax.dynamic_slice_in_dim(routes, tensor_rank * share_rows, share_rows, 0)
     across_routes = lax.dynamic_slice_in_dim(routes, (1 - tensor_rank) * share_rows, share_rows, 0)
@@ -1270,15 +1318,15 @@
     starts_row = lax.dynamic_index_in_dim(starts, tensor_rank, 0, keepdims=False)
     limits = piece_limits(starts_row, share_rows)
 
-    def half_forward(joined_weights):
+    def half_forward(joined_weights, after=()):
         query, key, value = project(
-            normed, joined_weights, tables, query_width, key_width, score_scale
+            normed, joined_weights, tables, query_width, key_width, score_scale, after
         )
         attended, lse = attend(query, key, value, limits)
         return attended, (query, key, value, lse)
 
     attended_own, saved_own = half_forward(joined_own)
-    attended_other, saved_other = half_forward(joined_other)
+    attended_other, saved_other = half_forward(joined_other, (counts,))
     middle_share = (
         inputs_share
         + jnp.dot(attended_own, w_out, preferred_element_type=jnp.float32)
@@ -1294,7 +1342,8 @@
     fractions = counts / (total_tokens * choices_count)
 
     group_gates = jnp.concatenate(spread(gate_low), axis=0)
-    place, begins, ends, gates = placement(group_routes, group_gates, first_expert, experts)
+    gates = gate_table(group_routes, group_gates, first_expert, experts)
+    place, begins, ends = placement(group_routes, first_expert, experts)
     gather_from = gather_tables(begins, ends, slots)
     blocks = gather_from[2]
     cot_slots = gather_rows(gather_from, place, None, cotangent_rows, slots, 0, experts)[0]
@@ -1312,7 +1361,7 @@
         if index == FIRST_PART:
             later_part = gather_rows(
                 gather_from, place, gates, mixed_rows, slots, FIRST_PART, experts - FIRST_PART,
-                (carried[1],),
+                (carried,),
             )
         if later_part is None:
             (x_slots, slot_gates), x_first = first_part, 0
@@ -1322,49 +1371,58 @@
         if index == 2:
             waits = [chips[0].one(slot_gates)]
         elif index == 4:
-            waits = [chips[1].one(carried[1]), chips[0].two(carried[1])]
+            waits = [chips[0].two(carried)]
+        elif index == 5:
+            waits = [chips[1].one(carried)]
         elif index == 6:
-            waits = [chips[2].one(carried[1])]
-        elif index == 7:
-            waits = [chips[3].one(carried[1]), chips[1].two(carried[1])]
-        elif index == 9:
-            waits = [chips[4].one(carried[1])]
+            waits = [chips[2].one(carried)]
+        elif index == 8:
+            waits = [chips[3].one(carried), chips[1].two(carried)]
         far_first = int(index in FAR_FIRST)
-        *carried, send, keep = expert_call(
+        carried, send, keep = expert_call(
             blocks, misc, x_slots, cot_slots, slot_gates, weights, carried, slots,
             index, 1, x_first, 0, depth, far_first, waits,
         )
         chips.append(ChipSum((send, keep), rank, far_first))
-    waits = [chips[5].one(carried[1])] + [chips[i].two(carried[1]) for i in (2, 3)]
+    waits = [chips[4].one(carried), chips[5].one(carried)]
+    done = [chips[0].three(carried)]
+    waits += done
 
     combine_from = combine_tables(begins, ends, slots)
     tiles = place.shape[1] // 4
-    turned_routes = group_routes.T
     names = first_expert + jnp.arange(experts, dtype=jnp.int32)
 
-    def combined(start, count, after):
-        y, dx, gate_grads = combine_rows(combine_from, place, *carried, start, count, after)
-        gate_grads = gate_grads[:experts].reshape(experts, 1, count * BLOCK)
-        rows = turned_routes[:, start * BLOCK : (start + count) * BLOCK]
-        hit = rows[None, :, :] == names[:, None, None]
-        return y, dx, jnp.sum(jnp.where(hit, gate_grads, 0.0), axis=0)
-
-    y_far, dx_far, gg_far = combined(2 * tiles, 2 * tiles, waits)
-    waits = [chips[6].one(dx_far), chips[4].two(dx_far)]
-    dx_far, y_far, gg_far = flip(dx_far, 1), flip(y_far, 1), flip(gg_far, 1)
-    y_cross, dx_cross, gg_cross = combined(tiles, tiles, waits)
-    dx_send = add_low(dx_cross, dx_far[share_rows:])
+    def combined(quarter, after):
+        y, dx, gate_grads = combine_rows(
+            combine_from, place, carried, quarter * tiles, tiles, after
+        )
+        gate_grads = gate_grads[:, :experts] + gate_grads[:, 64 : 64 + experts]
+        rows = group_routes[quarter * share_rows : (quarter + 1) * share_rows]
+        hit = rows[:, :, None] == names[None, None, :]
+        return y, dx, jnp.sum(jnp.where(hit, gate_grads[:, None, :], 0.0), axis=2)
+
+    far = combined(3, waits)
+    waits = [chips[2].two(far[1])]
+    done.append(chips[1].three(far[1]))
+    waits.append(done[1])
+    far_y, far_dx, far_gg = (flip(value, 1) for value in far)
+    cross = combined(1, waits)
+    dx_send = add_low(cross[1], far_dx)
     dx_across = swap(dx_send)
-    gg_across = swap(gg_cross + gg_far[:, share_rows:])
-    y_near, dx_near, gg_near = combined(0, tiles, [dx_send])
-    waits = [chips[7].one(dx_near)] + [chips[i].two(dx_near) for i in (5, 6)]
-    waits.append(chips[8].one(dx_near))
+    gg_across = swap(cross[2] + far_gg)
+    waits = [dx_send, chips[6].one(cross[1]), chips[3].two(cross[1])]
+    next_door = combined(2, waits)
+    door_y, door_dx, door_gg = (flip(value, 1) for value in next_door)
+    y_send = add_low(cross[0], far_y)
+    y_across = swap(order(y_send, dx_send))
+    near = combined(0, [y_send, next_door[1]])
+    waits = [chips[7].one(near[1]), chips[5].two(near[1])]
+    done += [chips[2].three(near[1]), chips[3].three(near[1])]
+    waits += done[2:]
     mixed_grad_share = (
-        dx_near.astype(jnp.float32)
-        + dx_far[:share_rows].astype(jnp.float32)
-        + dx_across.astype(jnp.float32)
-    )
-    gates_grad_share = (gg_near + gg_far[:, :share_rows] + gg_across).T
+        near[1].astype(jnp.float32) + door_dx.astype(jnp.float32) + dx_across.astype(jnp.float32)
+    )
+    gates_grad_share = near[2] + door_gg + gg_across
 
     upstream = cotangent.astype(jnp.float32)
     chosen_grad = gate_soft * (
@@ -1392,31 +1450,50 @@
     middle_grad = upstream + middle_from_norm
     middle_low = middle_grad.astype(jnp.bfloat16)
 
-    def half_back(saved, out_weights, after):
+    def half_back(saved, out_weights):
         attended_grad = dot_nt(middle_low, out_weights).astype(jnp.bfloat16)
-        grads = attend_back(saved, attended_grad, limits, tables, score_scale, after)
-        return jnp.concatenate(grads, axis=1)
-
-    other_grads = half_back(saved_other, out_other, waits)
-    y_across = swap(order(add_low(y_cross, y_far[share_rows:]), other_grads))
+
+        def part(chosen, after):
+            return attend_back(
+                saved, attended_grad, limits, tables, score_scale, chosen, after
+            )
+
+        return part
+
+    waits += [chips[8].one(middle_low), chips[4].two(middle_low), chips[6].two(middle_low)]
+    pairs = key_width // 128
+    other_grads = jnp.concatenate(
+        half_back(saved_other, out_other)((0, pairs), waits), axis=1
+    )
     expert_share = (
-        y_near.astype(jnp.float32)
-        + y_far[:share_rows].astype(jnp.float32)
-        + y_across.astype(jnp.float32)
+        near[0].astype(jnp.float32)
+        + door_y.astype(jnp.float32)
+        + order(y_across, other_grads).astype(jnp.float32)
     )
     output_share = (middle_share + expert_share).astype(jnp.bfloat16)
-    other_weight_grads = dot_tn(normed, other_grads)
-    waits = [chips[9].one(other_grads)] + [chips[i].two(other_grads) for i in (7, 8)]
-    out_grads = (
-        dot_tn(middle_low, attended_own),
-        dot_tn(order(middle_low, other_grads), attended_other),
-    )
-    own_grads = half_back(saved_own, w_out, waits)
-    out_total, _ = sum_heads(*out_grads, rank, ((), (), (own_grads,)))
+    joined_held = core_sum(dot_tn(normed, other_grads), core)
+    joined_across = swap(joined_held)
+    marked = order(middle_low, other_grads)
+    out_held = core_sum(dot_tn(marked, attended_other), core)
+    out_across = swap(order(out_held, joined_held))
+    out_kept = core_sum(dot_tn(marked, attended_own), core)
+    waits = [chips[9].one(other_grads), chips[7].two(other_grads)]
+    done += [chips[i].three(other_grads) for i in (4, 5, 6)]
+    waits += done[4:]
+    waits += [joined_held, out_held, out_kept, output_share]
+    own_part = half_back(saved_own, w_out)
+    front = own_part((0, pairs // 2), waits)
+    back = own_part((pairs // 2, pairs - pairs // 2), [joined_across, front[0]])
+    own_grads = jnp.concatenate(
+        [part for both in zip(front, back) for part in both], axis=1
+    )
+    out_half = add_low(out_kept, order(out_across, own_grads))
     own_weight_grads = dot_tn(normed, own_grads)
-    joined_total, _ = sum_heads(own_weight_grads, other_weight_grads, rank)
-    chips[9].two(own_weight_grads)
-    sums = [chip.three(own_weight_grads) for chip in chips]
+    joined_total = plane_sum(add_low(core_sum(own_weight_grads, core), joined_across), rank)
+    out_total = plane_sum(out_half, rank, own_weight_grads)
+    chips[8].two(own_grads)
+    chips[9].two(own_grads)
+    sums = done + [chips[i].three(own_weight_grads) for i in (7, 8, 9)]
     other_normed = dot_nt(other_grads, joined_other)
     own_normed = dot_nt(own_grads, joined_own)
     input_pullback = jax.vjp(normalize, inputs_share, norm_gains)[1]
@@ -1434,7 +1511,7 @@
     router_total = small[expert_count + 2 * model_width :].reshape(router_grad.shape)
     balance = expert_count * expert_count * fractions * prob_sums / total_tokens
 
-    mine = jnp.concatenate(sums, axis=0).reshape(experts, 3, 2, depth // 2, -1)
+    mine = jnp.stack(sums, axis=0).reshape(experts, 3, 2, depth // 2, -1)
     theirs = flip(pick_index(mine, 1 - core, 2), 1)
     mine = pick_index(mine, core, 2)
     expert_total = jnp.where(

time: 1480 us -> 1380 us (0.932)
  Pallas kernels: 679 us -> 611 us
  waiting for transfers between devices: 312 us -> 245 us
  starting transfers between devices: 86 us -> 134 us
  local copies, waits for them, and re-layouts: 148 us -> 120 us
    ppermute x12, waiting for transfers between devices: 98.2 us -> 20 us  [swap(): return lax.ppermute(value, 'tensor', [(0, 1), (1, 0)])]
    pallas_call x10 -> x0, local copies, waits for them, and re-layouts: 31 us -> none  [expert_call(): pl.pallas_call(functools.partial(expert_kernel, first, split, depth, far_...]
    pallas_call x10, Pallas kernels: 241 us -> 210 us  [expert_call(): pl.pallas_call(functools.partial(expert_kernel, first, split, depth, far_...]
    ppermute x65 -> x68, starting transfers between devices: 62.5 us -> 88.5 us  [flip(): return lax.ppermute(value, 'dp', [(i, i ^ bit) for i in range(size)])]
    convert_element_type x30 -> x41, other arithmetic: 80.4 us -> 104 us  [add_low(): (left.astype(jnp.float32) + right.astype(jnp.float32)).astype(jnp.bfloat16)]
    convert_element_type x14 -> x5, local copies, waits for them, and re-layouts: 28.8 us -> 6.4 us  [the longest x4 5.2 us: core_sum(): got = flip(pick_index(value, 1 - core, 1).astype(jnp.bfloat16), 1)]
    ppermute x12, starting transfers between devices: 23.5 us -> 45.6 us  [swap(): return lax.ppermute(value, 'tensor', [(0, 1), (1, 0)])]
    unnamed x13 -> x4, other arithmetic: 20.8 us -> 0.01 us
  transfers between devices with their start and end apart: 77 -> 80, of which waited for: 25 -> 18; matrix products, arithmetic and copies ran while one was open for 25% -> 26% of each run, Pallas kernels for 40% -> 40%
where the time goes in v3:
time: 1380 us; the launch traced here: 1370 us
  Pallas kernels  611 us (44%)
  waiting for transfers between devices  245 us (18%)
  other arithmetic  176 us (13%)
  starting transfers between devices  134 us (10%)
  local copies, waits for them, and re-layouts  120 us (9%)
  matrix products  78 us (6%)
    ppermute x68, waiting for transfers between devices, flip(): return lax.ppermute(value, 'dp', [(i, i ^ bit) for i in range(size)])  225 us
    pallas_call x10, Pallas kernels, expert_call(): pl.pallas_call(functools.partial(expert_kernel, first, split, depth, far_...  210 us
    pallas_call x3, Pallas kernels, gather_rows(): pl.pallas_call(functools.partial(gather_kernel, len(sources), with_gates,...  169 us
    convert_element_type x41, other arithmetic, add_low(): (left.astype(jnp.float32) + right.astype(jnp.float32)).astype(jnp.bfloat16)  104 us
    ppermute x68, starting transfers between devices, flip(): return lax.ppermute(value, 'dp', [(i, i ^ bit) for i in range(size)])  88.5 us
    pallas_call x4, Pallas kernels, combine_rows(): pl.pallas_call(functools.partial(combine_kernel, first), grid_spec=pltpu....  83.6 us
    pallas_call x3, Pallas kernels, attend_back(): pl.pallas_call(functools.partial(back_kernel, wide // HD, score_scale, le...  82.4 us
    pallas_call x2, Pallas kernels, attend(): pl.pallas_call(functools.partial(attend_kernel, wide // HD), grid=(pairs,...  48.9 us
  transfers between devices with their start and end apart: 80, of which 18 were waited for; matrix products, arithmetic and copies ran while one was open for 26% of the time, Pallas kernels for 40%

profile of v3, /device:TPU:0, one launch (start us, length us, event | category | flops | bytes accessed | tf_op | source)
XLA Modules:
  0.0 1369.4 jit_solution(16222497160172419780)
XLA Ops:
  35.8 24.4 %shard_map.238 = (bf16[1024,768]{1,0:T(8,128)(2,1)}, f32[2,1024,128]{2,1,0:T(8,128)}) custom-call(bf16[1024,768]{1,0:T(8,128)(2,1)} %get-tuple-element.117.query_ref, bf16[1024,256]{1,0:T(8,128)(2,1)} %get-tuple-element.118.key_ref, bf16[1024,256]{1,0:T(8,128)(2,1)} %get-tuple-element.119.value_ref, s32[1024,1]{1,0:T(8,128)} %select_select_fusion.limit_ref), custom_call_target="tpu_custom_call" | custom-call | tf_op jit(solution)/shard_map/pallas_call | solution.py:758
  70.2 26.9 %collective-permute-done.5 = f32[40]{0:T(128)S(1)} collective-permute-done((f32[40]{0:T(128)S(1)}, f32[40]{0:T(128)S(1)}, u32[]{:S(2)}, u32[]{:S(2)}) %collective-permute-start.5) | collective-permute-done | bytes 192 | tf_op jit(solution)/shard_map/ppermute | solution.py:568
  133.6 24.5 %shard_map.240 = (bf16[1024,768]{1,0:T(8,128)(2,1)}, f32[2,1024,128]{2,1,0:T(8,128)}) custom-call(bf16[1024,768]{1,0:T(8,128)(2,1)} %get-tuple-element.121.query_ref, bf16[1024,256]{1,0:T(8,128)(2,1)} %get-tuple-element.122.key_ref, bf16[1024,256]{1,0:T(8,128)(2,1)} %get-tuple-element.123.value_ref, s32[1024,1]{1,0:T(8,128)} %select_select_fusion.limit_ref), custom_call_target="tpu_custom_call" | custom-call | tf_op jit(solution)/shard_map/pallas_call | solution.py:758
  191.7 77.4 %shard_map.241.rest_5_.c_ref = bf16[12800,1536]{1,0:T(8,128)(2,1)} custom-call(s32[10,5]{1,0:T(8,128)} %copy-done.89, s32[10,5]{1,0:T(8,128)} %compare_select_fusion.3.high_ref, s32[10]{0:T(128)} %negate_maximum_fusion.blocks_ref, s32[10,16,1,256]{3,2,1,0:T(1,128)} %add_select_fusion.place_ref, bf16[1024,1536]{1,0:T(8,128)(2,1)} %rest_0_, ...), custom_call_target="tpu_custom_call" | custom-call | tf_op jit(solution)/shard_map/pallas_call | solution.py:277
  288.3 21.3 %shard_map.242 = (bf16[2560,1536]{1,0:T(8,128)(2,1)}, f32[2560,128]{1,0:T(8,128)}) custom-call(s32[2,5]{1,0:T(2,128)} %slice.161.low_ref, s32[2,5]{1,0:T(2,128)} %slice.162.high_ref, s32[2]{0:T(128)} %bitcast.391, s32[2,16,1,256]{3,2,1,0:T(1,128)} %copy.138.place_ref, bf16[4096,128]{1,0:T(8,128)(2,1)} %pad_bitcast_fusion.rest_0_, ...), custom_call_target="tpu_custom_call" | custom-call | tf_op jit(solution)/shard_map/pallas_call | solution.py:277
  334.3 20.4 %shard_map.244 = (bf16[12800,3200]{1,0:T(8,128)(2,1)}, bf16[2,2,3,192,512]{4,3,2,1,0:T(8,128)(2,1)}, bf16[2,2,3,192,512]{4,3,2,1,0:T(8,128)(2,1)}) custom-call(s32[10]{0:T(128)} %negate_maximum_fusion.blocks_ref, s32[3]{0:T(128)} %pad_add_fusion.1.misc_ref, bf16[2560,1536]{1,0:T(8,128)(2,1)} %get-tuple-element.128.x_ref, ...), custom_call_target="tpu_custom_call", output_to_operand_aliasing={{0}: (8, {})} | custom-call | tf_op jit(solution)/shard_map/pallas_call | solution.py:451
  357.4 70.2 %shard_map.245 = (bf16[10240,1536]{1,0:T(8,128)(2,1)}, f32[10240,128]{1,0:T(8,128)}) custom-call(s32[8,5]{1,0:T(8,128)} %slice.158.low_ref, s32[8,5]{1,0:T(8,128)} %slice.159.high_ref, s32[8]{0:T(128)} %slice.125.blocks_ref, s32[8,16,1,256]{3,2,1,0:T(1,128)} %copy.139.place_ref, bf16[4096,128]{1,0:T(8,128)(2,1)} %pad_bitcast_fusion.rest_0_, ...), custom_call_target="tpu_custom_call" | custom-call | tf_op jit(solution)/shard_map/pallas_call | solution.py:277
  435.3 24.3 %shard_map.246 = (bf16[12800,3200]{1,0:T(8,128)(2,1)}, bf16[2,2,3,192,512]{4,3,2,1,0:T(8,128)(2,1)}, bf16[2,2,3,192,512]{4,3,2,1,0:T(8,128)(2,1)}) custom-call(s32[10]{0:T(128)} %negate_maximum_fusion.blocks_ref, s32[3]{0:T(128)} %pad_add_fusion.1.misc_ref, bf16[10240,1536]{1,0:T(8,128)(2,1)} %get-tuple-element.132.x_ref, ...), custom_call_target="tpu_custom_call", output_to_operand_aliasing={{0}: (8, {})} | custom-call | tf_op jit(solution)/shard_map/pallas_call | solution.py:451
  460.6 28.3 %shard_map.247 = (bf16[12800,3200]{1,0:T(8,128)(2,1)}, bf16[2,2,3,192,512]{4,3,2,1,0:T(8,128)(2,1)}, bf16[2,2,3,192,512]{4,3,2,1,0:T(8,128)(2,1)}) custom-call(s32[10]{0:T(128)} %negate_maximum_fusion.blocks_ref, s32[3]{0:T(128)} %pad_add_fusion.1.misc_ref, bf16[10240,1536]{1,0:T(8,128)(2,1)} %get-tuple-element.132.x_ref, ...), custom_call_target="tpu_custom_call", output_to_operand_aliasing={{0}: (8, {})} | custom-call | tf_op jit(solution)/shard_map/pallas_call | solution.py:451
  491.2 24.3 %shard_map.248 = (bf16[12800,3200]{1,0:T(8,128)(2,1)}, bf16[2,2,3,192,512]{4,3,2,1,0:T(8,128)(2,1)}, bf16[2,2,3,192,512]{4,3,2,1,0:T(8,128)(2,1)}) custom-call(s32[10]{0:T(128)} %negate_maximum_fusion.blocks_ref, s32[3]{0:T(128)} %pad_add_fusion.1.misc_ref, bf16[10240,1536]{1,0:T(8,128)(2,1)} %get-tuple-element.132.x_ref, ...), custom_call_target="tpu_custom_call", output_to_operand_aliasing={{0}: (8, {})} | custom-call | tf_op jit(solution)/shard_map/pallas_call | solution.py:451
  558.3 20.2 %shard_map.250 = (bf16[12800,3200]{1,0:T(8,128)(2,1)}, bf16[2,2,3,192,512]{4,3,2,1,0:T(8,128)(2,1)}, bf16[2,2,3,192,512]{4,3,2,1,0:T(8,128)(2,1)}) custom-call(s32[10]{0:T(128)} %negate_maximum_fusion.blocks_ref, s32[3]{0:T(128)} %pad_add_fusion.1.misc_ref, bf16[10240,1536]{1,0:T(8,128)(2,1)} %get-tuple-element.132.x_ref, ...), custom_call_target="tpu_custom_call", output_to_operand_aliasing={{0}: (8, {})} | custom-call | tf_op jit(solution)/shard_map/pallas_call | solution.py:451
  599.2 26.1 %collective-permute-done.28 = bf16[2,3,192,512]{3,2,1,0:T(8,128)(2,1)} collective-permute-done((bf16[2,3,192,512]{3,2,1,0:T(8,128)(2,1)S(1)}, bf16[2,3,192,512]{3,2,1,0:T(8,128)(2,1)}, u32[]{:S(2)}, u32[]{:S(2)}) %collective-permute-start.28) | collective-permute-done | bytes 1179680 | tf_op jit(solution)/shard_map/ppermute | solution.py:568
  627.3 20.0 %shard_map.252 = (bf16[12800,3200]{1,0:T(8,128)(2,1)}, bf16[2,2,3,192,512]{4,3,2,1,0:T(8,128)(2,1)}, bf16[2,2,3,192,512]{4,3,2,1,0:T(8,128)(2,1)}) custom-call(s32[10]{0:T(128)} %negate_maximum_fusion.blocks_ref, s32[3]{0:T(128)} %pad_add_fusion.1.misc_ref, bf16[10240,1536]{1,0:T(8,128)(2,1)} %get-tuple-element.132.x_ref, ...), custom_call_target="tpu_custom_call", output_to_operand_aliasing={{0}: (8, {})} | custom-call | tf_op jit(solution)/shard_map/pallas_call | solution.py:451
  647.4 24.3 %shard_map.253 = (bf16[12800,3200]{1,0:T(8,128)(2,1)}, bf16[2,2,3,192,512]{4,3,2,1,0:T(8,128)(2,1)}, bf16[2,2,3,192,512]{4,3,2,1,0:T(8,128)(2,1)}) custom-call(s32[10]{0:T(128)} %negate_maximum_fusion.blocks_ref, s32[3]{0:T(128)} %pad_add_fusion.1.misc_ref, bf16[10240,1536]{1,0:T(8,128)(2,1)} %get-tuple-element.132.x_ref, ...), custom_call_target="tpu_custom_call", output_to_operand_aliasing={{0}: (8, {})} | custom-call | tf_op jit(solution)/shard_map/pallas_call | solution.py:451
  681.9 22.4 %shard_map.254 = (bf16[1024,1536]{1,0:T(8,128)(2,1)}, bf16[1024,1536]{1,0:T(8,128)(2,1)}, f32[1024,128]{1,0:T(8,128)}) custom-call(s32[16,96]{1,0:T(8,128)} %copy-done.79, s32[16,96]{1,0:T(8,128)} %get-tuple-element.323.piece_ref, s32[16,96]{1,0:T(8,128)} %get-tuple-element.322.source_ref, s32[16]{0:T(128)} %get-tuple-element.286.groups_ref, ...), custom_call_target="tpu_custom_call" | custom-call | tf_op jit(solution)/shard_map/pallas_call | solution.py:543
  729.3 63.2 %collective-permute-done.33 = bf16[3,192,512]{2,1,0:T(8,128)(2,1)} collective-permute-done((bf16[3,192,512]{2,1,0:T(8,128)(2,1)}, bf16[3,192,512]{2,1,0:T(8,128)(2,1)}, u32[]{:S(2)}, u32[]{:S(2)}) %collective-permute-start.33) | collective-permute-done | bytes 589856 | tf_op jit(solution)/shard_map/ppermute | solution.py:568
  802.5 21.0 %shard_map.255 = (bf16[1024,1536]{1,0:T(8,128)(2,1)}, bf16[1024,1536]{1,0:T(8,128)(2,1)}, f32[1024,128]{1,0:T(8,128)}) custom-call(s32[16,96]{1,0:T(8,128)} %copy-done.79, s32[16,96]{1,0:T(8,128)} %get-tuple-element.323.piece_ref, s32[16,96]{1,0:T(8,128)} %get-tuple-element.322.source_ref, s32[16]{0:T(128)} %get-tuple-element.286.groups_ref, ...), custom_call_target="tpu_custom_call" | custom-call | tf_op jit(solution)/shard_map/pallas_call | solution.py:543
  842.6 27.5 %collective-permute-start.41 = (bf16[1024,1536]{1,0:T(8,128)(2,1)}, bf16[1024,1536]{1,0:T(8,128)(2,1)}, u32[]{:S(2)}, u32[]{:S(2)}) collective-permute-start(bf16[1024,1536]{1,0:T(8,128)(2,1)} %add_convert_fusion.1.rest_0_), channel_id=1, source_target_pairs={{0,1},{1,0},{2,3},{3,2},{4,5},{5,4},{6,7},{7,6},{8,9},{9,8},{10,11... | collective-permute-start | bytes 9437192 | tf_op jit(solution)/shard_map/ppermute | solution.py:572
  897.6 21.3 %shard_map.257 = (bf16[1024,1536]{1,0:T(8,128)(2,1)}, bf16[1024,1536]{1,0:T(8,128)(2,1)}, f32[1024,128]{1,0:T(8,128)}) custom-call(s32[16,96]{1,0:T(8,128)} %copy-done.79, s32[16,96]{1,0:T(8,128)} %get-tuple-element.323.piece_ref, s32[16,96]{1,0:T(8,128)} %get-tuple-element.322.source_ref, s32[16]{0:T(128)} %get-tuple-element.286.groups_ref, ...), custom_call_target="tpu_custom_call" | custom-call | tf_op jit(solution)/shard_map/pallas_call | solution.py:543
  943.5 32.1 %collective-permute-done.46 = bf16[2,3,192,512]{3,2,1,0:T(8,128)(2,1)} collective-permute-done((bf16[2,3,192,512]{3,2,1,0:T(8,128)(2,1)}, bf16[2,3,192,512]{3,2,1,0:T(8,128)(2,1)}, u32[]{:S(2)}, u32[]{:S(2)}) %collective-permute-start.46) | collective-permute-done | bytes 1179680 | tf_op jit(solution)/shard_map/ppermute | solution.py:568
  1011.8 25.2 %collective-permute-done.51 = bf16[2,3,192,512]{3,2,1,0:T(8,128)(2,1)S(1)} collective-permute-done((bf16[2,3,192,512]{3,2,1,0:T(8,128)(2,1)}, bf16[2,3,192,512]{3,2,1,0:T(8,128)(2,1)S(1)}, u32[]{:S(2)}, u32[]{:S(2)}) %collective-permute-start.51) | collective-permute-done | bytes 1179680 | tf_op jit(solution)/shard_map/ppermute | solution.py:568
  1048.8 39.9 %shard_map.258 = (bf16[1024,768]{1,0:T(8,128)(2,1)}, bf16[1024,256]{1,0:T(8,128)(2,1)}, bf16[1024,256]{1,0:T(8,128)(2,1)}) custom-call(bf16[1024,768]{1,0:T(8,128)(2,1)} %get-tuple-element.121.query_ref, bf16[1024,256]{1,0:T(8,128)(2,1)} %get-tuple-element.122.key_ref, bf16[1024,256]{1,0:T(8,128)(2,1)} %get-tuple-element.123.value_ref, ...), custom_call_target="tpu_custom_call" | custom-call | tf_op jit(solution)/shard_map/pallas_call | solution.py:869
  1156.9 21.2 %shard_map.259 = (bf16[1024,384]{1,0:T(8,128)(2,1)}, bf16[1024,128]{1,0:T(8,128)(2,1)}, bf16[1024,128]{1,0:T(8,128)(2,1)}) custom-call(bf16[1024,768]{1,0:T(8,128)(2,1)} %get-tuple-element.117.query_ref, bf16[1024,256]{1,0:T(8,128)(2,1)} %get-tuple-element.118.key_ref, bf16[1024,256]{1,0:T(8,128)(2,1)} %get-tuple-element.119.value_ref, ...), custom_call_target="tpu_custom_call" | custom-call | tf_op jit(solution)/shard_map/pallas_call | solution.py:869
  1180.2 21.4 %shard_map.260 = (bf16[1024,384]{1,0:T(8,128)(2,1)}, bf16[1024,128]{1,0:T(8,128)(2,1)}, bf16[1024,128]{1,0:T(8,128)(2,1)}) custom-call(bf16[1024,768]{1,0:T(8,128)(2,1)} %get-tuple-element.117.query_ref, bf16[1024,256]{1,0:T(8,128)(2,1)} %get-tuple-element.118.key_ref, bf16[1024,256]{1,0:T(8,128)(2,1)} %get-tuple-element.119.value_ref, ...), custom_call_target="tpu_custom_call" | custom-call | tf_op jit(solution)/shard_map/pallas_call | solution.py:869
  (645 shorter events, 636.4 us)
Async XLA Ops:
  182.3 86.9 %collective-permute-start.17 = (bf16[1024,1536]{1,0:T(8,128)(2,1)}, bf16[1024,1536]{1,0:T(8,128)(2,1)}, u32[]{:S(2)}, u32[]{:S(2)}) collective-permute-start(bf16[1024,1536]{1,0:T(8,128)(2,1)} %multiply_convert_fusion.rest_1_), channel_id=1, source_target_pairs={{0,1},{1,0},{2,3},{3,2},{4,5},{5,4},{6,7},{7,6},{8,9},{9,8},{10,11... | collective-permute-start | bytes 9437192 | tf_op jit(solution)/shard_map/ppermute | solution.py:572
  191.6 96.7 %collective-permute-start.21 = (bf16[1024,1536]{1,0:T(8,128)(2,1)}, bf16[1024,1536]{1,0:T(8,128)(2,1)}, u32[]{:S(2)}, u32[]{:S(2)}) collective-permute-start(bf16[1024,1536]{1,0:T(8,128)(2,1)} %multiply_convert_fusion.rest_1_), channel_id=1, source_target_pairs={{0,2},{2,0},{4,6},{6,4},{8,10},{10,8},{12,14},{14,12},{16,18},{18,... | collective-permute-start | bytes 9437192 | tf_op jit(solution)/shard_map/ppermute | solution.py:568
  325.3 102.4 %collective-permute-start.23 = (bf16[2,2,3,192,512]{4,3,2,1,0:T(8,128)(2,1)}, bf16[2,2,3,192,512]{4,3,2,1,0:T(8,128)(2,1)}, u32[]{:S(2)}, u32[]{:S(2)}) collective-permute-start(bf16[2,2,3,192,512]{4,3,2,1,0:T(8,128)(2,1)} %get-tuple-element.135), channel_id=1, source_target_pairs={{0,4},{2,6},{4,0},{6,2},{8,12},{10,14},{12,8},{14,10},{16,20},{18,... | collective-permute-start | bytes 7077896 | tf_op jit(solution)/shard_map/ppermute | solution.py:568
  354.8 160.8 %collective-permute-start.25 = (bf16[2,2,3,192,512]{4,3,2,1,0:T(8,128)(2,1)}, bf16[2,2,3,192,512]{4,3,2,1,0:T(8,128)(2,1)}, u32[]{:S(2)}, u32[]{:S(2)}) collective-permute-start(bf16[2,2,3,192,512]{4,3,2,1,0:T(8,128)(2,1)} %get-tuple-element.142), channel_id=1, source_target_pairs={{0,4},{2,6},{4,0},{6,2},{8,12},{10,14},{12,8},{14,10},{16,20},{18,... | collective-permute-start | bytes 7077896 | tf_op jit(solution)/shard_map/ppermute | solution.py:568
  459.6 91.2 %collective-permute-start.26 = (bf16[2,2,3,192,512]{4,3,2,1,0:T(8,128)(2,1)}, bf16[2,2,3,192,512]{4,3,2,1,0:T(8,128)(2,1)}, u32[]{:S(2)}, u32[]{:S(2)}) collective-permute-start(bf16[2,2,3,192,512]{4,3,2,1,0:T(8,128)(2,1)} %get-tuple-element.146), channel_id=1, source_target_pairs={{0,8},{2,10},{4,12},{6,14},{8,0},{10,2},{12,4},{14,6},{16,24},{18,... | collective-permute-start | bytes 7077896 | tf_op jit(solution)/shard_map/ppermute | solution.py:568
  488.9 105.7 %collective-permute-start.27 = (bf16[2,2,3,192,512]{4,3,2,1,0:T(8,128)(2,1)}, bf16[2,2,3,192,512]{4,3,2,1,0:T(8,128)(2,1)}, u32[]{:S(2)}, u32[]{:S(2)}) collective-permute-start(bf16[2,2,3,192,512]{4,3,2,1,0:T(8,128)(2,1)} %get-tuple-element.151), channel_id=1, source_target_pairs={{0,4},{2,6},{4,0},{6,2},{8,12},{10,14},{12,8},{14,10},{16,20},{18,... | collective-permute-start | bytes 7077896 | tf_op jit(solution)/shard_map/ppermute | solution.py:568
  536.1 138.2 %collective-permute-start.31 = (bf16[2,2,3,192,512]{4,3,2,1,0:T(8,128)(2,1)}, bf16[2,2,3,192,512]{4,3,2,1,0:T(8,128)(2,1)}, u32[]{:S(2)}, u32[]{:S(2)}) collective-permute-start(bf16[2,2,3,192,512]{4,3,2,1,0:T(8,128)(2,1)} %get-tuple-element.160), channel_id=1, source_target_pairs={{0,8},{2,10},{4,12},{6,14},{8,0},{10,2},{12,4},{14,6},{16,24},{18,... | collective-permute-start | bytes 7077896 | tf_op jit(solution)/shard_map/ppermute | solution.py:568
  541.2 133.0 %collective-permute-start.30 = (bf16[2,2,3,192,512]{4,3,2,1,0:T(8,128)(2,1)}, bf16[2,2,3,192,512]{4,3,2,1,0:T(8,128)(2,1)}, u32[]{:S(2)}, u32[]{:S(2)}) collective-permute-start(bf16[2,2,3,192,512]{4,3,2,1,0:T(8,128)(2,1)} %get-tuple-element.157), channel_id=1, source_target_pairs={{0,4},{2,6},{4,0},{6,2},{8,12},{10,14},{12,8},{14,10},{16,20},{18,... | collective-permute-start | bytes 7077896 | tf_op jit(solution)/shard_map/ppermute | solution.py:568
  549.1 76.1 %collective-permute-start.28 = (bf16[2,3,192,512]{3,2,1,0:T(8,128)(2,1)S(1)}, bf16[2,3,192,512]{3,2,1,0:T(8,128)(2,1)}, u32[]{:S(2)}, u32[]{:S(2)}) collective-permute-start(bf16[2,3,192,512]{3,2,1,0:T(8,128)(2,1)S(1)} %copy-done.18), channel_id=1, source_target_pairs={{0,8},{2,10},{4,12},{6,14},{8,0},{10,2},{12,4},{14,6},{16,24},{18,... | collective-permute-start | bytes 3538952 | tf_op jit(solution)/shard_map/ppermute | solution.py:568
  550.8 120.9 %collective-permute-start.32 = (bf16[3,192,512]{2,1,0:T(8,128)(2,1)}, bf16[3,192,512]{2,1,0:T(8,128)(2,1)}, u32[]{:S(2)}, u32[]{:S(2)}) collective-permute-start(bf16[3,192,512]{2,1,0:T(8,128)(2,1)} %fusion.62.rest_1_), channel_id=1, source_target_pairs={{0,16},{2,18},{4,20},{6,22},{8,24},{10,26},{12,28},{14,30},{16,0},... | collective-permute-start | bytes 1769480 | tf_op jit(solution)/shard_map/ppermute | solution.py:568
  704.3 133.9 %collective-permute-start.35 = (bf16[1024,1536]{1,0:T(8,128)(2,1)}, bf16[1024,1536]{1,0:T(8,128)(2,1)}, u32[]{:S(2)}, u32[]{:S(2)}) collective-permute-start(bf16[1024,1536]{1,0:T(8,128)(2,1)} %get-tuple-element.163), channel_id=1, source_target_pairs={{0,2},{2,0},{4,6},{6,4},{8,10},{10,8},{12,14},{14,12},{16,18},{18,... | collective-permute-start | bytes 9437192 | tf_op jit(solution)/shard_map/ppermute | solution.py:568
  704.3 125.5 %collective-permute-start.36 = (bf16[2,2,3,192,512]{4,3,2,1,0:T(8,128)(2,1)}, bf16[2,2,3,192,512]{4,3,2,1,0:T(8,128)(2,1)}, u32[]{:S(2)}, u32[]{:S(2)}) collective-permute-start(bf16[2,2,3,192,512]{4,3,2,1,0:T(8,128)(2,1)} %get-tuple-element.170), channel_id=1, source_target_pairs={{0,4},{2,6},{4,0},{6,2},{8,12},{10,14},{12,8},{14,10},{16,20},{18,... | collective-permute-start | bytes 7077896 | tf_op jit(solution)/shard_map/ppermute | solution.py:568
  704.4 91.9 %collective-permute-start.29 = (bf16[2,3,192,512]{3,2,1,0:T(8,128)(2,1)}, bf16[2,3,192,512]{3,2,1,0:T(8,128)(2,1)}, u32[]{:S(2)}, u32[]{:S(2)}) collective-permute-start(bf16[2,3,192,512]{3,2,1,0:T(8,128)(2,1)} %get-tuple-element.309.rest_1_), channel_id=1, source_target_pairs={{0,16},{2,18},{4,20},{6,22},{8,24},{10,26},{12,28},{14,30},{16,0},... | collective-permute-start | bytes 3538952 | tf_op jit(solution)/shard_map/ppermute | solution.py:568
  720.6 168.5 %collective-permute-start.34 = (bf16[1024,1536]{1,0:T(8,128)(2,1)}, bf16[1024,1536]{1,0:T(8,128)(2,1)}, u32[]{:S(2)}, u32[]{:S(2)}) collective-permute-start(bf16[1024,1536]{1,0:T(8,128)(2,1)} %get-tuple-element.167), channel_id=1, source_target_pairs={{0,2},{2,0},{4,6},{6,4},{8,10},{10,8},{12,14},{14,12},{16,18},{18,... | collective-permute-start | bytes 9437192 | tf_op jit(solution)/shard_map/ppermute | solution.py:568
  796.3 131.6 %collective-permute-start.45 = (bf16[2,2,3,192,512]{4,3,2,1,0:T(8,128)(2,1)}, bf16[2,2,3,192,512]{4,3,2,1,0:T(8,128)(2,1)}, u32[]{:S(2)}, u32[]{:S(2)}) collective-permute-start(bf16[2,2,3,192,512]{4,3,2,1,0:T(8,128)(2,1)} %get-tuple-element.184), channel_id=1, source_target_pairs={{0,4},{2,6},{4,0},{6,2},{8,12},{10,14},{12,8},{14,10},{16,20},{18,... | collective-permute-start | bytes 7077896 | tf_op jit(solution)/shard_map/ppermute | solution.py:568
  828.1 95.2 %collective-permute-start.47 = (bf16[3,192,512]{2,1,0:T(8,128)(2,1)}, bf16[3,192,512]{2,1,0:T(8,128)(2,1)}, u32[]{:S(2)}, u32[]{:S(2)}) collective-permute-start(bf16[3,192,512]{2,1,0:T(8,128)(2,1)} %fusion.64.rest_0_), channel_id=1, source_target_pairs={{0,4},{2,6},{4,0},{6,2},{8,12},{10,14},{12,8},{14,10},{16,20},{18,... | collective-permute-start | bytes 1769480 | tf_op jit(solution)/shard_map/ppermute | solution.py:568
  829.8 91.3 %collective-permute-start.48 = (bf16[3,192,512]{2,1,0:T(8,128)(2,1)S(1)}, bf16[3,192,512]{2,1,0:T(8,128)(2,1)}, u32[]{:S(2)}, u32[]{:S(2)}) collective-permute-start(bf16[3,192,512]{2,1,0:T(8,128)(2,1)S(1)} %fusion.67.rest_2_), channel_id=1, source_target_pairs={{0,16},{2,18},{4,20},{6,22},{8,24},{10,26},{12,28},{14,30},{16,0},... | collective-permute-start | bytes 1769480 | tf_op jit(solution)/shard_map/ppermute | solution.py:568
  842.6 150.2 %collective-permute-start.41 = (bf16[1024,1536]{1,0:T(8,128)(2,1)}, bf16[1024,1536]{1,0:T(8,128)(2,1)}, u32[]{:S(2)}, u32[]{:S(2)}) collective-permute-start(bf16[1024,1536]{1,0:T(8,128)(2,1)} %add_convert_fusion.1.rest_0_), channel_id=1, source_target_pairs={{0,1},{1,0},{2,3},{3,2},{4,5},{5,4},{6,7},{7,6},{8,9},{9,8},{10,11... | collective-permute-start | bytes 9437192 | tf_op jit(solution)/shard_map/ppermute | solution.py:572
  889.1 105.8 %collective-permute-start.40 = (bf16[1024,1536]{1,0:T(8,128)(2,1)}, bf16[1024,1536]{1,0:T(8,128)(2,1)}, u32[]{:S(2)}, u32[]{:S(2)}) collective-permute-start(bf16[1024,1536]{1,0:T(8,128)(2,1)} %get-tuple-element.173.rest_1_), channel_id=1, source_target_pairs={{0,2},{2,0},{4,6},{6,4},{8,10},{10,8},{12,14},{14,12},{16,18},{18,... | collective-permute-start | bytes 9437192 | tf_op jit(solution)/shard_map/ppermute | solution.py:568
  923.3 209.6 %collective-permute-start.52 = (bf16[2,2,3,192,512]{4,3,2,1,0:T(8,128)(2,1)}, bf16[2,2,3,192,512]{4,3,2,1,0:T(8,128)(2,1)}, u32[]{:S(2)}, u32[]{:S(2)}) collective-permute-start(bf16[2,2,3,192,512]{4,3,2,1,0:T(8,128)(2,1)} %get-tuple-element.200), channel_id=1, source_target_pairs={{0,4},{2,6},{4,0},{6,2},{8,12},{10,14},{12,8},{14,10},{16,20},{18,... | collective-permute-start | bytes 7077896 | tf_op jit(solution)/shard_map/ppermute | solution.py:568
  994.9 99.1 %collective-permute-start.39 = (bf16[1024,1536]{1,0:T(8,128)(2,1)}, bf16[1024,1536]{1,0:T(8,128)(2,1)}, u32[]{:S(2)}, u32[]{:S(2)}) collective-permute-start(bf16[1024,1536]{1,0:T(8,128)(2,1)} %add_convert_fusion.2.rest_0_), channel_id=1, source_target_pairs={{0,1},{1,0},{2,3},{3,2},{4,5},{5,4},{6,7},{7,6},{8,9},{9,8},{10,11... | collective-permute-start | bytes 9437192 | tf_op jit(solution)/shard_map/ppermute | solution.py:572
  1037.6 94.9 %collective-permute-start.53 = (bf16[2,3,192,512]{3,2,1,0:T(8,128)(2,1)S(1)}, bf16[2,3,192,512]{3,2,1,0:T(8,128)(2,1)}, u32[]{:S(2)}, u32[]{:S(2)}) collective-permute-start(bf16[2,3,192,512]{3,2,1,0:T(8,128)(2,1)S(1)} %copy-done.38), channel_id=1, source_target_pairs={{0,8},{2,10},{4,12},{6,14},{8,0},{10,2},{12,4},{14,6},{16,24},{18,... | collective-permute-start | bytes 3538952 | tf_op jit(solution)/shard_map/ppermute | solution.py:568
  1140.1 77.3 %collective-permute-start.75 = (bf16[2,3,192,512]{3,2,1,0:T(8,128)(2,1)}, bf16[2,3,192,512]{3,2,1,0:T(8,128)(2,1)}, u32[]{:S(2)}, u32[]{:S(2)}) collective-permute-start(bf16[2,3,192,512]{3,2,1,0:T(8,128)(2,1)} %get-tuple-element.297.rest_4_), channel_id=1, source_target_pairs={{0,8},{2,10},{4,12},{6,14},{8,0},{10,2},{12,4},{14,6},{16,24},{18,... | collective-permute-start | bytes 3538952 | tf_op jit(solution)/shard_map/ppermute | solution.py:568
  1146.0 107.4 %collective-permute-start.74 = (bf16[3,192,512]{2,1,0:T(8,128)(2,1)}, bf16[3,192,512]{2,1,0:T(8,128)(2,1)}, u32[]{:S(2)}, u32[]{:S(2)}) collective-permute-start(bf16[3,192,512]{2,1,0:T(8,128)(2,1)} %fusion.73.rest_1_), channel_id=1, source_target_pairs={{0,16},{2,18},{4,20},{6,22},{8,24},{10,26},{12,28},{14,30},{16,0},... | collective-permute-start | bytes 1769480 | tf_op jit(solution)/shard_map/ppermute | solution.py:568
  (186 other events, 4085.6 us)

commit v4 on v3

--- a/solution.py
+++ b/solution.py
@@ -82,9 +82,10 @@
 
 
 BLOCK = 256
-PART = 256
+PART = 128
 PIECE_ROWS = 32
 GROUP = 8
+DEEP = 4
 VMEM_LIMIT = 60 * 1024 * 1024
 
 
@@ -220,27 +221,19 @@
             gate_buffer[slot] = jnp.zeros(gate_buffer.shape[1:], gate_buffer.dtype)
         rows = lax.broadcasted_iota(jnp.int32, (PART, BLOCK), 0) + part * PART
 
-        def step(pair, carry):
-            pick = jnp.concatenate(
-                [
-                    jnp.where(rows == place_ref[expert, 2 * pair + i], 1.0, 0.0)
-                    for i in range(2)
-                ],
-                axis=1,
-            ).astype(jnp.bfloat16)
-            start = pl.multiple_of(pair * 2 * BLOCK, 2 * BLOCK)
+        def step(tile, carry):
+            pick = jnp.where(rows == place_ref[expert, tile], 1.0, 0.0).astype(jnp.bfloat16)
+            start = pl.multiple_of(tile * BLOCK, BLOCK)
             buffer[slot] += jnp.dot(
-                pick, held[pl.ds(start, 2 * BLOCK), :], preferred_element_type=jnp.float32
+                pick, held[pl.ds(start, BLOCK), :], preferred_element_type=jnp.float32
             ).astype(buffer.dtype)
             if with_gates:
                 gate_buffer[slot] += jnp.dot(
-                    pick, gates_ref[pl.ds(start, 2 * BLOCK), :], preferred_element_type=jnp.float32
+                    pick, gates_ref[pl.ds(start, BLOCK), :], preferred_element_type=jnp.float32
                 )
             return carry
 
-        lax.fori_loop(
-            low_ref[expert, part] // 2, (high_ref[expert, part] + 1) // 2, step, 0
-        )
+        lax.fori_loop(low_ref[expert, part], high_ref[expert, part], step, 0)
         for copy in copies_of(part, slot):
             copy.start()
         return carry
@@ -422,12 +415,12 @@
         return (misc[0] + first + expert, 0, 0)
 
     def grads_index(expert, block, blocks, misc):
-        return (0, 0, 0, 0, 0)
+        return (0, 0, expert, 0, 0)
 
     out_shape = [jax.ShapeDtypeStruct((experts * slots, 2 * width + 128), jnp.bfloat16)]
     out_specs = [pl.BlockSpec((BLOCK, 2 * width + 128), rows_index(0))]
     if split:
-        out_shape += [jax.ShapeDtypeStruct((2, 2, 3, depth, hidden), jnp.bfloat16)] * 2
+        out_shape += [jax.ShapeDtypeStruct((2, 2, 3 * count, depth, hidden), jnp.bfloat16)] * 2
         out_specs += [pl.BlockSpec((2, 2, 3, depth, hidden), grads_index)] * 2
     else:
         out_shape += [jax.ShapeDtypeStruct((count, 3, width, hidden), jnp.bfloat16)]
@@ -471,14 +464,21 @@
 
 
 def combine_kernel(
-    first, owner_ref, piece_ref, source_ref, groups_ref, begin_ref, place_ref, yd_ref, *rest
+    first, owner_ref, piece_ref, source_ref, groups_ref, begin_ref, tile_ref, place_ref, yd_ref, *rest
 ):
-    y_out, dx_out, gate_out, buffer, total, sems = rest[-6:]
-    columns = y_out.shape[1]
+    yd_out, gate_out, buffer, total, sems = rest[-5:]
+    columns = yd_out.shape[1]
     step = pl.program_id(0)
     tile = first + step
 
-    def copies(which_tile, group, slot):
+    head = begin_ref[first]
+    final = first + pl.num_programs(0) - 1
+    stop = begin_ref[final] + groups_ref[final]
+
+    def copies(place):
+        which_tile = tile_ref[place]
+        group = place - begin_ref[which_tile]
+        slot = (place - head) % DEEP
         made = []
         for i in range(GROUP):
             source = pl.multiple_of(
@@ -495,18 +495,20 @@
 
     @pl.when(step == 0)
     def _():
-        for copy in copies(tile, 0, begin_ref[tile] % 2):
-            copy.start()
+        for ahead in range(DEEP - 1):
+
+            @pl.when(head + ahead < stop)
+            def _():
+                for copy in copies(head + ahead):
+                    copy.start()
 
     def one(group, carry):
-        slot = (begin_ref[tile] + group) % 2
-        last = group + 1 == groups_ref[tile]
-        next_tile = jnp.where(last, tile + 1, tile)
-        next_group = jnp.where(last, 0, group + 1)
-
-        @pl.when(jnp.logical_not(last & (step == pl.num_programs(0) - 1)))
+        place = begin_ref[tile] + group
+        slot = (place - head) % DEEP
+
+        @pl.when(place + DEEP - 1 < stop)
         def _():
-            for copy in copies(next_tile, next_group, 1 - slot):
+            for copy in copies(place + DEEP - 1):
                 copy.start()
 
         picks = []
@@ -518,7 +520,7 @@
             )
             picks.append(jnp.where(rows == place_ref[owner_ref[tile, entry], step], 1.0, 0.0))
         picked = jnp.concatenate(picks, axis=0).T.astype(jnp.bfloat16)
-        for copy in copies(tile, group, slot):
+        for copy in copies(place):
             copy.wait()
         fresh = group == 0
         for begin in range(0, total.shape[1], 640):
@@ -528,39 +530,43 @@
         return carry
 
     lax.fori_loop(0, groups_ref[tile], one, 0)
-    y_out[...] = total[:, :columns].astype(y_out.dtype)
-    dx_out[...] = total[:, columns : 2 * columns].astype(dx_out.dtype)
-    gate_out[...] = total[:, 2 * columns :]
+    yd_out[...] = total[:, :columns].astype(yd_out.dtype)
+    gate_out[...] = total[:, columns:]
 
 
 def combine_rows(tables, place, yd, first, count, after=()):
     owner, piece, source, groups, width = tables
-    begin = jnp.cumsum(groups) - groups
+    ends = jnp.cumsum(groups)
+    begin = ends - groups
+    most = groups.shape[0] * (width // GROUP)
+    tile_of = jnp.minimum(
+        jnp.sum((ends[None, :] <= jnp.arange(most)[:, None]).astype(jnp.int32), axis=1),
+        groups.shape[0] - 1,
+    )
     experts = place.shape[0]
     whole_width = yd.shape[1]
-    columns = (whole_width - 128) // 2
+    columns = whole_width - 128
     row_block = lambda wide: pl.BlockSpec((BLOCK, wide), lambda t, *_: (t, 0))
     return pl.pallas_call(
         functools.partial(combine_kernel, first),
         grid_spec=pltpu.PrefetchScalarGridSpec(
-            num_scalar_prefetch=5,
+            num_scalar_prefetch=6,
             grid=(count,),
             in_specs=[pl.BlockSpec((experts, count, 1, BLOCK), lambda *_: (0, first // count, 0, 0))]
             + [pl.BlockSpec(memory_space=pl.ANY)] * (1 + len(after)),
-            out_specs=[row_block(columns), row_block(columns), row_block(128)],
+            out_specs=[row_block(columns), row_block(128)],
             scratch_shapes=[
-                pltpu.VMEM((2, GROUP * PIECE_ROWS, whole_width), jnp.bfloat16),
+                pltpu.VMEM((DEEP, GROUP * PIECE_ROWS, whole_width), jnp.bfloat16),
                 pltpu.VMEM((BLOCK, whole_width), jnp.float32),
-                pltpu.SemaphoreType.DMA((2, GROUP)),
+                pltpu.SemaphoreType.DMA((DEEP, GROUP)),
             ],
         ),
         out_shape=[
             jax.ShapeDtypeStruct((count * BLOCK, columns), jnp.bfloat16),
-            jax.ShapeDtypeStruct((count * BLOCK, columns), jnp.bfloat16),
             jax.ShapeDtypeStruct((count * BLOCK, 128), jnp.float32),
         ],
         compiler_params=pltpu.CompilerParams(vmem_limit_bytes=VMEM_LIMIT),
-    )(owner, piece, source, groups, begin, place, yd, *after)
+    )(owner, piece, source, groups, begin, tile_of, place, yd, *after)
 
 
 def flip(value, bit):
@@ -712,7 +718,8 @@
     )(normed, weights, *tables, *after)
 
 
-def attend_kernel(per_pair, query_ref, key_ref, value_ref, limit_ref, out_ref, lse_ref):
+def attend_kernel(per_pair, query_ref, key_ref, value_ref, limit_ref, *rest):
+    out_ref, lse_ref = rest[-2:]
     step = pl.program_id(1)
 
     def work(keys):
@@ -751,7 +758,7 @@
         work(2 * HALF)
 
 
-def attend(query, key, value, limits):
+def attend(query, key, value, limits, after=()):
     rows, query_width = query.shape
     pairs = key.shape[1] // 128
     wide = query_width // pairs
@@ -763,7 +770,8 @@
             pl.BlockSpec((rows, 128), lambda p, i: (0, p)),
             pl.BlockSpec((rows, 128), lambda p, i: (0, p)),
             pl.BlockSpec((ROWS, 1), lambda p, i: (i, 0)),
-        ],
+        ]
+        + [pl.BlockSpec(memory_space=pl.ANY)] * len(after),
         out_specs=[
             pl.BlockSpec((ROWS, wide), lambda p, i: (i, p)),
             pl.BlockSpec((1, ROWS, 128), lambda p, i: (p, i, 0)),
@@ -773,7 +781,7 @@
             jax.ShapeDtypeStruct((pairs, rows, 128), jnp.float32),
         ],
         compiler_params=pltpu.CompilerParams(vmem_limit_bytes=VMEM_LIMIT),
-    )(query, key, value, limits)
+    )(query, key, value, limits, *after)
 
 
 def back_kernel(
@@ -1259,8 +1267,8 @@
     return [value, across, flip(value, 1), flip(across, 1)]
 
 
-FIRST_PART = 2
-FAR_FIRST = (2, 5)
+CHUNK = 2
+FAR_FIRST = -1
 
 
 def shards_pair(
@@ -1310,7 +1318,7 @@
         own_routes[:, :, None] == jnp.arange(expert_count, dtype=jnp.int32)[None, None, :]
     ).astype(jnp.float32)
     counts = all_sum(jnp.sum(route_onehot, axis=(0, 1)))
-    cotangent_rows = spread(order(cotangent, joined_piece, out_piece))
+    cotangent_rows = spread(order(cotangent, joined_piece))
 
     inputs_share = tokens.astype(jnp.float32)
     normed = normalize(inputs_share, norm_gains).astype(jnp.bfloat16)
@@ -1318,14 +1326,14 @@
     starts_row = lax.dynamic_index_in_dim(starts, tensor_rank, 0, keepdims=False)
     limits = piece_limits(starts_row, share_rows)
 
-    def half_forward(joined_weights, after=()):
+    def half_forward(joined_weights, after=(), later=()):
         query, key, value = project(
             normed, joined_weights, tables, query_width, key_width, score_scale, after
         )
-        attended, lse = attend(query, key, value, limits)
+        attended, lse = attend(query, key, value, limits, later)
         return attended, (query, key, value, lse)
 
-    attended_own, saved_own = half_forward(joined_own)
+    attended_own, saved_own = half_forward(joined_own, (), (joined_piece,))
     attended_other, saved_other = half_forward(joined_other, (counts,))
     middle_share = (
         inputs_share
@@ -1352,77 +1360,62 @@
     misc = jnp.stack([core * experts, side, (rank // 4) % 2])
     weights = (w_gate, w_up, w_down)
     first_part = gather_rows(
-        gather_from, place, gates, mixed_rows, slots, 0, FIRST_PART, (cot_slots, counts)
+        gather_from, place, gates, mixed_rows, slots, 0, CHUNK, (cot_slots, counts)
     )
     later_part = None
     carried = None
     chips = []
-    for index in range(experts):
-        if index == FIRST_PART:
+    for index in range(experts // CHUNK):
+        if index == 1:
             later_part = gather_rows(
-                gather_from, place, gates, mixed_rows, slots, FIRST_PART, experts - FIRST_PART,
-                (carried,),
+                gather_from, place, gates, mixed_rows, slots, CHUNK, experts - CHUNK, (carried,)
             )
-        if later_part is None:
-            (x_slots, slot_gates), x_first = first_part, 0
-        else:
-            (x_slots, slot_gates), x_first = later_part, FIRST_PART
+        (x_slots, slot_gates), x_first = (later_part, CHUNK) if index else (first_part, 0)
         waits = []
         if index == 2:
-            waits = [chips[0].one(slot_gates)]
+            waits = [chips[0].one(carried)]
         elif index == 4:
             waits = [chips[0].two(carried)]
-        elif index == 5:
-            waits = [chips[1].one(carried)]
-        elif index == 6:
-            waits = [chips[2].one(carried)]
-        elif index == 8:
-            waits = [chips[3].one(carried), chips[1].two(carried)]
-        far_first = int(index in FAR_FIRST)
+        far_first = int(index == FAR_FIRST)
         carried, send, keep = expert_call(
             blocks, misc, x_slots, cot_slots, slot_gates, weights, carried, slots,
-            index, 1, x_first, 0, depth, far_first, waits,
+            index * CHUNK, CHUNK, x_first, 0, depth, far_first, waits,
         )
         chips.append(ChipSum((send, keep), rank, far_first))
-    waits = [chips[4].one(carried), chips[5].one(carried)]
-    done = [chips[0].three(carried)]
-    waits += done
+    waits = [chips[1].one(carried)]
 
     combine_from = combine_tables(begins, ends, slots)
     tiles = place.shape[1] // 4
     names = first_expert + jnp.arange(experts, dtype=jnp.int32)
 
     def combined(quarter, after):
-        y, dx, gate_grads = combine_rows(
-            combine_from, place, carried, quarter * tiles, tiles, after
-        )
+        yd, gate_grads = combine_rows(combine_from, place, carried, quarter * tiles, tiles, after)
         gate_grads = gate_grads[:, :experts] + gate_grads[:, 64 : 64 + experts]
         rows = group_routes[quarter * share_rows : (quarter + 1) * share_rows]
         hit = rows[:, :, None] == names[None, None, :]
-        return y, dx, jnp.sum(jnp.where(hit, gate_grads[:, None, :], 0.0), axis=2)
+        return yd, jnp.sum(jnp.where(hit, gate_grads[:, None, :], 0.0), axis=2)
 
     far = combined(3, waits)
-    waits = [chips[2].two(far[1])]
-    done.append(chips[1].three(far[1]))
-    waits.append(done[1])
-    far_y, far_dx, far_gg = (flip(value, 1) for value in far)
-    cross = combined(1, waits)
-    dx_send = add_low(cross[1], far_dx)
+    far_yd, far_gg = (flip(value, 1) for value in far)
+    cross = combined(1, [far[0]])
+    dx_send = add_low(cross[0][:, model_width:], far_yd[:, model_width:])
     dx_across = swap(dx_send)
-    gg_across = swap(cross[2] + far_gg)
-    waits = [dx_send, chips[6].one(cross[1]), chips[3].two(cross[1])]
-    next_door = combined(2, waits)
-    door_y, door_dx, door_gg = (flip(value, 1) for value in next_door)
-    y_send = add_low(cross[0], far_y)
-    y_across = swap(order(y_send, dx_send))
-    near = combined(0, [y_send, next_door[1]])
-    waits = [chips[7].one(near[1]), chips[5].two(near[1])]
-    done += [chips[2].three(near[1]), chips[3].three(near[1])]
-    waits += done[2:]
+    gg_across = swap(cross[1] + far_gg)
+    next_door = combined(2, [dx_send])
+    door_yd, door_gg = (flip(value, 1) for value in next_door)
+    y_send = add_low(cross[0][:, :model_width], far_yd[:, :model_width])
+    near = combined(0, [next_door[0]])
+    y_across = swap(order(y_send, near[0]))
+    waits = [chips[2].one(near[0]), chips[1].two(near[0])]
+    done = [chips[0].three(near[0])]
+    waits += done
+    near_yd = order(near[0], *waits)
     mixed_grad_share = (
-        near[1].astype(jnp.float32) + door_dx.astype(jnp.float32) + dx_across.astype(jnp.float32)
-    )
-    gates_grad_share = near[2] + door_gg + gg_across
+        near_yd[:, model_width:].astype(jnp.float32)
+        + door_yd[:, model_width:].astype(jnp.float32)
+        + dx_across.astype(jnp.float32)
+    )
+    gates_grad_share = near[1] + door_gg + gg_across
 
     upstream = cotangent.astype(jnp.float32)
     chosen_grad = gate_soft * (
@@ -1460,14 +1453,17 @@
 
         return part
 
-    waits += [chips[8].one(middle_low), chips[4].two(middle_low), chips[6].two(middle_low)]
     pairs = key_width // 128
     other_grads = jnp.concatenate(
         half_back(saved_other, out_other)((0, pairs), waits), axis=1
     )
+    waits = [chips[3].one(other_grads), chips[2].two(other_grads)]
+    done.append(chips[1].three(other_grads))
+    waits.append(done[1])
+    other_grads = order(other_grads, *waits)
     expert_share = (
-        near[0].astype(jnp.float32)
-        + door_y.astype(jnp.float32)
+        near[0][:, :model_width].astype(jnp.float32)
+        + door_yd[:, :model_width].astype(jnp.float32)
         + order(y_across, other_grads).astype(jnp.float32)
     )
     output_share = (middle_share + expert_share).astype(jnp.bfloat16)
@@ -1477,10 +1473,7 @@
     out_held = core_sum(dot_tn(marked, attended_other), core)
     out_across = swap(order(out_held, joined_held))
     out_kept = core_sum(dot_tn(marked, attended_own), core)
-    waits = [chips[9].one(other_grads), chips[7].two(other_grads)]
-    done += [chips[i].three(other_grads) for i in (4, 5, 6)]
-    waits += done[4:]
-    waits += [joined_held, out_held, out_kept, output_share]
+    waits = [joined_held, out_held, out_kept, output_share]
     own_part = half_back(saved_own, w_out)
     front = own_part((0, pairs // 2), waits)
     back = own_part((pairs // 2, pairs - pairs // 2), [joined_across, front[0]])
@@ -1489,13 +1482,15 @@
     )
     out_half = add_low(out_kept, order(out_across, own_grads))
     own_weight_grads = dot_tn(normed, own_grads)
-    joined_total = plane_sum(add_low(core_sum(own_weight_grads, core), joined_across), rank)
+    own_held = core_sum(own_weight_grads, core)
+    joined_total = plane_sum(add_low(own_held, joined_across), rank)
     out_total = plane_sum(out_half, rank, own_weight_grads)
-    chips[8].two(own_grads)
-    chips[9].two(own_grads)
-    sums = done + [chips[i].three(own_weight_grads) for i in (7, 8, 9)]
+    chips[4].one(own_weight_grads)
+    chips[3].two(own_grads)
+    chips[4].two(own_weight_grads)
+    sums = done + [chips[i].three(own_weight_grads) for i in (2, 3, 4)]
     other_normed = dot_nt(other_grads, joined_other)
-    own_normed = dot_nt(own_grads, joined_own)
+    own_normed = dot_nt(order(own_grads, own_held), joined_own)
     input_pullback = jax.vjp(normalize, inputs_share, norm_gains)[1]
     input_from_norm, norm_gain_grad = input_pullback(other_normed + own_normed)
     input_grad_share = middle_grad + input_from_norm
@@ -1511,14 +1506,17 @@
     router_total = small[expert_count + 2 * model_width :].reshape(router_grad.shape)
     balance = expert_count * expert_count * fractions * prob_sums / total_tokens
 
-    mine = jnp.stack(sums, axis=0).reshape(experts, 3, 2, depth // 2, -1)
+    mine = jnp.concatenate(sums, axis=0).reshape(experts, 3, 2, depth // 2, -1)
     theirs = flip(pick_index(mine, 1 - core, 2), 1)
     mine = pick_index(mine, core, 2)
-    expert_total = jnp.where(
-        core == 0,
-        jnp.concatenate([mine, theirs], axis=0),
-        jnp.concatenate([theirs, mine], axis=0),
-    ).astype(jnp.float32)
+    def placed(kind):
+        own_kind, other_kind = mine[:, kind], theirs[:, kind]
+        return jnp.where(
+            core == 0,
+            jnp.concatenate([own_kind, other_kind], axis=0),
+            jnp.concatenate([other_kind, own_kind], axis=0),
+        ).astype(jnp.float32)
+
     return (
         output_share,
         balance,
@@ -1530,9 +1528,9 @@
         out_total.T,
         mix_gain_total,
         router_total,
-        expert_total[:, 0],
-        expert_total[:, 1],
-        expert_total[:, 2].transpose(0, 2, 1),
+        placed(0),
+        placed(1),
+        placed(2).transpose(0, 2, 1),
     )
 
 

time: 1380 us -> 1240 us (0.90)
  waiting for transfers between devices: 245 us -> 191 us
  other arithmetic: 176 us -> 152 us
  starting transfers between devices: 134 us -> 116 us
  local copies, waits for them, and re-layouts: 120 us -> 103 us
  Pallas kernels: 611 us -> 595 us
    ppermute x68 -> x51, waiting for transfers between devices: 225 us -> 181 us  [flip(): return lax.ppermute(value, 'dp', [(i, i ^ bit) for i in range(size)])]
    convert_element_type x41 -> x20, other arithmetic: 104 us -> 74.4 us  [add_low(): (left.astype(jnp.float32) + right.astype(jnp.float32)).astype(jnp.bfloat16)]
    unnamed x4 -> x12, other arithmetic: 0.01 us -> 14 us
    ppermute x68 -> x51, starting transfers between devices: 88.5 us -> 77.3 us  [flip(): return lax.ppermute(value, 'dp', [(i, i ^ bit) for i in range(size)])]
    unnamed x280 -> x229, local copies, waits for them, and re-layouts: 36.4 us -> 30.5 us
    pallas_call x10 -> x5, Pallas kernels: 210 us -> 210 us  [expert_call(): pl.pallas_call(functools.partial(expert_kernel, first, split, depth, far_...]
  transfers between devices with their start and end apart: 80 -> 63, of which waited for: 18 -> 17; matrix products, arithmetic and copies ran while one was open for 26% -> 23% of each run, Pallas kernels for 40% -> 40%
where the time goes in v4:
time: 1240 us
  Pallas kernels  595 us (48%)
  waiting for transfers between devices  191 us (15%)
  other arithmetic  152 us (12%)
  starting transfers between devices  116 us (9%)
  local copies, waits for them, and re-layouts  103 us (8%)
  matrix products  74.8 us (6%)
    pallas_call x5, Pallas kernels, expert_call(): pl.pallas_call(functools.partial(expert_kernel, first, split, depth, far_...  210 us
    ppermute x51, waiting for transfers between devices, flip(): return lax.ppermute(value, 'dp', [(i, i ^ bit) for i in range(size)])  181 us
    pallas_call x3, Pallas kernels, gather_rows(): pl.pallas_call(functools.partial(gather_kernel, len(sources), with_gates,...  165 us
    pallas_call x3, Pallas kernels, attend_back(): pl.pallas_call(functools.partial(back_kernel, wide // HD, score_scale, le...  82.5 us
    ppermute x51, starting transfers between devices, flip(): return lax.ppermute(value, 'dp', [(i, i ^ bit) for i in range(size)])  77.3 us
    convert_element_type x20, other arithmetic, add_low(): (left.astype(jnp.float32) + right.astype(jnp.float32)).astype(jnp.bfloat16)  74.4 us
    pallas_call x4, Pallas kernels, combine_rows(): pl.pallas_call(functools.partial(combine_kernel, first), grid_spec=pltpu....  70.8 us
    pallas_call x2, Pallas kernels, attend(): pl.pallas_call(functools.partial(attend_kernel, wide // HD), grid=(pairs,...  48.9 us
  transfers between devices with their start and end apart: 63, of which 17 were waited for; matrix products, arithmetic and copies ran while one was open for 23% of the time, Pallas kernels for 40%

profile of v4, /device:TPU:0, one launch (start us, length us, event | category | flops | bytes accessed | tf_op | source)
XLA Modules:
  0.0 1236.9 jit_solution(18306262154092575399)
XLA Ops:
  57.4 24.4 %shard_map.238 = (bf16[1024,768]{1,0:T(8,128)(2,1)}, f32[2,1024,128]{2,1,0:T(8,128)}) custom-call(bf16[1024,768]{1,0:T(8,128)(2,1)} %get-tuple-element.86.query_ref, bf16[1024,256]{1,0:T(8,128)(2,1)} %get-tuple-element.87.key_ref, bf16[1024,256]{1,0:T(8,128)(2,1)} %get-tuple-element.88.value_ref, s32[1024,1]{1,0:T(8,128)} %select_select_fusion.limit_ref, ...), custom_call_target="tpu_custom_call" | custom-call | tf_op jit(solution)/shard_map/pallas_call | solution.py:765
  109.3 24.5 %shard_map.240 = (bf16[1024,768]{1,0:T(8,128)(2,1)}, f32[2,1024,128]{2,1,0:T(8,128)}) custom-call(bf16[1024,768]{1,0:T(8,128)(2,1)} %get-tuple-element.90.query_ref, bf16[1024,256]{1,0:T(8,128)(2,1)} %get-tuple-element.91.key_ref, bf16[1024,256]{1,0:T(8,128)(2,1)} %get-tuple-element.92.value_ref, s32[1024,1]{1,0:T(8,128)} %select_select_fusion.limit_ref), custom_call_target="tpu_custom_call" | custom-call | tf_op jit(solution)/shard_map/pallas_call | solution.py:765
  154.8 76.7 %shard_map.241.rest_5_.c_ref = bf16[12800,1536]{1,0:T(8,128)(2,1)} custom-call(s32[10,10]{1,0:T(8,128)} %copy-done.61, s32[10,10]{1,0:T(8,128)} %compare_select_fusion.3.high_ref, s32[10]{0:T(128)} %negate_maximum_fusion.blocks_ref, s32[10,16,1,256]{3,2,1,0:T(1,128)} %add_select_fusion.place_ref, bf16[1024,1536]{1,0:T(8,128)(2,1)} %rest_0_, ...), custom_call_target="tpu_custom_call" | custom-call | tf_op jit(solution)/shard_map/pallas_call | solution.py:270
  248.7 21.3 %shard_map.242 = (bf16[2560,1536]{1,0:T(8,128)(2,1)}, f32[2560,128]{1,0:T(8,128)}) custom-call(s32[2,10]{1,0:T(2,128)} %slice.205.low_ref, s32[2,10]{1,0:T(2,128)} %slice.206.high_ref, s32[2]{0:T(128)} %bitcast.321, s32[2,16,1,256]{3,2,1,0:T(1,128)} %copy.133.place_ref, bf16[4096,128]{1,0:T(8,128)(2,1)} %pad_bitcast_fusion.rest_0_, ...), custom_call_target="tpu_custom_call" | custom-call | tf_op jit(solution)/shard_map/pallas_call | solution.py:270
  270.1 42.9 %shard_map.243 = (bf16[12800,3200]{1,0:T(8,128)(2,1)}, bf16[2,2,6,192,512]{4,3,2,1,0:T(8,128)(2,1)}, bf16[2,2,6,192,512]{4,3,2,1,0:T(8,128)(2,1)}) custom-call(s32[10]{0:T(128)} %negate_maximum_fusion.blocks_ref, s32[3]{0:T(128)} %pad_add_fusion.1.misc_ref, bf16[2560,1536]{1,0:T(8,128)(2,1)} %get-tuple-element.97.x_ref, ...), custom_call_target="tpu_custom_call" | custom-call | tf_op jit(solution)/shard_map/pallas_call | solution.py:444
  315.6 66.4 %shard_map.244 = (bf16[10240,1536]{1,0:T(8,128)(2,1)}, f32[10240,128]{1,0:T(8,128)}) custom-call(s32[8,10]{1,0:T(8,128)} %slice.202.low_ref, s32[8,10]{1,0:T(8,128)} %slice.203.high_ref, s32[8]{0:T(128)} %slice.158.blocks_ref, s32[8,16,1,256]{3,2,1,0:T(1,128)} %copy.134.place_ref, bf16[4096,128]{1,0:T(8,128)(2,1)} %pad_bitcast_fusion.rest_0_, ...), custom_call_target="tpu_custom_call" | custom-call | tf_op jit(solution)/shard_map/pallas_call | solution.py:270
  382.1 42.9 %shard_map.245 = (bf16[12800,3200]{1,0:T(8,128)(2,1)}, bf16[2,2,6,192,512]{4,3,2,1,0:T(8,128)(2,1)}, bf16[2,2,6,192,512]{4,3,2,1,0:T(8,128)(2,1)}) custom-call(s32[10]{0:T(128)} %negate_maximum_fusion.blocks_ref, s32[3]{0:T(128)} %pad_add_fusion.1.misc_ref, bf16[10240,1536]{1,0:T(8,128)(2,1)} %get-tuple-element.100.x_ref, ...), custom_call_target="tpu_custom_call", output_to_operand_aliasing={{0}: (8, {})} | custom-call | tf_op jit(solution)/shard_map/pallas_call | solution.py:444
  439.0 38.7 %shard_map.246 = (bf16[12800,3200]{1,0:T(8,128)(2,1)}, bf16[2,2,6,192,512]{4,3,2,1,0:T(8,128)(2,1)}, bf16[2,2,6,192,512]{4,3,2,1,0:T(8,128)(2,1)}) custom-call(s32[10]{0:T(128)} %negate_maximum_fusion.blocks_ref, s32[3]{0:T(128)} %pad_add_fusion.1.misc_ref, bf16[10240,1536]{1,0:T(8,128)(2,1)} %get-tuple-element.100.x_ref, ...), custom_call_target="tpu_custom_call", output_to_operand_aliasing={{0}: (8, {})} | custom-call | tf_op jit(solution)/shard_map/pallas_call | solution.py:444
  477.7 42.9 %shard_map.247 = (bf16[12800,3200]{1,0:T(8,128)(2,1)}, bf16[2,2,6,192,512]{4,3,2,1,0:T(8,128)(2,1)}, bf16[2,2,6,192,512]{4,3,2,1,0:T(8,128)(2,1)}) custom-call(s32[10]{0:T(128)} %negate_maximum_fusion.blocks_ref, s32[3]{0:T(128)} %pad_add_fusion.1.misc_ref, bf16[10240,1536]{1,0:T(8,128)(2,1)} %get-tuple-element.100.x_ref, ...), custom_call_target="tpu_custom_call", output_to_operand_aliasing={{0}: (8, {})} | custom-call | tf_op jit(solution)/shard_map/pallas_call | solution.py:444
  523.6 43.0 %shard_map.248 = (bf16[12800,3200]{1,0:T(8,128)(2,1)}, bf16[2,2,6,192,512]{4,3,2,1,0:T(8,128)(2,1)}, bf16[2,2,6,192,512]{4,3,2,1,0:T(8,128)(2,1)}) custom-call(s32[10]{0:T(128)} %negate_maximum_fusion.blocks_ref, s32[3]{0:T(128)} %pad_add_fusion.1.misc_ref, bf16[10240,1536]{1,0:T(8,128)(2,1)} %get-tuple-element.100.x_ref, ...), custom_call_target="tpu_custom_call", output_to_operand_aliasing={{0}: (8, {})} | custom-call | tf_op jit(solution)/shard_map/pallas_call | solution.py:444
  574.2 17.9 %shard_map.249 = (bf16[1024,3072]{1,0:T(8,128)(2,1)}, f32[1024,128]{1,0:T(8,128)}) custom-call(s32[16,96]{1,0:T(8,128)} %copy-done.53, s32[16,96]{1,0:T(8,128)} %get-tuple-element.262.piece_ref, s32[16,96]{1,0:T(8,128)} %get-tuple-element.261.source_ref, s32[16]{0:T(128)} %get-tuple-element.230.groups_ref, s32[16]{0:T(128)} %get-tuple-element.229.begin_ref, ...), custom_call_target="tpu_custom_call" | custom-call | tf_op jit(solution)/shard_map/pallas_call | solution.py:550
  592.1 16.2 %collective-permute-start.26 = (bf16[1024,3072]{1,0:T(8,128)(2,1)}, bf16[1024,3072]{1,0:T(8,128)(2,1)}, u32[]{:S(2)}, u32[]{:S(2)}) collective-permute-start(bf16[1024,3072]{1,0:T(8,128)(2,1)} %get-tuple-element.113.rest_0_), channel_id=1, source_target_pairs={{0,2},{2,0},{4,6},{6,4},{8,10},{10,8},{12,14},{14,12},{16,18},{18,... | collective-permute-start | bytes 18874376 | tf_op jit(solution)/shard_map/ppermute | solution.py:574
  608.3 16.8 %shard_map.250 = (bf16[1024,3072]{1,0:T(8,128)(2,1)}, f32[1024,128]{1,0:T(8,128)}) custom-call(s32[16,96]{1,0:T(8,128)} %copy-done.53, s32[16,96]{1,0:T(8,128)} %get-tuple-element.262.piece_ref, s32[16,96]{1,0:T(8,128)} %get-tuple-element.261.source_ref, s32[16]{0:T(128)} %get-tuple-element.230.groups_ref, s32[16]{0:T(128)} %get-tuple-element.229.begin_ref, ...), custom_call_target="tpu_custom_call" | custom-call | tf_op jit(solution)/shard_map/pallas_call | solution.py:550
  632.3 17.9 %shard_map.251 = (bf16[1024,3072]{1,0:T(8,128)(2,1)}, f32[1024,128]{1,0:T(8,128)}) custom-call(s32[16,96]{1,0:T(8,128)} %copy-done.53, s32[16,96]{1,0:T(8,128)} %get-tuple-element.262.piece_ref, s32[16,96]{1,0:T(8,128)} %get-tuple-element.261.source_ref, s32[16]{0:T(128)} %get-tuple-element.230.groups_ref, s32[16]{0:T(128)} %get-tuple-element.229.begin_ref, ...), custom_call_target="tpu_custom_call" | custom-call | tf_op jit(solution)/shard_map/pallas_call | solution.py:550
  688.7 18.2 %shard_map.252 = (bf16[1024,3072]{1,0:T(8,128)(2,1)}, f32[1024,128]{1,0:T(8,128)}) custom-call(s32[16,96]{1,0:T(8,128)} %copy-done.53, s32[16,96]{1,0:T(8,128)} %get-tuple-element.262.piece_ref, s32[16,96]{1,0:T(8,128)} %get-tuple-element.261.source_ref, s32[16]{0:T(128)} %get-tuple-element.230.groups_ref, s32[16]{0:T(128)} %get-tuple-element.229.begin_ref, ...), custom_call_target="tpu_custom_call" | custom-call | tf_op jit(solution)/shard_map/pallas_call | solution.py:550
  710.2 26.2 %collective-permute-done.31 = bf16[6,192,512]{2,1,0:T(8,128)(2,1)} collective-permute-done((bf16[6,192,512]{2,1,0:T(8,128)(2,1)}, bf16[6,192,512]{2,1,0:T(8,128)(2,1)}, u32[]{:S(2)}, u32[]{:S(2)}) %collective-permute-start.31) | collective-permute-done | bytes 1179680 | tf_op jit(solution)/shard_map/ppermute | solution.py:574
  738.6 24.4 %collective-permute-done.29 = bf16[2,2,6,192,512]{4,3,2,1,0:T(8,128)(2,1)} collective-permute-done((bf16[2,2,6,192,512]{4,3,2,1,0:T(8,128)(2,1)}, bf16[2,2,6,192,512]{4,3,2,1,0:T(8,128)(2,1)}, u32[]{:S(2)}, u32[]{:S(2)}) %collective-permute-start.29) | collective-permute-done | bytes 4718624 | tf_op jit(solution)/shard_map/ppermute | solution.py:574
  814.4 40.0 %shard_map.253 = (bf16[1024,768]{1,0:T(8,128)(2,1)}, bf16[1024,256]{1,0:T(8,128)(2,1)}, bf16[1024,256]{1,0:T(8,128)(2,1)}) custom-call(bf16[1024,768]{1,0:T(8,128)(2,1)} %get-tuple-element.90.query_ref, bf16[1024,256]{1,0:T(8,128)(2,1)} %get-tuple-element.91.key_ref, bf16[1024,256]{1,0:T(8,128)(2,1)} %get-tuple-element.92.value_ref, ...), custom_call_target="tpu_custom_call" | custom-call | tf_op jit(solution)/shard_map/pallas_call | solution.py:877
  856.3 18.3 %collective-permute-done.37 = bf16[2,6,192,512]{3,2,1,0:T(8,128)(2,1)} collective-permute-done((bf16[2,6,192,512]{3,2,1,0:T(8,128)(2,1)}, bf16[2,6,192,512]{3,2,1,0:T(8,128)(2,1)}, u32[]{:S(2)}, u32[]{:S(2)}) %collective-permute-start.37) | collective-permute-done | bytes 2359328 | tf_op jit(solution)/shard_map/ppermute | solution.py:574
  938.6 21.0 %shard_map.254 = (bf16[1024,384]{1,0:T(8,128)(2,1)}, bf16[1024,128]{1,0:T(8,128)(2,1)}, bf16[1024,128]{1,0:T(8,128)(2,1)}) custom-call(bf16[1024,768]{1,0:T(8,128)(2,1)} %get-tuple-element.86.query_ref, bf16[1024,256]{1,0:T(8,128)(2,1)} %get-tuple-element.87.key_ref, bf16[1024,256]{1,0:T(8,128)(2,1)} %get-tuple-element.88.value_ref, ...), custom_call_target="tpu_custom_call" | custom-call | tf_op jit(solution)/shard_map/pallas_call | solution.py:877
  970.9 21.6 %shard_map.255 = (bf16[1024,384]{1,0:T(8,128)(2,1)}, bf16[1024,128]{1,0:T(8,128)(2,1)}, bf16[1024,128]{1,0:T(8,128)(2,1)}) custom-call(bf16[1024,768]{1,0:T(8,128)(2,1)} %get-tuple-element.86.query_ref, bf16[1024,256]{1,0:T(8,128)(2,1)} %get-tuple-element.87.key_ref, bf16[1024,256]{1,0:T(8,128)(2,1)} %get-tuple-element.88.value_ref, ...), custom_call_target="tpu_custom_call" | custom-call | tf_op jit(solution)/shard_map/pallas_call | solution.py:877
  1080.0 33.3 %collective-permute-done.55 = bf16[96,768]{1,0:T(8,128)(2,1)} collective-permute-done((bf16[96,768]{1,0:T(8,128)(2,1)}, bf16[96,768]{1,0:T(8,128)(2,1)}, u32[]{:S(2)}, u32[]{:S(2)}) %collective-permute-start.55) | collective-permute-done | bytes 147488 | tf_op jit(solution)/shard_map/ppermute | solution.py:574
  1126.0 22.9 %collective-permute-done.46 = f32[64552]{0:T(1024)S(1)} collective-permute-done((f32[64552]{0:T(1024)S(1)}, f32[64552]{0:T(1024)S(1)}, u32[]{:S(2)}, u32[]{:S(2)}) %collective-permute-start.46) | collective-permute-done | bytes 258240 | tf_op jit(solution)/shard_map/ppermute | solution.py:574
  1155.3 27.2 %collective-permute-done.47 = f32[64552]{0:T(1024)S(1)} collective-permute-done((f32[64552]{0:T(1024)S(1)}, f32[64552]{0:T(1024)S(1)}, u32[]{:S(2)}, u32[]{:S(2)}) %collective-permute-start.47) | collective-permute-done | bytes 258240 | tf_op jit(solution)/shard_map/ppermute | solution.py:574
  (547 shorter events, 486.4 us)
Async XLA Ops:
  56.4 85.8 %collective-permute-start.18 = (bf16[1024,1536]{1,0:T(8,128)(2,1)}, bf16[1024,1536]{1,0:T(8,128)(2,1)}, u32[]{:S(2)}, u32[]{:S(2)}) collective-permute-start(bf16[1024,1536]{1,0:T(8,128)(2,1)} %rest_0_), channel_id=1, source_target_pairs={{0,1},{1,0},{2,3},{3,2},{4,5},{5,4},{6,7},{7,6},{8,9},{9,8},{10,11... | collective-permute-start | bytes 9437192 | tf_op jit(solution)/shard_map/ppermute | solution.py:578
  92.5 62.3 %collective-permute-start.19 = (bf16[1024,1536]{1,0:T(8,128)(2,1)}, bf16[1024,1536]{1,0:T(8,128)(2,1)}, u32[]{:S(2)}, u32[]{:S(2)}) collective-permute-start(bf16[1024,1536]{1,0:T(8,128)(2,1)} %rest_0_), channel_id=1, source_target_pairs={{0,2},{2,0},{4,6},{6,4},{8,10},{10,8},{12,14},{14,12},{16,18},{18,... | collective-permute-start | bytes 9437192 | tf_op jit(solution)/shard_map/ppermute | solution.py:574
  145.4 86.2 %collective-permute-start.17 = (bf16[1024,1536]{1,0:T(8,128)(2,1)}, bf16[1024,1536]{1,0:T(8,128)(2,1)}, u32[]{:S(2)}, u32[]{:S(2)}) collective-permute-start(bf16[1024,1536]{1,0:T(8,128)(2,1)} %multiply_convert_fusion.rest_1_), channel_id=1, source_target_pairs={{0,1},{1,0},{2,3},{3,2},{4,5},{5,4},{6,7},{7,6},{8,9},{9,8},{10,11... | collective-permute-start | bytes 9437192 | tf_op jit(solution)/shard_map/ppermute | solution.py:578
  154.5 94.2 %collective-permute-start.21 = (bf16[1024,1536]{1,0:T(8,128)(2,1)}, bf16[1024,1536]{1,0:T(8,128)(2,1)}, u32[]{:S(2)}, u32[]{:S(2)}) collective-permute-start(bf16[1024,1536]{1,0:T(8,128)(2,1)} %multiply_convert_fusion.rest_1_), channel_id=1, source_target_pairs={{0,2},{2,0},{4,6},{6,4},{8,10},{10,8},{12,14},{14,12},{16,18},{18,... | collective-permute-start | bytes 9437192 | tf_op jit(solution)/shard_map/ppermute | solution.py:574
  313.0 113.4 %collective-permute-start.23 = (bf16[2,2,6,192,512]{4,3,2,1,0:T(8,128)(2,1)}, bf16[2,2,6,192,512]{4,3,2,1,0:T(8,128)(2,1)}, u32[]{:S(2)}, u32[]{:S(2)}) collective-permute-start(bf16[2,2,6,192,512]{4,3,2,1,0:T(8,128)(2,1)} %get-tuple-element.104), channel_id=1, source_target_pairs={{0,4},{2,6},{4,0},{6,2},{8,12},{10,14},{12,8},{14,10},{16,20},{18,... | collective-permute-start | bytes 14155784 | tf_op jit(solution)/shard_map/ppermute | solution.py:574
  425.0 141.5 %collective-permute-start.25 = (bf16[2,2,6,192,512]{4,3,2,1,0:T(8,128)(2,1)}, bf16[2,2,6,192,512]{4,3,2,1,0:T(8,128)(2,1)}, u32[]{:S(2)}, u32[]{:S(2)}) collective-permute-start(bf16[2,2,6,192,512]{4,3,2,1,0:T(8,128)(2,1)} %get-tuple-element.111), channel_id=1, source_target_pairs={{0,4},{2,6},{4,0},{6,2},{8,12},{10,14},{12,8},{14,10},{16,20},{18,... | collective-permute-start | bytes 14155784 | tf_op jit(solution)/shard_map/ppermute | solution.py:574
  434.1 86.5 %collective-permute-start.24 = (bf16[2,6,192,512]{3,2,1,0:T(8,128)(2,1)}, bf16[2,6,192,512]{3,2,1,0:T(8,128)(2,1)}, u32[]{:S(2)}, u32[]{:S(2)}) collective-permute-start(bf16[2,6,192,512]{3,2,1,0:T(8,128)(2,1)} %get-tuple-element.244.rest_1_), channel_id=1, source_target_pairs={{0,8},{2,10},{4,12},{6,14},{8,0},{10,2},{12,4},{14,6},{16,24},{18,... | collective-permute-start | bytes 7077896 | tf_op jit(solution)/shard_map/ppermute | solution.py:574
  650.2 146.6 %collective-permute-start.27 = (bf16[1024,3072]{1,0:T(8,128)(2,1)}, bf16[1024,3072]{1,0:T(8,128)(2,1)}, u32[]{:S(2)}, u32[]{:S(2)}) collective-permute-start(bf16[1024,3072]{1,0:T(8,128)(2,1)} %get-tuple-element.115.rest_0_), channel_id=1, source_target_pairs={{0,2},{2,0},{4,6},{6,4},{8,10},{10,8},{12,14},{14,12},{16,18},{18,... | collective-permute-start | bytes 18874376 | tf_op jit(solution)/shard_map/ppermute | solution.py:574
  650.3 112.7 %collective-permute-start.29 = (bf16[2,2,6,192,512]{4,3,2,1,0:T(8,128)(2,1)}, bf16[2,2,6,192,512]{4,3,2,1,0:T(8,128)(2,1)}, u32[]{:S(2)}, u32[]{:S(2)}) collective-permute-start(bf16[2,2,6,192,512]{4,3,2,1,0:T(8,128)(2,1)} %get-tuple-element.119), channel_id=1, source_target_pairs={{0,4},{2,6},{4,0},{6,2},{8,12},{10,14},{12,8},{14,10},{16,20},{18,... | collective-permute-start | bytes 14155784 | tf_op jit(solution)/shard_map/ppermute | solution.py:574
  660.1 78.5 %collective-permute-start.30 = (bf16[2,6,192,512]{3,2,1,0:T(8,128)(2,1)}, bf16[2,6,192,512]{3,2,1,0:T(8,128)(2,1)}, u32[]{:S(2)}, u32[]{:S(2)}) collective-permute-start(bf16[2,6,192,512]{3,2,1,0:T(8,128)(2,1)} %get-tuple-element.242.rest_0_), channel_id=1, source_target_pairs={{0,8},{2,10},{4,12},{6,14},{8,0},{10,2},{12,4},{14,6},{16,24},{18,... | collective-permute-start | bytes 7077896 | tf_op jit(solution)/shard_map/ppermute | solution.py:574
  660.1 136.6 %collective-permute-start.32 = (bf16[1024,1536]{1,0:T(8,128)(2,1)}, bf16[1024,1536]{1,0:T(8,128)(2,1)}, u32[]{:S(2)}, u32[]{:S(2)}) collective-permute-start(bf16[1024,1536]{1,0:T(8,128)(2,1)} %get-tuple-element.233.rest_0_), channel_id=1, source_target_pairs={{0,1},{1,0},{2,3},{3,2},{4,5},{5,4},{6,7},{7,6},{8,9},{9,8},{10,11... | collective-permute-start | bytes 9437192 | tf_op jit(solution)/shard_map/ppermute | solution.py:578
  736.4 138.2 %collective-permute-start.36 = (bf16[2,2,6,192,512]{4,3,2,1,0:T(8,128)(2,1)}, bf16[2,2,6,192,512]{4,3,2,1,0:T(8,128)(2,1)}, u32[]{:S(2)}, u32[]{:S(2)}) collective-permute-start(bf16[2,2,6,192,512]{4,3,2,1,0:T(8,128)(2,1)} %get-tuple-element.133), channel_id=1, source_target_pairs={{0,4},{2,6},{4,0},{6,2},{8,12},{10,14},{12,8},{14,10},{16,20},{18,... | collective-permute-start | bytes 14155784 | tf_op jit(solution)/shard_map/ppermute | solution.py:574
  786.6 69.7 %collective-permute-start.38 = (bf16[6,192,512]{2,1,0:T(8,128)(2,1)}, bf16[6,192,512]{2,1,0:T(8,128)(2,1)}, u32[]{:S(2)}, u32[]{:S(2)}) collective-permute-start(bf16[6,192,512]{2,1,0:T(8,128)(2,1)} %fusion.40.rest_1_), channel_id=1, source_target_pairs={{0,16},{2,18},{4,20},{6,22},{8,24},{10,26},{12,28},{14,30},{16,0},... | collective-permute-start | bytes 3538952 | tf_op jit(solution)/shard_map/ppermute | solution.py:574
  796.4 78.2 %collective-permute-start.37 = (bf16[2,6,192,512]{3,2,1,0:T(8,128)(2,1)}, bf16[2,6,192,512]{3,2,1,0:T(8,128)(2,1)}, u32[]{:S(2)}, u32[]{:S(2)}) collective-permute-start(bf16[2,6,192,512]{3,2,1,0:T(8,128)(2,1)} %get-tuple-element.240.rest_0_), channel_id=1, source_target_pairs={{0,8},{2,10},{4,12},{6,14},{8,0},{10,2},{12,4},{14,6},{16,24},{18,... | collective-permute-start | bytes 7077896 | tf_op jit(solution)/shard_map/ppermute | solution.py:574
  796.7 107.8 %collective-permute-start.28 = (bf16[1024,1536]{1,0:T(8,128)(2,1)}, bf16[1024,1536]{1,0:T(8,128)(2,1)}, u32[]{:S(2)}, u32[]{:S(2)}) collective-permute-start(bf16[1024,1536]{1,0:T(8,128)(2,1)} %get-tuple-element.117), channel_id=1, source_target_pairs={{0,1},{1,0},{2,3},{3,2},{4,5},{5,4},{6,7},{7,6},{8,9},{9,8},{10,11... | collective-permute-start | bytes 9437192 | tf_op jit(solution)/shard_map/ppermute | solution.py:578
  902.4 129.4 %collective-permute-start.59 = (bf16[2,2,6,192,512]{4,3,2,1,0:T(8,128)(2,1)}, bf16[2,2,6,192,512]{4,3,2,1,0:T(8,128)(2,1)}, u32[]{:S(2)}, u32[]{:S(2)}) collective-permute-start(bf16[2,2,6,192,512]{4,3,2,1,0:T(8,128)(2,1)} %get-tuple-element.155), channel_id=1, source_target_pairs={{0,4},{2,6},{4,0},{6,2},{8,12},{10,14},{12,8},{14,10},{16,20},{18,... | collective-permute-start | bytes 14155784 | tf_op jit(solution)/shard_map/ppermute | solution.py:574
  904.5 127.3 %collective-permute-start.56 = (bf16[6,192,512]{2,1,0:T(8,128)(2,1)}, bf16[6,192,512]{2,1,0:T(8,128)(2,1)}, u32[]{:S(2)}, u32[]{:S(2)}) collective-permute-start(bf16[6,192,512]{2,1,0:T(8,128)(2,1)} %fusion.42), channel_id=1, source_target_pairs={{0,16},{2,18},{4,20},{6,22},{8,24},{10,26},{12,28},{14,30},{16,0},... | collective-permute-start | bytes 3538952 | tf_op jit(solution)/shard_map/ppermute | solution.py:574
  933.3 66.4 %collective-permute-start.52 = (bf16[8,96,768]{2,1,0:T(8,128)(2,1)}, bf16[8,96,768]{2,1,0:T(8,128)(2,1)}, u32[]{:S(2)}, u32[]{:S(2)}) collective-permute-start(bf16[8,96,768]{2,1,0:T(8,128)(2,1)} %fusion.32.rest_1_), channel_id=1, source_target_pairs={{0,1},{1,0},{2,3},{3,2},{4,5},{5,4},{6,7},{7,6},{8,9},{9,8},{10,11... | collective-permute-start | bytes 3538952 | tf_op jit(solution)/shard_map/ppermute | solution.py:578
  937.3 83.8 %collective-permute-start.57 = (bf16[2,6,192,512]{3,2,1,0:T(8,128)(2,1)}, bf16[2,6,192,512]{3,2,1,0:T(8,128)(2,1)}, u32[]{:S(2)}, u32[]{:S(2)}) collective-permute-start(bf16[2,6,192,512]{3,2,1,0:T(8,128)(2,1)} %get-tuple-element.238), channel_id=1, source_target_pairs={{0,8},{2,10},{4,12},{6,14},{8,0},{10,2},{12,4},{14,6},{16,24},{18,... | collective-permute-start | bytes 7077896 | tf_op jit(solution)/shard_map/ppermute | solution.py:574
  1031.5 83.5 %collective-permute-start.58 = (bf16[6,192,512]{2,1,0:T(8,128)(2,1)}, bf16[6,192,512]{2,1,0:T(8,128)(2,1)S(1)}, u32[]{:S(2)}, u32[]{:S(2)}) collective-permute-start(bf16[6,192,512]{2,1,0:T(8,128)(2,1)} %fusion.48), channel_id=1, source_target_pairs={{0,16},{2,18},{4,20},{6,22},{8,24},{10,26},{12,28},{14,30},{16,0},... | collective-permute-start | bytes 3538952 | tf_op jit(solution)/shard_map/ppermute | solution.py:574
  1039.7 77.9 %collective-permute-start.60 = (bf16[2,6,192,512]{3,2,1,0:T(8,128)(2,1)}, bf16[2,6,192,512]{3,2,1,0:T(8,128)(2,1)}, u32[]{:S(2)}, u32[]{:S(2)}) collective-permute-start(bf16[2,6,192,512]{3,2,1,0:T(8,128)(2,1)} %get-tuple-element.236), channel_id=1, source_target_pairs={{0,8},{2,10},{4,12},{6,14},{8,0},{10,2},{12,4},{14,6},{16,24},{18,... | collective-permute-start | bytes 7077896 | tf_op jit(solution)/shard_map/ppermute | solution.py:574
  1042.5 70.9 %collective-permute-start.55 = (bf16[96,768]{1,0:T(8,128)(2,1)}, bf16[96,768]{1,0:T(8,128)(2,1)}, u32[]{:S(2)}, u32[]{:S(2)}) collective-permute-start(bf16[96,768]{1,0:T(8,128)(2,1)} %dynamic-slice_bitcast_fusion.5), channel_id=1, source_target_pairs={{0,16},{2,18},{4,20},{6,22},{8,24},{10,26},{12,28},{14,30},{16,0},... | collective-permute-start | bytes 442376 | tf_op jit(solution)/shard_map/ppermute | solution.py:574
  1074.3 79.8 %collective-permute-start.49 = (bf16[4,96,1280]{2,1,0:T(8,128)(2,1)S(1)}, bf16[4,96,1280]{2,1,0:T(8,128)(2,1)S(1)}, u32[]{:S(2)}, u32[]{:S(2)}) collective-permute-start(bf16[4,96,1280]{2,1,0:T(8,128)(2,1)S(1)} %dynamic-slice_bitcast_fusion), channel_id=1, source_target_pairs={{0,4},{2,6},{4,0},{6,2},{8,12},{10,14},{12,8},{14,10},{16,20},{18,... | collective-permute-start | bytes 2949128 | tf_op jit(solution)/shard_map/ppermute | solution.py:574
  1119.3 63.7 %collective-permute-start.61 = (bf16[6,192,512]{2,1,0:T(8,128)(2,1)S(1)}, bf16[6,192,512]{2,1,0:T(8,128)(2,1)S(1)}, u32[]{:S(2)}, u32[]{:S(2)}) collective-permute-start(bf16[6,192,512]{2,1,0:T(8,128)(2,1)S(1)} %fusion.51), channel_id=1, source_target_pairs={{0,16},{2,18},{4,20},{6,22},{8,24},{10,26},{12,28},{14,30},{16,0},... | collective-permute-start | bytes 3538952 | tf_op jit(solution)/shard_map/ppermute | solution.py:574
  (148 other events, 2931.5 us)

commit v5 on v4

--- a/solution.py
+++ b/solution.py
@@ -466,8 +466,8 @@
 def combine_kernel(
     first, owner_ref, piece_ref, source_ref, groups_ref, begin_ref, tile_ref, place_ref, yd_ref, *rest
 ):
-    yd_out, gate_out, buffer, total, sems = rest[-5:]
-    columns = yd_out.shape[1]
+    y_out, dx_out, gate_out, buffer, total, sems = rest[-6:]
+    columns = y_out.shape[1]
     step = pl.program_id(0)
     tile = first + step
 
@@ -530,8 +530,9 @@
         return carry
 
     lax.fori_loop(0, groups_ref[tile], one, 0)
-    yd_out[...] = total[:, :columns].astype(yd_out.dtype)
-    gate_out[...] = total[:, columns:]
+    y_out[...] = total[:, :columns].astype(y_out.dtype)
+    dx_out[...] = total[:, columns : 2 * columns].astype(dx_out.dtype)
+    gate_out[...] = total[:, 2 * columns :]
 
 
 def combine_rows(tables, place, yd, first, count, after=()):
@@ -545,7 +546,7 @@
     )
     experts = place.shape[0]
     whole_width = yd.shape[1]
-    columns = whole_width - 128
+    columns = (whole_width - 128) // 2
     row_block = lambda wide: pl.BlockSpec((BLOCK, wide), lambda t, *_: (t, 0))
     return pl.pallas_call(
         functools.partial(combine_kernel, first),
@@ -554,7 +555,7 @@
             grid=(count,),
             in_specs=[pl.BlockSpec((experts, count, 1, BLOCK), lambda *_: (0, first // count, 0, 0))]
             + [pl.BlockSpec(memory_space=pl.ANY)] * (1 + len(after)),
-            out_specs=[row_block(columns), row_block(128)],
+            out_specs=[row_block(columns), row_block(columns), row_block(128)],
             scratch_shapes=[
                 pltpu.VMEM((DEEP, GROUP * PIECE_ROWS, whole_width), jnp.bfloat16),
                 pltpu.VMEM((BLOCK, whole_width), jnp.float32),
@@ -562,6 +563,7 @@
             ],
         ),
         out_shape=[
+            jax.ShapeDtypeStruct((count * BLOCK, columns), jnp.bfloat16),
             jax.ShapeDtypeStruct((count * BLOCK, columns), jnp.bfloat16),
             jax.ShapeDtypeStruct((count * BLOCK, 128), jnp.float32),
         ],
@@ -1317,7 +1319,10 @@
     route_onehot = (
         own_routes[:, :, None] == jnp.arange(expert_count, dtype=jnp.int32)[None, None, :]
     ).astype(jnp.float32)
-    counts = all_sum(jnp.sum(route_onehot, axis=(0, 1)))
+    hops = [jnp.sum(route_onehot, axis=(0, 1))]
+    for bit in (1, 2, 4, 8):
+        hops.append(hops[-1] + flip(hops[-1], bit))
+    counts = hops[-1] + swap(hops[-1])
     cotangent_rows = spread(order(cotangent, joined_piece))
 
     inputs_share = tokens.astype(jnp.float32)
@@ -1333,8 +1338,8 @@
         attended, lse = attend(query, key, value, limits, later)
         return attended, (query, key, value, lse)
 
-    attended_own, saved_own = half_forward(joined_own, (), (joined_piece,))
-    attended_other, saved_other = half_forward(joined_other, (counts,))
+    attended_own, saved_own = half_forward(joined_own, (), (joined_piece, hops[1]))
+    attended_other, saved_other = half_forward(joined_other, (hops[2],), (hops[3],))
     middle_share = (
         inputs_share
         + jnp.dot(attended_own, w_out, preferred_element_type=jnp.float32)
@@ -1354,7 +1359,9 @@
     place, begins, ends = placement(group_routes, first_expert, experts)
     gather_from = gather_tables(begins, ends, slots)
     blocks = gather_from[2]
-    cot_slots = gather_rows(gather_from, place, None, cotangent_rows, slots, 0, experts)[0]
+    cot_slots = gather_rows(
+        gather_from, place, None, cotangent_rows, slots, 0, experts, (hops[4],)
+    )[0]
     mixed_across = order(swap(mixed_share), cot_slots)
     mixed_rows = [mixed_share, mixed_across, flip(mixed_share, 1), flip(mixed_across, 1)]
     misc = jnp.stack([core * experts, side, (rank // 4) % 2])
@@ -1389,33 +1396,32 @@
     names = first_expert + jnp.arange(experts, dtype=jnp.int32)
 
     def combined(quarter, after):
-        yd, gate_grads = combine_rows(combine_from, place, carried, quarter * tiles, tiles, after)
+        y, dx, gate_grads = combine_rows(
+            combine_from, place, carried, quarter * tiles, tiles, after
+        )
         gate_grads = gate_grads[:, :experts] + gate_grads[:, 64 : 64 + experts]
         rows = group_routes[quarter * share_rows : (quarter + 1) * share_rows]
         hit = rows[:, :, None] == names[None, None, :]
-        return yd, jnp.sum(jnp.where(hit, gate_grads[:, None, :], 0.0), axis=2)
+        return y, dx, jnp.sum(jnp.where(hit, gate_grads[:, None, :], 0.0), axis=2)
 
     far = combined(3, waits)
-    far_yd, far_gg = (flip(value, 1) for value in far)
+    far_y, far_dx, far_gg = (flip(value, 1) for value in far)
     cross = combined(1, [far[0]])
-    dx_send = add_low(cross[0][:, model_width:], far_yd[:, model_width:])
+    dx_send = add_low(cross[1], far_dx)
     dx_across = swap(dx_send)
-    gg_across = swap(cross[1] + far_gg)
-    next_door = combined(2, [dx_send])
-    door_yd, door_gg = (flip(value, 1) for value in next_door)
-    y_send = add_low(cross[0][:, :model_width], far_yd[:, :model_width])
+    gg_across = swap(cross[2] + far_gg)
+    next_door = combined(2, [dx_send, chips[2].one(cross[1])])
+    door_y, door_dx, door_gg = (flip(value, 1) for value in next_door)
+    y_send = add_low(cross[0], far_y)
     near = combined(0, [next_door[0]])
     y_across = swap(order(y_send, near[0]))
-    waits = [chips[2].one(near[0]), chips[1].two(near[0])]
-    done = [chips[0].three(near[0])]
-    waits += done
-    near_yd = order(near[0], *waits)
+    waits = [chips[1].two(near[0])]
     mixed_grad_share = (
-        near_yd[:, model_width:].astype(jnp.float32)
-        + door_yd[:, model_width:].astype(jnp.float32)
+        order(near[1], *waits).astype(jnp.float32)
+        + door_dx.astype(jnp.float32)
         + dx_across.astype(jnp.float32)
     )
-    gates_grad_share = near[1] + door_gg + gg_across
+    gates_grad_share = near[2] + door_gg + gg_across
 
     upstream = cotangent.astype(jnp.float32)
     chosen_grad = gate_soft * (
@@ -1455,15 +1461,17 @@
 
     pairs = key_width // 128
     other_grads = jnp.concatenate(
-        half_back(saved_other, out_other)((0, pairs), waits), axis=1
-    )
-    waits = [chips[3].one(other_grads), chips[2].two(other_grads)]
-    done.append(chips[1].three(other_grads))
-    waits.append(done[1])
+        half_back(saved_other, out_other)(
+            (0, pairs), [*waits, chips[3].one(middle_low)]
+        ),
+        axis=1,
+    )
+    done = [chips[0].three(other_grads)]
+    waits = [chips[2].two(other_grads), *done]
     other_grads = order(other_grads, *waits)
     expert_share = (
-        near[0][:, :model_width].astype(jnp.float32)
-        + door_yd[:, :model_width].astype(jnp.float32)
+        near[0].astype(jnp.float32)
+        + door_y.astype(jnp.float32)
         + order(y_across, other_grads).astype(jnp.float32)
     )
     output_share = (middle_share + expert_share).astype(jnp.bfloat16)
@@ -1473,10 +1481,11 @@
     out_held = core_sum(dot_tn(marked, attended_other), core)
     out_across = swap(order(out_held, joined_held))
     out_kept = core_sum(dot_tn(marked, attended_own), core)
-    waits = [joined_held, out_held, out_kept, output_share]
+    done.append(chips[1].three(joined_held))
+    waits = [chips[4].one(joined_held), done[1], joined_held, out_held, out_kept, output_share]
     own_part = half_back(saved_own, w_out)
     front = own_part((0, pairs // 2), waits)
-    back = own_part((pairs // 2, pairs - pairs // 2), [joined_across, front[0]])
+    back = own_part((pairs // 2, pairs - pairs // 2), [joined_across, front[0], chips[3].two(front[0])])
     own_grads = jnp.concatenate(
         [part for both in zip(front, back) for part in both], axis=1
     )
@@ -1485,10 +1494,9 @@
     own_held = core_sum(own_weight_grads, core)
     joined_total = plane_sum(add_low(own_held, joined_across), rank)
     out_total = plane_sum(out_half, rank, own_weight_grads)
-    chips[4].one(own_weight_grads)
-    chips[3].two(own_grads)
-    chips[4].two(own_weight_grads)
-    sums = done + [chips[i].three(own_weight_grads) for i in (2, 3, 4)]
+    done.append(chips[2].three(own_grads))
+    chips[4].two(own_grads)
+    sums = done + [chips[i].three(own_weight_grads) for i in (3, 4)]
     other_normed = dot_nt(other_grads, joined_other)
     own_normed = dot_nt(order(own_grads, own_held), joined_own)
     input_pullback = jax.vjp(normalize, inputs_share, norm_gains)[1]

time: 1240 us -> 1200 us (0.968)
  starting transfers between devices: 116 us -> 45.8 us
  Pallas kernels: 595 us -> 636 us
  local copies, waits for them, and re-layouts: 103 us -> 87.2 us
    ppermute x51 -> x53, starting transfers between devices: 77.3 us -> 39.4 us  [flip(): return lax.ppermute(value, 'dp', [(i, i ^ bit) for i in range(size)])]
    ppermute x12, starting transfers between devices: 38.7 us -> 6.44 us  [swap(): return lax.ppermute(value, 'tensor', [(0, 1), (1, 0)])]
    pallas_call x5, Pallas kernels: 210 us -> 235 us  [expert_call(): pl.pallas_call(functools.partial(expert_kernel, first, split, depth, far_...]
    ppermute x51 -> x53, waiting for transfers between devices: 181 us -> 188 us  [flip(): return lax.ppermute(value, 'dp', [(i, i ^ bit) for i in range(size)])]
    unnamed x229 -> x257, local copies, waits for them, and re-layouts: 30.5 us -> 27.3 us
    convert_element_type x20 -> x21, other arithmetic: 74.4 us -> 76.8 us  [add_low(): (left.astype(jnp.float32) + right.astype(jnp.float32)).astype(jnp.bfloat16)]
  transfers between devices with their start and end apart: 63 -> 65, of which waited for: 17 -> 20; matrix products, arithmetic and copies ran while one was open for 23% -> 23% of each run, Pallas kernels for 40% -> 47%
where the time goes in v5:
time: 1200 us
  Pallas kernels  636 us (53%)
  waiting for transfers between devices  197 us (16%)
  other arithmetic  154 us (13%)
  local copies, waits for them, and re-layouts  87.2 us (7%)
  matrix products  74.2 us (6%)
  starting transfers between devices  45.8 us (4%)
    pallas_call x5, Pallas kernels, expert_call(): pl.pallas_call(functools.partial(expert_kernel, first, split, depth, far_...  235 us
    ppermute x53, waiting for transfers between devices, flip(): return lax.ppermute(value, 'dp', [(i, i ^ bit) for i in range(size)])  188 us
    pallas_call x3, Pallas kernels, gather_rows(): pl.pallas_call(functools.partial(gather_kernel, len(sources), with_gates,...  175 us
    pallas_call x3, Pallas kernels, attend_back(): pl.pallas_call(functools.partial(back_kernel, wide // HD, score_scale, le...  82.3 us
    pallas_call x4, Pallas kernels, combine_rows(): pl.pallas_call(functools.partial(combine_kernel, first), grid_spec=pltpu....  77.8 us
    convert_element_type x21, other arithmetic, add_low(): (left.astype(jnp.float32) + right.astype(jnp.float32)).astype(jnp.bfloat16)  76.8 us
    pallas_call x2, Pallas kernels, attend(): pl.pallas_call(functools.partial(attend_kernel, wide // HD), grid=(pairs,...  48.9 us
    ppermute x53, starting transfers between devices, flip(): return lax.ppermute(value, 'dp', [(i, i ^ bit) for i in range(size)])  39.4 us
  transfers between devices with their start and end apart: 65, of which 20 were waited for; matrix products, arithmetic and copies ran while one was open for 23% of the time, Pallas kernels for 47%

profile of v5, /device:TPU:0, one launch (start us, length us, event | category | flops | bytes accessed | tf_op | source)
XLA Modules:
  0.0 1200.8 jit_solution(12393640853836782811)
XLA Ops:
  49.9 24.4 %shard_map.238 = (bf16[1024,768]{1,0:T(8,128)(2,1)}, f32[2,1024,128]{2,1,0:T(8,128)}) custom-call(bf16[1024,768]{1,0:T(8,128)(2,1)} %get-tuple-element.90.query_ref, bf16[1024,256]{1,0:T(8,128)(2,1)} %get-tuple-element.91.key_ref, bf16[1024,256]{1,0:T(8,128)(2,1)} %get-tuple-element.92.value_ref, s32[1024,1]{1,0:T(8,128)} %select_select_fusion.limit_ref, ...), custom_call_target="tpu_custom_call" | custom-call | tf_op jit(solution)/shard_map/pallas_call | solution.py:767
  101.7 24.6 %shard_map.240 = (bf16[1024,768]{1,0:T(8,128)(2,1)}, f32[2,1024,128]{2,1,0:T(8,128)}) custom-call(bf16[1024,768]{1,0:T(8,128)(2,1)} %get-tuple-element.94.query_ref, bf16[1024,256]{1,0:T(8,128)(2,1)} %get-tuple-element.95.key_ref, bf16[1024,256]{1,0:T(8,128)(2,1)} %get-tuple-element.96.value_ref, s32[1024,1]{1,0:T(8,128)} %select_select_fusion.limit_ref, ...), custom_call_target="tpu_custom_call" | custom-call | tf_op jit(solution)/shard_map/pallas_call | solution.py:767
  149.8 82.1 %shard_map.241.rest_5_.c_ref = bf16[12800,1536]{1,0:T(8,128)(2,1)} custom-call(s32[10,10]{1,0:T(8,128)} %copy-done.69, s32[10,10]{1,0:T(8,128)} %compare_select_fusion.3.high_ref, s32[10]{0:T(128)} %negate_maximum_fusion.blocks_ref, s32[10,16,1,256]{3,2,1,0:T(1,128)} %add_select_fusion.place_ref, bf16[1024,1536]{1,0:T(8,128)(2,1)} %rest_0_, ...), custom_call_target="tpu_custom_call" | custom-call | tf_op jit(solution)/shard_map/pallas_call | solution.py:270
  248.6 22.6 %shard_map.242 = (bf16[2560,1536]{1,0:T(8,128)(2,1)}, f32[2560,128]{1,0:T(8,128)}) custom-call(s32[2,10]{1,0:T(2,128)} %slice.173.low_ref, s32[2,10]{1,0:T(2,128)} %slice.174.high_ref, s32[2]{0:T(128)} %bitcast.319, s32[2,16,1,256]{3,2,1,0:T(1,128)} %copy.133.place_ref, bf16[4096,128]{1,0:T(8,128)(2,1)} %pad_bitcast_fusion.rest_0_, ...), custom_call_target="tpu_custom_call" | custom-call | tf_op jit(solution)/shard_map/pallas_call | solution.py:270
  271.2 47.2 %shard_map.243 = (bf16[12800,3200]{1,0:T(8,128)(2,1)}, bf16[2,2,6,192,512]{4,3,2,1,0:T(8,128)(2,1)}, bf16[2,2,6,192,512]{4,3,2,1,0:T(8,128)(2,1)}) custom-call(s32[10]{0:T(128)} %negate_maximum_fusion.blocks_ref, s32[3]{0:T(128)} %pad_add_fusion.1.misc_ref, bf16[2560,1536]{1,0:T(8,128)(2,1)} %get-tuple-element.101.x_ref, ...), custom_call_target="tpu_custom_call" | custom-call | tf_op jit(solution)/shard_map/pallas_call | solution.py:444
  321.0 70.6 %shard_map.244 = (bf16[10240,1536]{1,0:T(8,128)(2,1)}, f32[10240,128]{1,0:T(8,128)}) custom-call(s32[8,10]{1,0:T(8,128)} %slice.170.low_ref, s32[8,10]{1,0:T(8,128)} %slice.171.high_ref, s32[8]{0:T(128)} %slice.134.blocks_ref, s32[8,16,1,256]{3,2,1,0:T(1,128)} %copy.134.place_ref, bf16[4096,128]{1,0:T(8,128)(2,1)} %pad_bitcast_fusion.rest_0_, ...), custom_call_target="tpu_custom_call" | custom-call | tf_op jit(solution)/shard_map/pallas_call | solution.py:270
  391.6 50.9 %shard_map.245 = (bf16[12800,3200]{1,0:T(8,128)(2,1)}, bf16[2,2,6,192,512]{4,3,2,1,0:T(8,128)(2,1)}, bf16[2,2,6,192,512]{4,3,2,1,0:T(8,128)(2,1)}) custom-call(s32[10]{0:T(128)} %negate_maximum_fusion.blocks_ref, s32[3]{0:T(128)} %pad_add_fusion.1.misc_ref, bf16[10240,1536]{1,0:T(8,128)(2,1)} %get-tuple-element.104.x_ref, ...), custom_call_target="tpu_custom_call", output_to_operand_aliasing={{0}: (8, {})} | custom-call | tf_op jit(solution)/shard_map/pallas_call | solution.py:444
  454.8 42.7 %shard_map.246 = (bf16[12800,3200]{1,0:T(8,128)(2,1)}, bf16[2,2,6,192,512]{4,3,2,1,0:T(8,128)(2,1)}, bf16[2,2,6,192,512]{4,3,2,1,0:T(8,128)(2,1)}) custom-call(s32[10]{0:T(128)} %negate_maximum_fusion.blocks_ref, s32[3]{0:T(128)} %pad_add_fusion.1.misc_ref, bf16[10240,1536]{1,0:T(8,128)(2,1)} %get-tuple-element.104.x_ref, ...), custom_call_target="tpu_custom_call", output_to_operand_aliasing={{0}: (8, {})} | custom-call | tf_op jit(solution)/shard_map/pallas_call | solution.py:444
  500.6 42.9 %shard_map.247 = (bf16[12800,3200]{1,0:T(8,128)(2,1)}, bf16[2,2,6,192,512]{4,3,2,1,0:T(8,128)(2,1)}, bf16[2,2,6,192,512]{4,3,2,1,0:T(8,128)(2,1)}) custom-call(s32[10]{0:T(128)} %negate_maximum_fusion.blocks_ref, s32[3]{0:T(128)} %pad_add_fusion.1.misc_ref, bf16[10240,1536]{1,0:T(8,128)(2,1)} %get-tuple-element.104.x_ref, ...), custom_call_target="tpu_custom_call", output_to_operand_aliasing={{0}: (8, {})} | custom-call | tf_op jit(solution)/shard_map/pallas_call | solution.py:444
  546.6 50.8 %shard_map.248 = (bf16[12800,3200]{1,0:T(8,128)(2,1)}, bf16[2,2,6,192,512]{4,3,2,1,0:T(8,128)(2,1)}, bf16[2,2,6,192,512]{4,3,2,1,0:T(8,128)(2,1)}) custom-call(s32[10]{0:T(128)} %negate_maximum_fusion.blocks_ref, s32[3]{0:T(128)} %pad_add_fusion.1.misc_ref, bf16[10240,1536]{1,0:T(8,128)(2,1)} %get-tuple-element.104.x_ref, ...), custom_call_target="tpu_custom_call", output_to_operand_aliasing={{0}: (8, {})} | custom-call | tf_op jit(solution)/shard_map/pallas_call | solution.py:444
  605.1 19.7 %shard_map.249 = (bf16[1024,1536]{1,0:T(8,128)(2,1)}, bf16[1024,1536]{1,0:T(8,128)(2,1)}, f32[1024,128]{1,0:T(8,128)}) custom-call(s32[16,96]{1,0:T(8,128)} %copy-done.59, s32[16,96]{1,0:T(8,128)} %get-tuple-element.268.piece_ref, s32[16,96]{1,0:T(8,128)} %get-tuple-element.267.source_ref, s32[16]{0:T(128)} %get-tuple-element.238.groups_ref, ...), custom_call_target="tpu_custom_call" | custom-call | tf_op jit(solution)/shard_map/pallas_call | solution.py:551
  630.9 19.4 %shard_map.250 = (bf16[1024,1536]{1,0:T(8,128)(2,1)}, bf16[1024,1536]{1,0:T(8,128)(2,1)}, f32[1024,128]{1,0:T(8,128)}) custom-call(s32[16,96]{1,0:T(8,128)} %copy-done.59, s32[16,96]{1,0:T(8,128)} %get-tuple-element.268.piece_ref, s32[16,96]{1,0:T(8,128)} %get-tuple-element.267.source_ref, s32[16]{0:T(128)} %get-tuple-element.238.groups_ref, ...), custom_call_target="tpu_custom_call" | custom-call | tf_op jit(solution)/shard_map/pallas_call | solution.py:551
  662.6 19.6 %shard_map.251 = (bf16[1024,1536]{1,0:T(8,128)(2,1)}, bf16[1024,1536]{1,0:T(8,128)(2,1)}, f32[1024,128]{1,0:T(8,128)}) custom-call(s32[16,96]{1,0:T(8,128)} %copy-done.59, s32[16,96]{1,0:T(8,128)} %get-tuple-element.268.piece_ref, s32[16,96]{1,0:T(8,128)} %get-tuple-element.267.source_ref, s32[16]{0:T(128)} %get-tuple-element.238.groups_ref, ...), custom_call_target="tpu_custom_call" | custom-call | tf_op jit(solution)/shard_map/pallas_call | solution.py:551
  698.2 19.1 %shard_map.252 = (bf16[1024,1536]{1,0:T(8,128)(2,1)}, bf16[1024,1536]{1,0:T(8,128)(2,1)}, f32[1024,128]{1,0:T(8,128)}) custom-call(s32[16,96]{1,0:T(8,128)} %copy-done.59, s32[16,96]{1,0:T(8,128)} %get-tuple-element.268.piece_ref, s32[16,96]{1,0:T(8,128)} %get-tuple-element.267.source_ref, s32[16]{0:T(128)} %get-tuple-element.238.groups_ref, ...), custom_call_target="tpu_custom_call" | custom-call | tf_op jit(solution)/shard_map/pallas_call | solution.py:551
  725.2 19.8 %collective-permute-done.31 = bf16[2,6,192,512]{3,2,1,0:T(8,128)(2,1)} collective-permute-done((bf16[2,6,192,512]{3,2,1,0:T(8,128)(2,1)}, bf16[2,6,192,512]{3,2,1,0:T(8,128)(2,1)}, u32[]{:S(2)}, u32[]{:S(2)}) %collective-permute-start.31) | collective-permute-done | bytes 2359328 | tf_op jit(solution)/shard_map/ppermute | solution.py:576
  769.4 29.9 %collective-permute-done.37 = bf16[2,2,6,192,512]{4,3,2,1,0:T(8,128)(2,1)} collective-permute-done((bf16[2,2,6,192,512]{4,3,2,1,0:T(8,128)(2,1)}, bf16[2,2,6,192,512]{4,3,2,1,0:T(8,128)(2,1)}, u32[]{:S(2)}, u32[]{:S(2)}) %collective-permute-start.37) | collective-permute-done | bytes 4718624 | tf_op jit(solution)/shard_map/ppermute | solution.py:576
  805.8 39.9 %shard_map.253 = (bf16[1024,768]{1,0:T(8,128)(2,1)}, bf16[1024,256]{1,0:T(8,128)(2,1)}, bf16[1024,256]{1,0:T(8,128)(2,1)}) custom-call(bf16[1024,768]{1,0:T(8,128)(2,1)} %get-tuple-element.94.query_ref, bf16[1024,256]{1,0:T(8,128)(2,1)} %get-tuple-element.95.key_ref, bf16[1024,256]{1,0:T(8,128)(2,1)} %get-tuple-element.96.value_ref, ...), custom_call_target="tpu_custom_call" | custom-call | tf_op jit(solution)/shard_map/pallas_call | solution.py:879
  913.2 21.0 %shard_map.254 = (bf16[1024,384]{1,0:T(8,128)(2,1)}, bf16[1024,128]{1,0:T(8,128)(2,1)}, bf16[1024,128]{1,0:T(8,128)(2,1)}) custom-call(bf16[1024,768]{1,0:T(8,128)(2,1)} %get-tuple-element.90.query_ref, bf16[1024,256]{1,0:T(8,128)(2,1)} %get-tuple-element.91.key_ref, bf16[1024,256]{1,0:T(8,128)(2,1)} %get-tuple-element.92.value_ref, ...), custom_call_target="tpu_custom_call" | custom-call | tf_op jit(solution)/shard_map/pallas_call | solution.py:879
  936.4 16.3 %collective-permute-done.46 = bf16[2,6,192,512]{3,2,1,0:T(8,128)(2,1)} collective-permute-done((bf16[2,6,192,512]{3,2,1,0:T(8,128)(2,1)}, bf16[2,6,192,512]{3,2,1,0:T(8,128)(2,1)}, u32[]{:S(2)}, u32[]{:S(2)}) %collective-permute-start.46) | collective-permute-done | bytes 2359328 | tf_op jit(solution)/shard_map/ppermute | solution.py:576
  955.8 21.4 %shard_map.255 = (bf16[1024,384]{1,0:T(8,128)(2,1)}, bf16[1024,128]{1,0:T(8,128)(2,1)}, bf16[1024,128]{1,0:T(8,128)(2,1)}) custom-call(bf16[1024,768]{1,0:T(8,128)(2,1)} %get-tuple-element.90.query_ref, bf16[1024,256]{1,0:T(8,128)(2,1)} %get-tuple-element.91.key_ref, bf16[1024,256]{1,0:T(8,128)(2,1)} %get-tuple-element.92.value_ref, ...), custom_call_target="tpu_custom_call" | custom-call | tf_op jit(solution)/shard_map/pallas_call | solution.py:879
  994.7 32.4 %collective-permute-done.62 = bf16[2,6,192,512]{3,2,1,0:T(8,128)(2,1)} collective-permute-done((bf16[2,6,192,512]{3,2,1,0:T(8,128)(2,1)}, bf16[2,6,192,512]{3,2,1,0:T(8,128)(2,1)}, u32[]{:S(2)}, u32[]{:S(2)}) %collective-permute-start.62) | collective-permute-done | bytes 2359328 | tf_op jit(solution)/shard_map/ppermute | solution.py:576
  1042.4 18.3 %collective-permute-done.58 = bf16[2,96,768]{2,1,0:T(8,128)(2,1)} collective-permute-done((bf16[2,96,768]{2,1,0:T(8,128)(2,1)}, bf16[2,96,768]{2,1,0:T(8,128)(2,1)}, u32[]{:S(2)}, u32[]{:S(2)}) %collective-permute-start.58) | collective-permute-done | bytes 294944 | tf_op jit(solution)/shard_map/ppermute | solution.py:576
  1067.7 20.2 %collective-permute-done.59 = bf16[96,768]{1,0:T(8,128)(2,1)S(1)} collective-permute-done((bf16[96,768]{1,0:T(8,128)(2,1)S(1)}, bf16[96,768]{1,0:T(8,128)(2,1)S(1)}, u32[]{:S(2)}, u32[]{:S(2)}) %collective-permute-start.59) | collective-permute-done | bytes 147488 | tf_op jit(solution)/shard_map/ppermute | solution.py:576
  1122.8 20.6 %collective-permute-done.49 = f32[64552]{0:T(1024)S(1)} collective-permute-done((f32[64552]{0:T(1024)S(1)}, f32[64552]{0:T(1024)S(1)}, u32[]{:S(2)}, u32[]{:S(2)}) %collective-permute-start.49) | collective-permute-done | bytes 258240 | tf_op jit(solution)/shard_map/ppermute | solution.py:576
  (579 shorter events, 418.8 us)
Async XLA Ops:
  47.9 86.8 %collective-permute-start.16 = (bf16[1024,1536]{1,0:T(8,128)(2,1)}, bf16[1024,1536]{1,0:T(8,128)(2,1)}, u32[]{:S(2)}, u32[]{:S(2)}) collective-permute-start(bf16[1024,1536]{1,0:T(8,128)(2,1)} %rest_0_), channel_id=1, source_target_pairs={{0,1},{1,0},{2,3},{3,2},{4,5},{5,4},{6,7},{7,6},{8,9},{9,8},{10,11... | collective-permute-start | bytes 9437192 | tf_op jit(solution)/shard_map/ppermute | solution.py:580
  85.1 64.6 %collective-permute-start.17 = (bf16[1024,1536]{1,0:T(8,128)(2,1)}, bf16[1024,1536]{1,0:T(8,128)(2,1)}, u32[]{:S(2)}, u32[]{:S(2)}) collective-permute-start(bf16[1024,1536]{1,0:T(8,128)(2,1)} %rest_0_), channel_id=1, source_target_pairs={{0,2},{2,0},{4,6},{6,4},{8,10},{10,8},{12,14},{14,12},{16,18},{18,... | collective-permute-start | bytes 9437192 | tf_op jit(solution)/shard_map/ppermute | solution.py:576
  137.8 94.0 %collective-permute-start.15 = (bf16[1024,1536]{1,0:T(8,128)(2,1)}, bf16[1024,1536]{1,0:T(8,128)(2,1)}, u32[]{:S(2)}, u32[]{:S(2)}) collective-permute-start(bf16[1024,1536]{1,0:T(8,128)(2,1)} %multiply_convert_fusion.rest_1_), channel_id=1, source_target_pairs={{0,1},{1,0},{2,3},{3,2},{4,5},{5,4},{6,7},{7,6},{8,9},{9,8},{10,11... | collective-permute-start | bytes 9437192 | tf_op jit(solution)/shard_map/ppermute | solution.py:580
  149.7 98.9 %collective-permute-start.20 = (bf16[1024,1536]{1,0:T(8,128)(2,1)}, bf16[1024,1536]{1,0:T(8,128)(2,1)}, u32[]{:S(2)}, u32[]{:S(2)}) collective-permute-start(bf16[1024,1536]{1,0:T(8,128)(2,1)} %multiply_convert_fusion.rest_1_), channel_id=1, source_target_pairs={{0,2},{2,0},{4,6},{6,4},{8,10},{10,8},{12,14},{14,12},{16,18},{18,... | collective-permute-start | bytes 9437192 | tf_op jit(solution)/shard_map/ppermute | solution.py:576
  318.4 124.7 %collective-permute-start.23 = (bf16[2,2,6,192,512]{4,3,2,1,0:T(8,128)(2,1)}, bf16[2,2,6,192,512]{4,3,2,1,0:T(8,128)(2,1)}, u32[]{:S(2)}, u32[]{:S(2)}) collective-permute-start(bf16[2,2,6,192,512]{4,3,2,1,0:T(8,128)(2,1)} %get-tuple-element.108), channel_id=1, source_target_pairs={{0,4},{2,6},{4,0},{6,2},{8,12},{10,14},{12,8},{14,10},{16,20},{18,... | collective-permute-start | bytes 14155784 | tf_op jit(solution)/shard_map/ppermute | solution.py:576
  442.5 154.9 %collective-permute-start.25 = (bf16[2,2,6,192,512]{4,3,2,1,0:T(8,128)(2,1)}, bf16[2,2,6,192,512]{4,3,2,1,0:T(8,128)(2,1)}, u32[]{:S(2)}, u32[]{:S(2)}) collective-permute-start(bf16[2,2,6,192,512]{4,3,2,1,0:T(8,128)(2,1)} %get-tuple-element.115), channel_id=1, source_target_pairs={{0,4},{2,6},{4,0},{6,2},{8,12},{10,14},{12,8},{14,10},{16,20},{18,... | collective-permute-start | bytes 14155784 | tf_op jit(solution)/shard_map/ppermute | solution.py:576
  450.9 92.7 %collective-permute-start.24 = (bf16[2,6,192,512]{3,2,1,0:T(8,128)(2,1)}, bf16[2,6,192,512]{3,2,1,0:T(8,128)(2,1)}, u32[]{:S(2)}, u32[]{:S(2)}) collective-permute-start(bf16[2,6,192,512]{3,2,1,0:T(8,128)(2,1)} %get-tuple-element.250.rest_1_), channel_id=1, source_target_pairs={{0,8},{2,10},{4,12},{6,14},{8,0},{10,2},{12,4},{14,6},{16,24},{18,... | collective-permute-start | bytes 7077896 | tf_op jit(solution)/shard_map/ppermute | solution.py:576
  497.5 152.8 %collective-permute-start.27 = (bf16[2,2,6,192,512]{4,3,2,1,0:T(8,128)(2,1)}, bf16[2,2,6,192,512]{4,3,2,1,0:T(8,128)(2,1)}, u32[]{:S(2)}, u32[]{:S(2)}) collective-permute-start(bf16[2,2,6,192,512]{4,3,2,1,0:T(8,128)(2,1)} %get-tuple-element.121), channel_id=1, source_target_pairs={{0,4},{2,6},{4,0},{6,2},{8,12},{10,14},{12,8},{14,10},{16,20},{18,... | collective-permute-start | bytes 14155784 | tf_op jit(solution)/shard_map/ppermute | solution.py:576
  626.0 93.5 %collective-permute-start.29 = (bf16[1024,1536]{1,0:T(8,128)(2,1)}, bf16[1024,1536]{1,0:T(8,128)(2,1)}, u32[]{:S(2)}, u32[]{:S(2)}) collective-permute-start(bf16[1024,1536]{1,0:T(8,128)(2,1)} %get-tuple-element.117.rest_0_), channel_id=1, source_target_pairs={{0,2},{2,0},{4,6},{6,4},{8,10},{10,8},{12,14},{14,12},{16,18},{18,... | collective-permute-start | bytes 9437192 | tf_op jit(solution)/shard_map/ppermute | solution.py:576
  662.5 88.4 %collective-permute-start.33 = (bf16[1024,1536]{1,0:T(8,128)(2,1)}, bf16[1024,1536]{1,0:T(8,128)(2,1)}, u32[]{:S(2)}, u32[]{:S(2)}) collective-permute-start(bf16[1024,1536]{1,0:T(8,128)(2,1)} %add_convert_fusion.2.rest_0_), channel_id=1, source_target_pairs={{0,1},{1,0},{2,3},{3,2},{4,5},{5,4},{6,7},{7,6},{8,9},{9,8},{10,11... | collective-permute-start | bytes 9437192 | tf_op jit(solution)/shard_map/ppermute | solution.py:580
  682.2 68.8 %collective-permute-start.32 = (bf16[1024,1536]{1,0:T(8,128)(2,1)}, bf16[1024,1536]{1,0:T(8,128)(2,1)}, u32[]{:S(2)}, u32[]{:S(2)}) collective-permute-start(bf16[1024,1536]{1,0:T(8,128)(2,1)} %get-tuple-element.130), channel_id=1, source_target_pairs={{0,2},{2,0},{4,6},{6,4},{8,10},{10,8},{12,14},{14,12},{16,18},{18,... | collective-permute-start | bytes 9437192 | tf_op jit(solution)/shard_map/ppermute | solution.py:576
  695.0 104.2 %collective-permute-start.37 = (bf16[2,2,6,192,512]{4,3,2,1,0:T(8,128)(2,1)}, bf16[2,2,6,192,512]{4,3,2,1,0:T(8,128)(2,1)}, u32[]{:S(2)}, u32[]{:S(2)}) collective-permute-start(bf16[2,2,6,192,512]{4,3,2,1,0:T(8,128)(2,1)} %get-tuple-element.137), channel_id=1, source_target_pairs={{0,4},{2,6},{4,0},{6,2},{8,12},{10,14},{12,8},{14,10},{16,20},{18,... | collective-permute-start | bytes 14155784 | tf_op jit(solution)/shard_map/ppermute | solution.py:576
  748.2 99.3 %collective-permute-start.39 = (bf16[6,192,512]{2,1,0:T(8,128)(2,1)}, bf16[6,192,512]{2,1,0:T(8,128)(2,1)}, u32[]{:S(2)}, u32[]{:S(2)}) collective-permute-start(bf16[6,192,512]{2,1,0:T(8,128)(2,1)} %fusion.39.rest_1_), channel_id=1, source_target_pairs={{0,16},{2,18},{4,20},{6,22},{8,24},{10,26},{12,28},{14,30},{16,0},... | collective-permute-start | bytes 3538952 | tf_op jit(solution)/shard_map/ppermute | solution.py:576
  749.0 98.7 %collective-permute-start.38 = (bf16[2,6,192,512]{3,2,1,0:T(8,128)(2,1)}, bf16[2,6,192,512]{3,2,1,0:T(8,128)(2,1)}, u32[]{:S(2)}, u32[]{:S(2)}) collective-permute-start(bf16[2,6,192,512]{3,2,1,0:T(8,128)(2,1)} %get-tuple-element.246.rest_1_), channel_id=1, source_target_pairs={{0,8},{2,10},{4,12},{6,14},{8,0},{10,2},{12,4},{14,6},{16,24},{18,... | collective-permute-start | bytes 7077896 | tf_op jit(solution)/shard_map/ppermute | solution.py:576
  751.0 119.0 %collective-permute-start.28 = (bf16[1024,1536]{1,0:T(8,128)(2,1)}, bf16[1024,1536]{1,0:T(8,128)(2,1)}, u32[]{:S(2)}, u32[]{:S(2)}) collective-permute-start(bf16[1024,1536]{1,0:T(8,128)(2,1)} %get-tuple-element.123.rest_0_), channel_id=1, source_target_pairs={{0,2},{2,0},{4,6},{6,4},{8,10},{10,8},{12,14},{14,12},{16,18},{18,... | collective-permute-start | bytes 9437192 | tf_op jit(solution)/shard_map/ppermute | solution.py:576
  751.1 104.1 %collective-permute-start.30 = (bf16[1024,1536]{1,0:T(8,128)(2,1)}, bf16[1024,1536]{1,0:T(8,128)(2,1)}, u32[]{:S(2)}, u32[]{:S(2)}) collective-permute-start(bf16[1024,1536]{1,0:T(8,128)(2,1)} %add_convert_fusion.1), channel_id=1, source_target_pairs={{0,1},{1,0},{2,3},{3,2},{4,5},{5,4},{6,7},{7,6},{8,9},{9,8},{10,11... | collective-permute-start | bytes 9437192 | tf_op jit(solution)/shard_map/ppermute | solution.py:580
  799.2 103.4 %collective-permute-start.40 = (bf16[2,2,6,192,512]{4,3,2,1,0:T(8,128)(2,1)}, bf16[2,2,6,192,512]{4,3,2,1,0:T(8,128)(2,1)}, u32[]{:S(2)}, u32[]{:S(2)}) collective-permute-start(bf16[2,2,6,192,512]{4,3,2,1,0:T(8,128)(2,1)} %get-tuple-element.148), channel_id=1, source_target_pairs={{0,4},{2,6},{4,0},{6,2},{8,12},{10,14},{12,8},{14,10},{16,20},{18,... | collective-permute-start | bytes 14155784 | tf_op jit(solution)/shard_map/ppermute | solution.py:576
  847.7 105.0 %collective-permute-start.46 = (bf16[2,6,192,512]{3,2,1,0:T(8,128)(2,1)}, bf16[2,6,192,512]{3,2,1,0:T(8,128)(2,1)}, u32[]{:S(2)}, u32[]{:S(2)}) collective-permute-start(bf16[2,6,192,512]{3,2,1,0:T(8,128)(2,1)} %get-tuple-element.244.rest_1_), channel_id=1, source_target_pairs={{0,8},{2,10},{4,12},{6,14},{8,0},{10,2},{12,4},{14,6},{16,24},{18,... | collective-permute-start | bytes 7077896 | tf_op jit(solution)/shard_map/ppermute | solution.py:576
  887.2 68.5 %collective-permute-start.45 = (bf16[8,96,1280]{2,1,0:T(8,128)(2,1)}, bf16[8,96,1280]{2,1,0:T(8,128)(2,1)}, u32[]{:S(2)}, u32[]{:S(2)}) collective-permute-start(bf16[8,96,1280]{2,1,0:T(8,128)(2,1)} %fusion.10.rest_2_), channel_id=1, source_target_pairs={{0,1},{1,0},{2,3},{3,2},{4,5},{5,4},{6,7},{7,6},{8,9},{9,8},{10,11... | collective-permute-start | bytes 5898248 | tf_op jit(solution)/shard_map/ppermute | solution.py:580
  894.1 144.6 %collective-permute-start.60 = (bf16[6,192,512]{2,1,0:T(8,128)(2,1)}, bf16[6,192,512]{2,1,0:T(8,128)(2,1)}, u32[]{:S(2)}, u32[]{:S(2)}) collective-permute-start(bf16[6,192,512]{2,1,0:T(8,128)(2,1)} %fusion.41), channel_id=1, source_target_pairs={{0,16},{2,18},{4,20},{6,22},{8,24},{10,26},{12,28},{14,30},{16,0},... | collective-permute-start | bytes 3538952 | tf_op jit(solution)/shard_map/ppermute | solution.py:576
  902.6 80.8 %collective-permute-start.56 = (bf16[8,96,768]{2,1,0:T(8,128)(2,1)}, bf16[8,96,768]{2,1,0:T(8,128)(2,1)}, u32[]{:S(2)}, u32[]{:S(2)}) collective-permute-start(bf16[8,96,768]{2,1,0:T(8,128)(2,1)} %fusion.32.rest_3_), channel_id=1, source_target_pairs={{0,1},{1,0},{2,3},{3,2},{4,5},{5,4},{6,7},{7,6},{8,9},{9,8},{10,11... | collective-permute-start | bytes 3538952 | tf_op jit(solution)/shard_map/ppermute | solution.py:580
  909.1 118.0 %collective-permute-start.62 = (bf16[2,6,192,512]{3,2,1,0:T(8,128)(2,1)}, bf16[2,6,192,512]{3,2,1,0:T(8,128)(2,1)}, u32[]{:S(2)}, u32[]{:S(2)}) collective-permute-start(bf16[2,6,192,512]{3,2,1,0:T(8,128)(2,1)} %get-tuple-element.242.rest_0_), channel_id=1, source_target_pairs={{0,8},{2,10},{4,12},{6,14},{8,0},{10,2},{12,4},{14,6},{16,24},{18,... | collective-permute-start | bytes 7077896 | tf_op jit(solution)/shard_map/ppermute | solution.py:576
  955.7 83.0 %collective-permute-start.61 = (bf16[6,192,512]{2,1,0:T(8,128)(2,1)}, bf16[6,192,512]{2,1,0:T(8,128)(2,1)}, u32[]{:S(2)}, u32[]{:S(2)}) collective-permute-start(bf16[6,192,512]{2,1,0:T(8,128)(2,1)} %fusion.44.rest_2_), channel_id=1, source_target_pairs={{0,16},{2,18},{4,20},{6,22},{8,24},{10,26},{12,28},{14,30},{16,0},... | collective-permute-start | bytes 3538952 | tf_op jit(solution)/shard_map/ppermute | solution.py:576
  994.7 94.0 %collective-permute-start.47 = (bf16[8,96,1280]{2,1,0:T(8,128)(2,1)}, bf16[8,96,1280]{2,1,0:T(8,128)(2,1)}, u32[]{:S(2)}, u32[]{:S(2)}) collective-permute-start(bf16[8,96,1280]{2,1,0:T(8,128)(2,1)} %fusion.34), channel_id=1, source_target_pairs={{0,2},{2,0},{4,6},{6,4},{8,10},{10,8},{12,14},{14,12},{16,18},{18,... | collective-permute-start | bytes 5898248 | tf_op jit(solution)/shard_map/ppermute | solution.py:576
  (164 other events, 2965.6 us)

commit v6 on v5

--- a/solution.py
+++ b/solution.py
@@ -629,16 +629,17 @@
     return add_low(pick_index(value, core, 1), got)
 
 
-def plane_sum(total, rank, *after):
+def plane_sum(total, rank, marks=((), (), ())):
     side, low_bit, high_bit = (rank // 2) % 2, (rank // 4) % 2, rank // 8
     part, columns = total.shape[1:]
     total = total.reshape(4, 2, part, columns)
-    got = order(flip(pick_index(total, 1 - side, 1), 2), *after)
-    total = add_low(pick_index(total, side, 1), got).reshape(2, 2, part, columns)
-    got = flip(pick_index(total, 1 - low_bit, 1), 4)
-    total = add_low(pick_index(total, low_bit, 1), got)
-    got = flip(pick_index(total, 1 - high_bit, 0), 8)
-    return pick_index(total, high_bit, 0).astype(jnp.float32) + got.astype(jnp.float32)
+    got = order(flip(pick_index(total, 1 - side, 1), 2), *marks[0])
+    first = add_low(pick_index(total, side, 1), got).reshape(2, 2, part, columns)
+    got = order(flip(pick_index(first, 1 - low_bit, 1), 4), *marks[1])
+    second = add_low(pick_index(first, low_bit, 1), got)
+    got = order(flip(pick_index(second, 1 - high_bit, 0), 8), *marks[2])
+    last = pick_index(second, high_bit, 0).astype(jnp.float32) + got.astype(jnp.float32)
+    return last, first, second
 
 
 def fetch_other(weights, core, side, after=()):
@@ -1338,8 +1339,8 @@
         attended, lse = attend(query, key, value, limits, later)
         return attended, (query, key, value, lse)
 
-    attended_own, saved_own = half_forward(joined_own, (), (joined_piece, hops[1]))
-    attended_other, saved_other = half_forward(joined_other, (hops[2],), (hops[3],))
+    attended_own, saved_own = half_forward(joined_own, (), (joined_piece,))
+    attended_other, saved_other = half_forward(joined_other, (hops[1],), (hops[2],))
     middle_share = (
         inputs_share
         + jnp.dot(attended_own, w_out, preferred_element_type=jnp.float32)
@@ -1360,14 +1361,14 @@
     gather_from = gather_tables(begins, ends, slots)
     blocks = gather_from[2]
     cot_slots = gather_rows(
-        gather_from, place, None, cotangent_rows, slots, 0, experts, (hops[4],)
+        gather_from, place, None, cotangent_rows, slots, 0, experts, (hops[3],)
     )[0]
     mixed_across = order(swap(mixed_share), cot_slots)
     mixed_rows = [mixed_share, mixed_across, flip(mixed_share, 1), flip(mixed_across, 1)]
     misc = jnp.stack([core * experts, side, (rank // 4) % 2])
     weights = (w_gate, w_up, w_down)
     first_part = gather_rows(
-        gather_from, place, gates, mixed_rows, slots, 0, CHUNK, (cot_slots, counts)
+        gather_from, place, gates, mixed_rows, slots, 0, CHUNK, (cot_slots, hops[4])
     )
     later_part = None
     carried = None
@@ -1375,21 +1376,24 @@
     for index in range(experts // CHUNK):
         if index == 1:
             later_part = gather_rows(
-                gather_from, place, gates, mixed_rows, slots, CHUNK, experts - CHUNK, (carried,)
+                gather_from, place, gates, mixed_rows, slots, CHUNK, experts - CHUNK, (carried, counts)
             )
         (x_slots, slot_gates), x_first = (later_part, CHUNK) if index else (first_part, 0)
         waits = []
         if index == 2:
             waits = [chips[0].one(carried)]
+        elif index == 3:
+            waits = [chips[0].two(carried)]
         elif index == 4:
-            waits = [chips[0].two(carried)]
+            waits = [chips[1].one(carried)]
         far_first = int(index == FAR_FIRST)
         carried, send, keep = expert_call(
             blocks, misc, x_slots, cot_slots, slot_gates, weights, carried, slots,
             index * CHUNK, CHUNK, x_first, 0, depth, far_first, waits,
         )
         chips.append(ChipSum((send, keep), rank, far_first))
-    waits = [chips[1].one(carried)]
+    done = [chips[0].three(carried)]
+    waits = [chips[1].two(carried), done[0]]
 
     combine_from = combine_tables(begins, ends, slots)
     tiles = place.shape[1] // 4
@@ -1415,9 +1419,8 @@
     y_send = add_low(cross[0], far_y)
     near = combined(0, [next_door[0]])
     y_across = swap(order(y_send, near[0]))
-    waits = [chips[1].two(near[0])]
     mixed_grad_share = (
-        order(near[1], *waits).astype(jnp.float32)
+        near[1].astype(jnp.float32)
         + door_dx.astype(jnp.float32)
         + dx_across.astype(jnp.float32)
     )
@@ -1459,15 +1462,22 @@
 
         return part
 
+    early = [
+        jnp.concatenate(
+            [jnp.sum(probabilities, axis=0), mix_gain_grad, router_grad.reshape(-1)]
+        )
+    ]
+    early.append(early[-1] + order(flip(early[-1], 1), middle_low))
+    middle_sum = chips[3].one(middle_low)
+    chips[4].parts = (order(chips[4].parts[0], middle_sum), chips[4].parts[1])
     pairs = key_width // 128
     other_grads = jnp.concatenate(
         half_back(saved_other, out_other)(
-            (0, pairs), [*waits, chips[3].one(middle_low)]
+            (0, pairs), [early[1], middle_sum]
         ),
         axis=1,
     )
-    done = [chips[0].three(other_grads)]
-    waits = [chips[2].two(other_grads), *done]
+    waits = [chips[2].two(other_grads)]
     other_grads = order(other_grads, *waits)
     expert_share = (
         near[0].astype(jnp.float32)
@@ -1482,36 +1492,38 @@
     out_across = swap(order(out_held, joined_held))
     out_kept = core_sum(dot_tn(marked, attended_own), core)
     done.append(chips[1].three(joined_held))
-    waits = [chips[4].one(joined_held), done[1], joined_held, out_held, out_kept, output_share]
+    early.append(early[-1] + order(flip(early[-1], 2), joined_held))
+    waits = [early[2], chips[4].one(joined_held), done[1], joined_held, out_held, out_kept, output_share]
     own_part = half_back(saved_own, w_out)
     front = own_part((0, pairs // 2), waits)
     back = own_part((pairs // 2, pairs - pairs // 2), [joined_across, front[0], chips[3].two(front[0])])
+    early.append(early[-1] + order(flip(early[-1], 4), back[0]))
+    early.append(early[-1] + flip(early[-1], 8))
     own_grads = jnp.concatenate(
         [part for both in zip(front, back) for part in both], axis=1
     )
     out_half = add_low(out_kept, order(out_across, own_grads))
     own_weight_grads = dot_tn(normed, own_grads)
     own_held = core_sum(own_weight_grads, core)
-    joined_total = plane_sum(add_low(own_held, joined_across), rank)
-    out_total = plane_sum(out_half, rank, own_weight_grads)
-    done.append(chips[2].three(own_grads))
-    chips[4].two(own_grads)
-    sums = done + [chips[i].three(own_weight_grads) for i in (3, 4)]
+    joined_half = add_low(own_held, joined_across)
+    joined_total, joined_first, joined_second = plane_sum(joined_half, rank)
+    out_total, _, _ = plane_sum(
+        out_half, rank, ((joined_half,), (joined_first,), (joined_second,))
+    )
+    done.append(chips[2].three(joined_half))
+    chips[4].two(joined_half)
+    sums = done + [chips[i].three(joined_first) for i in (3, 4)]
     other_normed = dot_nt(other_grads, joined_other)
     own_normed = dot_nt(order(own_grads, own_held), joined_own)
     input_pullback = jax.vjp(normalize, inputs_share, norm_gains)[1]
     input_from_norm, norm_gain_grad = input_pullback(other_normed + own_normed)
     input_grad_share = middle_grad + input_from_norm
     key_end = query_width + key_width
-    small = all_sum(
-        jnp.concatenate(
-            [jnp.sum(probabilities, axis=0), mix_gain_grad, norm_gain_grad, router_grad.reshape(-1)]
-        )
-    )
+    small = early[-1] + swap(early[-1])
     prob_sums = small[:expert_count]
     mix_gain_total = small[expert_count : expert_count + model_width]
-    norm_gain_total = small[expert_count + model_width : expert_count + 2 * model_width]
-    router_total = small[expert_count + 2 * model_width :].reshape(router_grad.shape)
+    router_total = small[expert_count + model_width :].reshape(router_grad.shape)
+    norm_gain_total = all_sum(norm_gain_grad)
     balance = expert_count * expert_count * fractions * prob_sums / total_tokens
 
     mine = jnp.concatenate(sums, axis=0).reshape(experts, 3, 2, depth // 2, -1)

time: 1200 us -> 1300 us (1.083)
  waiting for transfers between devices: 197 us -> 271 us
  Pallas kernels: 636 us -> 612 us
  starting transfers between devices: 45.8 us -> 69.4 us
  other arithmetic: 154 us -> 173 us
    ppermute x53 -> x57, waiting for transfers between devices: 188 us -> 239 us  [flip(): return lax.ppermute(value, 'dp', [(i, i ^ bit) for i in range(size)])]
    ppermute x12 -> x13, waiting for transfers between devices: 9.01 us -> 32 us  [swap(): return lax.ppermute(value, 'tensor', [(0, 1), (1, 0)])]
    ppermute x12 -> x13, starting transfers between devices: 6.44 us -> 24.6 us  [swap(): return lax.ppermute(value, 'tensor', [(0, 1), (1, 0)])]
    pallas_call x5, Pallas kernels: 235 us -> 218 us  [expert_call(): pl.pallas_call(functools.partial(expert_kernel, first, split, depth, far_...]
    ppermute x53 -> x57, starting transfers between devices: 39.4 us -> 44.8 us  [flip(): return lax.ppermute(value, 'dp', [(i, i ^ bit) for i in range(size)])]
    unnamed x257 -> x227, local copies, waits for them, and re-layouts: 27.3 us -> 31.1 us
  transfers between devices with their start and end apart: 65 -> 70, of which waited for: 20 -> 21; matrix products, arithmetic and copies ran while one was open for 23% -> 22% of each run, Pallas kernels for 47% -> 41%
where the time goes in v6:
time: 1300 us; the launch traced here: 1290 us
  Pallas kernels  612 us (47%)
  waiting for transfers between devices  271 us (21%)
  other arithmetic  173 us (13%)
  local copies, waits for them, and re-layouts  91.8 us (7%)
  starting transfers between devices  69.4 us (5%)
  matrix products  66 us (5%)
    ppermute x57, waiting for transfers between devices, flip(): return lax.ppermute(value, 'dp', [(i, i ^ bit) for i in range(size)])  239 us
    pallas_call x5, Pallas kernels, expert_call(): pl.pallas_call(functools.partial(expert_kernel, first, split, depth, far_...  218 us
    pallas_call x3, Pallas kernels, gather_rows(): pl.pallas_call(functools.partial(gather_kernel, len(sources), with_gates,...  170 us
    pallas_call x3, Pallas kernels, attend_back(): pl.pallas_call(functools.partial(back_kernel, wide // HD, score_scale, le...  82.6 us
    pallas_call x4, Pallas kernels, combine_rows(): pl.pallas_call(functools.partial(combine_kernel, first), grid_spec=pltpu....  75.4 us
    convert_element_type x21, other arithmetic, add_low(): (left.astype(jnp.float32) + right.astype(jnp.float32)).astype(jnp.bfloat16)  75.2 us
    pallas_call x2, Pallas kernels, attend(): pl.pallas_call(functools.partial(attend_kernel, wide // HD), grid=(pairs,...  48.7 us
    ppermute x57, starting transfers between devices, flip(): return lax.ppermute(value, 'dp', [(i, i ^ bit) for i in range(size)])  44.8 us
  transfers between devices with their start and end apart: 70, of which 21 were waited for; matrix products, arithmetic and copies ran while one was open for 22% of the time, Pallas kernels for 41%

profile of v6, /device:TPU:0, one launch (start us, length us, event | category | flops | bytes accessed | tf_op | source)
XLA Modules:
  0.0 1287.9 jit_solution(8218676762154583992)
XLA Ops:
  49.9 24.3 %shard_map.238 = (bf16[1024,768]{1,0:T(8,128)(2,1)}, f32[2,1024,128]{2,1,0:T(8,128)}) custom-call(bf16[1024,768]{1,0:T(8,128)(2,1)} %get-tuple-element.95.query_ref, bf16[1024,256]{1,0:T(8,128)(2,1)} %get-tuple-element.96.key_ref, bf16[1024,256]{1,0:T(8,128)(2,1)} %get-tuple-element.97.value_ref, s32[1024,1]{1,0:T(8,128)} %select_select_fusion.limit_ref, ...), custom_call_target="tpu_custom_call" | custom-call | tf_op jit(solution)/shard_map/pallas_call | solution.py:768
  102.2 24.3 %shard_map.240 = (bf16[1024,768]{1,0:T(8,128)(2,1)}, f32[2,1024,128]{2,1,0:T(8,128)}) custom-call(bf16[1024,768]{1,0:T(8,128)(2,1)} %get-tuple-element.99.query_ref, bf16[1024,256]{1,0:T(8,128)(2,1)} %get-tuple-element.100.key_ref, bf16[1024,256]{1,0:T(8,128)(2,1)} %get-tuple-element.101.value_ref, s32[1024,1]{1,0:T(8,128)} %select_select_fusion.limit_ref, ...), custom_call_target="tpu_custom_call" | custom-call | tf_op jit(solution)/shard_map/pallas_call | solution.py:768
  149.1 79.4 %shard_map.241.rest_5_.c_ref = bf16[12800,1536]{1,0:T(8,128)(2,1)} custom-call(s32[10,10]{1,0:T(8,128)} %copy-done.63, s32[10,10]{1,0:T(8,128)} %compare_select_fusion.3.high_ref, s32[10]{0:T(128)} %negate_maximum_fusion.blocks_ref, s32[10,16,1,256]{3,2,1,0:T(1,128)} %add_select_fusion.place_ref, bf16[1024,1536]{1,0:T(8,128)(2,1)} %rest_0_, ...), custom_call_target="tpu_custom_call" | custom-call | tf_op jit(solution)/shard_map/pallas_call | solution.py:270
  248.7 22.8 %shard_map.242 = (bf16[2560,1536]{1,0:T(8,128)(2,1)}, f32[2560,128]{1,0:T(8,128)}) custom-call(s32[2,10]{1,0:T(2,128)} %slice.169.low_ref, s32[2,10]{1,0:T(2,128)} %slice.170.high_ref, s32[2]{0:T(128)} %bitcast.314, s32[2,16,1,256]{3,2,1,0:T(1,128)} %copy.133.place_ref, bf16[4096,128]{1,0:T(8,128)(2,1)} %pad_bitcast_fusion.rest_0_, ...), custom_call_target="tpu_custom_call" | custom-call | tf_op jit(solution)/shard_map/pallas_call | solution.py:270
  271.6 42.4 %shard_map.243 = (bf16[12800,3200]{1,0:T(8,128)(2,1)}, bf16[2,2,6,192,512]{4,3,2,1,0:T(8,128)(2,1)}, bf16[2,2,6,192,512]{4,3,2,1,0:T(8,128)(2,1)}) custom-call(s32[10]{0:T(128)} %negate_maximum_fusion.blocks_ref, s32[3]{0:T(128)} %pad_add_fusion.1.misc_ref, bf16[2560,1536]{1,0:T(8,128)(2,1)} %get-tuple-element.106.x_ref, ...), custom_call_target="tpu_custom_call" | custom-call | tf_op jit(solution)/shard_map/pallas_call | solution.py:444
  320.8 67.6 %shard_map.244 = (bf16[10240,1536]{1,0:T(8,128)(2,1)}, f32[10240,128]{1,0:T(8,128)}) custom-call(s32[8,10]{1,0:T(8,128)} %slice.166.low_ref, s32[8,10]{1,0:T(8,128)} %slice.167.high_ref, s32[8]{0:T(128)} %slice.131.blocks_ref, s32[8,16,1,256]{3,2,1,0:T(1,128)} %copy.134.place_ref, bf16[4096,128]{1,0:T(8,128)(2,1)} %pad_bitcast_fusion.rest_0_, ...), custom_call_target="tpu_custom_call" | custom-call | tf_op jit(solution)/shard_map/pallas_call | solution.py:270
  388.4 46.9 %shard_map.245 = (bf16[12800,3200]{1,0:T(8,128)(2,1)}, bf16[2,2,6,192,512]{4,3,2,1,0:T(8,128)(2,1)}, bf16[2,2,6,192,512]{4,3,2,1,0:T(8,128)(2,1)}) custom-call(s32[10]{0:T(128)} %negate_maximum_fusion.blocks_ref, s32[3]{0:T(128)} %pad_add_fusion.1.misc_ref, bf16[10240,1536]{1,0:T(8,128)(2,1)} %get-tuple-element.109.x_ref, ...), custom_call_target="tpu_custom_call", output_to_operand_aliasing={{0}: (8, {})} | custom-call | tf_op jit(solution)/shard_map/pallas_call | solution.py:444
  446.7 42.9 %shard_map.246 = (bf16[12800,3200]{1,0:T(8,128)(2,1)}, bf16[2,2,6,192,512]{4,3,2,1,0:T(8,128)(2,1)}, bf16[2,2,6,192,512]{4,3,2,1,0:T(8,128)(2,1)}) custom-call(s32[10]{0:T(128)} %negate_maximum_fusion.blocks_ref, s32[3]{0:T(128)} %pad_add_fusion.1.misc_ref, bf16[10240,1536]{1,0:T(8,128)(2,1)} %get-tuple-element.109.x_ref, ...), custom_call_target="tpu_custom_call", output_to_operand_aliasing={{0}: (8, {})} | custom-call | tf_op jit(solution)/shard_map/pallas_call | solution.py:444
  499.7 42.8 %shard_map.247 = (bf16[12800,3200]{1,0:T(8,128)(2,1)}, bf16[2,2,6,192,512]{4,3,2,1,0:T(8,128)(2,1)}, bf16[2,2,6,192,512]{4,3,2,1,0:T(8,128)(2,1)}) custom-call(s32[10]{0:T(128)} %negate_maximum_fusion.blocks_ref, s32[3]{0:T(128)} %pad_add_fusion.1.misc_ref, bf16[10240,1536]{1,0:T(8,128)(2,1)} %get-tuple-element.109.x_ref, ...), custom_call_target="tpu_custom_call", output_to_operand_aliasing={{0}: (8, {})} | custom-call | tf_op jit(solution)/shard_map/pallas_call | solution.py:444
  563.2 42.8 %shard_map.248 = (bf16[12800,3200]{1,0:T(8,128)(2,1)}, bf16[2,2,6,192,512]{4,3,2,1,0:T(8,128)(2,1)}, bf16[2,2,6,192,512]{4,3,2,1,0:T(8,128)(2,1)}) custom-call(s32[10]{0:T(128)} %negate_maximum_fusion.blocks_ref, s32[3]{0:T(128)} %pad_add_fusion.1.misc_ref, bf16[10240,1536]{1,0:T(8,128)(2,1)} %get-tuple-element.109.x_ref, ...), custom_call_target="tpu_custom_call", output_to_operand_aliasing={{0}: (8, {})} | custom-call | tf_op jit(solution)/shard_map/pallas_call | solution.py:444
  606.0 17.1 %collective-permute-done.27 = bf16[6,192,512]{2,1,0:T(8,128)(2,1)} collective-permute-done((bf16[6,192,512]{2,1,0:T(8,128)(2,1)S(1)}, bf16[6,192,512]{2,1,0:T(8,128)(2,1)}, u32[]{:S(2)}, u32[]{:S(2)}) %collective-permute-start.27) | collective-permute-done | bytes 1179680 | tf_op jit(solution)/shard_map/ppermute | solution.py:576
  629.8 19.1 %shard_map.249 = (bf16[1024,1536]{1,0:T(8,128)(2,1)}, bf16[1024,1536]{1,0:T(8,128)(2,1)}, f32[1024,128]{1,0:T(8,128)}) custom-call(s32[16,96]{1,0:T(8,128)} %copy-done.55, s32[16,96]{1,0:T(8,128)} %get-tuple-element.277.piece_ref, s32[16,96]{1,0:T(8,128)} %get-tuple-element.276.source_ref, s32[16]{0:T(128)} %get-tuple-element.249.groups_ref, ...), custom_call_target="tpu_custom_call" | custom-call | tf_op jit(solution)/shard_map/pallas_call | solution.py:551
  660.5 19.5 %shard_map.250 = (bf16[1024,1536]{1,0:T(8,128)(2,1)}, bf16[1024,1536]{1,0:T(8,128)(2,1)}, f32[1024,128]{1,0:T(8,128)}) custom-call(s32[16,96]{1,0:T(8,128)} %copy-done.55, s32[16,96]{1,0:T(8,128)} %get-tuple-element.277.piece_ref, s32[16,96]{1,0:T(8,128)} %get-tuple-element.276.source_ref, s32[16]{0:T(128)} %get-tuple-element.249.groups_ref, ...), custom_call_target="tpu_custom_call" | custom-call | tf_op jit(solution)/shard_map/pallas_call | solution.py:551
  697.2 18.7 %shard_map.251 = (bf16[1024,1536]{1,0:T(8,128)(2,1)}, bf16[1024,1536]{1,0:T(8,128)(2,1)}, f32[1024,128]{1,0:T(8,128)}) custom-call(s32[16,96]{1,0:T(8,128)} %copy-done.55, s32[16,96]{1,0:T(8,128)} %get-tuple-element.277.piece_ref, s32[16,96]{1,0:T(8,128)} %get-tuple-element.276.source_ref, s32[16]{0:T(128)} %get-tuple-element.249.groups_ref, ...), custom_call_target="tpu_custom_call" | custom-call | tf_op jit(solution)/shard_map/pallas_call | solution.py:551
  720.7 18.2 %shard_map.252 = (bf16[1024,1536]{1,0:T(8,128)(2,1)}, bf16[1024,1536]{1,0:T(8,128)(2,1)}, f32[1024,128]{1,0:T(8,128)}) custom-call(s32[16,96]{1,0:T(8,128)} %copy-done.55, s32[16,96]{1,0:T(8,128)} %get-tuple-element.277.piece_ref, s32[16,96]{1,0:T(8,128)} %get-tuple-element.276.source_ref, s32[16]{0:T(128)} %get-tuple-element.249.groups_ref, ...), custom_call_target="tpu_custom_call" | custom-call | tf_op jit(solution)/shard_map/pallas_call | solution.py:551
  800.7 50.5 %collective-permute-done.39 = bf16[2,2,6,192,512]{4,3,2,1,0:T(8,128)(2,1)} collective-permute-done((bf16[2,2,6,192,512]{4,3,2,1,0:T(8,128)(2,1)}, bf16[2,2,6,192,512]{4,3,2,1,0:T(8,128)(2,1)}, u32[]{:S(2)}, u32[]{:S(2)}) %collective-permute-start.39) | collective-permute-done | bytes 4718624 | tf_op jit(solution)/shard_map/ppermute | solution.py:576
  858.3 39.8 %shard_map.253 = (bf16[1024,768]{1,0:T(8,128)(2,1)}, bf16[1024,256]{1,0:T(8,128)(2,1)}, bf16[1024,256]{1,0:T(8,128)(2,1)}) custom-call(bf16[1024,768]{1,0:T(8,128)(2,1)} %get-tuple-element.99.query_ref, bf16[1024,256]{1,0:T(8,128)(2,1)} %get-tuple-element.100.key_ref, bf16[1024,256]{1,0:T(8,128)(2,1)} %get-tuple-element.101.value_ref, ...), custom_call_target="tpu_custom_call" | custom-call | tf_op jit(solution)/shard_map/pallas_call | solution.py:880
  944.8 22.4 %collective-permute-done.41 = f32[63016]{0:T(1024)S(1)} collective-permute-done((f32[63016]{0:T(1024)S(1)}, f32[63016]{0:T(1024)S(1)}, u32[]{:S(2)}, u32[]{:S(2)}) %collective-permute-start.41) | collective-permute-done | bytes 252096 | tf_op jit(solution)/shard_map/ppermute | solution.py:576
  977.8 21.2 %shard_map.254 = (bf16[1024,384]{1,0:T(8,128)(2,1)}, bf16[1024,128]{1,0:T(8,128)(2,1)}, bf16[1024,128]{1,0:T(8,128)(2,1)}) custom-call(bf16[1024,768]{1,0:T(8,128)(2,1)} %get-tuple-element.95.query_ref, bf16[1024,256]{1,0:T(8,128)(2,1)} %get-tuple-element.96.key_ref, bf16[1024,256]{1,0:T(8,128)(2,1)} %get-tuple-element.97.value_ref, ...), custom_call_target="tpu_custom_call" | custom-call | tf_op jit(solution)/shard_map/pallas_call | solution.py:880
  1004.2 21.6 %shard_map.255 = (bf16[1024,384]{1,0:T(8,128)(2,1)}, bf16[1024,128]{1,0:T(8,128)(2,1)}, bf16[1024,128]{1,0:T(8,128)(2,1)}) custom-call(bf16[1024,768]{1,0:T(8,128)(2,1)} %get-tuple-element.95.query_ref, bf16[1024,256]{1,0:T(8,128)(2,1)} %get-tuple-element.96.key_ref, bf16[1024,256]{1,0:T(8,128)(2,1)} %get-tuple-element.97.value_ref, ...), custom_call_target="tpu_custom_call" | custom-call | tf_op jit(solution)/shard_map/pallas_call | solution.py:880
  1060.2 12.3 collective-permute-done.61
  1072.9 46.7 %collective-permute-done.50 = f32[63016]{0:T(1024)} collective-permute-done((f32[63016]{0:T(1024)}, f32[63016]{0:T(1024)}, u32[]{:S(2)}, u32[]{:S(2)}) %collective-permute-start.50) | collective-permute-done | bytes 252096 | tf_op jit(solution)/shard_map/ppermute | solution.py:576
  1157.7 20.5 %collective-permute-done.54 = f32[1536]{0:T(1024)S(1)} collective-permute-done((f32[1536]{0:T(1024)S(1)}, f32[1536]{0:T(1024)S(1)}, u32[]{:S(2)}, u32[]{:S(2)}) %collective-permute-start.54) | collective-permute-done | bytes 6176 | tf_op jit(solution)/shard_map/ppermute | solution.py:576
  1196.3 41.0 %collective-permute-done.68 = bf16[6,192,512]{2,1,0:T(8,128)(2,1)S(1)} collective-permute-done((bf16[6,192,512]{2,1,0:T(8,128)(2,1)S(1)}, bf16[6,192,512]{2,1,0:T(8,128)(2,1)S(1)}, u32[]{:S(2)}, u32[]{:S(2)}) %collective-permute-start.68) | collective-permute-done | bytes 1179680 | tf_op jit(solution)/shard_map/ppermute | solution.py:576
  (563 shorter events, 478.2 us)
Async XLA Ops:
  47.9 87.0 %collective-permute-start.15 = (bf16[1024,1536]{1,0:T(8,128)(2,1)}, bf16[1024,1536]{1,0:T(8,128)(2,1)}, u32[]{:S(2)}, u32[]{:S(2)}) collective-permute-start(bf16[1024,1536]{1,0:T(8,128)(2,1)} %rest_0_), channel_id=1, source_target_pairs={{0,1},{1,0},{2,3},{3,2},{4,5},{5,4},{6,7},{7,6},{8,9},{9,8},{10,11... | collective-permute-start | bytes 9437192 | tf_op jit(solution)/shard_map/ppermute | solution.py:580
  138.0 90.5 %collective-permute-start.14 = (bf16[1024,1536]{1,0:T(8,128)(2,1)}, bf16[1024,1536]{1,0:T(8,128)(2,1)}, u32[]{:S(2)}, u32[]{:S(2)}) collective-permute-start(bf16[1024,1536]{1,0:T(8,128)(2,1)} %multiply_convert_fusion.rest_1_), channel_id=1, source_target_pairs={{0,1},{1,0},{2,3},{3,2},{4,5},{5,4},{6,7},{7,6},{8,9},{9,8},{10,11... | collective-permute-start | bytes 9437192 | tf_op jit(solution)/shard_map/ppermute | solution.py:580
  149.1 99.6 %collective-permute-start.19 = (bf16[1024,1536]{1,0:T(8,128)(2,1)}, bf16[1024,1536]{1,0:T(8,128)(2,1)}, u32[]{:S(2)}, u32[]{:S(2)}) collective-permute-start(bf16[1024,1536]{1,0:T(8,128)(2,1)} %multiply_convert_fusion.rest_1_), channel_id=1, source_target_pairs={{0,2},{2,0},{4,6},{6,4},{8,10},{10,8},{12,14},{14,12},{16,18},{18,... | collective-permute-start | bytes 9437192 | tf_op jit(solution)/shard_map/ppermute | solution.py:576
  314.0 123.1 %collective-permute-start.23 = (bf16[2,2,6,192,512]{4,3,2,1,0:T(8,128)(2,1)}, bf16[2,2,6,192,512]{4,3,2,1,0:T(8,128)(2,1)}, u32[]{:S(2)}, u32[]{:S(2)}) collective-permute-start(bf16[2,2,6,192,512]{4,3,2,1,0:T(8,128)(2,1)} %get-tuple-element.113), channel_id=1, source_target_pairs={{0,4},{2,6},{4,0},{6,2},{8,12},{10,14},{12,8},{14,10},{16,20},{18,... | collective-permute-start | bytes 14155784 | tf_op jit(solution)/shard_map/ppermute | solution.py:576
  435.3 107.2 %collective-permute-start.25 = (bf16[2,2,6,192,512]{4,3,2,1,0:T(8,128)(2,1)}, bf16[2,2,6,192,512]{4,3,2,1,0:T(8,128)(2,1)}, u32[]{:S(2)}, u32[]{:S(2)}) collective-permute-start(bf16[2,2,6,192,512]{4,3,2,1,0:T(8,128)(2,1)} %get-tuple-element.119), channel_id=1, source_target_pairs={{0,4},{2,6},{4,0},{6,2},{8,12},{10,14},{12,8},{14,10},{16,20},{18,... | collective-permute-start | bytes 14155784 | tf_op jit(solution)/shard_map/ppermute | solution.py:576
  550.2 76.9 %collective-permute-start.26 = (bf16[2,6,192,512]{3,2,1,0:T(8,128)(2,1)}, bf16[2,6,192,512]{3,2,1,0:T(8,128)(2,1)}, u32[]{:S(2)}, u32[]{:S(2)}) collective-permute-start(bf16[2,6,192,512]{3,2,1,0:T(8,128)(2,1)} %get-tuple-element.259.rest_1_), channel_id=1, source_target_pairs={{0,8},{2,10},{4,12},{6,14},{8,0},{10,2},{12,4},{14,6},{16,24},{18,... | collective-permute-start | bytes 7077896 | tf_op jit(solution)/shard_map/ppermute | solution.py:576
  550.3 129.6 %collective-permute-start.29 = (bf16[2,2,6,192,512]{4,3,2,1,0:T(8,128)(2,1)}, bf16[2,2,6,192,512]{4,3,2,1,0:T(8,128)(2,1)}, u32[]{:S(2)}, u32[]{:S(2)}) collective-permute-start(bf16[2,2,6,192,512]{4,3,2,1,0:T(8,128)(2,1)} %get-tuple-element.128), channel_id=1, source_target_pairs={{0,4},{2,6},{4,0},{6,2},{8,12},{10,14},{12,8},{14,10},{16,20},{18,... | collective-permute-start | bytes 14155784 | tf_op jit(solution)/shard_map/ppermute | solution.py:576
  554.8 68.2 %collective-permute-start.27 = (bf16[6,192,512]{2,1,0:T(8,128)(2,1)S(1)}, bf16[6,192,512]{2,1,0:T(8,128)(2,1)}, u32[]{:S(2)}, u32[]{:S(2)}) collective-permute-start(bf16[6,192,512]{2,1,0:T(8,128)(2,1)S(1)} %copy-done.17), channel_id=1, source_target_pairs={{0,16},{2,18},{4,20},{6,22},{8,24},{10,26},{12,28},{14,30},{16,0},... | collective-permute-start | bytes 3538952 | tf_op jit(solution)/shard_map/ppermute | solution.py:576
  650.0 97.2 %collective-permute-start.31 = (bf16[1024,1536]{1,0:T(8,128)(2,1)}, bf16[1024,1536]{1,0:T(8,128)(2,1)}, u32[]{:S(2)}, u32[]{:S(2)}) collective-permute-start(bf16[1024,1536]{1,0:T(8,128)(2,1)} %get-tuple-element.124.rest_0_), channel_id=1, source_target_pairs={{0,2},{2,0},{4,6},{6,4},{8,10},{10,8},{12,14},{14,12},{16,18},{18,... | collective-permute-start | bytes 9437192 | tf_op jit(solution)/shard_map/ppermute | solution.py:576
  692.3 86.4 %collective-permute-start.34 = (bf16[1024,1536]{1,0:T(8,128)(2,1)}, bf16[1024,1536]{1,0:T(8,128)(2,1)}, u32[]{:S(2)}, u32[]{:S(2)}) collective-permute-start(bf16[1024,1536]{1,0:T(8,128)(2,1)} %add_convert_fusion.2.rest_0_), channel_id=1, source_target_pairs={{0,1},{1,0},{2,3},{3,2},{4,5},{5,4},{6,7},{7,6},{8,9},{9,8},{10,11... | collective-permute-start | bytes 9437192 | tf_op jit(solution)/shard_map/ppermute | solution.py:580
  746.7 104.5 %collective-permute-start.39 = (bf16[2,2,6,192,512]{4,3,2,1,0:T(8,128)(2,1)}, bf16[2,2,6,192,512]{4,3,2,1,0:T(8,128)(2,1)}, u32[]{:S(2)}, u32[]{:S(2)}) collective-permute-start(bf16[2,2,6,192,512]{4,3,2,1,0:T(8,128)(2,1)} %get-tuple-element.143), channel_id=1, source_target_pairs={{0,4},{2,6},{4,0},{6,2},{8,12},{10,14},{12,8},{14,10},{16,20},{18,... | collective-permute-start | bytes 14155784 | tf_op jit(solution)/shard_map/ppermute | solution.py:576
  754.3 190.5 %collective-permute-start.46 = (bf16[6,192,512]{2,1,0:T(8,128)(2,1)}, bf16[6,192,512]{2,1,0:T(8,128)(2,1)}, u32[]{:S(2)}, u32[]{:S(2)}) collective-permute-start(bf16[6,192,512]{2,1,0:T(8,128)(2,1)} %fusion.40.rest_0_), channel_id=1, source_target_pairs={{0,16},{2,18},{4,20},{6,22},{8,24},{10,26},{12,28},{14,30},{16,0},... | collective-permute-start | bytes 3538952 | tf_op jit(solution)/shard_map/ppermute | solution.py:576
  765.4 134.6 %collective-permute-start.40 = (bf16[2,6,192,512]{3,2,1,0:T(8,128)(2,1)}, bf16[2,6,192,512]{3,2,1,0:T(8,128)(2,1)}, u32[]{:S(2)}, u32[]{:S(2)}) collective-permute-start(bf16[2,6,192,512]{3,2,1,0:T(8,128)(2,1)} %get-tuple-element.257.rest_1_), channel_id=1, source_target_pairs={{0,8},{2,10},{4,12},{6,14},{8,0},{10,2},{12,4},{14,6},{16,24},{18,... | collective-permute-start | bytes 7077896 | tf_op jit(solution)/shard_map/ppermute | solution.py:576
  778.7 135.7 %collective-permute-start.32 = (bf16[1024,1536]{1,0:T(8,128)(2,1)}, bf16[1024,1536]{1,0:T(8,128)(2,1)}, u32[]{:S(2)}, u32[]{:S(2)}) collective-permute-start(bf16[1024,1536]{1,0:T(8,128)(2,1)} %add_convert_fusion.1), channel_id=1, source_target_pairs={{0,1},{1,0},{2,3},{3,2},{4,5},{5,4},{6,7},{7,6},{8,9},{9,8},{10,11... | collective-permute-start | bytes 9437192 | tf_op jit(solution)/shard_map/ppermute | solution.py:580
  789.6 67.7 %collective-permute-start.38 = (f32[63016]{0:T(1024)S(1)}, f32[63016]{0:T(1024)S(1)}, u32[]{:S(2)}, u32[]{:S(2)}) collective-permute-start(f32[63016]{0:T(1024)S(1)} %concatenate.63), channel_id=1, source_target_pairs={{0,2},{2,0},{4,6},{6,4},{8,10},{10,8},{12,14},{14,12},{16,18},{18,... | collective-permute-start | bytes 756200 | tf_op jit(solution)/shard_map/ppermute | solution.py:576
  851.2 77.1 %collective-permute-start.30 = (bf16[1024,1536]{1,0:T(8,128)(2,1)}, bf16[1024,1536]{1,0:T(8,128)(2,1)}, u32[]{:S(2)}, u32[]{:S(2)}) collective-permute-start(bf16[1024,1536]{1,0:T(8,128)(2,1)} %get-tuple-element.130.rest_0_), channel_id=1, source_target_pairs={{0,2},{2,0},{4,6},{6,4},{8,10},{10,8},{12,14},{14,12},{16,18},{18,... | collective-permute-start | bytes 9437192 | tf_op jit(solution)/shard_map/ppermute | solution.py:576
  857.3 114.2 %collective-permute-start.45 = (bf16[2,2,6,192,512]{4,3,2,1,0:T(8,128)(2,1)}, bf16[2,2,6,192,512]{4,3,2,1,0:T(8,128)(2,1)}, u32[]{:S(2)}, u32[]{:S(2)}) collective-permute-start(bf16[2,2,6,192,512]{4,3,2,1,0:T(8,128)(2,1)} %get-tuple-element.155), channel_id=1, source_target_pairs={{0,4},{2,6},{4,0},{6,2},{8,12},{10,14},{12,8},{14,10},{16,20},{18,... | collective-permute-start | bytes 14155784 | tf_op jit(solution)/shard_map/ppermute | solution.py:576
  926.0 73.0 %collective-permute-start.49 = (bf16[2,6,192,512]{3,2,1,0:T(8,128)(2,1)}, bf16[2,6,192,512]{3,2,1,0:T(8,128)(2,1)}, u32[]{:S(2)}, u32[]{:S(2)}) collective-permute-start(bf16[2,6,192,512]{3,2,1,0:T(8,128)(2,1)} %get-tuple-element.255.rest_1_), channel_id=1, source_target_pairs={{0,8},{2,10},{4,12},{6,14},{8,0},{10,2},{12,4},{14,6},{16,24},{18,... | collective-permute-start | bytes 7077896 | tf_op jit(solution)/shard_map/ppermute | solution.py:576
  928.3 75.9 %collective-permute-start.44 = (bf16[8,96,1280]{2,1,0:T(8,128)(2,1)}, bf16[8,96,1280]{2,1,0:T(8,128)(2,1)}, u32[]{:S(2)}, u32[]{:S(2)}) collective-permute-start(bf16[8,96,1280]{2,1,0:T(8,128)(2,1)} %fusion.10.rest_3_), channel_id=1, source_target_pairs={{0,1},{1,0},{2,3},{3,2},{4,5},{5,4},{6,7},{7,6},{8,9},{9,8},{10,11... | collective-permute-start | bytes 5898248 | tf_op jit(solution)/shard_map/ppermute | solution.py:580
  1043.8 89.3 %collective-permute-start.52 = (bf16[8,96,1280]{2,1,0:T(8,128)(2,1)}, bf16[8,96,1280]{2,1,0:T(8,128)(2,1)}, u32[]{:S(2)}, u32[]{:S(2)}) collective-permute-start(bf16[8,96,1280]{2,1,0:T(8,128)(2,1)} %fusion.34), channel_id=1, source_target_pairs={{0,2},{2,0},{4,6},{6,4},{8,10},{10,8},{12,14},{14,12},{16,18},{18,... | collective-permute-start | bytes 5898248 | tf_op jit(solution)/shard_map/ppermute | solution.py:576
  1057.3 121.0 %collective-permute-start.65 = (bf16[6,192,512]{2,1,0:T(8,128)(2,1)}, bf16[6,192,512]{2,1,0:T(8,128)(2,1)}, u32[]{:S(2)}, u32[]{:S(2)}) collective-permute-start(bf16[6,192,512]{2,1,0:T(8,128)(2,1)} %fusion.42), channel_id=1, source_target_pairs={{0,16},{2,18},{4,20},{6,22},{8,24},{10,26},{12,28},{14,30},{16,0},... | collective-permute-start | bytes 3538952 | tf_op jit(solution)/shard_map/ppermute | solution.py:576
  1057.3 135.6 %collective-permute-start.66 = (bf16[6,192,512]{2,1,0:T(8,128)(2,1)}, bf16[6,192,512]{2,1,0:T(8,128)(2,1)}, u32[]{:S(2)}, u32[]{:S(2)}) collective-permute-start(bf16[6,192,512]{2,1,0:T(8,128)(2,1)} %fusion.44.rest_2_), channel_id=1, source_target_pairs={{0,16},{2,18},{4,20},{6,22},{8,24},{10,26},{12,28},{14,30},{16,0},... | collective-permute-start | bytes 3538952 | tf_op jit(solution)/shard_map/ppermute | solution.py:576
  1072.5 109.9 %collective-permute-start.67 = (bf16[2,6,192,512]{3,2,1,0:T(8,128)(2,1)}, bf16[2,6,192,512]{3,2,1,0:T(8,128)(2,1)}, u32[]{:S(2)}, u32[]{:S(2)}) collective-permute-start(bf16[2,6,192,512]{3,2,1,0:T(8,128)(2,1)} %get-tuple-element.253.rest_1_), channel_id=1, source_target_pairs={{0,8},{2,10},{4,12},{6,14},{8,0},{10,2},{12,4},{14,6},{16,24},{18,... | collective-permute-start | bytes 7077896 | tf_op jit(solution)/shard_map/ppermute | solution.py:576
  1178.3 78.7 %collective-permute-start.63 = (bf16[2,96,768]{2,1,0:T(8,128)(2,1)S(1)}, bf16[2,96,768]{2,1,0:T(8,128)(2,1)S(1)}, u32[]{:S(2)}, u32[]{:S(2)}) collective-permute-start(bf16[2,96,768]{2,1,0:T(8,128)(2,1)S(1)} %dynamic-slice_bitcast_fusion.3), channel_id=1, source_target_pairs={{0,8},{2,10},{4,12},{6,14},{8,0},{10,2},{12,4},{14,6},{16,24},{18,... | collective-permute-start | bytes 884744 | tf_op jit(solution)/shard_map/ppermute | solution.py:576
  (154 other events, 2919.4 us)

commit v7 on v5

--- a/solution.py
+++ b/solution.py
@@ -1381,15 +1381,18 @@
         waits = []
         if index == 2:
             waits = [chips[0].one(carried)]
+        elif index == 3:
+            waits = [chips[0].two(carried)]
         elif index == 4:
-            waits = [chips[0].two(carried)]
+            waits = [chips[1].one(carried)]
         far_first = int(index == FAR_FIRST)
         carried, send, keep = expert_call(
             blocks, misc, x_slots, cot_slots, slot_gates, weights, carried, slots,
             index * CHUNK, CHUNK, x_first, 0, depth, far_first, waits,
         )
         chips.append(ChipSum((send, keep), rank, far_first))
-    waits = [chips[1].one(carried)]
+    done = [chips[0].three(carried)]
+    waits = [chips[1].two(carried), done[0]]
 
     combine_from = combine_tables(begins, ends, slots)
     tiles = place.shape[1] // 4
@@ -1415,9 +1418,8 @@
     y_send = add_low(cross[0], far_y)
     near = combined(0, [next_door[0]])
     y_across = swap(order(y_send, near[0]))
-    waits = [chips[1].two(near[0])]
     mixed_grad_share = (
-        order(near[1], *waits).astype(jnp.float32)
+        near[1].astype(jnp.float32)
         + door_dx.astype(jnp.float32)
         + dx_across.astype(jnp.float32)
     )
@@ -1462,12 +1464,11 @@
     pairs = key_width // 128
     other_grads = jnp.concatenate(
         half_back(saved_other, out_other)(
-            (0, pairs), [*waits, chips[3].one(middle_low)]
+            (0, pairs), [chips[3].one(middle_low)]
         ),
         axis=1,
     )
-    done = [chips[0].three(other_grads)]
-    waits = [chips[2].two(other_grads), *done]
+    waits = [chips[2].two(other_grads)]
     other_grads = order(other_grads, *waits)
     expert_share = (
         near[0].astype(jnp.float32)
@@ -1492,13 +1493,15 @@
     out_half = add_low(out_kept, order(out_across, own_grads))
     own_weight_grads = dot_tn(normed, own_grads)
     own_held = core_sum(own_weight_grads, core)
-    joined_total = plane_sum(add_low(own_held, joined_across), rank)
-    out_total = plane_sum(out_half, rank, own_weight_grads)
-    done.append(chips[2].three(own_grads))
-    chips[4].two(own_grads)
-    sums = done + [chips[i].three(own_weight_grads) for i in (3, 4)]
+    half = jnp.concatenate([add_low(own_held, joined_across), out_half], axis=-1)
+    both_total = plane_sum(half, rank)
+    joined_total = both_total[:, : query_width + 2 * key_width]
+    out_total = both_total[:, query_width + 2 * key_width :]
+    done.append(chips[2].three(half))
+    chips[4].two(half)
+    sums = done + [chips[i].three(half) for i in (3, 4)]
     other_normed = dot_nt(other_grads, joined_other)
-    own_normed = dot_nt(order(own_grads, own_held), joined_own)
+    own_normed = dot_nt(order(own_grads, half), joined_own)
     input_pullback = jax.vjp(normalize, inputs_share, norm_gains)[1]
     input_from_norm, norm_gain_grad = input_pullback(other_normed + own_normed)
     input_grad_share = middle_grad + input_from_norm

time: 1200 us -> 1240 us (1.033)
  starting transfers between devices: 45.8 us -> 66 us
  other arithmetic: 154 us -> 169 us
  local copies, waits for them, and re-layouts: 87.2 us -> 102 us
    ppermute x12, waiting for transfers between devices: 9.01 us -> 38.6 us  [swap(): return lax.ppermute(value, 'tensor', [(0, 1), (1, 0)])]
    ppermute x53 -> x50, waiting for transfers between devices: 188 us -> 165 us  [flip(): return lax.ppermute(value, 'dp', [(i, i ^ bit) for i in range(size)])]
    ppermute x12, starting transfers between devices: 6.44 us -> 29.5 us  [swap(): return lax.ppermute(value, 'tensor', [(0, 1), (1, 0)])]
    ppermute x53 -> x50, starting transfers between devices: 39.4 us -> 36.5 us  [flip(): return lax.ppermute(value, 'dp', [(i, i ^ bit) for i in range(size)])]
    unnamed x257 -> x253, local copies, waits for them, and re-layouts: 27.3 us -> 29.4 us
    convert_element_type x21 -> x19, other arithmetic: 76.8 us -> 77.3 us  [add_low(): (left.astype(jnp.float32) + right.astype(jnp.float32)).astype(jnp.bfloat16)]
  transfers between devices with their start and end apart: 65 -> 62, of which waited for: 20 -> 17; matrix products, arithmetic and copies ran while one was open for 23% -> 24% of each run, Pallas kernels for 47% -> 43%
where the time goes in v7:
time: 1240 us; the launch traced here: 1250 us
  Pallas kernels  631 us (51%)
  waiting for transfers between devices  203 us (16%)
  other arithmetic  169 us (14%)
  local copies, waits for them, and re-layouts  102 us (8%)
  matrix products  69.5 us (6%)
  starting transfers between devices  66 us (5%)
    pallas_call x5, Pallas kernels, expert_call(): pl.pallas_call(functools.partial(expert_kernel, first, split, depth, far_...  229 us
    pallas_call x3, Pallas kernels, gather_rows(): pl.pallas_call(functools.partial(gather_kernel, len(sources), with_gates,...  176 us
    ppermute x50, waiting for transfers between devices, flip(): return lax.ppermute(value, 'dp', [(i, i ^ bit) for i in range(size)])  165 us
    pallas_call x3, Pallas kernels, attend_back(): pl.pallas_call(functools.partial(back_kernel, wide // HD, score_scale, le...  82.4 us
    convert_element_type x19, other arithmetic, add_low(): (left.astype(jnp.float32) + right.astype(jnp.float32)).astype(jnp.bfloat16)  77.3 us
    pallas_call x4, Pallas kernels, combine_rows(): pl.pallas_call(functools.partial(combine_kernel, first), grid_spec=pltpu....  76.8 us
    pallas_call x2, Pallas kernels, attend(): pl.pallas_call(functools.partial(attend_kernel, wide // HD), grid=(pairs,...  48.9 us
    ppermute x12, waiting for transfers between devices, swap(): return lax.ppermute(value, 'tensor', [(0, 1), (1, 0)])  38.6 us
  transfers between devices with their start and end apart: 62, of which 17 were waited for; matrix products, arithmetic and copies ran while one was open for 24% of the time, Pallas kernels for 43%

profile of v7, /device:TPU:0, one launch (start us, length us, event | category | flops | bytes accessed | tf_op | source)
XLA Modules:
  0.0 1245.3 jit_solution(15577790852324541568)
XLA Ops:
  49.9 24.4 %shard_map.238 = (bf16[1024,768]{1,0:T(8,128)(2,1)}, f32[2,1024,128]{2,1,0:T(8,128)}) custom-call(bf16[1024,768]{1,0:T(8,128)(2,1)} %get-tuple-element.88.query_ref, bf16[1024,256]{1,0:T(8,128)(2,1)} %get-tuple-element.89.key_ref, bf16[1024,256]{1,0:T(8,128)(2,1)} %get-tuple-element.90.value_ref, s32[1024,1]{1,0:T(8,128)} %select_select_fusion.limit_ref, ...), custom_call_target="tpu_custom_call" | custom-call | tf_op jit(solution)/shard_map/pallas_call | solution.py:767
  101.8 24.6 %shard_map.240 = (bf16[1024,768]{1,0:T(8,128)(2,1)}, f32[2,1024,128]{2,1,0:T(8,128)}) custom-call(bf16[1024,768]{1,0:T(8,128)(2,1)} %get-tuple-element.92.query_ref, bf16[1024,256]{1,0:T(8,128)(2,1)} %get-tuple-element.93.key_ref, bf16[1024,256]{1,0:T(8,128)(2,1)} %get-tuple-element.94.value_ref, s32[1024,1]{1,0:T(8,128)} %select_select_fusion.limit_ref, ...), custom_call_target="tpu_custom_call" | custom-call | tf_op jit(solution)/shard_map/pallas_call | solution.py:767
  149.7 82.2 %shard_map.241.rest_5_.c_ref = bf16[12800,1536]{1,0:T(8,128)(2,1)} custom-call(s32[10,10]{1,0:T(8,128)} %copy-done.68, s32[10,10]{1,0:T(8,128)} %compare_select_fusion.3.high_ref, s32[10]{0:T(128)} %negate_maximum_fusion.blocks_ref, s32[10,16,1,256]{3,2,1,0:T(1,128)} %add_select_fusion.place_ref, bf16[1024,1536]{1,0:T(8,128)(2,1)} %rest_0_, ...), custom_call_target="tpu_custom_call" | custom-call | tf_op jit(solution)/shard_map/pallas_call | solution.py:270
  248.7 22.3 %shard_map.242 = (bf16[2560,1536]{1,0:T(8,128)(2,1)}, f32[2560,128]{1,0:T(8,128)}) custom-call(s32[2,10]{1,0:T(2,128)} %slice.181.low_ref, s32[2,10]{1,0:T(2,128)} %slice.182.high_ref, s32[2]{0:T(128)} %bitcast.297, s32[2,16,1,256]{3,2,1,0:T(1,128)} %copy.130.place_ref, bf16[4096,128]{1,0:T(8,128)(2,1)} %pad_bitcast_fusion.rest_0_, ...), custom_call_target="tpu_custom_call" | custom-call | tf_op jit(solution)/shard_map/pallas_call | solution.py:270
  271.0 47.1 %shard_map.243 = (bf16[12800,3200]{1,0:T(8,128)(2,1)}, bf16[2,2,6,192,512]{4,3,2,1,0:T(8,128)(2,1)}, bf16[2,2,6,192,512]{4,3,2,1,0:T(8,128)(2,1)}) custom-call(s32[10]{0:T(128)} %negate_maximum_fusion.blocks_ref, s32[3]{0:T(128)} %pad_add_fusion.1.misc_ref, bf16[2560,1536]{1,0:T(8,128)(2,1)} %get-tuple-element.99.x_ref, ...), custom_call_target="tpu_custom_call" | custom-call | tf_op jit(solution)/shard_map/pallas_call | solution.py:444
  320.7 71.1 %shard_map.244 = (bf16[10240,1536]{1,0:T(8,128)(2,1)}, f32[10240,128]{1,0:T(8,128)}) custom-call(s32[8,10]{1,0:T(8,128)} %slice.178.low_ref, s32[8,10]{1,0:T(8,128)} %slice.179.high_ref, s32[8]{0:T(128)} %slice.141.blocks_ref, s32[8,16,1,256]{3,2,1,0:T(1,128)} %copy.131.place_ref, bf16[4096,128]{1,0:T(8,128)(2,1)} %pad_bitcast_fusion.rest_0_, ...), custom_call_target="tpu_custom_call" | custom-call | tf_op jit(solution)/shard_map/pallas_call | solution.py:270
  391.8 46.5 %shard_map.245 = (bf16[12800,3200]{1,0:T(8,128)(2,1)}, bf16[2,2,6,192,512]{4,3,2,1,0:T(8,128)(2,1)}, bf16[2,2,6,192,512]{4,3,2,1,0:T(8,128)(2,1)}) custom-call(s32[10]{0:T(128)} %negate_maximum_fusion.blocks_ref, s32[3]{0:T(128)} %pad_add_fusion.1.misc_ref, bf16[10240,1536]{1,0:T(8,128)(2,1)} %get-tuple-element.102.x_ref, ...), custom_call_target="tpu_custom_call", output_to_operand_aliasing={{0}: (8, {})} | custom-call | tf_op jit(solution)/shard_map/pallas_call | solution.py:444
  448.5 46.5 %shard_map.246 = (bf16[12800,3200]{1,0:T(8,128)(2,1)}, bf16[2,2,6,192,512]{4,3,2,1,0:T(8,128)(2,1)}, bf16[2,2,6,192,512]{4,3,2,1,0:T(8,128)(2,1)}) custom-call(s32[10]{0:T(128)} %negate_maximum_fusion.blocks_ref, s32[3]{0:T(128)} %pad_add_fusion.1.misc_ref, bf16[10240,1536]{1,0:T(8,128)(2,1)} %get-tuple-element.102.x_ref, ...), custom_call_target="tpu_custom_call", output_to_operand_aliasing={{0}: (8, {})} | custom-call | tf_op jit(solution)/shard_map/pallas_call | solution.py:444
  498.0 42.7 %shard_map.247 = (bf16[12800,3200]{1,0:T(8,128)(2,1)}, bf16[2,2,6,192,512]{4,3,2,1,0:T(8,128)(2,1)}, bf16[2,2,6,192,512]{4,3,2,1,0:T(8,128)(2,1)}) custom-call(s32[10]{0:T(128)} %negate_maximum_fusion.blocks_ref, s32[3]{0:T(128)} %pad_add_fusion.1.misc_ref, bf16[10240,1536]{1,0:T(8,128)(2,1)} %get-tuple-element.102.x_ref, ...), custom_call_target="tpu_custom_call", output_to_operand_aliasing={{0}: (8, {})} | custom-call | tf_op jit(solution)/shard_map/pallas_call | solution.py:444
  560.8 46.7 %shard_map.248 = (bf16[12800,3200]{1,0:T(8,128)(2,1)}, bf16[2,2,6,192,512]{4,3,2,1,0:T(8,128)(2,1)}, bf16[2,2,6,192,512]{4,3,2,1,0:T(8,128)(2,1)}) custom-call(s32[10]{0:T(128)} %negate_maximum_fusion.blocks_ref, s32[3]{0:T(128)} %pad_add_fusion.1.misc_ref, bf16[10240,1536]{1,0:T(8,128)(2,1)} %get-tuple-element.102.x_ref, ...), custom_call_target="tpu_custom_call", output_to_operand_aliasing={{0}: (8, {})} | custom-call | tf_op jit(solution)/shard_map/pallas_call | solution.py:444
  615.1 18.9 %shard_map.249 = (bf16[1024,1536]{1,0:T(8,128)(2,1)}, bf16[1024,1536]{1,0:T(8,128)(2,1)}, f32[1024,128]{1,0:T(8,128)}) custom-call(s32[16,96]{1,0:T(8,128)} %copy-done.60, s32[16,96]{1,0:T(8,128)} %get-tuple-element.265.piece_ref, s32[16,96]{1,0:T(8,128)} %get-tuple-element.264.source_ref, s32[16]{0:T(128)} %get-tuple-element.233.groups_ref, ...), custom_call_target="tpu_custom_call" | custom-call | tf_op jit(solution)/shard_map/pallas_call | solution.py:551
  644.1 19.5 %shard_map.250 = (bf16[1024,1536]{1,0:T(8,128)(2,1)}, bf16[1024,1536]{1,0:T(8,128)(2,1)}, f32[1024,128]{1,0:T(8,128)}) custom-call(s32[16,96]{1,0:T(8,128)} %copy-done.60, s32[16,96]{1,0:T(8,128)} %get-tuple-element.265.piece_ref, s32[16,96]{1,0:T(8,128)} %get-tuple-element.264.source_ref, s32[16]{0:T(128)} %get-tuple-element.233.groups_ref, ...), custom_call_target="tpu_custom_call" | custom-call | tf_op jit(solution)/shard_map/pallas_call | solution.py:551
  675.9 21.8 %collective-permute-start.34 = (bf16[1024,1536]{1,0:T(8,128)(2,1)}, bf16[1024,1536]{1,0:T(8,128)(2,1)}, u32[]{:S(2)}, u32[]{:S(2)}) collective-permute-start(bf16[1024,1536]{1,0:T(8,128)(2,1)} %add_convert_fusion.2.rest_0_), channel_id=1, source_target_pairs={{0,1},{1,0},{2,3},{3,2},{4,5},{5,4},{6,7},{7,6},{8,9},{9,8},{10,11... | collective-permute-start | bytes 9437192 | tf_op jit(solution)/shard_map/ppermute | solution.py:580
  697.8 19.5 %shard_map.251 = (bf16[1024,1536]{1,0:T(8,128)(2,1)}, bf16[1024,1536]{1,0:T(8,128)(2,1)}, f32[1024,128]{1,0:T(8,128)}) custom-call(s32[16,96]{1,0:T(8,128)} %copy-done.60, s32[16,96]{1,0:T(8,128)} %get-tuple-element.265.piece_ref, s32[16,96]{1,0:T(8,128)} %get-tuple-element.264.source_ref, s32[16]{0:T(128)} %get-tuple-element.233.groups_ref, ...), custom_call_target="tpu_custom_call" | custom-call | tf_op jit(solution)/shard_map/pallas_call | solution.py:551
  723.2 18.9 %shard_map.252 = (bf16[1024,1536]{1,0:T(8,128)(2,1)}, bf16[1024,1536]{1,0:T(8,128)(2,1)}, f32[1024,128]{1,0:T(8,128)}) custom-call(s32[16,96]{1,0:T(8,128)} %copy-done.60, s32[16,96]{1,0:T(8,128)} %get-tuple-element.265.piece_ref, s32[16,96]{1,0:T(8,128)} %get-tuple-element.264.source_ref, s32[16]{0:T(128)} %get-tuple-element.233.groups_ref, ...), custom_call_target="tpu_custom_call" | custom-call | tf_op jit(solution)/shard_map/pallas_call | solution.py:551
  788.5 35.3 %collective-permute-done.38 = bf16[2,2,6,192,512]{4,3,2,1,0:T(8,128)(2,1)} collective-permute-done((bf16[2,2,6,192,512]{4,3,2,1,0:T(8,128)(2,1)}, bf16[2,2,6,192,512]{4,3,2,1,0:T(8,128)(2,1)}, u32[]{:S(2)}, u32[]{:S(2)}) %collective-permute-start.38) | collective-permute-done | bytes 4718624 | tf_op jit(solution)/shard_map/ppermute | solution.py:576
  833.9 40.0 %shard_map.253 = (bf16[1024,768]{1,0:T(8,128)(2,1)}, bf16[1024,256]{1,0:T(8,128)(2,1)}, bf16[1024,256]{1,0:T(8,128)(2,1)}) custom-call(bf16[1024,768]{1,0:T(8,128)(2,1)} %get-tuple-element.92.query_ref, bf16[1024,256]{1,0:T(8,128)(2,1)} %get-tuple-element.93.key_ref, bf16[1024,256]{1,0:T(8,128)(2,1)} %get-tuple-element.94.value_ref, ...), custom_call_target="tpu_custom_call" | custom-call | tf_op jit(solution)/shard_map/pallas_call | solution.py:879
  934.4 21.0 %shard_map.254 = (bf16[1024,384]{1,0:T(8,128)(2,1)}, bf16[1024,128]{1,0:T(8,128)(2,1)}, bf16[1024,128]{1,0:T(8,128)(2,1)}) custom-call(bf16[1024,768]{1,0:T(8,128)(2,1)} %get-tuple-element.88.query_ref, bf16[1024,256]{1,0:T(8,128)(2,1)} %get-tuple-element.89.key_ref, bf16[1024,256]{1,0:T(8,128)(2,1)} %get-tuple-element.90.value_ref, ...), custom_call_target="tpu_custom_call" | custom-call | tf_op jit(solution)/shard_map/pallas_call | solution.py:879
  960.6 21.4 %shard_map.255 = (bf16[1024,384]{1,0:T(8,128)(2,1)}, bf16[1024,128]{1,0:T(8,128)(2,1)}, bf16[1024,128]{1,0:T(8,128)(2,1)}) custom-call(bf16[1024,768]{1,0:T(8,128)(2,1)} %get-tuple-element.88.query_ref, bf16[1024,256]{1,0:T(8,128)(2,1)} %get-tuple-element.89.key_ref, bf16[1024,256]{1,0:T(8,128)(2,1)} %get-tuple-element.90.value_ref, ...), custom_call_target="tpu_custom_call" | custom-call | tf_op jit(solution)/shard_map/pallas_call | solution.py:879
  1014.1 14.5 %collective-permute-done.48 = bf16[8,96,768]{2,1,0:T(8,128)(2,1)} collective-permute-done((bf16[8,96,768]{2,1,0:T(8,128)(2,1)}, bf16[8,96,768]{2,1,0:T(8,128)(2,1)}, u32[]{:S(2)}, u32[]{:S(2)}) %collective-permute-start.48) | collective-permute-done | bytes 1179680 | tf_op jit(solution)/shard_map/ppermute | solution.py:580
  1034.6 62.3 %collective-permute-done.59 = bf16[2,6,192,512]{3,2,1,0:T(8,128)(2,1)} collective-permute-done((bf16[2,6,192,512]{3,2,1,0:T(8,128)(2,1)}, bf16[2,6,192,512]{3,2,1,0:T(8,128)(2,1)}, u32[]{:S(2)}, u32[]{:S(2)}) %collective-permute-start.59) | collective-permute-done | bytes 2359328 | tf_op jit(solution)/shard_map/ppermute | solution.py:576
  1124.8 17.4 %collective-permute-done.58 = bf16[6,192,512]{2,1,0:T(8,128)(2,1)} collective-permute-done((bf16[6,192,512]{2,1,0:T(8,128)(2,1)}, bf16[6,192,512]{2,1,0:T(8,128)(2,1)}, u32[]{:S(2)}, u32[]{:S(2)}) %collective-permute-start.58) | collective-permute-done | bytes 1179680 | tf_op jit(solution)/shard_map/ppermute | solution.py:576
  1155.6 17.1 %collective-permute-done.51 = f32[64552]{0:T(1024)S(1)} collective-permute-done((f32[64552]{0:T(1024)S(1)}, f32[64552]{0:T(1024)S(1)}, u32[]{:S(2)}, u32[]{:S(2)}) %collective-permute-start.51) | collective-permute-done | bytes 258240 | tf_op jit(solution)/shard_map/ppermute | solution.py:576
  1217.2 17.0 %collective-permute-done.56 = bf16[96,2048]{1,0:T(8,128)(2,1)S(1)} collective-permute-done((bf16[96,2048]{1,0:T(8,128)(2,1)S(1)}, bf16[96,2048]{1,0:T(8,128)(2,1)S(1)}, u32[]{:S(2)}, u32[]{:S(2)}) %collective-permute-start.56) | collective-permute-done | bytes 393248 | tf_op jit(solution)/shard_map/ppermute | solution.py:576
  (565 shorter events, 441.2 us)
Async XLA Ops:
  47.9 86.8 %collective-permute-start.16 = (bf16[1024,1536]{1,0:T(8,128)(2,1)}, bf16[1024,1536]{1,0:T(8,128)(2,1)}, u32[]{:S(2)}, u32[]{:S(2)}) collective-permute-start(bf16[1024,1536]{1,0:T(8,128)(2,1)} %rest_0_), channel_id=1, source_target_pairs={{0,1},{1,0},{2,3},{3,2},{4,5},{5,4},{6,7},{7,6},{8,9},{9,8},{10,11... | collective-permute-start | bytes 9437192 | tf_op jit(solution)/shard_map/ppermute | solution.py:580
  85.1 64.6 %collective-permute-start.17 = (bf16[1024,1536]{1,0:T(8,128)(2,1)}, bf16[1024,1536]{1,0:T(8,128)(2,1)}, u32[]{:S(2)}, u32[]{:S(2)}) collective-permute-start(bf16[1024,1536]{1,0:T(8,128)(2,1)} %rest_0_), channel_id=1, source_target_pairs={{0,2},{2,0},{4,6},{6,4},{8,10},{10,8},{12,14},{14,12},{16,18},{18,... | collective-permute-start | bytes 9437192 | tf_op jit(solution)/shard_map/ppermute | solution.py:576
  137.8 94.1 %collective-permute-start.15 = (bf16[1024,1536]{1,0:T(8,128)(2,1)}, bf16[1024,1536]{1,0:T(8,128)(2,1)}, u32[]{:S(2)}, u32[]{:S(2)}) collective-permute-start(bf16[1024,1536]{1,0:T(8,128)(2,1)} %multiply_convert_fusion.rest_1_), channel_id=1, source_target_pairs={{0,1},{1,0},{2,3},{3,2},{4,5},{5,4},{6,7},{7,6},{8,9},{9,8},{10,11... | collective-permute-start | bytes 9437192 | tf_op jit(solution)/shard_map/ppermute | solution.py:580
  149.7 99.0 %collective-permute-start.20 = (bf16[1024,1536]{1,0:T(8,128)(2,1)}, bf16[1024,1536]{1,0:T(8,128)(2,1)}, u32[]{:S(2)}, u32[]{:S(2)}) collective-permute-start(bf16[1024,1536]{1,0:T(8,128)(2,1)} %multiply_convert_fusion.rest_1_), channel_id=1, source_target_pairs={{0,2},{2,0},{4,6},{6,4},{8,10},{10,8},{12,14},{14,12},{16,18},{18,... | collective-permute-start | bytes 9437192 | tf_op jit(solution)/shard_map/ppermute | solution.py:576
  318.1 122.7 %collective-permute-start.23 = (bf16[2,2,6,192,512]{4,3,2,1,0:T(8,128)(2,1)}, bf16[2,2,6,192,512]{4,3,2,1,0:T(8,128)(2,1)}, u32[]{:S(2)}, u32[]{:S(2)}) collective-permute-start(bf16[2,2,6,192,512]{4,3,2,1,0:T(8,128)(2,1)} %get-tuple-element.106), channel_id=1, source_target_pairs={{0,4},{2,6},{4,0},{6,2},{8,12},{10,14},{12,8},{14,10},{16,20},{18,... | collective-permute-start | bytes 14155784 | tf_op jit(solution)/shard_map/ppermute | solution.py:576
  438.3 102.4 %collective-permute-start.25 = (bf16[2,2,6,192,512]{4,3,2,1,0:T(8,128)(2,1)}, bf16[2,2,6,192,512]{4,3,2,1,0:T(8,128)(2,1)}, u32[]{:S(2)}, u32[]{:S(2)}) collective-permute-start(bf16[2,2,6,192,512]{4,3,2,1,0:T(8,128)(2,1)} %get-tuple-element.112), channel_id=1, source_target_pairs={{0,4},{2,6},{4,0},{6,2},{8,12},{10,14},{12,8},{14,10},{16,20},{18,... | collective-permute-start | bytes 14155784 | tf_op jit(solution)/shard_map/ppermute | solution.py:576
  548.5 63.9 %collective-permute-start.26 = (bf16[2,6,192,512]{3,2,1,0:T(8,128)(2,1)}, bf16[2,6,192,512]{3,2,1,0:T(8,128)(2,1)}, u32[]{:S(2)}, u32[]{:S(2)}) collective-permute-start(bf16[2,6,192,512]{3,2,1,0:T(8,128)(2,1)} %get-tuple-element.243.rest_1_), channel_id=1, source_target_pairs={{0,8},{2,10},{4,12},{6,14},{8,0},{10,2},{12,4},{14,6},{16,24},{18,... | collective-permute-start | bytes 7077896 | tf_op jit(solution)/shard_map/ppermute | solution.py:576
  550.6 113.0 %collective-permute-start.29 = (bf16[2,2,6,192,512]{4,3,2,1,0:T(8,128)(2,1)}, bf16[2,2,6,192,512]{4,3,2,1,0:T(8,128)(2,1)}, u32[]{:S(2)}, u32[]{:S(2)}) collective-permute-start(bf16[2,2,6,192,512]{4,3,2,1,0:T(8,128)(2,1)} %get-tuple-element.121), channel_id=1, source_target_pairs={{0,4},{2,6},{4,0},{6,2},{8,12},{10,14},{12,8},{14,10},{16,20},{18,... | collective-permute-start | bytes 14155784 | tf_op jit(solution)/shard_map/ppermute | solution.py:576
  635.1 114.9 %collective-permute-start.31 = (bf16[1024,1536]{1,0:T(8,128)(2,1)}, bf16[1024,1536]{1,0:T(8,128)(2,1)}, u32[]{:S(2)}, u32[]{:S(2)}) collective-permute-start(bf16[1024,1536]{1,0:T(8,128)(2,1)} %get-tuple-element.117.rest_0_), channel_id=1, source_target_pairs={{0,2},{2,0},{4,6},{6,4},{8,10},{10,8},{12,14},{14,12},{16,18},{18,... | collective-permute-start | bytes 9437192 | tf_op jit(solution)/shard_map/ppermute | solution.py:576
  675.9 96.7 %collective-permute-start.34 = (bf16[1024,1536]{1,0:T(8,128)(2,1)}, bf16[1024,1536]{1,0:T(8,128)(2,1)}, u32[]{:S(2)}, u32[]{:S(2)}) collective-permute-start(bf16[1024,1536]{1,0:T(8,128)(2,1)} %add_convert_fusion.2.rest_0_), channel_id=1, source_target_pairs={{0,1},{1,0},{2,3},{3,2},{4,5},{5,4},{6,7},{7,6},{8,9},{9,8},{10,11... | collective-permute-start | bytes 9437192 | tf_op jit(solution)/shard_map/ppermute | solution.py:580
  717.3 55.4 %collective-permute-start.33 = (bf16[1024,1536]{1,0:T(8,128)(2,1)}, bf16[1024,1536]{1,0:T(8,128)(2,1)}, u32[]{:S(2)}, u32[]{:S(2)}) collective-permute-start(bf16[1024,1536]{1,0:T(8,128)(2,1)} %get-tuple-element.128), channel_id=1, source_target_pairs={{0,2},{2,0},{4,6},{6,4},{8,10},{10,8},{12,14},{14,12},{16,18},{18,... | collective-permute-start | bytes 9437192 | tf_op jit(solution)/shard_map/ppermute | solution.py:576
  718.9 104.9 %collective-permute-start.38 = (bf16[2,2,6,192,512]{4,3,2,1,0:T(8,128)(2,1)}, bf16[2,2,6,192,512]{4,3,2,1,0:T(8,128)(2,1)}, u32[]{:S(2)}, u32[]{:S(2)}) collective-permute-start(bf16[2,2,6,192,512]{4,3,2,1,0:T(8,128)(2,1)} %get-tuple-element.135), channel_id=1, source_target_pairs={{0,4},{2,6},{4,0},{6,2},{8,12},{10,14},{12,8},{14,10},{16,20},{18,... | collective-permute-start | bytes 14155784 | tf_op jit(solution)/shard_map/ppermute | solution.py:576
  755.5 169.0 %collective-permute-start.40 = (bf16[2,2,6,192,512]{4,3,2,1,0:T(8,128)(2,1)}, bf16[2,2,6,192,512]{4,3,2,1,0:T(8,128)(2,1)}, u32[]{:S(2)}, u32[]{:S(2)}) collective-permute-start(bf16[2,2,6,192,512]{4,3,2,1,0:T(8,128)(2,1)} %get-tuple-element.145), channel_id=1, source_target_pairs={{0,4},{2,6},{4,0},{6,2},{8,12},{10,14},{12,8},{14,10},{16,20},{18,... | collective-permute-start | bytes 14155784 | tf_op jit(solution)/shard_map/ppermute | solution.py:576
  767.0 151.0 %collective-permute-start.42 = (bf16[6,192,512]{2,1,0:T(8,128)(2,1)}, bf16[6,192,512]{2,1,0:T(8,128)(2,1)}, u32[]{:S(2)}, u32[]{:S(2)}) collective-permute-start(bf16[6,192,512]{2,1,0:T(8,128)(2,1)} %fusion.41.rest_0_), channel_id=1, source_target_pairs={{0,16},{2,18},{4,20},{6,22},{8,24},{10,26},{12,28},{14,30},{16,0},... | collective-permute-start | bytes 3538952 | tf_op jit(solution)/shard_map/ppermute | solution.py:576
  772.6 103.2 %collective-permute-start.39 = (bf16[2,6,192,512]{3,2,1,0:T(8,128)(2,1)}, bf16[2,6,192,512]{3,2,1,0:T(8,128)(2,1)}, u32[]{:S(2)}, u32[]{:S(2)}) collective-permute-start(bf16[2,6,192,512]{3,2,1,0:T(8,128)(2,1)} %get-tuple-element.241.rest_1_), channel_id=1, source_target_pairs={{0,8},{2,10},{4,12},{6,14},{8,0},{10,2},{12,4},{14,6},{16,24},{18,... | collective-permute-start | bytes 7077896 | tf_op jit(solution)/shard_map/ppermute | solution.py:576
  772.7 107.5 %collective-permute-start.32 = (bf16[1024,1536]{1,0:T(8,128)(2,1)}, bf16[1024,1536]{1,0:T(8,128)(2,1)}, u32[]{:S(2)}, u32[]{:S(2)}) collective-permute-start(bf16[1024,1536]{1,0:T(8,128)(2,1)} %add_convert_fusion.1), channel_id=1, source_target_pairs={{0,1},{1,0},{2,3},{3,2},{4,5},{5,4},{6,7},{7,6},{8,9},{9,8},{10,11... | collective-permute-start | bytes 9437192 | tf_op jit(solution)/shard_map/ppermute | solution.py:580
  823.8 71.2 %collective-permute-start.30 = (bf16[1024,1536]{1,0:T(8,128)(2,1)}, bf16[1024,1536]{1,0:T(8,128)(2,1)}, u32[]{:S(2)}, u32[]{:S(2)}) collective-permute-start(bf16[1024,1536]{1,0:T(8,128)(2,1)} %get-tuple-element.123.rest_0_), channel_id=1, source_target_pairs={{0,2},{2,0},{4,6},{6,4},{8,10},{10,8},{12,14},{14,12},{16,18},{18,... | collective-permute-start | bytes 9437192 | tf_op jit(solution)/shard_map/ppermute | solution.py:576
  875.8 81.7 %collective-permute-start.46 = (bf16[2,6,192,512]{3,2,1,0:T(8,128)(2,1)}, bf16[2,6,192,512]{3,2,1,0:T(8,128)(2,1)}, u32[]{:S(2)}, u32[]{:S(2)}) collective-permute-start(bf16[2,6,192,512]{3,2,1,0:T(8,128)(2,1)} %get-tuple-element.239.rest_0_), channel_id=1, source_target_pairs={{0,8},{2,10},{4,12},{6,14},{8,0},{10,2},{12,4},{14,6},{16,24},{18,... | collective-permute-start | bytes 7077896 | tf_op jit(solution)/shard_map/ppermute | solution.py:576
  999.9 97.0 %collective-permute-start.59 = (bf16[2,6,192,512]{3,2,1,0:T(8,128)(2,1)}, bf16[2,6,192,512]{3,2,1,0:T(8,128)(2,1)}, u32[]{:S(2)}, u32[]{:S(2)}) collective-permute-start(bf16[2,6,192,512]{3,2,1,0:T(8,128)(2,1)} %get-tuple-element.237.rest_0_), channel_id=1, source_target_pairs={{0,8},{2,10},{4,12},{6,14},{8,0},{10,2},{12,4},{14,6},{16,24},{18,... | collective-permute-start | bytes 7077896 | tf_op jit(solution)/shard_map/ppermute | solution.py:576
  1008.7 133.5 %collective-permute-start.57 = (bf16[6,192,512]{2,1,0:T(8,128)(2,1)}, bf16[6,192,512]{2,1,0:T(8,128)(2,1)}, u32[]{:S(2)}, u32[]{:S(2)}) collective-permute-start(bf16[6,192,512]{2,1,0:T(8,128)(2,1)} %fusion.43), channel_id=1, source_target_pairs={{0,16},{2,18},{4,20},{6,22},{8,24},{10,26},{12,28},{14,30},{16,0},... | collective-permute-start | bytes 3538952 | tf_op jit(solution)/shard_map/ppermute | solution.py:576
  1014.0 128.2 %collective-permute-start.58 = (bf16[6,192,512]{2,1,0:T(8,128)(2,1)}, bf16[6,192,512]{2,1,0:T(8,128)(2,1)}, u32[]{:S(2)}, u32[]{:S(2)}) collective-permute-start(bf16[6,192,512]{2,1,0:T(8,128)(2,1)} %fusion.45.rest_2_), channel_id=1, source_target_pairs={{0,16},{2,18},{4,20},{6,22},{8,24},{10,26},{12,28},{14,30},{16,0},... | collective-permute-start | bytes 3538952 | tf_op jit(solution)/shard_map/ppermute | solution.py:576
  1106.4 68.3 %collective-permute-start.60 = (bf16[6,192,512]{2,1,0:T(8,128)(2,1)}, bf16[6,192,512]{2,1,0:T(8,128)(2,1)S(1)}, u32[]{:S(2)}, u32[]{:S(2)}) collective-permute-start(bf16[6,192,512]{2,1,0:T(8,128)(2,1)} %fusion.52), channel_id=1, source_target_pairs={{0,16},{2,18},{4,20},{6,22},{8,24},{10,26},{12,28},{14,30},{16,0},... | collective-permute-start | bytes 3538952 | tf_op jit(solution)/shard_map/ppermute | solution.py:576
  1107.6 75.1 %collective-permute-start.54 = (bf16[4,96,2048]{2,1,0:T(8,128)(2,1)}, bf16[4,96,2048]{2,1,0:T(8,128)(2,1)}, u32[]{:S(2)}, u32[]{:S(2)}) collective-permute-start(bf16[4,96,2048]{2,1,0:T(8,128)(2,1)} %dynamic-slice_bitcast_fusion), channel_id=1, source_target_pairs={{0,4},{2,6},{4,0},{6,2},{8,12},{10,14},{12,8},{14,10},{16,20},{18,... | collective-permute-start | bytes 4718600 | tf_op jit(solution)/shard_map/ppermute | solution.py:576
  1182.6 53.2 %collective-permute-start.61 = (bf16[10,3,96,512]{3,2,0,1:T(8,128)(2,1)}, bf16[10,3,96,512]{3,2,0,1:T(8,128)(2,1)}, u32[]{:S(2)}, u32[]{:S(2)}) collective-permute-start(bf16[10,3,96,512]{3,2,0,1:T(8,128)(2,1)} %bitcast.254), channel_id=1, source_target_pairs={{0,2},{2,0},{4,6},{6,4},{8,10},{10,8},{12,14},{14,12},{16,18},{18,... | collective-permute-start | bytes 8847368 | tf_op jit(solution)/shard_map/ppermute | solution.py:576
  (159 other events, 2830.1 us)

commit v8 on v7

--- a/solution.py
+++ b/solution.py
@@ -1498,13 +1498,13 @@
     joined_total = both_total[:, : query_width + 2 * key_width]
     out_total = both_total[:, query_width + 2 * key_width :]
     done.append(chips[2].three(half))
-    chips[4].two(half)
-    sums = done + [chips[i].three(half) for i in (3, 4)]
+    chips[4].two(own_grads)
     other_normed = dot_nt(other_grads, joined_other)
     own_normed = dot_nt(order(own_grads, half), joined_own)
     input_pullback = jax.vjp(normalize, inputs_share, norm_gains)[1]
     input_from_norm, norm_gain_grad = input_pullback(other_normed + own_normed)
     input_grad_share = middle_grad + input_from_norm
+    sums = done + [chips[i].three(norm_gain_grad) for i in (3, 4)]
     key_end = query_width + key_width
     small = all_sum(
         jnp.concatenate(

time: 1240 us -> 1260 us (1.016)
  starting transfers between devices: 66 us -> 97.9 us
  Pallas kernels: 631 us -> 613 us
    ppermute x50, starting transfers between devices: 36.5 us -> 80.8 us  [flip(): return lax.ppermute(value, 'dp', [(i, i ^ bit) for i in range(size)])]
    unnamed x253 -> x255, local copies, waits for them, and re-layouts: 29.4 us -> 31.2 us
  transfers between devices with their start and end apart: 62 -> 62, of which waited for: 17 -> 19; matrix products, arithmetic and copies ran while one was open for 24% -> 24% of each run, Pallas kernels for 43% -> 44%
where the time goes in v8:
time: 1260 us
  Pallas kernels  613 us (49%)
  waiting for transfers between devices  206 us (16%)
  other arithmetic  164 us (13%)
  local copies, waits for them, and re-layouts  104 us (8%)
  starting transfers between devices  97.9 us (8%)
  matrix products  70.7 us (6%)
    pallas_call x5, Pallas kernels, expert_call(): pl.pallas_call(functools.partial(expert_kernel, first, split, depth, far_...  218 us
    pallas_call x3, Pallas kernels, gather_rows(): pl.pallas_call(functools.partial(gather_kernel, len(sources), with_gates,...  171 us
    ppermute x50, waiting for transfers between devices, flip(): return lax.ppermute(value, 'dp', [(i, i ^ bit) for i in range(size)])  169 us
    pallas_call x3, Pallas kernels, attend_back(): pl.pallas_call(functools.partial(back_kernel, wide // HD, score_scale, le...  82.3 us
    ppermute x50, starting transfers between devices, flip(): return lax.ppermute(value, 'dp', [(i, i ^ bit) for i in range(size)])  80.8 us
    pallas_call x4, Pallas kernels, combine_rows(): pl.pallas_call(functools.partial(combine_kernel, first), grid_spec=pltpu....  75.2 us
    convert_element_type x19, other arithmetic, add_low(): (left.astype(jnp.float32) + right.astype(jnp.float32)).astype(jnp.bfloat16)  74.3 us
    pallas_call x2, Pallas kernels, attend(): pl.pallas_call(functools.partial(attend_kernel, wide // HD), grid=(pairs,...  48.9 us
  transfers between devices with their start and end apart: 62, of which 19 were waited for; matrix products, arithmetic and copies ran while one was open for 24% of the time, Pallas kernels for 44%

profile of v8, /device:TPU:0, one launch (start us, length us, event | category | flops | bytes accessed | tf_op | source)
XLA Modules:
  0.0 1259.8 jit_solution(9178296790116620357)
XLA Ops:
  49.9 24.4 %shard_map.238 = (bf16[1024,768]{1,0:T(8,128)(2,1)}, f32[2,1024,128]{2,1,0:T(8,128)}) custom-call(bf16[1024,768]{1,0:T(8,128)(2,1)} %get-tuple-element.88.query_ref, bf16[1024,256]{1,0:T(8,128)(2,1)} %get-tuple-element.89.key_ref, bf16[1024,256]{1,0:T(8,128)(2,1)} %get-tuple-element.90.value_ref, s32[1024,1]{1,0:T(8,128)} %select_select_fusion.limit_ref, ...), custom_call_target="tpu_custom_call" | custom-call | tf_op jit(solution)/shard_map/pallas_call | solution.py:767
  101.7 24.6 %shard_map.240 = (bf16[1024,768]{1,0:T(8,128)(2,1)}, f32[2,1024,128]{2,1,0:T(8,128)}) custom-call(bf16[1024,768]{1,0:T(8,128)(2,1)} %get-tuple-element.92.query_ref, bf16[1024,256]{1,0:T(8,128)(2,1)} %get-tuple-element.93.key_ref, bf16[1024,256]{1,0:T(8,128)(2,1)} %get-tuple-element.94.value_ref, s32[1024,1]{1,0:T(8,128)} %select_select_fusion.limit_ref, ...), custom_call_target="tpu_custom_call" | custom-call | tf_op jit(solution)/shard_map/pallas_call | solution.py:767
  149.7 79.9 %shard_map.241.rest_5_.c_ref = bf16[12800,1536]{1,0:T(8,128)(2,1)} custom-call(s32[10,10]{1,0:T(8,128)} %copy-done.69, s32[10,10]{1,0:T(8,128)} %compare_select_fusion.3.high_ref, s32[10]{0:T(128)} %negate_maximum_fusion.blocks_ref, s32[10,16,1,256]{3,2,1,0:T(1,128)} %add_select_fusion.place_ref, bf16[1024,1536]{1,0:T(8,128)(2,1)} %rest_0_, ...), custom_call_target="tpu_custom_call" | custom-call | tf_op jit(solution)/shard_map/pallas_call | solution.py:270
  246.8 21.9 %shard_map.242 = (bf16[2560,1536]{1,0:T(8,128)(2,1)}, f32[2560,128]{1,0:T(8,128)}) custom-call(s32[2,10]{1,0:T(2,128)} %slice.181.low_ref, s32[2,10]{1,0:T(2,128)} %slice.182.high_ref, s32[2]{0:T(128)} %bitcast.297, s32[2,16,1,256]{3,2,1,0:T(1,128)} %copy.130.place_ref, bf16[4096,128]{1,0:T(8,128)(2,1)} %pad_bitcast_fusion.rest_0_, ...), custom_call_target="tpu_custom_call" | custom-call | tf_op jit(solution)/shard_map/pallas_call | solution.py:270
  268.7 38.7 %shard_map.243 = (bf16[12800,3200]{1,0:T(8,128)(2,1)}, bf16[2,2,6,192,512]{4,3,2,1,0:T(8,128)(2,1)}, bf16[2,2,6,192,512]{4,3,2,1,0:T(8,128)(2,1)}) custom-call(s32[10]{0:T(128)} %negate_maximum_fusion.blocks_ref, s32[3]{0:T(128)} %pad_add_fusion.1.misc_ref, bf16[2560,1536]{1,0:T(8,128)(2,1)} %get-tuple-element.99.x_ref, ...), custom_call_target="tpu_custom_call" | custom-call | tf_op jit(solution)/shard_map/pallas_call | solution.py:444
  316.0 69.0 %shard_map.244 = (bf16[10240,1536]{1,0:T(8,128)(2,1)}, f32[10240,128]{1,0:T(8,128)}) custom-call(s32[8,10]{1,0:T(8,128)} %slice.178.low_ref, s32[8,10]{1,0:T(8,128)} %slice.179.high_ref, s32[8]{0:T(128)} %slice.141.blocks_ref, s32[8,16,1,256]{3,2,1,0:T(1,128)} %copy.131.place_ref, bf16[4096,128]{1,0:T(8,128)(2,1)} %pad_bitcast_fusion.rest_0_, ...), custom_call_target="tpu_custom_call" | custom-call | tf_op jit(solution)/shard_map/pallas_call | solution.py:270
  385.0 38.6 %shard_map.245 = (bf16[12800,3200]{1,0:T(8,128)(2,1)}, bf16[2,2,6,192,512]{4,3,2,1,0:T(8,128)(2,1)}, bf16[2,2,6,192,512]{4,3,2,1,0:T(8,128)(2,1)}) custom-call(s32[10]{0:T(128)} %negate_maximum_fusion.blocks_ref, s32[3]{0:T(128)} %pad_add_fusion.1.misc_ref, bf16[10240,1536]{1,0:T(8,128)(2,1)} %get-tuple-element.102.x_ref, ...), custom_call_target="tpu_custom_call", output_to_operand_aliasing={{0}: (8, {})} | custom-call | tf_op jit(solution)/shard_map/pallas_call | solution.py:444
  433.3 42.7 %shard_map.246 = (bf16[12800,3200]{1,0:T(8,128)(2,1)}, bf16[2,2,6,192,512]{4,3,2,1,0:T(8,128)(2,1)}, bf16[2,2,6,192,512]{4,3,2,1,0:T(8,128)(2,1)}) custom-call(s32[10]{0:T(128)} %negate_maximum_fusion.blocks_ref, s32[3]{0:T(128)} %pad_add_fusion.1.misc_ref, bf16[10240,1536]{1,0:T(8,128)(2,1)} %get-tuple-element.102.x_ref, ...), custom_call_target="tpu_custom_call", output_to_operand_aliasing={{0}: (8, {})} | custom-call | tf_op jit(solution)/shard_map/pallas_call | solution.py:444
  481.0 51.2 %shard_map.247 = (bf16[12800,3200]{1,0:T(8,128)(2,1)}, bf16[2,2,6,192,512]{4,3,2,1,0:T(8,128)(2,1)}, bf16[2,2,6,192,512]{4,3,2,1,0:T(8,128)(2,1)}) custom-call(s32[10]{0:T(128)} %negate_maximum_fusion.blocks_ref, s32[3]{0:T(128)} %pad_add_fusion.1.misc_ref, bf16[10240,1536]{1,0:T(8,128)(2,1)} %get-tuple-element.102.x_ref, ...), custom_call_target="tpu_custom_call", output_to_operand_aliasing={{0}: (8, {})} | custom-call | tf_op jit(solution)/shard_map/pallas_call | solution.py:444
  556.1 46.9 %shard_map.248 = (bf16[12800,3200]{1,0:T(8,128)(2,1)}, bf16[2,2,6,192,512]{4,3,2,1,0:T(8,128)(2,1)}, bf16[2,2,6,192,512]{4,3,2,1,0:T(8,128)(2,1)}) custom-call(s32[10]{0:T(128)} %negate_maximum_fusion.blocks_ref, s32[3]{0:T(128)} %pad_add_fusion.1.misc_ref, bf16[10240,1536]{1,0:T(8,128)(2,1)} %get-tuple-element.102.x_ref, ...), custom_call_target="tpu_custom_call", output_to_operand_aliasing={{0}: (8, {})} | custom-call | tf_op jit(solution)/shard_map/pallas_call | solution.py:444
  619.0 19.7 %shard_map.249 = (bf16[1024,1536]{1,0:T(8,128)(2,1)}, bf16[1024,1536]{1,0:T(8,128)(2,1)}, f32[1024,128]{1,0:T(8,128)}) custom-call(s32[16,96]{1,0:T(8,128)} %copy-done.61, s32[16,96]{1,0:T(8,128)} %get-tuple-element.265.piece_ref, s32[16,96]{1,0:T(8,128)} %get-tuple-element.264.source_ref, s32[16]{0:T(128)} %get-tuple-element.233.groups_ref, ...), custom_call_target="tpu_custom_call" | custom-call | tf_op jit(solution)/shard_map/pallas_call | solution.py:551
  653.2 19.5 %shard_map.250 = (bf16[1024,1536]{1,0:T(8,128)(2,1)}, bf16[1024,1536]{1,0:T(8,128)(2,1)}, f32[1024,128]{1,0:T(8,128)}) custom-call(s32[16,96]{1,0:T(8,128)} %copy-done.61, s32[16,96]{1,0:T(8,128)} %get-tuple-element.265.piece_ref, s32[16,96]{1,0:T(8,128)} %get-tuple-element.264.source_ref, s32[16]{0:T(128)} %get-tuple-element.233.groups_ref, ...), custom_call_target="tpu_custom_call" | custom-call | tf_op jit(solution)/shard_map/pallas_call | solution.py:551
  690.1 17.8 %shard_map.251 = (bf16[1024,1536]{1,0:T(8,128)(2,1)}, bf16[1024,1536]{1,0:T(8,128)(2,1)}, f32[1024,128]{1,0:T(8,128)}) custom-call(s32[16,96]{1,0:T(8,128)} %copy-done.61, s32[16,96]{1,0:T(8,128)} %get-tuple-element.265.piece_ref, s32[16,96]{1,0:T(8,128)} %get-tuple-element.264.source_ref, s32[16]{0:T(128)} %get-tuple-element.233.groups_ref, ...), custom_call_target="tpu_custom_call" | custom-call | tf_op jit(solution)/shard_map/pallas_call | solution.py:551
  714.8 18.3 %shard_map.252 = (bf16[1024,1536]{1,0:T(8,128)(2,1)}, bf16[1024,1536]{1,0:T(8,128)(2,1)}, f32[1024,128]{1,0:T(8,128)}) custom-call(s32[16,96]{1,0:T(8,128)} %copy-done.61, s32[16,96]{1,0:T(8,128)} %get-tuple-element.265.piece_ref, s32[16,96]{1,0:T(8,128)} %get-tuple-element.264.source_ref, s32[16]{0:T(128)} %get-tuple-element.233.groups_ref, ...), custom_call_target="tpu_custom_call" | custom-call | tf_op jit(solution)/shard_map/pallas_call | solution.py:551
  790.1 25.0 %collective-permute-done.38 = bf16[2,2,6,192,512]{4,3,2,1,0:T(8,128)(2,1)} collective-permute-done((bf16[2,2,6,192,512]{4,3,2,1,0:T(8,128)(2,1)}, bf16[2,2,6,192,512]{4,3,2,1,0:T(8,128)(2,1)}, u32[]{:S(2)}, u32[]{:S(2)}) %collective-permute-start.38) | collective-permute-done | bytes 4718624 | tf_op jit(solution)/shard_map/ppermute | solution.py:576
  825.3 40.0 %shard_map.253 = (bf16[1024,768]{1,0:T(8,128)(2,1)}, bf16[1024,256]{1,0:T(8,128)(2,1)}, bf16[1024,256]{1,0:T(8,128)(2,1)}) custom-call(bf16[1024,768]{1,0:T(8,128)(2,1)} %get-tuple-element.92.query_ref, bf16[1024,256]{1,0:T(8,128)(2,1)} %get-tuple-element.93.key_ref, bf16[1024,256]{1,0:T(8,128)(2,1)} %get-tuple-element.94.value_ref, ...), custom_call_target="tpu_custom_call" | custom-call | tf_op jit(solution)/shard_map/pallas_call | solution.py:879
  867.1 13.4 %collective-permute-start.46 = (bf16[2,6,192,512]{3,2,1,0:T(8,128)(2,1)}, bf16[2,6,192,512]{3,2,1,0:T(8,128)(2,1)}, u32[]{:S(2)}, u32[]{:S(2)}) collective-permute-start(bf16[2,6,192,512]{3,2,1,0:T(8,128)(2,1)} %get-tuple-element.239.rest_0_), channel_id=1, source_target_pairs={{0,8},{2,10},{4,12},{6,14},{8,0},{10,2},{12,4},{14,6},{16,24},{18,... | collective-permute-start | bytes 7077896 | tf_op jit(solution)/shard_map/ppermute | solution.py:576
  939.2 21.0 %shard_map.254 = (bf16[1024,384]{1,0:T(8,128)(2,1)}, bf16[1024,128]{1,0:T(8,128)(2,1)}, bf16[1024,128]{1,0:T(8,128)(2,1)}) custom-call(bf16[1024,768]{1,0:T(8,128)(2,1)} %get-tuple-element.88.query_ref, bf16[1024,256]{1,0:T(8,128)(2,1)} %get-tuple-element.89.key_ref, bf16[1024,256]{1,0:T(8,128)(2,1)} %get-tuple-element.90.value_ref, ...), custom_call_target="tpu_custom_call" | custom-call | tf_op jit(solution)/shard_map/pallas_call | solution.py:879
  965.3 21.4 %shard_map.255 = (bf16[1024,384]{1,0:T(8,128)(2,1)}, bf16[1024,128]{1,0:T(8,128)(2,1)}, bf16[1024,128]{1,0:T(8,128)(2,1)}) custom-call(bf16[1024,768]{1,0:T(8,128)(2,1)} %get-tuple-element.88.query_ref, bf16[1024,256]{1,0:T(8,128)(2,1)} %get-tuple-element.89.key_ref, bf16[1024,256]{1,0:T(8,128)(2,1)} %get-tuple-element.90.value_ref, ...), custom_call_target="tpu_custom_call" | custom-call | tf_op jit(solution)/shard_map/pallas_call | solution.py:879
  1016.3 17.0 %collective-permute-done.48 = bf16[8,96,768]{2,1,0:T(8,128)(2,1)} collective-permute-done((bf16[8,96,768]{2,1,0:T(8,128)(2,1)}, bf16[8,96,768]{2,1,0:T(8,128)(2,1)}, u32[]{:S(2)}, u32[]{:S(2)}) %collective-permute-start.48) | collective-permute-done | bytes 1179680 | tf_op jit(solution)/shard_map/ppermute | solution.py:580
  1053.3 9.8 fusion.8
  1063.1 55.2 %collective-permute-done.57 = bf16[6,192,512]{2,1,0:T(8,128)(2,1)} collective-permute-done((bf16[6,192,512]{2,1,0:T(8,128)(2,1)}, bf16[6,192,512]{2,1,0:T(8,128)(2,1)}, u32[]{:S(2)}, u32[]{:S(2)}) %collective-permute-start.57) | collective-permute-done | bytes 1179680 | tf_op jit(solution)/shard_map/ppermute | solution.py:576
  1118.3 50.4 %collective-permute-done.60 = bf16[6,192,512]{2,1,0:T(8,128)(2,1)S(1)} collective-permute-done((bf16[6,192,512]{2,1,0:T(8,128)(2,1)S(1)}, bf16[6,192,512]{2,1,0:T(8,128)(2,1)S(1)}, u32[]{:S(2)}, u32[]{:S(2)}) %collective-permute-start.60) | collective-permute-done | bytes 1179680 | tf_op jit(solution)/shard_map/ppermute | solution.py:576
  1233.3 15.5 %collective-permute-done.56 = bf16[96,2048]{1,0:T(8,128)(2,1)S(1)} collective-permute-done((bf16[96,2048]{1,0:T(8,128)(2,1)S(1)}, bf16[96,2048]{1,0:T(8,128)(2,1)S(1)}, u32[]{:S(2)}, u32[]{:S(2)}) %collective-permute-start.56) | collective-permute-done | bytes 393248 | tf_op jit(solution)/shard_map/ppermute | solution.py:576
  (567 shorter events, 472.9 us)
Async XLA Ops:
  47.9 86.7 %collective-permute-start.16 = (bf16[1024,1536]{1,0:T(8,128)(2,1)}, bf16[1024,1536]{1,0:T(8,128)(2,1)}, u32[]{:S(2)}, u32[]{:S(2)}) collective-permute-start(bf16[1024,1536]{1,0:T(8,128)(2,1)} %rest_0_), channel_id=1, source_target_pairs={{0,1},{1,0},{2,3},{3,2},{4,5},{5,4},{6,7},{7,6},{8,9},{9,8},{10,11... | collective-permute-start | bytes 9437192 | tf_op jit(solution)/shard_map/ppermute | solution.py:580
  85.1 64.6 %collective-permute-start.17 = (bf16[1024,1536]{1,0:T(8,128)(2,1)}, bf16[1024,1536]{1,0:T(8,128)(2,1)}, u32[]{:S(2)}, u32[]{:S(2)}) collective-permute-start(bf16[1024,1536]{1,0:T(8,128)(2,1)} %rest_0_), channel_id=1, source_target_pairs={{0,2},{2,0},{4,6},{6,4},{8,10},{10,8},{12,14},{14,12},{16,18},{18,... | collective-permute-start | bytes 9437192 | tf_op jit(solution)/shard_map/ppermute | solution.py:576
  137.8 91.8 %collective-permute-start.15 = (bf16[1024,1536]{1,0:T(8,128)(2,1)}, bf16[1024,1536]{1,0:T(8,128)(2,1)}, u32[]{:S(2)}, u32[]{:S(2)}) collective-permute-start(bf16[1024,1536]{1,0:T(8,128)(2,1)} %multiply_convert_fusion.rest_1_), channel_id=1, source_target_pairs={{0,1},{1,0},{2,3},{3,2},{4,5},{5,4},{6,7},{7,6},{8,9},{9,8},{10,11... | collective-permute-start | bytes 9437192 | tf_op jit(solution)/shard_map/ppermute | solution.py:580
  149.7 97.1 %collective-permute-start.20 = (bf16[1024,1536]{1,0:T(8,128)(2,1)}, bf16[1024,1536]{1,0:T(8,128)(2,1)}, u32[]{:S(2)}, u32[]{:S(2)}) collective-permute-start(bf16[1024,1536]{1,0:T(8,128)(2,1)} %multiply_convert_fusion.rest_1_), channel_id=1, source_target_pairs={{0,2},{2,0},{4,6},{6,4},{8,10},{10,8},{12,14},{14,12},{16,18},{18,... | collective-permute-start | bytes 9437192 | tf_op jit(solution)/shard_map/ppermute | solution.py:576
  307.3 116.3 %collective-permute-start.23 = (bf16[2,2,6,192,512]{4,3,2,1,0:T(8,128)(2,1)}, bf16[2,2,6,192,512]{4,3,2,1,0:T(8,128)(2,1)}, u32[]{:S(2)}, u32[]{:S(2)}) collective-permute-start(bf16[2,2,6,192,512]{4,3,2,1,0:T(8,128)(2,1)} %get-tuple-element.106), channel_id=1, source_target_pairs={{0,4},{2,6},{4,0},{6,2},{8,12},{10,14},{12,8},{14,10},{16,20},{18,... | collective-permute-start | bytes 14155784 | tf_op jit(solution)/shard_map/ppermute | solution.py:576
  423.6 108.6 %collective-permute-start.25 = (bf16[2,2,6,192,512]{4,3,2,1,0:T(8,128)(2,1)}, bf16[2,2,6,192,512]{4,3,2,1,0:T(8,128)(2,1)}, u32[]{:S(2)}, u32[]{:S(2)}) collective-permute-start(bf16[2,2,6,192,512]{4,3,2,1,0:T(8,128)(2,1)} %get-tuple-element.112), channel_id=1, source_target_pairs={{0,4},{2,6},{4,0},{6,2},{8,12},{10,14},{12,8},{14,10},{16,20},{18,... | collective-permute-start | bytes 14155784 | tf_op jit(solution)/shard_map/ppermute | solution.py:576
  540.0 76.4 %collective-permute-start.26 = (bf16[2,6,192,512]{3,2,1,0:T(8,128)(2,1)}, bf16[2,6,192,512]{3,2,1,0:T(8,128)(2,1)}, u32[]{:S(2)}, u32[]{:S(2)}) collective-permute-start(bf16[2,6,192,512]{3,2,1,0:T(8,128)(2,1)} %get-tuple-element.243.rest_1_), channel_id=1, source_target_pairs={{0,8},{2,10},{4,12},{6,14},{8,0},{10,2},{12,4},{14,6},{16,24},{18,... | collective-permute-start | bytes 7077896 | tf_op jit(solution)/shard_map/ppermute | solution.py:576
  540.0 132.7 %collective-permute-start.29 = (bf16[2,2,6,192,512]{4,3,2,1,0:T(8,128)(2,1)}, bf16[2,2,6,192,512]{4,3,2,1,0:T(8,128)(2,1)}, u32[]{:S(2)}, u32[]{:S(2)}) collective-permute-start(bf16[2,2,6,192,512]{4,3,2,1,0:T(8,128)(2,1)} %get-tuple-element.121), channel_id=1, source_target_pairs={{0,4},{2,6},{4,0},{6,2},{8,12},{10,14},{12,8},{14,10},{16,20},{18,... | collective-permute-start | bytes 14155784 | tf_op jit(solution)/shard_map/ppermute | solution.py:576
  547.2 64.9 %collective-permute-start.27 = (bf16[6,192,512]{2,1,0:T(8,128)(2,1)S(1)}, bf16[6,192,512]{2,1,0:T(8,128)(2,1)}, u32[]{:S(2)}, u32[]{:S(2)}) collective-permute-start(bf16[6,192,512]{2,1,0:T(8,128)(2,1)S(1)} %copy-done.21), channel_id=1, source_target_pairs={{0,16},{2,18},{4,20},{6,22},{8,24},{10,26},{12,28},{14,30},{16,0},... | collective-permute-start | bytes 3538952 | tf_op jit(solution)/shard_map/ppermute | solution.py:576
  644.8 96.9 %collective-permute-start.31 = (bf16[1024,1536]{1,0:T(8,128)(2,1)}, bf16[1024,1536]{1,0:T(8,128)(2,1)}, u32[]{:S(2)}, u32[]{:S(2)}) collective-permute-start(bf16[1024,1536]{1,0:T(8,128)(2,1)} %get-tuple-element.117.rest_0_), channel_id=1, source_target_pairs={{0,2},{2,0},{4,6},{6,4},{8,10},{10,8},{12,14},{14,12},{16,18},{18,... | collective-permute-start | bytes 9437192 | tf_op jit(solution)/shard_map/ppermute | solution.py:576
  685.0 82.5 %collective-permute-start.34 = (bf16[1024,1536]{1,0:T(8,128)(2,1)}, bf16[1024,1536]{1,0:T(8,128)(2,1)}, u32[]{:S(2)}, u32[]{:S(2)}) collective-permute-start(bf16[1024,1536]{1,0:T(8,128)(2,1)} %add_convert_fusion.2.rest_0_), channel_id=1, source_target_pairs={{0,1},{1,0},{2,3},{3,2},{4,5},{5,4},{6,7},{7,6},{8,9},{9,8},{10,11... | collective-permute-start | bytes 9437192 | tf_op jit(solution)/shard_map/ppermute | solution.py:580
  707.9 66.7 %collective-permute-start.33 = (bf16[1024,1536]{1,0:T(8,128)(2,1)}, bf16[1024,1536]{1,0:T(8,128)(2,1)}, u32[]{:S(2)}, u32[]{:S(2)}) collective-permute-start(bf16[1024,1536]{1,0:T(8,128)(2,1)} %get-tuple-element.128), channel_id=1, source_target_pairs={{0,2},{2,0},{4,6},{6,4},{8,10},{10,8},{12,14},{14,12},{16,18},{18,... | collective-permute-start | bytes 9437192 | tf_op jit(solution)/shard_map/ppermute | solution.py:576
  710.1 105.0 %collective-permute-start.38 = (bf16[2,2,6,192,512]{4,3,2,1,0:T(8,128)(2,1)}, bf16[2,2,6,192,512]{4,3,2,1,0:T(8,128)(2,1)}, u32[]{:S(2)}, u32[]{:S(2)}) collective-permute-start(bf16[2,2,6,192,512]{4,3,2,1,0:T(8,128)(2,1)} %get-tuple-element.135), channel_id=1, source_target_pairs={{0,4},{2,6},{4,0},{6,2},{8,12},{10,14},{12,8},{14,10},{16,20},{18,... | collective-permute-start | bytes 14155784 | tf_op jit(solution)/shard_map/ppermute | solution.py:576
  748.7 172.0 %collective-permute-start.40 = (bf16[2,2,6,192,512]{4,3,2,1,0:T(8,128)(2,1)}, bf16[2,2,6,192,512]{4,3,2,1,0:T(8,128)(2,1)}, u32[]{:S(2)}, u32[]{:S(2)}) collective-permute-start(bf16[2,2,6,192,512]{4,3,2,1,0:T(8,128)(2,1)} %get-tuple-element.145), channel_id=1, source_target_pairs={{0,4},{2,6},{4,0},{6,2},{8,12},{10,14},{12,8},{14,10},{16,20},{18,... | collective-permute-start | bytes 14155784 | tf_op jit(solution)/shard_map/ppermute | solution.py:576
  758.5 162.2 %collective-permute-start.42 = (bf16[6,192,512]{2,1,0:T(8,128)(2,1)}, bf16[6,192,512]{2,1,0:T(8,128)(2,1)}, u32[]{:S(2)}, u32[]{:S(2)}) collective-permute-start(bf16[6,192,512]{2,1,0:T(8,128)(2,1)} %fusion.41.rest_0_), channel_id=1, source_target_pairs={{0,16},{2,18},{4,20},{6,22},{8,24},{10,26},{12,28},{14,30},{16,0},... | collective-permute-start | bytes 3538952 | tf_op jit(solution)/shard_map/ppermute | solution.py:576
  767.5 99.6 %collective-permute-start.39 = (bf16[2,6,192,512]{3,2,1,0:T(8,128)(2,1)}, bf16[2,6,192,512]{3,2,1,0:T(8,128)(2,1)}, u32[]{:S(2)}, u32[]{:S(2)}) collective-permute-start(bf16[2,6,192,512]{3,2,1,0:T(8,128)(2,1)} %get-tuple-element.241.rest_1_), channel_id=1, source_target_pairs={{0,8},{2,10},{4,12},{6,14},{8,0},{10,2},{12,4},{14,6},{16,24},{18,... | collective-permute-start | bytes 7077896 | tf_op jit(solution)/shard_map/ppermute | solution.py:576
  774.6 108.6 %collective-permute-start.32 = (bf16[1024,1536]{1,0:T(8,128)(2,1)}, bf16[1024,1536]{1,0:T(8,128)(2,1)}, u32[]{:S(2)}, u32[]{:S(2)}) collective-permute-start(bf16[1024,1536]{1,0:T(8,128)(2,1)} %add_convert_fusion.1), channel_id=1, source_target_pairs={{0,1},{1,0},{2,3},{3,2},{4,5},{5,4},{6,7},{7,6},{8,9},{9,8},{10,11... | collective-permute-start | bytes 9437192 | tf_op jit(solution)/shard_map/ppermute | solution.py:580
  815.1 82.9 %collective-permute-start.30 = (bf16[1024,1536]{1,0:T(8,128)(2,1)}, bf16[1024,1536]{1,0:T(8,128)(2,1)}, u32[]{:S(2)}, u32[]{:S(2)}) collective-permute-start(bf16[1024,1536]{1,0:T(8,128)(2,1)} %get-tuple-element.123.rest_0_), channel_id=1, source_target_pairs={{0,2},{2,0},{4,6},{6,4},{8,10},{10,8},{12,14},{14,12},{16,18},{18,... | collective-permute-start | bytes 9437192 | tf_op jit(solution)/shard_map/ppermute | solution.py:576
  867.1 95.2 %collective-permute-start.46 = (bf16[2,6,192,512]{3,2,1,0:T(8,128)(2,1)}, bf16[2,6,192,512]{3,2,1,0:T(8,128)(2,1)}, u32[]{:S(2)}, u32[]{:S(2)}) collective-permute-start(bf16[2,6,192,512]{3,2,1,0:T(8,128)(2,1)} %get-tuple-element.239.rest_0_), channel_id=1, source_target_pairs={{0,8},{2,10},{4,12},{6,14},{8,0},{10,2},{12,4},{14,6},{16,24},{18,... | collective-permute-start | bytes 7077896 | tf_op jit(solution)/shard_map/ppermute | solution.py:576
  927.0 107.9 %collective-permute-start.59 = (bf16[2,6,192,512]{3,2,1,0:T(8,128)(2,1)}, bf16[2,6,192,512]{3,2,1,0:T(8,128)(2,1)}, u32[]{:S(2)}, u32[]{:S(2)}) collective-permute-start(bf16[2,6,192,512]{3,2,1,0:T(8,128)(2,1)} %get-tuple-element.237.rest_0_), channel_id=1, source_target_pairs={{0,8},{2,10},{4,12},{6,14},{8,0},{10,2},{12,4},{14,6},{16,24},{18,... | collective-permute-start | bytes 7077896 | tf_op jit(solution)/shard_map/ppermute | solution.py:576
  1013.4 104.9 %collective-permute-start.57 = (bf16[6,192,512]{2,1,0:T(8,128)(2,1)}, bf16[6,192,512]{2,1,0:T(8,128)(2,1)}, u32[]{:S(2)}, u32[]{:S(2)}) collective-permute-start(bf16[6,192,512]{2,1,0:T(8,128)(2,1)} %fusion.43), channel_id=1, source_target_pairs={{0,16},{2,18},{4,20},{6,22},{8,24},{10,26},{12,28},{14,30},{16,0},... | collective-permute-start | bytes 3538952 | tf_op jit(solution)/shard_map/ppermute | solution.py:576
  1013.4 155.3 %collective-permute-start.58 = (bf16[6,192,512]{2,1,0:T(8,128)(2,1)}, bf16[6,192,512]{2,1,0:T(8,128)(2,1)}, u32[]{:S(2)}, u32[]{:S(2)}) collective-permute-start(bf16[6,192,512]{2,1,0:T(8,128)(2,1)} %fusion.45.rest_2_), channel_id=1, source_target_pairs={{0,16},{2,18},{4,20},{6,22},{8,24},{10,26},{12,28},{14,30},{16,0},... | collective-permute-start | bytes 3538952 | tf_op jit(solution)/shard_map/ppermute | solution.py:576
  1036.6 132.2 %collective-permute-start.60 = (bf16[6,192,512]{2,1,0:T(8,128)(2,1)S(1)}, bf16[6,192,512]{2,1,0:T(8,128)(2,1)S(1)}, u32[]{:S(2)}, u32[]{:S(2)}) collective-permute-start(bf16[6,192,512]{2,1,0:T(8,128)(2,1)S(1)} %fusion.52), channel_id=1, source_target_pairs={{0,16},{2,18},{4,20},{6,22},{8,24},{10,26},{12,28},{14,30},{16,0},... | collective-permute-start | bytes 3538952 | tf_op jit(solution)/shard_map/ppermute | solution.py:576
  1051.5 148.6 %collective-permute-start.54 = (bf16[4,96,2048]{2,1,0:T(8,128)(2,1)}, bf16[4,96,2048]{2,1,0:T(8,128)(2,1)}, u32[]{:S(2)}, u32[]{:S(2)}) collective-permute-start(bf16[4,96,2048]{2,1,0:T(8,128)(2,1)} %dynamic-slice_bitcast_fusion), channel_id=1, source_target_pairs={{0,4},{2,6},{4,0},{6,2},{8,12},{10,14},{12,8},{14,10},{16,20},{18,... | collective-permute-start | bytes 4718600 | tf_op jit(solution)/shard_map/ppermute | solution.py:576
  (160 other events, 2621.9 us)
